TPU v7x, 32 devices: a whole 2x2x4 slice. The times are simulated.
32 devices in a mesh: rep: 4 (over x, core), ep: 8 (over z, y).
Axes of the slice: x: 2, y: 2, z: 4, core: 2. Of those that a mesh axis runs over, the one named last changes fastest.
Arguments:
- tokens: bfloat16 [63040, 512], P(('rep', 'ep')), may hold values from -6 to 6
- cotangent: bfloat16 [63040, 512], P(('rep', 'ep')), may hold values from -6 to 6
- expert_ids: int32 [63040, 2], P(('rep', 'ep')), may hold values from 0 to 7, all different within a row
- priority: int32 [32, 1970], P(('rep', 'ep')), may hold values from 0 to 1969, each once within a row
- heads_in: float32 [512, 1536], P(('rep', 'ep')), may hold values from -0.25 to 0.25
- heads_in_first: float32 [512, 1536], P(('rep', 'ep')), may hold values from -448 to 448
- heads_in_second: float32 [512, 1536], P(('rep', 'ep')), may hold values from 5673.6 to 22694.4
- heads_out: float32 [512, 512], P(('rep', 'ep')), may hold values from -0.75 to 0.75
- heads_out_first: float32 [512, 512], P(('rep', 'ep')), may hold values from -448 to 448
- heads_out_second: float32 [512, 512], P(('rep', 'ep')), may hold values from 5673.6 to 22694.4
- router: float32 [512, 8], P(('rep', 'ep')), may hold values from -0.1875 to 0.1875
- router_first: float32 [512, 8], P(('rep', 'ep')), may hold values from -8192 to 8192
- router_second: float32 [512, 8], P(('rep', 'ep')), may hold values from 2017280 to 8069120
- scales: float32 [512, 5], P(('rep', 'ep')), may hold values from -0.5 to 1.4
- scales_first: float32 [512, 5], P(('rep', 'ep')), may hold values from -1536 to 1536
- scales_second: float32 [512, 5], P(('rep', 'ep')), may hold values from 63040 to 252160
- expert_in: float32 [8, 512, 2048], P('ep', None, 'rep'), may hold values from -0.25 to 0.25
- expert_in_first: float32 [8, 512, 2048], P('ep', None, 'rep'), may hold values from -224 to 224
- expert_in_second: float32 [8, 512, 2048], P('ep', None, 'rep'), may hold values from 1418.4 to 5673.6
- bias_in: float32 [8, 2048], P('ep', 'rep'), may hold values from -0.625 to 0.625
- bias_in_first: float32 [8, 2048], P('ep', 'rep'), may hold values from -224 to 224
- bias_in_second: float32 [8, 2048], P('ep', 'rep'), may hold values from 1418.4 to 5673.6
- expert_out: float32 [8, 2048, 512], P('ep', 'rep'), may hold values from -0.1875 to 0.1875
- expert_out_first: float32 [8, 2048, 512], P('ep', 'rep'), may hold values from -224 to 224
- expert_out_second: float32 [8, 2048, 512], P('ep', 'rep'), may hold values from 1418.4 to 5673.6
- bias_out: float32 [8, 512], P('ep', 'rep'), may hold values from -0.625 to 0.625
- bias_out_first: float32 [8, 512], P('ep', 'rep'), may hold values from -384 to 384
- bias_out_second: float32 [8, 512], P('ep', 'rep'), may hold values from 3940 to 15760
Outputs:
- output: float32 [63040, 512], P(('rep', 'ep'))
- input_grad: float32 [63040, 512], P(('rep', 'ep'))
- heads_in_first_new: float32 [512, 1536], P(('rep', 'ep'))
- heads_in_second_new: float32 [512, 1536], P(('rep', 'ep'))
- heads_in_new: float32 [512, 1536], P(('rep', 'ep'))
- heads_out_first_new: float32 [512, 512], P(('rep', 'ep'))
- heads_out_second_new: float32 [512, 512], P(('rep', 'ep'))
- heads_out_new: float32 [512, 512], P(('rep', 'ep'))
- router_first_new: float32 [512, 8], P(('rep', 'ep'))
- router_second_new: float32 [512, 8], P(('rep', 'ep'))
- router_new: float32 [512, 8], P(('rep', 'ep'))
- scales_first_new: float32 [512, 5], P(('rep', 'ep'))
- scales_second_new: float32 [512, 5], P(('rep', 'ep'))
- scales_new: float32 [512, 5], P(('rep', 'ep'))
- expert_in_first_new: float32 [8, 512, 2048], P('ep', None, 'rep')
- expert_in_second_new: float32 [8, 512, 2048], P('ep', None, 'rep')
- expert_in_new: float32 [8, 512, 2048], P('ep', None, 'rep')
- bias_in_first_new: float32 [8, 2048], P('ep', 'rep')
- bias_in_second_new: float32 [8, 2048], P('ep', 'rep')
- bias_in_new: float32 [8, 2048], P('ep', 'rep')
- expert_out_first_new: float32 [8, 2048, 512], P('ep', 'rep')
- expert_out_second_new: float32 [8, 2048, 512], P('ep', 'rep')
- expert_out_new: float32 [8, 2048, 512], P('ep', 'rep')
- bias_out_first_new: float32 [8, 512], P('ep', 'rep')
- bias_out_second_new: float32 [8, 512], P('ep', 'rep')
- bias_out_new: float32 [8, 512], P('ep', 'rep')
- norms: float32 [3, 12], replicated
Inputs may be any that keep to these rules, and one draw needn't show every extreme that they name: `expert_ids`: each token names 2 different experts. `priority`: each row is a permutation of its device's 1970 token positions.
All inputs are finite; a program needn't handle non-finite values.
Results may differ from a plain program's by a relative error of at most 0.014.
Values may be sent and summed in bfloat16 or wider, within the bound.
No kernel may reach another device: no remote copies, remote signals or barrier semaphores. Data moves between devices by JAX's collectives and lax.ppermute only.
A program may use at most 256 MiB of HBM per device.

v0:
```python
import jax
import jax.numpy as jnp
from jax import lax
from jax.sharding import PartitionSpec as P

HEADS = 8
HEAD = 64
FF = 2048
SEQ = 197
STEP = 5


BETA = 0.5
RATE = 0.3
DECAY = 0.01
EPSILON = 1e-06


def normalize(rows):
    centred = rows - jnp.mean(rows, axis=-1, keepdims=True)
    inverse = lax.rsqrt(jnp.mean(centred * centred, axis=-1, keepdims=True) + 1e-06)
    return (centred * inverse, inverse)


def norm_back(grad_rows, normed, inverse, gain):
    scaled = grad_rows * gain
    return inverse * (
        scaled
        - jnp.mean(scaled, axis=-1, keepdims=True)
        - normed * jnp.mean(scaled * normed, axis=-1, keepdims=True)
    )


def exact_gelu(values):
    return jax.nn.gelu(values, approximate=False)


def route_places(block_ids, ranking, experts):
    count = block_ids.shape[0]
    keys = jnp.arange(block_ids.shape[1], dtype=jnp.int32)[None, :] * count + ranking[:, None]
    ordered = (
        jnp.zeros((block_ids.size,), jnp.int32).at[keys.reshape(-1)].set(block_ids.reshape(-1))
    )
    hits = (ordered[:, None] == jnp.arange(experts, dtype=jnp.int32)[None, :]).astype(jnp.int32)
    before = jnp.cumsum(hits, axis=0) - hits
    place = jnp.sum(before * hits, axis=1)
    return place[keys]


def attention_scores(query, keyed, factor):
    return jnp.einsum("bqhd,bkhd->bhqk", query, keyed, preferred_element_type=jnp.float32) * factor


def moments(weight, grad, first, second):
    first_new = BETA * first + (1.0 - BETA) * grad
    second_new = BETA * second + (1.0 - BETA) * grad * grad
    step = (
        first_new / (1.0 - BETA**STEP) / (jnp.sqrt(second_new / (1.0 - BETA**STEP)) + EPSILON)
        + DECAY * weight
    )
    return (first_new, second_new, step)


def squares(array, per_column):
    if per_column:
        return jnp.sum(array * array, axis=0)
    return jnp.sum(array * array)[None]


def expert_front(rows, enter_weight, enter_bias):
    pre = jnp.einsum("sjcd,jdf->sjcf", rows, enter_weight, preferred_element_type=jnp.float32)
    return pre + enter_bias.astype(jnp.float32)[None, :, None, :]


def on_device(
    tokens,
    cotangent,
    expert_ids,
    priority,
    heads_in,
    heads_in_first,
    heads_in_second,
    heads_out,
    heads_out_first,
    heads_out_second,
    router,
    router_first,
    router_second,
    scales,
    scales_first,
    scales_second,
    expert_in,
    expert_in_first,
    expert_in_second,
    bias_in,
    bias_in_first,
    bias_in_second,
    expert_out,
    expert_out_first,
    expert_out_second,
    bias_out,
    bias_out_first,
    bias_out_second,
):
    in_matrix, out_matrix, router_matrix, scale_table = (
        lax.all_gather(heads_in.astype(jnp.bfloat16), ("rep", "ep"), axis=0, tiled=True),
        lax.all_gather(heads_out.astype(jnp.bfloat16), ("rep", "ep"), axis=0, tiled=True),
        lax.all_gather(router.astype(jnp.bfloat16), ("rep", "ep"), axis=0, tiled=True),
        lax.all_gather(scales.astype(jnp.bfloat16), ("rep", "ep"), axis=0, tiled=True),
    )
    enter_weight, enter_bias, leave_weight, leave_bias = (
        lax.all_gather(expert_in.astype(jnp.bfloat16), "rep", axis=2, tiled=True),
        lax.all_gather(bias_in.astype(jnp.bfloat16), "rep", axis=1, tiled=True),
        lax.all_gather(expert_out.astype(jnp.bfloat16), "rep", axis=1, tiled=True),
        lax.all_gather(bias_out.astype(jnp.bfloat16), "rep", axis=1, tiled=True),
    )
    gains = scale_table.astype(jnp.float32)
    inputs = tokens.astype(jnp.float32)
    count, width = inputs.shape
    images = count // SEQ
    factor = HEAD ** (-0.5)
    normed_one, inverse_one = normalize(inputs)
    entry = (normed_one * gains[:, 0] + gains[:, 1]).astype(jnp.bfloat16)
    projected = jnp.dot(entry, in_matrix, preferred_element_type=jnp.float32).astype(jnp.bfloat16)
    grid = projected.reshape(images, SEQ, 3, HEADS, HEAD)
    query = grid[:, :, 0]
    keyed = grid[:, :, 1]
    valued = grid[:, :, 2]
    scores = attention_scores(query, keyed, factor)
    peak = jnp.max(scores, axis=-1, keepdims=True)
    log_total = peak + jnp.log(jnp.sum(jnp.exp(scores - peak), axis=-1, keepdims=True))
    weights = jnp.exp(scores - log_total).astype(jnp.bfloat16)
    mixed = jnp.einsum("bhqk,bkhd->bqhd", weights, valued, preferred_element_type=jnp.float32)
    mixed = mixed.reshape(count, width).astype(jnp.bfloat16)
    hidden = inputs + jnp.dot(mixed, out_matrix, preferred_element_type=jnp.float32) + gains[:, 4]
    normed_two, inverse_two = normalize(hidden)
    routed = (normed_two * gains[:, 2] + gains[:, 3]).astype(jnp.bfloat16)
    logits = jnp.dot(routed, router_matrix, preferred_element_type=jnp.float32)
    experts = logits.shape[1]
    top = expert_ids.shape[1]
    choose = (expert_ids[:, :, None] == jnp.arange(experts, dtype=jnp.int32)[None, None, :]).astype(
        jnp.float32
    )
    picked = jnp.sum(choose * logits[:, None, :], axis=2)
    gates = jax.nn.softmax(picked, axis=1)
    places = route_places(expert_ids, priority[0], experts)
    capacity = (5 * top * count + 4 * experts - 1) // (4 * experts)
    groups = lax.axis_size("ep")
    local = experts // groups
    slots = experts * capacity
    slot = jnp.where(places < capacity, expert_ids * capacity + places, slots)
    pair_of_slot = (
        jnp.full((slots,), count * top, jnp.int32)
        .at[slot.reshape(-1)]
        .set(jnp.arange(count * top, dtype=jnp.int32), mode="drop")
    )
    token_of_slot = pair_of_slot // top
    padded_rows = jnp.concatenate([routed, jnp.zeros((1, width), jnp.bfloat16)], axis=0)
    outgoing = padded_rows[token_of_slot].reshape(groups, local, capacity, width)
    arrived = lax.all_to_all(outgoing, "ep", split_axis=0, concat_axis=0, tiled=True)
    pre = expert_front(arrived, enter_weight, enter_bias)
    act, gelu_back = jax.vjp(exact_gelu, pre)
    act_low = act.astype(jnp.bfloat16)
    result = jnp.einsum("sjcf,jfd->sjcd", act_low, leave_weight, preferred_element_type=jnp.float32)
    result = (result + leave_bias.astype(jnp.float32)[None, :, None, :]).astype(jnp.bfloat16)
    returned = lax.all_to_all(result, "ep", split_axis=0, concat_axis=0, tiled=True).reshape(
        slots, width
    )
    padded_back = jnp.concatenate([returned, jnp.zeros((1, width), jnp.bfloat16)], axis=0)
    picked_rows = padded_back[slot].astype(jnp.float32)
    output = hidden + jnp.sum(gates[:, :, None] * picked_rows, axis=1)
    grad_output = cotangent.astype(jnp.float32)
    grad_gates = jnp.sum(picked_rows * grad_output[:, None, :], axis=2)
    gate_list = jnp.concatenate([gates.reshape(-1), jnp.zeros((1,), jnp.float32)])
    padded_grad = jnp.concatenate([grad_output, jnp.zeros((1, width), jnp.float32)], axis=0)
    grad_slots = (padded_grad[token_of_slot] * gate_list[pair_of_slot][:, None]).astype(
        jnp.bfloat16
    )
    grad_arrived = lax.all_to_all(
        grad_slots.reshape(groups, local, capacity, width),
        "ep",
        split_axis=0,
        concat_axis=0,
        tiled=True,
    )
    grad_act = jnp.einsum(
        "sjcd,jfd->sjcf", grad_arrived, leave_weight, preferred_element_type=jnp.float32
    )
    grad_pre = gelu_back(grad_act)[0].astype(jnp.bfloat16)
    grad_leave = jnp.einsum(
        "sjcf,sjcd->jfd", act_low, grad_arrived, preferred_element_type=jnp.float32
    )
    grad_leave_bias = jnp.sum(grad_arrived, axis=(0, 2), dtype=jnp.float32)
    grad_enter = jnp.einsum("sjcd,sjcf->jdf", arrived, grad_pre, preferred_element_type=jnp.float32)
    grad_enter_bias = jnp.sum(grad_pre, axis=(0, 2), dtype=jnp.float32)
    grad_rows = jnp.einsum(
        "sjcf,jdf->sjcd", grad_pre, enter_weight, preferred_element_type=jnp.float32
    ).astype(jnp.bfloat16)
    grad_back = lax.all_to_all(grad_rows, "ep", split_axis=0, concat_axis=0, tiled=True).reshape(
        slots, width
    )
    padded_grad_back = jnp.concatenate([grad_back, jnp.zeros((1, width), jnp.bfloat16)], axis=0)
    grad_routed = jnp.sum(padded_grad_back[slot], axis=1, dtype=jnp.float32)
    grad_picked = gates * (grad_gates - jnp.sum(gates * grad_gates, axis=1, keepdims=True))
    grad_logits = jnp.sum(choose * grad_picked[:, :, None], axis=1).astype(jnp.bfloat16)
    grad_router = jnp.einsum("td,te->de", routed, grad_logits, preferred_element_type=jnp.float32)
    grad_routed = grad_routed + jnp.einsum(
        "te,de->td", grad_logits, router_matrix, preferred_element_type=jnp.float32
    )
    grad_gain_two = jnp.sum(grad_routed * normed_two, axis=0)
    grad_shift_two = jnp.sum(grad_routed, axis=0)
    grad_hidden = grad_output + norm_back(grad_routed, normed_two, inverse_two, gains[:, 2])
    grad_shift_out = jnp.sum(grad_hidden, axis=0)
    grad_mix_out = grad_hidden.astype(jnp.bfloat16)
    grad_out_matrix = jnp.einsum(
        "td,te->de", mixed, grad_mix_out, preferred_element_type=jnp.float32
    )
    grad_mixed = jnp.einsum(
        "te,de->td", grad_mix_out, out_matrix, preferred_element_type=jnp.float32
    )
    grad_mixed = grad_mixed.astype(jnp.bfloat16).reshape(images, SEQ, HEADS, HEAD)
    probs = jnp.exp(attention_scores(query, keyed, factor) - log_total)
    weights_again = probs.astype(jnp.bfloat16)
    grad_valued = jnp.einsum(
        "bhqk,bqhd->bkhd", weights_again, grad_mixed, preferred_element_type=jnp.float32
    )
    grad_probs = jnp.einsum(
        "bqhd,bkhd->bhqk", grad_mixed, valued, preferred_element_type=jnp.float32
    )
    grad_scores = (
        probs * (grad_probs - jnp.sum(probs * grad_probs, axis=-1, keepdims=True))
    ).astype(jnp.bfloat16)
    grad_query = (
        jnp.einsum("bhqk,bkhd->bqhd", grad_scores, keyed, preferred_element_type=jnp.float32)
        * factor
    )
    grad_keyed = (
        jnp.einsum("bhqk,bqhd->bkhd", grad_scores, query, preferred_element_type=jnp.float32)
        * factor
    )
    grad_projected = (
        jnp.stack([grad_query, grad_keyed, grad_valued], axis=2)
        .reshape(count, 3 * width)
        .astype(jnp.bfloat16)
    )
    grad_in_matrix = jnp.einsum(
        "td,te->de", entry, grad_projected, preferred_element_type=jnp.float32
    )
    grad_entry = jnp.einsum(
        "te,de->td", grad_projected, in_matrix, preferred_element_type=jnp.float32
    )
    grad_gain_one = jnp.sum(grad_entry * normed_one, axis=0)
    grad_shift_one = jnp.sum(grad_entry, axis=0)
    input_grad = grad_hidden + norm_back(grad_entry, normed_one, inverse_one, gains[:, 0])
    grad_scales = jnp.stack(
        [grad_gain_one, grad_shift_one, grad_gain_two, grad_shift_two, grad_shift_out], axis=1
    )
    summed_dense = (
        lax.psum_scatter(grad_in_matrix, ("rep", "ep"), scatter_dimension=0, tiled=True),
        lax.psum_scatter(grad_out_matrix, ("rep", "ep"), scatter_dimension=0, tiled=True),
        lax.psum_scatter(grad_router, ("rep", "ep"), scatter_dimension=0, tiled=True),
        lax.psum_scatter(grad_scales, ("rep", "ep"), scatter_dimension=0, tiled=True),
    )
    summed_expert = (
        lax.psum_scatter(
            grad_enter.astype(jnp.bfloat16), "rep", scatter_dimension=2, tiled=True
        ).astype(jnp.float32),
        lax.psum_scatter(
            grad_enter_bias.astype(jnp.bfloat16), "rep", scatter_dimension=1, tiled=True
        ).astype(jnp.float32),
        lax.psum_scatter(
            grad_leave.astype(jnp.bfloat16), "rep", scatter_dimension=1, tiled=True
        ).astype(jnp.float32),
        lax.psum_scatter(
            grad_leave_bias.astype(jnp.bfloat16), "rep", scatter_dimension=1, tiled=True
        ).astype(jnp.float32),
    )
    weights_now = (heads_in, heads_out, router, scales, expert_in, bias_in, expert_out, bias_out)
    grads_now = tuple(summed_dense) + tuple(summed_expert)
    firsts = (
        heads_in_first,
        heads_out_first,
        router_first,
        scales_first,
        expert_in_first,
        bias_in_first,
        expert_out_first,
        bias_out_first,
    )
    seconds = (
        heads_in_second,
        heads_out_second,
        router_second,
        scales_second,
        expert_in_second,
        bias_in_second,
        expert_out_second,
        bias_out_second,
    )
    states = [moments(w, g, f, s) for w, g, f, s in zip(weights_now, grads_now, firsts, seconds)]
    weight_terms = jnp.concatenate([squares(w, index == 3) for index, w in enumerate(weights_now)])
    step_terms = jnp.concatenate(
        [squares(state[2], index == 3) for index, state in enumerate(states)]
    )
    totals = lax.psum(jnp.stack([weight_terms, step_terms]), ("rep", "ep"))
    counts = jnp.array(
        [3 * width * width, width * width, width * experts]
        + [width] * 5
        + [experts * width * FF, experts * FF, experts * FF * width, experts * width],
        jnp.float32,
    )
    weight_rms = jnp.sqrt(totals[0] / counts)
    step_rms = jnp.sqrt(totals[1] / counts)
    trust = weight_rms / step_rms
    bounds = [(0, 1), (1, 2), (2, 3), (3, 8), (8, 9), (9, 10), (10, 11), (11, 12)]
    results = [output, input_grad]
    for weight, state, bound in zip(weights_now, states, bounds):
        results.extend([state[0], state[1], weight - RATE * trust[bound[0] : bound[1]] * state[2]])
    results.append(jnp.stack([weight_rms, step_rms, trust]))
    return tuple(results)


def solution(mesh):
    in_specs = (
        P(("rep", "ep"), None),
        P(("rep", "ep"), None),
        P(("rep", "ep"), None),
        P(("rep", "ep"), None),
        P(("rep", "ep"), None),
        P(("rep", "ep"), None),
        P(("rep", "ep"), None),
        P(("rep", "ep"), None),
        P(("rep", "ep"), None),
        P(("rep", "ep"), None),
        P(("rep", "ep"), None),
        P(("rep", "ep"), None),
        P(("rep", "ep"), None),
        P(("rep", "ep"), None),
        P(("rep", "ep"), None),
        P(("rep", "ep"), None),
        P("ep", None, "rep"),
        P("ep", None, "rep"),
        P("ep", None, "rep"),
        P("ep", "rep"),
        P("ep", "rep"),
        P("ep", "rep"),
        P("ep", "rep", None),
        P("ep", "rep", None),
        P("ep", "rep", None),
        P("ep", "rep"),
        P("ep", "rep"),
        P("ep", "rep"),
    )
    out_specs = (
        P(("rep", "ep"), None),
        P(("rep", "ep"), None),
        P(("rep", "ep"), None),
        P(("rep", "ep"), None),
        P(("rep", "ep"), None),
        P(("rep", "ep"), None),
        P(("rep", "ep"), None),
        P(("rep", "ep"), None),
        P(("rep", "ep"), None),
        P(("rep", "ep"), None),
        P(("rep", "ep"), None),
        P(("rep", "ep"), None),
        P(("rep", "ep"), None),
        P(("rep", "ep"), None),
        P("ep", None, "rep"),
        P("ep", None, "rep"),
        P("ep", None, "rep"),
        P("ep", "rep"),
        P("ep", "rep"),
        P("ep", "rep"),
        P("ep", "rep", None),
        P("ep", "rep", None),
        P("ep", "rep", None),
        P("ep", "rep"),
        P("ep", "rep"),
        P("ep", "rep"),
        P(),
    )
    return jax.shard_map(
        on_device, mesh=mesh, in_specs=in_specs, out_specs=out_specs, check_vma=False
    )
```

profile of v0, /device:TPU:0, one launch (start us, length us, event | category | flops | bytes accessed | tf_op | source)
XLA Modules:
  0.0 1979.4 jit_solution(5428876734154637648)
XLA Ops:
  12.4 70.2 %all-gather = bf16[32,16,5]{1,2,0:T(8,128)(2,1)S(1)} all-gather(bf16[1,16,5]{1,2,0:T(8,128)(2,1)S(1)} %convert_bitcast_fusion.5), channel_id=1, replica_groups=mesh['rep'=4,'ep'=8] {'rep','ep'}, dimensions={0}, use_global_device_ids=true | all-gather | bytes 5280 | tf_op jit(solution)/shard_map/all_gather | solution.py:109
  87.1 19.4 scatter_custom_fusion
  110.2 20.9 %gather_fusion = s32[3940]{0:T(1024)S(1)} fusion(s32[3940]{0:T(1024)S(1)} %fusion.102, s32[4096]{0:T(1024)S(1)} %pad_clamp_fusion.3), kind=kCustom, calls=%fused_computation | custom fusion | bytes 47280 | tf_op jit(solution)/shard_map/gather | solution.py:47
  138.0 19.4 scatter_custom_fusion.1
  158.9 67.4 %all_gather.26 = bf16[512,512]{1,0:T(8,128)(2,1)S(1)} all-gather(bf16[16,512]{1,0:T(8,128)(2,1)S(1)} %copy-done.47), channel_id=1, replica_groups=mesh['rep'=4,'ep'=8] {'rep','ep'}, dimensions={0}, use_global_device_ids=true | all-gather | bytes 540672 | tf_op jit(solution)/shard_map/all_gather | solution.py:107
  226.3 7.2 convolution_convert_fusion
  233.6 15.7 reshape.438
  249.3 8.8 fusion.139
  258.1 6.0 copy.196
  264.0 4.8 copy.197
  268.8 10.8 multiply_reduce_fusion.1
  279.7 10.3 exponential_reduce_fusion
  290.0 5.0 copy.195
  295.0 11.3 convert_bitcast_fusion.2
  306.3 6.0 copy.163
  312.3 6.3 convert_element_type.155
  326.9 15.1 gather_fusion.1
  346.7 163.6 %all-gather.1 = bf16[32,16,8]{1,2,0:T(8,128)(2,1)S(1)} all-gather(bf16[1,16,8]{1,2,0:T(8,128)(2,1)S(1)} %convert_bitcast_fusion.4), channel_id=1, replica_groups=mesh['rep'=4,'ep'=8] {'rep','ep'}, dimensions={0}, use_global_device_ids=true | all-gather | bytes 8448 | tf_op jit(solution)/shard_map/all_gather | solution.py:108
  514.6 18.4 gather_fusion.3
  536.9 25.8 %gather_fusion.4 = f32[4928]{0:T(1024)S(1)} fusion(f32[3941]{0:T(1024)S(1)} %pad_maximum_fusion.1, s32[5120]{0:T(1024)S(1)} %get-tuple-element.113), kind=kCustom, calls=%fused_computation.4 | custom fusion | bytes 59136 | tf_op jit(solution)/shard_map/gather | solution.py:176
  562.8 7.2 multiply_convert_fusion.1
  576.2 5.1 all_gather.29
  581.4 19.8 %all-gather.8.cloned.1.call-done = bf16[1,512,2048]{2,1,0:T(8,128)(2,1)} async-done(((bf16[1,512,512]{2,1,0:T(8,128)(2,1)}), bf16[1,512,2048]{2,1,0:T(8,128)(2,1)}) %all-gather.8.cloned.1.call-update) | async-done | bytes 2097168 | tf_op jit(solution)/shard_map/all_gather | solution.py:112
  601.2 21.0 %fusion.38 = f32[8,616,2048]{2,1,0:T(8,128)} fusion(bf16[8,1,616,512]{3,2,1,0:T(8,128)(2,1)} %all-to-all-done, bf16[1,512,2048]{2,1,0:T(8,128)(2,1)} %all-gather.8.cloned.1.call-done), kind=kOutput, calls=%fused_computation.70 | convolution fusion | flops 10334765056 | bytes 47513600 | tf_op jit(solution)/shard_map/sjcd,jdf->sjcf/dot_general | solution.py:71
  622.2 60.9 %all-to-all-done.2 = bf16[8,1,616,512]{3,2,1,0:T(8,128)(2,1)} async-done(((bf16[8,1,616,512]{3,2,1,0:T(8,128)(2,1)}), bf16[8,1,616,512]{3,2,1,0:T(8,128)(2,1)}, u32[]{:S(2)}, u32[]{:S(2)}) %all-to-all-start.2) | async-done | bytes 5046304 | tf_op jit(solution)/shard_map/all_to_all | solution.py:179
  683.1 107.0 %fusion.68 = bf16[1,2048,512]{2,1,0:T(8,128)(2,1)} fusion(bf16[8,1,616,512]{3,2,1,0:T(8,128)(2,1)} %all-to-all-done.2, f32[8,616,2048]{2,1,0:T(8,128)} %fusion.38, f32[2048]{0:T(1024)S(1)} %bitcast.377), kind=kOutput, calls=%fused_computation.103 | convolution fusion | flops 11001921536 | bytes 47521792 | tf_op jit(solution)/shard_map/sjcf,sjcd->jfd/dot_general | solution.py:190
  794.2 25.5 %reduce-scatter.23.cloned.1.call-done = bf16[1,512,512]{2,1,0:T(8,128)(2,1)} async-done(((bf16[1,2048,512]{2,1,0:T(8,128)(2,1)}), bf16[1,512,512]{2,1,0:T(8,128)(2,1)}) %reduce-scatter.23.cloned.1.call-update) | async-done | bytes 524304 | tf_op jit(solution)/shard_map/reduce_scatter | solution.py:271
  823.4 18.3 reduce-scatter.31.cloned.1.call-done
  843.8 5.0 all_gather.31
  848.9 17.5 all-gather.10.cloned.1.call-done
  866.4 93.2 %fusion.30 = bf16[8,1,616,512]{3,2,1,0:T(8,128)(2,1)} fusion(f32[512]{0:T(512)S(1)} %bitcast.385, bf16[1,2048,512]{2,1,0:T(8,128)(2,1)} %all-gather.10.cloned.1.call-done, f32[8,616,2048]{2,1,0:T(8,128)} %fusion.38, f32[2048]{0:T(1024)S(1)} %bitcast.378), kind=kOutput, calls=%fused_computation.64 | convolution fusion | flops 11005919232 | bytes 47523840 | tf_op jit(solution)/shard_map/sjcf,jfd->sjcd/dot_general | solution.py:164
  959.6 6.0 all-to-all-start.1
  965.6 106.0 %fusion.143 = (bf16[2048]{0:T(1024)(128)(2,1)S(1)}, bf16[8,1,616,2048]{3,2,0,1:T(8,128)(2,1)}) fusion(bf16[1,2048,512]{2,1,0:T(8,128)(2,1)S(1)} %copy-done.80, bf16[8,1,616,512]{3,2,1,0:T(8,128)(2,1)} %all-to-all-done.2, f32[2048]{0:T(1024)S(1)} %bitcast.379, f32[8,616,2048]{2,1,0:T(8,128)} %fusion.38), kind=kOutput, calls=%fused_computation.255 | convolution fusion | flops 11081611264 | bytes 67710976 | tf_op jit(solution)/shard_map/sjcd,jfd->sjcf/dot_general | solution.py:186
  1071.6 16.5 convert_bitcast_fusion
  1088.1 6.1 all-to-all-start.3
  1098.5 17.7 fusion.63
  1116.3 5.0 concatenate.22
  1121.3 15.7 gather_fusion.2
  1137.0 9.8 reshape.569
  1146.7 25.8 %multiply_reduce_fusion.2 = (f32[1970,2]{1,0:T(8,128)S(1)}, f32[1970,512]{1,0:T(8,128)}) fusion(f32[1970,2,512]{2,1,0:T(2,128)} %reshape.569, f32[1970,512]{1,0:T(8,128)} %convert_element_type.168, f32[1970,2]{1,0:T(8,128)S(1)} %copy-done.16), kind=kLoop, calls=%fused_computation.55 | loop fusion | flops 7056540 | bytes 16169760 | tf_op jit(solution)/shard_map/reduce_sum | solution.py:173
  1173.0 32.6 %all-to-all-done.3 = bf16[8,1,616,512]{3,2,1,0:T(8,128)(2,1)} async-done(((bf16[8,1,616,512]{3,2,1,0:T(8,128)(2,1)}), bf16[8,1,616,512]{3,2,1,0:T(8,128)(2,1)}, u32[]{:S(2)}, u32[]{:S(2)}) %all-to-all-start.3) | async-done | bytes 5046304 | tf_op jit(solution)/shard_map/all_to_all | solution.py:199
  1205.6 5.0 concatenate.25
  1210.6 15.6 gather_fusion.5
  1226.3 9.6 reshape.570
  1235.9 40.9 %reduce_sum.388 = f32[1970,512]{1,0:T(8,128)} reduce(f32[1970,2,512]{2,1,0:T(2,128)} %reshape.570, f32[]{:T(128)} %constant.53.clone.1), dimensions={1}, to_apply=%region_15.16 | reduce | flops 1008640 | bytes 12103684 | tf_op jit(solution)/shard_map/reduce_sum | solution.py:203
  1276.9 5.1 multiply_reduce_fusion.4
  1282.0 6.4 fusion.135
  1292.9 6.0 reshape.452
  1298.9 6.0 copy.177
  1304.9 11.8 multiply_reduce_fusion
  1316.7 12.3 multiply_convert_fusion
  1336.5 11.2 convert_bitcast_fusion.1
  1347.7 6.7 pad_maximum_fusion
  1354.4 15.3 copy.182
  1369.7 16.5 convert_element_type.180
  1386.3 9.5 fusion.52
  1399.9 5.0 fusion.98
  1405.1 8.3 fusion.125
  1420.4 108.0 %reduce-scatter.27.cloned.1.call-done = f32[16,5]{1,0:T(8,128)} async-done(((f32[512,5]{1,0:T(8,128)}), f32[16,5]{1,0:T(8,128)}) %reduce-scatter.27.cloned.1.call-update) | async-done | bytes 336
  1529.3 131.5 %reduce-scatter.25.cloned.1.call-done = f32[16,8]{1,0:T(8,128)} async-done(((f32[512,8]{1,0:T(8,128)}), f32[16,8]{1,0:T(8,128)}) %reduce-scatter.25.cloned.1.call-update) | async-done | bytes 528
  1662.2 132.4 %reduce-scatter.19.cloned.1.call-done = f32[16,512]{1,0:T(8,128)} async-done(((f32[512,512]{1,0:T(8,128)}), f32[16,512]{1,0:T(8,128)}) %reduce-scatter.19.cloned.1.call-update) | async-done | bytes 32784 | tf_op jit(solution)/shard_map/reduce_scatter | solution.py:260
  1796.1 102.8 %reduce-scatter.17.cloned.1.call-done = f32[16,1536]{1,0:T(8,128)} async-done(((f32[512,1536]{1,0:T(8,128)}), f32[16,1536]{1,0:T(8,128)}) %reduce-scatter.17.cloned.1.call-update) | async-done | bytes 98320 | tf_op jit(solution)/shard_map/reduce_scatter | solution.py:259
  1909.7 5.5 fusion.51
  1915.1 39.9 %psum.7 = f32[2,12]{1,0:T(2,128)S(1)} all-reduce(f32[2,12]{1,0:T(2,128)S(1)} %pad_maximum_fusion.3), channel_id=1, replica_groups=mesh['rep'=4,'ep'=8] {'rep','ep'}, use_global_device_ids=true, to_apply=%region_55.56 | all-reduce | flops 24 | bytes 192 | tf_op jit(solution)/shard_map/psum | solution.py:305
  (300 shorter events, 112.4 us)
Async XLA Ops:
  8.0 218.3 %all-gather.6.cloned.1.call-start = ((), (), s32[]{:S(2)}) async-start(), calls=%async_computation.12 | async-start | bytes 1622016 | tf_op jit(solution)/shard_map/all_gather | solution.py:106
  110.1 47.3 %copy-start.7 = (bf16[1970,512]{1,0:T(8,128)(2,1)S(1)}, bf16[1970,512]{1,0:T(8,128)(2,1)}, u32[]{:S(2)}) copy-start(bf16[1970,512]{1,0:T(8,128)(2,1)} %param.29) | copy-start | bytes 6051844
  110.1 48.7 %copy-start.48 = (f32[512,5]{0,1:T(8,128)S(1)}, f32[512,5]{0,1:T(8,128)}, u32[]{:S(2)}) copy-start(f32[512,5]{0,1:T(8,128)} %reshape.575) | copy-start | bytes 30724
  110.1 48.7 %copy-start.47 = (bf16[16,512]{1,0:T(8,128)(2,1)S(1)}, bf16[16,512]{1,0:T(8,128)(2,1)}, u32[]{:S(2)}) copy-start(bf16[16,512]{1,0:T(8,128)(2,1)} %convert_element_type.156) | copy-start | bytes 49156
  157.8 91.5 %copy-start.43 = (f32[1970]{0:T(1024)}, f32[1970]{0:T(1024)S(1)}, u32[]{:S(2)}) copy-start(f32[1970]{0:T(1024)S(1)} %broadcast_multiply_fusion.6) | copy-start | bytes 23644
  158.8 90.4 %copy-start.52 = (f32[1970]{0:T(1024)}, f32[1970]{0:T(1024)S(1)}, u32[]{:S(2)}) copy-start(f32[1970]{0:T(1024)S(1)} %add_rsqrt_fusion.1) | copy-start | bytes 23644
  158.9 90.4 %copy-start.64 = (f32[512,1]{0,1:T(1,128)}, f32[512,1]{0,1:T(1,128)S(1)}, u32[]{:S(2)}) copy-start(f32[512,1]{0,1:T(1,128)S(1)} %get-tuple-element.84) | copy-start | bytes 6148
  158.9 90.4 %copy-start.70 = (f32[512,1]{0,1:T(1,128)}, f32[512,1]{0,1:T(1,128)S(1)}, u32[]{:S(2)}) copy-start(f32[512,1]{0,1:T(1,128)S(1)} %get-tuple-element.83) | copy-start | bytes 6148
  158.9 164.2 %copy-start.56 = (f32[512,1]{0,1:T(1,128)}, f32[512,1]{0,1:T(1,128)S(1)}, u32[]{:S(2)}) copy-start(f32[512,1]{0,1:T(1,128)S(1)} %get-tuple-element.80) | copy-start | bytes 6148
  226.3 92.3 %copy-start.19 = (bf16[512,512]{1,0:T(8,128)(2,1)}, bf16[512,512]{1,0:T(8,128)(2,1)S(1)}, u32[]{:S(2)}) copy-start(bf16[512,512]{1,0:T(8,128)(2,1)S(1)} %all_gather.26) | copy-start | bytes 1572868
  342.0 227.9 %all-to-all-start = ((bf16[8,1,616,512]{3,2,1,0:T(8,128)(2,1)}), bf16[8,1,616,512]{3,2,1,0:T(8,128)(2,1)}, u32[]{:S(2)}, u32[]{:S(2)}) async-start(bf16[8,1,616,512]{3,2,1,0:T(8,128)(2,1)} %bitcast.361), calls=%async_computation | async-start | bytes 10092544 | tf_op jit(solution)/shard_map/all_to_all | solution.py:160
  569.9 113.1 %all-to-all-start.2 = ((bf16[8,1,616,512]{3,2,1,0:T(8,128)(2,1)}), bf16[8,1,616,512]{3,2,1,0:T(8,128)(2,1)}, u32[]{:S(2)}, u32[]{:S(2)}) async-start(bf16[8,1,616,512]{3,2,1,0:T(8,128)(2,1)} %multiply_convert_fusion.1), calls=%async_computation.2 | async-start | bytes 10092544 | tf_op jit(solution)/shard_map/all_to_all | solution.py:179
  574.6 26.6 %all-gather.8.cloned.1.call-start = ((), (), s32[]{:S(2)}) async-start(), calls=%async_computation.13 | async-start | bytes 2621440 | tf_op jit(solution)/shard_map/all_gather | solution.py:112
  575.5 244.2 %reduce-scatter.23.cloned.1.call-start = ((), (), s32[]{:S(2)}) async-start(), calls=%async_computation.18 | async-start | bytes 2621440 | tf_op jit(solution)/shard_map/reduce_scatter | solution.py:271
  683.1 136.6 %copy-start.17 = (f32[1,512,512]{2,1,0:T(8,128)S(1)}, f32[1,512,512]{2,1,0:T(8,128)}, u32[]{:S(2)}) copy-start(f32[1,512,512]{2,1,0:T(8,128)} %param.51) | copy-start | bytes 3145732
  683.1 136.6 %copy-start.23 = (f32[1,512,512]{2,1,0:T(8,128)S(1)}, f32[1,512,512]{2,1,0:T(8,128)}, u32[]{:S(2)}) copy-start(f32[1,512,512]{2,1,0:T(8,128)} %param.52) | copy-start | bytes 3145732
  683.1 136.6 %copy-start.24 = (f32[1,512,512]{2,1,0:T(8,128)S(1)}, f32[1,512,512]{2,1,0:T(8,128)}, u32[]{:S(2)}) copy-start(f32[1,512,512]{2,1,0:T(8,128)} %param.53) | copy-start | bytes 3145732
  683.1 159.5 %copy-start.72 = (f32[1,128]{1,0:T(1,128)S(1)}, f32[1,128]{1,0:T(1,128)}, u32[]{:S(2)}) copy-start(f32[1,128]{1,0:T(1,128)} %param.54) | copy-start | bytes 1540
  683.1 159.5 %copy-start.77 = (f32[1,128]{1,0:T(1,128)S(1)}, f32[1,128]{1,0:T(1,128)}, u32[]{:S(2)}) copy-start(f32[1,128]{1,0:T(1,128)} %param.56) | copy-start | bytes 1540
  683.1 159.5 %copy-start.78 = (f32[1,128]{1,0:T(1,128)S(1)}, f32[1,128]{1,0:T(1,128)}, u32[]{:S(2)}) copy-start(f32[1,128]{1,0:T(1,128)} %param.55) | copy-start | bytes 1540
  790.1 51.7 %reduce-scatter.31.cloned.1.call-start = ((), (), s32[]{:S(2)}) async-start(), calls=%async_computation.22 | async-start | bytes 163840
  794.1 72.3 %all-gather.10.cloned.1.call-start = ((), (), s32[]{:S(2)}) async-start(), calls=%async_computation.14 | async-start | bytes 2621440 | tf_op jit(solution)/shard_map/all_gather | solution.py:114
  866.4 99.2 %copy-start.80 = (bf16[1,2048,512]{2,1,0:T(8,128)(2,1)S(1)}, bf16[1,2048,512]{2,1,0:T(8,128)(2,1)}, u32[]{:S(2)}) copy-start(bf16[1,2048,512]{2,1,0:T(8,128)(2,1)} %all-gather.10.cloned.1.call-done) | copy-start | bytes 6291460
  959.6 128.5 %all-to-all-start.1 = ((bf16[8,1,616,512]{3,2,1,0:T(8,128)(2,1)}), bf16[8,1,616,512]{3,2,1,0:T(8,128)(2,1)}, u32[]{:S(2)}, u32[]{:S(2)}) async-start(bf16[8,1,616,512]{3,2,1,0:T(8,128)(2,1)} %fusion.30), calls=%async_computation.1 | async-start | bytes 10092544 | tf_op jit(solution)/shard_map/all_to_all | solution.py:166
  965.6 106.0 %copy-start.79 = (bf16[1,512,2048]{2,1,0:T(8,128)(2,1)S(1)}, bf16[1,512,2048]{2,1,0:T(8,128)(2,1)}, u32[]{:S(2)}) copy-start(bf16[1,512,2048]{2,1,0:T(8,128)(2,1)} %all-gather.8.cloned.1.call-done) | copy-start | bytes 6291460
  1088.1 117.5 %all-to-all-start.3 = ((bf16[8,1,616,512]{3,2,1,0:T(8,128)(2,1)}), bf16[8,1,616,512]{3,2,1,0:T(8,128)(2,1)}, u32[]{:S(2)}, u32[]{:S(2)}) async-start(bf16[8,1,616,512]{3,2,1,0:T(8,128)(2,1)} %convert_bitcast_fusion), calls=%async_computation.3 | async-start | bytes 10092544 | tf_op jit(solution)/shard_map/all_to_all | solution.py:199
  1094.2 319.3 %reduce-scatter.29.cloned.1.call-start = ((), (), s32[]{:S(2)}) async-start(), calls=%async_computation.21 | async-start | bytes 655360
  1098.5 317.3 %reduce-scatter.21.cloned.1.call-start = ((), (), s32[]{:S(2)}) async-start(), calls=%async_computation.17 | async-start | bytes 2621440 | tf_op jit(solution)/shard_map/reduce_scatter | solution.py:265
  1116.2 412.1 %reduce-scatter.27.cloned.1.call-start = ((), (), s32[]{:S(2)}) async-start(), calls=%async_computation.20 | async-start | bytes 270336
  1137.0 35.9 %copy-start.27 = (f32[1970,2]{0,1:T(2,128)S(1)}, f32[1970,2]{0,1:T(2,128)}, u32[]{:S(2)}) copy-start(f32[1970,2]{0,1:T(2,128)} %copy-done.26) | copy-start | bytes 47284
  1137.0 35.9 %copy-start.34 = (f32[1970]{0:T(1024)S(1)}, f32[1970]{0:T(1024)}, u32[]{:S(2)}) copy-start(f32[1970]{0:T(1024)} %copy-done.33) | copy-start | bytes 23644
  1137.0 35.9 %copy-start.38 = (f32[1970]{0:T(1024)S(1)}, f32[1970]{0:T(1024)}, u32[]{:S(2)}) copy-start(f32[1970]{0:T(1024)} %copy-done.37) | copy-start | bytes 23644
  1137.0 36.0 %copy-start.32 = (s32[1970,2]{0,1:T(2,128)S(1)}, s32[1970,2]{0,1:T(2,128)}, u32[]{:S(2)}) copy-start(s32[1970,2]{0,1:T(2,128)} %param.31) | copy-start | bytes 47284
  1226.2 50.6 %copy-start.36 = (f32[1970]{0:T(1024)S(1)}, f32[1970]{0:T(1024)}, u32[]{:S(2)}) copy-start(f32[1970]{0:T(1024)} %copy-done.35) | copy-start | bytes 23644
  1226.2 50.6 %copy-start.42 = (f32[1970]{0:T(1024)S(1)}, f32[1970]{0:T(1024)}, u32[]{:S(2)}) copy-start(f32[1970]{0:T(1024)} %copy-done.41) | copy-start | bytes 23644
  1226.2 50.6 %copy-start.46 = (bf16[512,8]{0,1:T(8,128)(2,1)S(1)}, bf16[512,8]{0,1:T(8,128)(2,1)}, u32[]{:S(2)}) copy-start(bf16[512,8]{0,1:T(8,128)(2,1)} %copy-done.45) | copy-start | bytes 24580
  1226.2 50.6 %copy-start.57 = (f32[512,1]{0,1:T(1,128)S(1)}, f32[512,1]{0,1:T(1,128)}, u32[]{:S(2)}) copy-start(f32[512,1]{0,1:T(1,128)} %copy-done.56) | copy-start | bytes 6148
  1354.4 31.9 %copy-start.8 = (bf16[1970,512]{1,0:T(8,128)(2,1)S(1)}, bf16[1970,512]{1,0:T(8,128)(2,1)}, u32[]{:S(2)}) copy-start(bf16[1970,512]{1,0:T(8,128)(2,1)} %param.29) | copy-start | bytes 6051844
  1354.4 31.9 %copy-start.44 = (f32[1970]{0:T(1024)S(1)}, f32[1970]{0:T(1024)}, u32[]{:S(2)}) copy-start(f32[1970]{0:T(1024)} %copy-done.43) | copy-start | bytes 23644
  1354.4 31.9 %copy-start.53 = (f32[1970]{0:T(1024)S(1)}, f32[1970]{0:T(1024)}, u32[]{:S(2)}) copy-start(f32[1970]{0:T(1024)} %copy-done.52) | copy-start | bytes 23644
  1354.4 31.9 %copy-start.65 = (f32[512,1]{0,1:T(1,128)S(1)}, f32[512,1]{0,1:T(1,128)}, u32[]{:S(2)}) copy-start(f32[512,1]{0,1:T(1,128)} %copy-done.64) | copy-start | bytes 6148
  1396.7 264.0 %reduce-scatter.25.cloned.1.call-start = ((), (), s32[]{:S(2)}) async-start(), calls=%async_computation.19 | async-start | bytes 270336
  1399.8 394.9 %reduce-scatter.19.cloned.1.call-start = ((), (), s32[]{:S(2)}) async-start(), calls=%async_computation.16 | async-start | bytes 1081344 | tf_op jit(solution)/shard_map/reduce_scatter | solution.py:260
  1405.0 124.2 %copy-start.49 = (f32[16,5]{0,1:T(8,128)S(1)}, f32[16,5]{0,1:T(8,128)}, u32[]{:S(2)}) copy-start(f32[16,5]{0,1:T(8,128)} %param.42) | copy-start | bytes 964
  1405.0 124.2 %copy-start.66 = (f32[16,5]{0,1:T(8,128)S(1)}, f32[16,5]{0,1:T(8,128)}, u32[]{:S(2)}) copy-start(f32[16,5]{0,1:T(8,128)} %param.43) | copy-start | bytes 964
  1405.0 124.2 %copy-start.67 = (f32[16,5]{0,1:T(8,128)S(1)}, f32[16,5]{0,1:T(8,128)}, u32[]{:S(2)}) copy-start(f32[16,5]{0,1:T(8,128)} %param.44) | copy-start | bytes 964
  1405.0 256.5 %copy-start.51 = (f32[16,8]{0,1:T(8,128)S(1)}, f32[16,8]{0,1:T(8,128)}, u32[]{:S(2)}) copy-start(f32[16,8]{0,1:T(8,128)} %param.39) | copy-start | bytes 1540
  1405.0 256.5 %copy-start.68 = (f32[16,8]{0,1:T(8,128)S(1)}, f32[16,8]{0,1:T(8,128)}, u32[]{:S(2)}) copy-start(f32[16,8]{0,1:T(8,128)} %param.40) | copy-start | bytes 1540
  1405.0 256.5 %copy-start.69 = (f32[16,8]{0,1:T(8,128)S(1)}, f32[16,8]{0,1:T(8,128)}, u32[]{:S(2)}) copy-start(f32[16,8]{0,1:T(8,128)} %param.41) | copy-start | bytes 1540
  1405.0 389.6 %copy-start.30 = (f32[16,512]{1,0:T(8,128)S(1)}, f32[16,512]{1,0:T(8,128)}, u32[]{:S(2)}) copy-start(f32[16,512]{1,0:T(8,128)} %param.36) | copy-start | bytes 98308
  1405.0 389.6 %copy-start.54 = (f32[16,512]{1,0:T(8,128)S(1)}, f32[16,512]{1,0:T(8,128)}, u32[]{:S(2)}) copy-start(f32[16,512]{1,0:T(8,128)} %param.37) | copy-start | bytes 98308
  1405.0 389.6 %copy-start.55 = (f32[16,512]{1,0:T(8,128)S(1)}, f32[16,512]{1,0:T(8,128)}, u32[]{:S(2)}) copy-start(f32[16,512]{1,0:T(8,128)} %param.38) | copy-start | bytes 98308
  1405.1 493.8 %copy-start.25 = (f32[16,1536]{1,0:T(8,128)S(1)}, f32[16,1536]{1,0:T(8,128)}, u32[]{:S(2)}) copy-start(f32[16,1536]{1,0:T(8,128)} %param.33) | copy-start | bytes 294916
  1405.1 493.8 %reduce-scatter.17.cloned.1.call-start = ((), (), s32[]{:S(2)}) async-start(), calls=%async_computation.15 | async-start | bytes 3244032 | tf_op jit(solution)/shard_map/reduce_scatter | solution.py:259
  1413.4 548.1 %copy-start.73 = (f32[1,128]{1,0:T(1,128)S(1)}, f32[1,128]{1,0:T(1,128)}, u32[]{:S(2)}) copy-start(f32[1,128]{1,0:T(1,128)} %param.54) | copy-start | bytes 1540
  1413.4 548.1 %copy-start.74 = (f32[1,128]{1,0:T(1,128)S(1)}, f32[1,128]{1,0:T(1,128)}, u32[]{:S(2)}) copy-start(f32[1,128]{1,0:T(1,128)} %get-tuple-element.100) | copy-start | bytes 1540
  1529.3 442.4 %copy-start.60 = (f32[16,5]{0,1:T(8,128)}, f32[16,5]{0,1:T(8,128)S(1)}, u32[]{:S(2)}) copy-start(f32[16,5]{0,1:T(8,128)S(1)} %get-tuple-element.61) | copy-start | bytes 964
  1529.3 442.4 %copy-start.61 = (f32[16,5]{0,1:T(8,128)}, f32[16,5]{0,1:T(8,128)S(1)}, u32[]{:S(2)}) copy-start(f32[16,5]{0,1:T(8,128)S(1)} %get-tuple-element.62) | copy-start | bytes 964
  1662.2 309.5 %copy-start.62 = (f32[16,8]{0,1:T(8,128)}, f32[16,8]{0,1:T(8,128)S(1)}, u32[]{:S(2)}) copy-start(f32[16,8]{0,1:T(8,128)S(1)} %get-tuple-element.65) | copy-start | bytes 1540
  1662.2 309.5 %copy-start.63 = (f32[16,8]{0,1:T(8,128)}, f32[16,8]{0,1:T(8,128)S(1)}, u32[]{:S(2)}) copy-start(f32[16,8]{0,1:T(8,128)S(1)} %get-tuple-element.66) | copy-start | bytes 1540
  1796.1 175.6 %copy-start.39 = (f32[16,512]{1,0:T(8,128)}, f32[16,512]{1,0:T(8,128)S(1)}, u32[]{:S(2)}) copy-start(f32[16,512]{1,0:T(8,128)S(1)} %get-tuple-element.67) | copy-start | bytes 98308
  1796.1 175.6 %copy-start.40 = (f32[16,512]{1,0:T(8,128)}, f32[16,512]{1,0:T(8,128)S(1)}, u32[]{:S(2)}) copy-start(f32[16,512]{1,0:T(8,128)S(1)} %get-tuple-element.68) | copy-start | bytes 98308
  1900.5 71.2 %copy-start.28 = (f32[16,1536]{1,0:T(8,128)}, f32[16,1536]{1,0:T(8,128)S(1)}, u32[]{:S(2)}) copy-start(f32[16,1536]{1,0:T(8,128)S(1)} %get-tuple-element.69) | copy-start | bytes 294916
  1900.5 71.2 %copy-start.29 = (f32[16,1536]{1,0:T(8,128)}, f32[16,1536]{1,0:T(8,128)S(1)}, u32[]{:S(2)}) copy-start(f32[16,1536]{1,0:T(8,128)S(1)} %get-tuple-element.70) | copy-start | bytes 294916
  (32 other events, 389.8 us)
Sparse Core Ops, SparseCore 0:
  12.3 57.8 all-gather.5
Sparse Core Ops, SparseCore 1:
  577.2 23.9 all-gather.7
  790.2 29.5 reduce-scatter.22
  822.1 19.6 reduce-scatter.30
  843.9 22.4 all-gather.9
  1098.5 22.0 reduce-scatter.28
  1123.3 31.3 reduce-scatter.20
  1396.8 131.5 reduce-scatter.26
  1531.1 129.6 reduce-scatter.24
  1663.4 131.2 reduce-scatter.18
  1801.0 97.8 reduce-scatter.16
where the time goes:
time: 1990 us; the launch traced here: 1980 us
  waiting for transfers between devices  650 us (33%)
  matrix products  459 us (23%)
  blocking collectives  351 us (18%)
  local copies, waits for them, and re-layouts  313 us (16%)
  other arithmetic  163 us (8%)
  starting transfers between devices  21.9 us (1%)
  between operations  21.5 us (1%)
    unnamed x15, waiting for transfers between devices  258 us
    all_gather x1, blocking collectives, on_device(): lax.all_gather(router.astype(jnp.bfloat16), ('rep', 'ep'), axis=0, tiled=...  164 us
    reduce_scatter x1, waiting for transfers between devices, on_device(): lax.psum_scatter(grad_out_matrix, ('rep', 'ep'), scatter_dimension=0, til...  132 us
    dot_general x1, matrix products, on_device(): jnp.einsum('sjcf,sjcd->jfd', act_low, grad_arrived, preferred_element_typ...  107 us
    dot_general x1, matrix products, on_device(): jnp.einsum('sjcd,jfd->sjcf', grad_arrived, leave_weight, preferred_elemen...  106 us
    reduce_scatter x1, waiting for transfers between devices, on_device(): lax.psum_scatter(grad_in_matrix, ('rep', 'ep'), scatter_dimension=0, tile...  103 us
    dot_general x1, matrix products, on_device(): jnp.einsum('sjcf,jfd->sjcd', act_low, leave_weight, preferred_element_typ...  93.2 us
    all_gather x1, blocking collectives, on_device(): lax.all_gather(scales.astype(jnp.bfloat16), ('rep', 'ep'), axis=0, tiled=...  70.2 us
  transfers between devices with their start and end apart: 15, of which 10 were waited for; matrix products, arithmetic and copies ran while one was open for 30% of the time, Pallas kernels for 0%

commit v1 on v0

--- a/solution.py
+++ b/solution.py
@@ -1,6 +1,10 @@
+import functools
+
 import jax
 import jax.numpy as jnp
 from jax import lax
+from jax.experimental import pallas as pl
+from jax.experimental.pallas import tpu as pltpu
 from jax.sharding import PartitionSpec as P
 
 HEADS = 8
@@ -67,12 +71,858 @@
     return jnp.sum(array * array)[None]
 
 
+def finish(totals, weights_now, states, width, experts):
+    counts = jnp.array(
+        [3 * width * width, width * width, width * experts]
+        + [width] * 5
+        + [experts * width * FF, experts * FF, experts * FF * width, experts * width],
+        jnp.float32,
+    )
+    weight_rms = jnp.sqrt(totals[0] / counts)
+    step_rms = jnp.sqrt(totals[1] / counts)
+    trust = weight_rms / step_rms
+    bounds = [(0, 1), (1, 2), (2, 3), (3, 8), (8, 9), (9, 10), (10, 11), (11, 12)]
+    results = []
+    for weight, state, bound in zip(weights_now, states, bounds):
+        results.extend([state[0], state[1], weight - RATE * trust[bound[0] : bound[1]] * state[2]])
+    results.append(jnp.stack([weight_rms, step_rms, trust]))
+    return tuple(results)
+
+
+PAD = 208
+WIN = 96
+VMEM = 60 * 1024 * 1024
+BF = jnp.bfloat16
+F32 = jnp.float32
+
+
+def dot_nn(a, b):
+    return lax.dot_general(a, b, (((1,), (0,)), ((), ())), preferred_element_type=F32)
+
+
+def dot_nt(a, b):
+    return lax.dot_general(a, b, (((1,), (1,)), ((), ())), preferred_element_type=F32)
+
+
+def dot_tn(a, b):
+    return lax.dot_general(a, b, (((0,), (0,)), ((), ())), preferred_element_type=F32)
+
+
+def lane_iota(rows, lanes):
+    return lax.broadcasted_iota(jnp.int32, (rows, lanes), 1)
+
+
+def row_iota(rows, lanes):
+    return lax.broadcasted_iota(jnp.int32, (rows, lanes), 0)
+
+
+def whole(shape):
+    return pl.BlockSpec(shape, lambda *_: (0,) * len(shape))
+
+
+def params(semantics=None, **kw):
+    return pltpu.CompilerParams(vmem_limit_bytes=VMEM, **kw)
+
+
+def assemble_kernel(place_ref, got_ref, in_ref, out_ref, router_ref, gains_ref, small_ref):
+    copies, rows = got_ref.shape[0], got_ref.shape[1]
+    width = out_ref.shape[1]
+
+    def body(j, carry):
+        place = pl.multiple_of(place_ref[j] * rows, rows)
+        in_ref[pl.ds(place, rows), :] = got_ref[j, :, : 3 * width]
+        out_ref[pl.ds(place, rows), :] = got_ref[j, :, 3 * width : 4 * width]
+        small_ref[pl.ds(place, rows), :] = got_ref[j, :, 4 * width :]
+        return carry
+
+    lax.fori_loop(0, copies, body, 0)
+    turned = small_ref[:, :128].astype(F32).T
+    experts = router_ref.shape[0]
+    router_ref[...] = turned[:experts].astype(BF)
+    gains_ref[...] = turned[experts : experts + 8]
+
+
+def assemble(place, got, experts):
+    copies, rows, lanes = got.shape
+    width = copies * rows
+    return pl.pallas_call(
+        assemble_kernel,
+        grid_spec=pltpu.PrefetchScalarGridSpec(
+            num_scalar_prefetch=1,
+            grid=(1,),
+            in_specs=[whole(got.shape)],
+            out_specs=[
+                whole((width, 3 * width)),
+                whole((width, width)),
+                whole((experts, width)),
+                whole((8, width)),
+                whole((width, lanes - 4 * width)),
+            ],
+        ),
+        out_shape=[
+            jax.ShapeDtypeStruct((width, 3 * width), BF),
+            jax.ShapeDtypeStruct((width, width), BF),
+            jax.ShapeDtypeStruct((experts, width), BF),
+            jax.ShapeDtypeStruct((8, width), F32),
+            jax.ShapeDtypeStruct((width, lanes - 4 * width), BF),
+        ],
+        compiler_params=params(),
+        name="assemble",
+    )(place, got)
+
+
+def places_kernel(capacity, rows_ref, cols_ref, lrow_ref, lcol_ref, meta_ref):
+    count = cols_ref.shape[0]
+    images = count // PAD
+    experts = lcol_ref.shape[1]
+    expert = lane_iota(count, experts).astype(F32)
+    first = (cols_ref[:, 1:2] == expert).astype(F32)
+    second = (cols_ref[:, 2:3] == expert).astype(F32)
+    first_low = first.astype(BF)
+    second_low = second.astype(BF)
+    total_first = jnp.sum(first, axis=0, keepdims=True)
+    lower = (lane_iota(PAD, PAD) < row_iota(PAD, PAD)).astype(F32).astype(BF)
+    ranking = rows_ref[0:1, :]
+    begin = jnp.zeros((1, experts), F32)
+    for i in range(images):
+        span = slice(i * PAD, (i + 1) * PAD)
+        ahead = (ranking < cols_ref[span, 0:1]).astype(F32).astype(BF)
+        rank_first = dot_nn(ahead, first_low)
+        rank_second = dot_nn(ahead, second_low) + total_first
+        place = first[span] * rank_first + second[span] * rank_second
+        kept = (first[span] + second[span]) * (place < capacity).astype(F32)
+        local = dot_nn(lower, kept.astype(BF))
+        local = jnp.where(kept > 0.0, local, -1.0)
+        lcol_ref[span, :] = local
+        lrow_ref[i] = local.T
+        here = jnp.sum(kept, axis=0, keepdims=True)
+        meta_ref[i : i + 1, :] = begin.astype(jnp.int32)
+        meta_ref[images + i : images + i + 1, :] = here.astype(jnp.int32)
+        begin = begin + here
+
+
+def find_places(rows, cols, capacity, experts):
+    count = cols.shape[0]
+    images = count // PAD
+    return pl.pallas_call(
+        functools.partial(places_kernel, capacity),
+        out_shape=[
+            jax.ShapeDtypeStruct((images, experts, PAD), F32),
+            jax.ShapeDtypeStruct((count, experts), F32),
+            jax.ShapeDtypeStruct((2 * images, experts), jnp.int32),
+        ],
+        compiler_params=params(),
+        name="places",
+    )(rows, cols)
+
+
+def spread_kernel(tok_ref, cot_ref, tpad_ref, cpad_ref):
+    count, width = tok_ref.shape
+    for source, target in ((tok_ref, tpad_ref), (cot_ref, cpad_ref)):
+        for i in range(count // SEQ):
+            rows = source[SEQ * i : SEQ * (i + 1), :].astype(F32)
+            rows = jnp.concatenate([rows, jnp.zeros((PAD - SEQ, width), F32)], axis=0)
+            target[PAD * i : PAD * (i + 1), :] = rows.astype(BF)
+
+
+def spread_rows(tokens, cotangent):
+    count, width = tokens.shape
+    shape = jax.ShapeDtypeStruct((count // SEQ * PAD, width), BF)
+    return pl.pallas_call(
+        spread_kernel, out_shape=[shape, shape], compiler_params=params(), name="spread_rows"
+    )(tokens, cotangent)
+
+
+def store_image(target, i, values):
+    for image in range(target.shape[0] // SEQ):
+
+        @pl.when(i == image)
+        def _(image=image):
+            target[SEQ * image : SEQ * (image + 1), :] = values[0:SEQ, :]
+
+
+def attention_kernel(
+    tok_ref, in_ref, out_ref, router_ref, gains_ref, ids_ref,
+    proj_ref, prob_ref, mixed_ref, hidden_ref, routed_ref, gcol_ref, grow_ref, mixed_all,
+):
+    width = tok_ref.shape[1]
+    x = tok_ref[...].astype(F32)
+    normed, _ = normalize(x)
+    entry = (normed * gains_ref[0:1, :] + gains_ref[1:2, :]).astype(BF)
+    proj_ref[...] = dot_nn(entry, in_ref[...]).astype(BF)
+    pair = 2 * HEAD
+    halves = lane_iota(PAD, pair) < HEAD
+    key_there = lane_iota(PAD, PAD) < SEQ
+    for p in range(HEADS // 2):
+        q = proj_ref[:, pair * p : pair * (p + 1)] * jnp.asarray(HEAD ** -0.5, BF)
+        k = proj_ref[:, width + pair * p : width + pair * (p + 1)]
+        v = proj_ref[:, 2 * width + pair * p : 2 * width + pair * (p + 1)]
+        sides = []
+        for s in range(2):
+            mine = halves if s == 0 else jnp.logical_not(halves)
+            scores = dot_nt(jnp.where(mine, q, jnp.zeros_like(q)), k)
+            scores = jnp.where(key_there, scores, -1e30)
+            peak = jnp.max(scores, axis=1, keepdims=True)
+            raised = jnp.exp(scores - peak)
+            total = jnp.sum(raised, axis=1, keepdims=True)
+            weights = (raised * (1.0 / total)).astype(BF)
+            prob_ref[0, 2 * p + s] = weights
+            sides.append(dot_nn(weights, v))
+        mixed_all[:, pair * p : pair * (p + 1)] = jnp.where(halves, sides[0], sides[1]).astype(BF)
+    mixed = mixed_all[...]
+    mixed_ref[...] = mixed
+    hidden = x + dot_nn(mixed, out_ref[...]) + gains_ref[4:5, :]
+    hidden_ref[...] = hidden
+    normed_two, _ = normalize(hidden)
+    routed = (normed_two * gains_ref[2:3, :] + gains_ref[3:4, :]).astype(BF)
+    routed_ref[...] = routed
+    logits = dot_nt(routed, router_ref[...])
+    experts = logits.shape[1]
+    expert = lane_iota(PAD, experts)
+    chosen = jnp.logical_or(ids_ref[:, 0:1] == expert, ids_ref[:, 1:2] == expert)
+    top = jnp.max(jnp.where(chosen, logits, -1e30), axis=1, keepdims=True)
+    raised = jnp.where(chosen, jnp.exp(jnp.where(chosen, logits - top, 0.0)), 0.0)
+    total = jnp.sum(raised, axis=1, keepdims=True)
+    gates = raised / jnp.where(total > 0.0, total, 1.0)
+    gcol_ref[...] = gates
+    grow_ref[0] = gates.T
+
+
+def attention(tok_pad, in_matrix, out_matrix, router, gains, ids_col):
+    padded, width = tok_pad.shape
+    images = padded // PAD
+    experts = router.shape[0]
+    row = lambda lanes: pl.BlockSpec((PAD, lanes), lambda i: (i, 0))
+    once = lambda a: pl.BlockSpec(a.shape, lambda i: (0, 0), pipeline_mode=pl.Buffered(1))
+    return pl.pallas_call(
+        attention_kernel,
+        grid=(images,),
+        in_specs=[row(width), once(in_matrix), once(out_matrix), once(router), once(gains), row(2)],
+        out_specs=[
+            row(3 * width),
+            pl.BlockSpec((1, HEADS, PAD, PAD), lambda i: (i, 0, 0, 0)),
+            row(width), row(width), row(width), row(experts),
+            pl.BlockSpec((1, experts, PAD), lambda i: (i, 0, 0)),
+        ],
+        out_shape=[
+            jax.ShapeDtypeStruct((padded, 3 * width), BF),
+            jax.ShapeDtypeStruct((images, HEADS, PAD, PAD), BF),
+            jax.ShapeDtypeStruct((padded, width), BF),
+            jax.ShapeDtypeStruct((padded, width), F32),
+            jax.ShapeDtypeStruct((padded, width), BF),
+            jax.ShapeDtypeStruct((padded, experts), F32),
+            jax.ShapeDtypeStruct((images, experts, PAD), F32),
+        ],
+        scratch_shapes=[pltpu.VMEM((PAD, width), BF)],
+        compiler_params=params(),
+        name="attention",
+    )(tok_pad, in_matrix, out_matrix, router, gains, ids_col)
+
+
+def window_count():
+    return -(-(15 + SEQ) // WIN)
+
+
+def gather_kernel(meta_ref, routed_ref, cot_ref, lrow_ref, grow_ref, r_ref, g_ref, rt_ref, gt_ref, r_all, g_all):
+    e = pl.program_id(0)
+    images = lrow_ref.shape[0]
+    listed = r_ref.shape[1]
+    r_all[...] = jnp.zeros_like(r_all)
+    g_all[...] = jnp.zeros_like(g_all)
+    row = row_iota(WIN, PAD).astype(F32)
+    for i in range(images):
+        start, here = meta_ref[i, e], meta_ref[images + i, e]
+        base = lax.shift_left(lax.shift_right_logical(start, 4), 4)
+        shift = (start - base).astype(F32)
+        local = lrow_ref[i, pl.ds(e, 1), :]
+        gate = grow_ref[i, pl.ds(e, 1), :]
+        for q in range(window_count()):
+            @pl.when(jnp.logical_and(here > 0, base + q * WIN < start + here))
+            def _(i=i, q=q, base=base, shift=shift, local=local, gate=gate):
+                pick = jnp.logical_and(local >= 0.0, local + (shift - q * WIN) == row)
+                low = pick.astype(F32).astype(BF)
+                slot_gate = jnp.sum(jnp.where(pick, gate, 0.0), axis=1, keepdims=True)
+                where = pl.ds(pl.multiple_of(base + q * WIN, 16), WIN)
+                r_all[where, :] += dot_nn(low, routed_ref[i * PAD : (i + 1) * PAD, :])
+                g_all[where, :] += slot_gate * dot_nn(low, cot_ref[i * PAD : (i + 1) * PAD, :])
+    r_ref[0] = r_all[0:listed, :].astype(BF)
+    g_ref[0] = g_all[0:listed, :].astype(BF)
+    rt_ref[0] = r_all[0:listed, :].T.astype(BF)
+    gt_ref[0] = g_all[0:listed, :].astype(BF).astype(F32).T.astype(BF)
+
+
+def gather(meta, routed, cot_pad, lrow, grow, listed):
+    width = routed.shape[1]
+    experts = lrow.shape[1]
+    once = lambda a: pl.BlockSpec(a.shape, lambda e, m: (0,) * a.ndim, pipeline_mode=pl.Buffered(1))
+    block = pl.BlockSpec((1, listed, width), lambda e, m: (e, 0, 0))
+    turned = pl.BlockSpec((1, width, listed), lambda e, m: (e, 0, 0))
+    return pl.pallas_call(
+        gather_kernel,
+        grid_spec=pltpu.PrefetchScalarGridSpec(
+            num_scalar_prefetch=1,
+            grid=(experts,),
+            in_specs=[once(routed), once(cot_pad), once(lrow), once(grow)],
+            out_specs=[block, block, turned, turned],
+            scratch_shapes=[pltpu.VMEM((listed + WIN, width), F32)] * 2,
+        ),
+        out_shape=[jax.ShapeDtypeStruct((experts, listed, width), BF)] * 2
+        + [jax.ShapeDtypeStruct((experts, width, listed), BF)] * 2,
+        compiler_params=params(),
+        name="gather",
+    )(meta, routed, cot_pad, lrow, grow)
+
+
+def gelu_both(pre):
+    bell = jnp.exp(-0.5 * (pre * pre))
+    t = pl.reciprocal(1.0 + (0.3275911 * 2.0**-0.5) * jnp.abs(pre))
+    tail = t * (0.127414796 + t * (-0.142248368 + t * (0.7107068705 + t * (-0.7265760135 + t * 0.5307027145))))
+    tail = tail * bell
+    phi = jnp.where(pre < 0.0, tail, 1.0 - tail)
+    return pre * phi, phi + pre * bell * 0.3989422804014327
+
+
+def expert_kernel(last, at_ref, *refs):
+    if last:
+        (r_ref, g_ref, rt_ref, gt_ref, w_ref, b_ref, ob_ref, y_in, d_in,
+         y_ref, d_ref, near_ref, far_ref, db_ref, y_all, d_all) = refs
+    else:
+        (r_ref, g_ref, rt_ref, gt_ref, w_ref, b_ref,
+         y_ref, d_ref, near_ref, far_ref, db_ref, obg_ref, y_all, d_all) = refs
+    rep = w_ref.shape[0]
+    rows, grads = r_ref[0], g_ref[0]
+    rows_t, grads_t = rt_ref[0], gt_ref[0]
+    if not last:
+        obg_ref[0] = jnp.sum(grads.astype(F32), axis=0, keepdims=True)
+    for r in range(rep):
+        place = lax.bitwise_xor(at_ref[0], r)
+        enter, leave = w_ref[place, 0, 0], w_ref[place, 0, 1]
+        pre = dot_nn(rows, enter) + b_ref[0, pl.ds(place, 1), :]
+        act, slope = gelu_both(pre)
+        act = act.astype(BF)
+        grad_pre = (dot_nn(grads, leave) * slope).astype(BF)
+        out = far_ref if r % 2 else near_ref
+        out[r // 2, 0, 0] = dot_nn(rows_t, grad_pre).astype(BF)
+        out[r // 2, 0, 1] = dot_nn(grads_t, act).astype(BF)
+        db_ref[0, pl.ds(place, 1), :] = jnp.sum(grad_pre.astype(F32), axis=0, keepdims=True)
+        y_part = dot_nt(act, leave)
+        d_part = dot_nt(grad_pre, enter)
+        if r == 0:
+            y_all[...] = y_part + y_in[0] if last else y_part
+            d_all[...] = d_part + d_in[0] if last else d_part
+        else:
+            y_all[...] += y_part
+            d_all[...] += d_part
+    if last:
+        y_ref[0] = (y_all[...] + ob_ref[0]).astype(BF)
+        d_ref[0] = d_all[...].astype(BF)
+    else:
+        y_ref[0] = y_all[...]
+        d_ref[0] = d_all[...]
+
+
+def expert_pass(at, lists, weights, bias, out_bias=None, carried=None):
+    last = carried is not None
+    rows = lists[0]
+    experts, listed, width = rows.shape
+    rep, _, _, _, cols = weights.shape
+    here = lambda e, at: lax.bitwise_xor(e, at[1])
+    block = pl.BlockSpec((1, listed, width), lambda e, at: (here(e, at), 0, 0))
+    turned = pl.BlockSpec((1, width, listed), lambda e, at: (here(e, at), 0, 0))
+    out_w = pl.BlockSpec((rep // 2, 1, 2, width, cols), lambda e, at: (0, e, 0, 0, 0))
+    in_specs = [
+        block, block, turned, turned,
+        pl.BlockSpec((rep, 1, 2, width, cols), lambda e, at: (0, here(e, at), 0, 0, 0)),
+        pl.BlockSpec((1, rep, cols), lambda e, at: (here(e, at), 0, 0)),
+    ]
+    args = list(lists) + [weights, bias]
+    kind = BF if last else F32
+    out_specs = [block, block, out_w, out_w, pl.BlockSpec((1, rep, cols), lambda e, at: (here(e, at), 0, 0))]
+    out_shape = [
+        jax.ShapeDtypeStruct(rows.shape, kind),
+        jax.ShapeDtypeStruct(rows.shape, kind),
+        jax.ShapeDtypeStruct((rep // 2, experts, 2, width, cols), BF),
+        jax.ShapeDtypeStruct((rep // 2, experts, 2, width, cols), BF),
+        jax.ShapeDtypeStruct((experts, rep, cols), F32),
+    ]
+    if last:
+        in_specs += [pl.BlockSpec((1, 1, width), lambda e, at: (here(e, at), 0, 0)), block, block]
+        args += [out_bias, *carried]
+    else:
+        out_specs.append(pl.BlockSpec((1, 1, width), lambda e, at: (here(e, at), 0, 0)))
+        out_shape.append(jax.ShapeDtypeStruct((experts, 1, width), F32))
+    flops = 12 * experts * listed * width * rep * cols
+    return pl.pallas_call(
+        functools.partial(expert_kernel, last),
+        grid_spec=pltpu.PrefetchScalarGridSpec(
+            num_scalar_prefetch=1,
+            grid=(experts,),
+            in_specs=in_specs,
+            out_specs=out_specs,
+            scratch_shapes=[pltpu.VMEM((listed, width), F32)] * 2,
+        ),
+        out_shape=out_shape,
+        compiler_params=params(),
+        cost_estimate=pl.CostEstimate(flops=flops, bytes_accessed=60_000_000, transcendentals=0),
+        name="experts_last" if last else "experts_first",
+    )(at, *args)
+
+
+def combine_kernel(
+    meta_ref, y_ref, d_ref, lcol_ref, gcol_ref, hidden_ref, cot_ref, mixed_ref, out_w_ref, router_ref, gains_ref,
+    out_ref, gh_ref, gm_ref, dout_ref, drouter_ref, dscale_ref, y_acc, g_acc, d_acc,
+):
+    i = pl.program_id(0)
+    images = pl.num_programs(0)
+    experts, listed, width = y_ref.shape
+    gates = gcol_ref[...]
+    local = lcol_ref[...]
+    go = cot_ref[...].astype(F32)
+    lane = lane_iota(PAD, WIN).astype(F32)
+    expert = lane_iota(PAD, experts)
+
+    def window(e, q, base, shift):
+        at = jnp.minimum(base + q * WIN, listed - WIN)
+        moved = (at - base).astype(F32)
+        spot = local[:, e : e + 1] + shift
+        pick = jnp.logical_and(spot == lane + moved, local[:, e : e + 1] >= 0.0)
+        pick = jnp.logical_and(pick, spot >= q * WIN)
+        low = pick.astype(F32).astype(BF)
+        where = pl.ds(pl.multiple_of(at, 16), WIN)
+        return dot_nn(low, y_ref[e, where, :]), dot_nn(low, d_ref[e, where, :])
+
+    y_sum = jnp.zeros((PAD, width), F32)
+    d_sum = jnp.zeros((PAD, width), F32)
+    grad_gates = jnp.zeros((PAD, experts), F32)
+    bases = []
+    for e in range(experts):
+        start = meta_ref[i, e]
+        base = lax.shift_left(lax.shift_right_logical(start, 4), 4)
+        bases.append((start, base))
+        y_tok, d_tok = window(e, 0, base, (start - base).astype(F32))
+        y_sum += gates[:, e : e + 1] * y_tok
+        d_sum += d_tok
+        gg = jnp.sum(go * y_tok, axis=1, keepdims=True)
+        grad_gates += jnp.where(expert == e, gg, 0.0)
+    y_acc[...] = y_sum
+    d_acc[...] = d_sum
+    g_acc[...] = grad_gates
+    for e in range(experts):
+        start, base = bases[e]
+        here = meta_ref[images + i, e]
+        for q in range(1, window_count()):
+            @pl.when(base + q * WIN < start + here)
+            def _(e=e, q=q, base=base, start=start):
+                y_tok, d_tok = window(e, q, base, (start - base).astype(F32))
+                y_acc[...] += gates[:, e : e + 1] * y_tok
+                d_acc[...] += d_tok
+                gg = jnp.sum(go * y_tok, axis=1, keepdims=True)
+                g_acc[...] += jnp.where(expert == e, gg, 0.0)
+    hidden = hidden_ref[...]
+    y_acc[...] += hidden
+    store_image(out_ref, i, y_acc)
+    grad_gates = g_acc[...]
+    pick = gates * (grad_gates - jnp.sum(gates * grad_gates, axis=1, keepdims=True))
+    logit_low = pick.astype(BF)
+    grad_routed = d_acc[...] + dot_nn(logit_low, router_ref[...])
+    normed, inverse = normalize(hidden)
+    routed = (normed * gains_ref[2:3, :] + gains_ref[3:4, :]).astype(BF)
+    grad_hidden = go + norm_back(grad_routed, normed, inverse, gains_ref[2:3, :])
+    gh_ref[...] = grad_hidden
+    grad_mix = grad_hidden.astype(BF)
+    gm_ref[...] = dot_nt(grad_mix, out_w_ref[...]).astype(BF)
+
+    @pl.when(i == 0)
+    def _():
+        dout_ref[...] = jnp.zeros_like(dout_ref)
+        drouter_ref[...] = jnp.zeros_like(drouter_ref)
+        dscale_ref[...] = jnp.zeros_like(dscale_ref)
+
+    dout_ref[...] += dot_tn(mixed_ref[...], grad_mix)
+    drouter_ref[...] += dot_tn(logit_low, routed)
+    dscale_ref[2:3, :] += jnp.sum(grad_routed * normed, axis=0, keepdims=True)
+    dscale_ref[3:4, :] += jnp.sum(grad_routed, axis=0, keepdims=True)
+    dscale_ref[4:5, :] += jnp.sum(grad_hidden, axis=0, keepdims=True)
+
+
+def combine(meta, y, d, lcol, gcol, hidden, cot_pad, mixed, out_matrix, router, gains):
+    padded, width = hidden.shape
+    images = padded // PAD
+    experts = y.shape[0]
+    row = lambda lanes: pl.BlockSpec((PAD, lanes), lambda i, m: (i, 0))
+    once = lambda a: pl.BlockSpec(a.shape, lambda i, m: (0,) * a.ndim, pipeline_mode=pl.Buffered(1))
+    return pl.pallas_call(
+        combine_kernel,
+        grid_spec=pltpu.PrefetchScalarGridSpec(
+            num_scalar_prefetch=1,
+            grid=(images,),
+            in_specs=[
+                once(y), once(d), row(experts), row(experts), row(width), row(width), row(width),
+                once(out_matrix), once(router), once(gains),
+            ],
+            out_specs=[
+                whole((images * SEQ, width)), row(width), row(width), whole((width, width)), whole((experts, width)),
+                whole((8, width)),
+            ],
+            scratch_shapes=[
+                pltpu.VMEM((PAD, width), F32), pltpu.VMEM((PAD, experts), F32), pltpu.VMEM((PAD, width), F32),
+            ],
+        ),
+        out_shape=[
+            jax.ShapeDtypeStruct((images * SEQ, width), F32),
+            jax.ShapeDtypeStruct((padded, width), F32),
+            jax.ShapeDtypeStruct((padded, width), BF),
+            jax.ShapeDtypeStruct((width, width), F32),
+            jax.ShapeDtypeStruct((experts, width), F32),
+            jax.ShapeDtypeStruct((8, width), F32),
+        ],
+        compiler_params=params(),
+        name="combine",
+    )(meta, y, d, lcol, gcol, hidden, cot_pad, mixed, out_matrix, router, gains)
+
+
+def attention_back_kernel(
+    place_ref, proj_ref, prob_ref, gm_ref, gh_ref, tpad_ref, in_ref, gains_ref, dout_ref, small_ref,
+    grad_ref, near_ref, far_ref, din_ref, dscale_ref, line_ref, dproj, grad_all,
+):
+    i = pl.program_id(0)
+    width = gm_ref.shape[1]
+    pair = 2 * HEAD
+    halves = lane_iota(PAD, pair) < HEAD
+    factor = HEAD ** -0.5
+    for p in range(HEADS // 2):
+        cut = slice(pair * p, pair * (p + 1))
+        q = proj_ref[:, cut]
+        k = proj_ref[:, width + pair * p : width + pair * (p + 1)]
+        v = proj_ref[:, 2 * width + pair * p : 2 * width + pair * (p + 1)]
+        gm = gm_ref[:, cut]
+        both = []
+        for s in range(2):
+            mine = halves if s == 0 else jnp.logical_not(halves)
+            low = prob_ref[0, 2 * p + s]
+            probs = low.astype(F32)
+            grad_probs = dot_nt(jnp.where(mine, gm, jnp.zeros_like(gm)), v)
+            middle = jnp.sum(probs * grad_probs, axis=1, keepdims=True)
+            grad_scores = (probs * (grad_probs - middle)).astype(BF)
+            both.append((dot_nn(grad_scores, k), dot_tn(grad_scores, q), dot_tn(low, gm)))
+        dproj[:, cut] = (jnp.where(halves, both[0][0], both[1][0]) * factor).astype(BF)
+        dproj[:, width + pair * p : width + pair * (p + 1)] = (
+            jnp.where(halves, both[0][1], both[1][1]) * factor
+        ).astype(BF)
+        dproj[:, 2 * width + pair * p : 2 * width + pair * (p + 1)] = jnp.where(
+            halves, both[0][2], both[1][2]
+        ).astype(BF)
+    normed, inverse = normalize(tpad_ref[...].astype(F32))
+    entry = (normed * gains_ref[0:1, :] + gains_ref[1:2, :]).astype(BF)
+    grads = dproj[...]
+    grad_entry = dot_nt(grads, in_ref[...])
+
+    @pl.when(i == 0)
+    def _():
+        din_ref[...] = jnp.zeros_like(din_ref)
+        dscale_ref[...] = jnp.zeros_like(dscale_ref)
+
+    din_ref[...] += dot_tn(entry, grads)
+    dscale_ref[0:1, :] += jnp.sum(grad_entry * normed, axis=0, keepdims=True)
+    dscale_ref[1:2, :] += jnp.sum(grad_entry, axis=0, keepdims=True)
+    grad = gh_ref[...] + norm_back(grad_entry, normed, inverse, gains_ref[0:1, :])
+    grad_all[...] = grad
+    store_image(grad_ref, i, grad_all)
+
+    @pl.when(i == pl.num_programs(0) - 1)
+    def _():
+        blocks, rows = 2 * near_ref.shape[0], near_ref.shape[1]
+        owner = lane_iota(blocks, width) // rows == row_iota(blocks, width)
+        spot = row_iota(width, 128) % rows
+        line = jnp.zeros((blocks, 128), F32)
+        for s in range(2):
+            spread = jnp.where(owner, dscale_ref[s : s + 1, :], 0.0)
+            chosen = (lane_iota(width, 128) == spot + s * rows).astype(F32)
+            line += lax.dot_general(
+                spread, chosen, (((1,), (0,)), ((), ())),
+                preferred_element_type=F32, precision=lax.Precision.HIGHEST,
+            )
+        line_ref[...] = line
+        scale_row = row_iota(8, 128) == 6
+        for side, out in ((0, near_ref), (1, far_ref)):
+            def body(j, carry, side=side, out=out):
+                place = place_ref[side * (blocks // 2) + j]
+                here = pl.ds(pl.multiple_of(place * rows, rows), rows)
+                out[j, :, : 3 * width] = din_ref[here, :].astype(BF)
+                out[j, :, 3 * width : 4 * width] = dout_ref[here, :].astype(BF)
+                small = small_ref[place] + jnp.where(scale_row, line_ref[pl.ds(place, 1), :], 0.0)
+                out[j, :, 4 * width :] = resplit(small)
+                return carry
+
+            lax.fori_loop(0, blocks // 2, body, 0)
+
+
+def attention_back(place, proj, probs, grad_mixed, grad_hidden, tok_pad, in_matrix, gains, grad_out, small):
+    padded, width = grad_hidden.shape
+    images = padded // PAD
+    blocks = small.shape[0]
+    rows = width // blocks
+    row = lambda lanes: pl.BlockSpec((PAD, lanes), lambda i, m: (i, 0))
+    once = lambda a: pl.BlockSpec(a.shape, lambda i, m: (0,) * a.ndim, pipeline_mode=pl.Buffered(1))
+    half = (blocks // 2, rows, 4 * width + 128)
+    return pl.pallas_call(
+        attention_back_kernel,
+        grid_spec=pltpu.PrefetchScalarGridSpec(
+            num_scalar_prefetch=1,
+            grid=(images,),
+            in_specs=[
+                row(3 * width), pl.BlockSpec((1, HEADS, PAD, PAD), lambda i, m: (i, 0, 0, 0)), row(width), row(width),
+                row(width), once(in_matrix), once(gains), once(grad_out), once(small),
+            ],
+            out_specs=[whole((images * SEQ, width)), whole(half), whole(half)],
+            scratch_shapes=[
+                pltpu.VMEM((width, 3 * width), F32), pltpu.VMEM((8, width), F32), pltpu.VMEM((blocks, 128), F32),
+                pltpu.VMEM((PAD, 3 * width), BF), pltpu.VMEM((PAD, width), F32),
+            ],
+        ),
+        out_shape=[
+            jax.ShapeDtypeStruct((images * SEQ, width), F32),
+            jax.ShapeDtypeStruct(half, BF),
+            jax.ShapeDtypeStruct(half, BF),
+        ],
+        compiler_params=params(),
+        name="attention_back",
+    )(place, proj, probs, grad_mixed, grad_hidden, tok_pad, in_matrix, gains, grad_out, small)
+
+
+X_BIT, CORE_BIT, Y_BIT = 16, 8, 1
+Z_BITS = (2, 4, 6)
+AXES = ("rep", "ep")
+
+
+def swap(array, bits):
+    devices = lax.axis_size("rep") * lax.axis_size("ep")
+    return lax.ppermute(array, AXES, [(d, d ^ bits) for d in range(devices)])
+
+
+def relative(position):
+    c, x, y, z = position >> 4 & 1, position >> 3 & 1, position >> 2 & 1, position & 3
+    return x * X_BIT + c * CORE_BIT + z * 2 + y * Y_BIT
+
+
+def gather_all(block):
+    zs = jnp.stack([block] + [swap(block, bits) for bits in Z_BITS])
+    others = [swap(zs, bits) for bits in (Y_BIT, X_BIT, X_BIT | Y_BIT)]
+    plane = jnp.stack([zs] + others)
+    return jnp.stack([plane, swap(plane, CORE_BIT)]).reshape((32,) + block.shape)
+
+
+def sum_everywhere(values):
+    for bits in (CORE_BIT, Y_BIT, X_BIT, 2, 4):
+        values = values + swap(values, bits)
+    return values
+
+
+def unsplit(block):
+    return block[:8] + block[8:]
+
+
+def resplit(small):
+    twice = jnp.concatenate([small, small], axis=0)
+    high = twice.astype(BF).astype(F32)
+    return jnp.where(row_iota(16, 128) < 8, high, twice - high).astype(BF)
+
+
+def block_sum_kernel(parts, terms, *refs):
+    ins, outs = refs[:terms], refs[terms:]
+    size = ins[0].shape[0] // parts
+    lanes = ins[0].shape[2]
+    for p in range(parts):
+        for j in range(size):
+            at = p * size + j
+            total = ins[0][at].astype(F32)
+            for t in ins[1:]:
+                total = total + t[at].astype(F32)
+            small = unsplit(total[:, lanes - 128 :])
+            outs[p][j, :, : lanes - 128] = total[:, : lanes - 128].astype(BF)
+            outs[p][j, :, lanes - 128 :] = resplit(small)
+
+
+def block_sum(terms, parts):
+    size = terms[0].shape[0] // parts
+    shape = (size,) + terms[0].shape[1:]
+    return pl.pallas_call(
+        functools.partial(block_sum_kernel, parts, len(terms)),
+        out_shape=[jax.ShapeDtypeStruct(shape, BF)] * parts,
+        compiler_params=params(),
+        name="block_sum",
+    )(*terms)
+
+
+def last_sum_kernel(*refs):
+    ins, (big_ref, small_ref) = refs[:-2], refs[-2:]
+    lanes = ins[0].shape[2]
+    total = ins[0][0].astype(F32)
+    for t in ins[1:]:
+        total = total + t[0].astype(F32)
+    big_ref[...] = total[:, : lanes - 128]
+    small_ref[...] = unsplit(total[:, lanes - 128 :])
+
+
+def last_sum(terms):
+    lanes = terms[0].shape[2]
+    return pl.pallas_call(
+        last_sum_kernel,
+        out_shape=[jax.ShapeDtypeStruct((16, lanes - 128), F32), jax.ShapeDtypeStruct((8, 128), F32)],
+        compiler_params=params(),
+        name="last_sum",
+    )(*terms)
+
+
+def scatter_dense(near, far):
+    parts = block_sum([near, swap(far, CORE_BIT)], 4)
+    got = [swap(parts[1], Y_BIT), swap(parts[2], X_BIT), swap(parts[3], X_BIT | Y_BIT)]
+    parts = block_sum([parts[0]] + got, 4)
+    return last_sum([parts[0]] + [swap(parts[z], Z_BITS[z - 1]) for z in (1, 2, 3)])
+
+
+def scatter_expert(near, far):
+    got = swap(far, CORE_BIT)
+    shape = (2, 4, 2) + near.shape[2:]
+    near, got = near.reshape(shape), got.reshape(shape)
+    add = lambda cut: near[cut] + got[cut]
+    every = slice(None)
+    a_keep, a_send = add((every, every, 0, 0)), add((every, every, 1, 0))
+    b_keep, b_send = add((0, every, every, 1)), add((1, every, every, 1))
+    a_got, b_got = swap(a_send, Y_BIT), swap(b_send, X_BIT)
+    a_far, b_far = a_keep[1] + a_got[1], b_keep[:, 1] + b_got[:, 1]
+    a_got2, b_got2 = swap(a_far, X_BIT), swap(b_far, Y_BIT)
+    total = lambda z: jnp.stack(
+        [a_keep[0, z] + a_got[0, z] + a_got2[z], b_keep[z, 0] + b_got[z, 0] + b_got2[z]]
+    )
+    result = total(0).astype(F32)
+    for z in (1, 2, 3):
+        result = result + swap(total(z), Z_BITS[z - 1]).astype(F32)
+    return result
+
+
+CHUNKS = 2
+
+
+def replicate_plan(
+    tokens, cotangent, expert_ids, priority,
+    heads_in, heads_in_first, heads_in_second, heads_out, heads_out_first, heads_out_second,
+    router, router_first, router_second, scales, scales_first, scales_second,
+    expert_in, expert_in_first, expert_in_second, bias_in, bias_in_first, bias_in_second,
+    expert_out, expert_out_first, expert_out_second, bias_out, bias_out_first, bias_out_second,
+):
+    count, width = tokens.shape
+    images = count // SEQ
+    experts = router.shape[1]
+    rep, ep = lax.axis_size("rep"), lax.axis_size("ep")
+    rep_me, ep_me = lax.axis_index("rep"), lax.axis_index("ep")
+    me = (rep_me * ep + ep_me).astype(jnp.int32)
+    at = jnp.stack([rep_me, ep_me]).astype(jnp.int32)
+    capacity = (5 * expert_ids.shape[1] * count + 4 * experts - 1) // (4 * experts)
+    listed = -(-capacity // 16) * 16
+    hidden_part = FF // rep
+    cols = hidden_part // CHUNKS
+
+    enter_low = expert_in[0].astype(BF)
+    leave_low = expert_out[0].astype(BF).T
+    pieces = [
+        jnp.stack([enter_low[:, k * cols : (k + 1) * cols], leave_low[:, k * cols : (k + 1) * cols]])
+        for k in range(CHUNKS)
+    ]
+    wide = [
+        lax.all_gather(piece[None], AXES, axis=0, tiled=True).reshape(rep, ep, 2, width, cols) for piece in pieces
+    ]
+
+    rows_here = heads_in.shape[0]
+    small = jnp.concatenate([router, scales], axis=1)
+    small = jnp.pad(small, ((0, 0), (0, 128 - small.shape[1])))
+    biases = jnp.concatenate([bias_in.reshape(-1, 128), bias_out.reshape(-1, 128)], axis=0)
+    biases = jnp.pad(biases, ((0, rows_here - biases.shape[0]), (0, 0)))
+    dense = jnp.concatenate([heads_in, heads_out, small, biases], axis=1).astype(BF)
+    order = jnp.array([relative(p) for p in range(rep * ep)], jnp.int32)
+    place = jnp.bitwise_xor(order, me)
+    in_matrix, out_matrix, router_matrix, gains, small_all = assemble(place, gather_all(dense), experts)
+    bias_all = small_all[:, 128:].reshape(rep, ep, rows_here, 128)
+    in_rows = hidden_part // 128
+    enter_bias = bias_all[:, :, :in_rows].reshape(rep, ep, hidden_part).astype(F32).transpose(1, 0, 2)
+    leave_bias = bias_all[:, :, in_rows].astype(F32).transpose(1, 0, 2).reshape(ep, 1, width)
+
+    spread = lambda a, fill: jnp.pad(
+        a.reshape(-1, images, SEQ), ((0, 0), (0, 0), (0, PAD - SEQ)), constant_values=fill
+    ).reshape(-1, images * PAD)
+    ids_rows = spread(expert_ids.T, -1)
+    rows = jnp.concatenate([spread(priority, count), ids_rows], axis=0).astype(F32)
+    rows = jnp.pad(rows, ((0, 5), (0, 0)))
+    lrow, lcol, meta = find_places(rows, rows.T, capacity, experts)
+
+    tok_pad, cot_pad = spread_rows(tokens, cotangent)
+    proj, probs, mixed, hidden, routed, gcol, grow = attention(
+        tok_pad, in_matrix, out_matrix, router_matrix, gains, ids_rows.T
+    )
+    lists = gather(meta, routed, cot_pad, lrow, grow, listed)
+
+    bias_cut = lambda k: enter_bias[:, :, k * cols : (k + 1) * cols]
+    near, far, grad_bias = [], [], []
+    y, d, n, f, b, grad_leave_bias = expert_pass(at, lists, wide[0], bias_cut(0))
+    near.append(n), far.append(f), grad_bias.append(b)
+    y, d, n, f, b = expert_pass(at, lists, wide[1], bias_cut(1), leave_bias, (y, d))
+    near.append(n), far.append(f), grad_bias.append(b)
+    expert_sums = [scatter_expert(n, f) for n, f in zip(near, far)]
+
+    output, grad_hidden, grad_mixed, grad_out, grad_router, grad_scale = combine(
+        meta, y, d, lcol, gcol, hidden, cot_pad, mixed, out_matrix, router_matrix, gains
+    )
+    devices = rep * ep
+    by_device = lambda a: jnp.pad(
+        a.reshape(a.shape[0], devices, rows_here).transpose(1, 0, 2).reshape(devices, 1, -1),
+        ((0, 0), (0, 0), (0, 128 - a.shape[0] * rows_here)),
+    )
+    small_grads = jnp.concatenate(
+        [
+            jnp.concatenate(grad_bias, axis=2).transpose(1, 0, 2).reshape(devices, in_rows, 128),
+            grad_leave_bias.reshape(ep, rep, 128).transpose(1, 0, 2).reshape(devices, 1, 128),
+            by_device(grad_router),
+            by_device(grad_scale[:5]),
+        ],
+        axis=1,
+    )
+    small_grads = jnp.pad(small_grads, ((0, 0), (0, 8 - small_grads.shape[1]), (0, 0)))
+    input_grad, near_dense, far_dense = attention_back(
+        place, proj, probs, grad_mixed, grad_hidden, tok_pad, in_matrix, gains, grad_out, small_grads
+    )
+    big, small = scatter_dense(near_dense, far_dense)
+    grads_now = (
+        big[:, : 3 * width],
+        big[:, 3 * width :],
+        small[in_rows + 1].reshape(experts, rows_here).T,
+        small[in_rows + 2, : 5 * rows_here].reshape(5, rows_here).T,
+        jnp.concatenate([total[0] for total in expert_sums], axis=1)[None],
+        small[:in_rows].reshape(1, hidden_part),
+        jnp.concatenate([total[1] for total in expert_sums], axis=1).T[None],
+        small[in_rows][None],
+    )
+    weights_now = (heads_in, heads_out, router, scales, expert_in, bias_in, expert_out, bias_out)
+    firsts = (
+        heads_in_first, heads_out_first, router_first, scales_first,
+        expert_in_first, bias_in_first, expert_out_first, bias_out_first,
+    )
+    seconds = (
+        heads_in_second, heads_out_second, router_second, scales_second,
+        expert_in_second, bias_in_second, expert_out_second, bias_out_second,
+    )
+    states = [moments(w, g, f, s) for w, g, f, s in zip(weights_now, grads_now, firsts, seconds)]
+    weight_terms = jnp.concatenate([squares(w, index == 3) for index, w in enumerate(weights_now)])
+    step_terms = jnp.concatenate([squares(state[2], index == 3) for index, state in enumerate(states)])
+    totals = sum_everywhere(jnp.stack([weight_terms, step_terms]))
+    return (output, input_grad) + finish(totals, weights_now, states, width, experts)
+
+
 def expert_front(rows, enter_weight, enter_bias):
     pre = jnp.einsum("sjcd,jdf->sjcf", rows, enter_weight, preferred_element_type=jnp.float32)
     return pre + enter_bias.astype(jnp.float32)[None, :, None, :]
 
 
-def on_device(
+def exchange_plan(
     tokens,
     cotangent,
     expert_ids,
@@ -303,21 +1153,7 @@
         [squares(state[2], index == 3) for index, state in enumerate(states)]
     )
     totals = lax.psum(jnp.stack([weight_terms, step_terms]), ("rep", "ep"))
-    counts = jnp.array(
-        [3 * width * width, width * width, width * experts]
-        + [width] * 5
-        + [experts * width * FF, experts * FF, experts * FF * width, experts * width],
-        jnp.float32,
-    )
-    weight_rms = jnp.sqrt(totals[0] / counts)
-    step_rms = jnp.sqrt(totals[1] / counts)
-    trust = weight_rms / step_rms
-    bounds = [(0, 1), (1, 2), (2, 3), (3, 8), (8, 9), (9, 10), (10, 11), (11, 12)]
-    results = [output, input_grad]
-    for weight, state, bound in zip(weights_now, states, bounds):
-        results.extend([state[0], state[1], weight - RATE * trust[bound[0] : bound[1]] * state[2]])
-    results.append(jnp.stack([weight_rms, step_rms, trust]))
-    return tuple(results)
+    return (output, input_grad) + finish(totals, weights_now, states, width, experts)
 
 
 def solution(mesh):
@@ -380,6 +1216,11 @@
         P("ep", "rep"),
         P(),
     )
+    replicated = mesh.shape["rep"] == 4 and mesh.shape["ep"] == 8
     return jax.shard_map(
-        on_device, mesh=mesh, in_specs=in_specs, out_specs=out_specs, check_vma=False
-    )
+        replicate_plan if replicated else exchange_plan,
+        mesh=mesh,
+        in_specs=in_specs,
+        out_specs=out_specs,
+        check_vma=False,
+    )

time: 1990 us -> 744 us (0.37)
  matrix products: 459 us -> 0 us
  waiting for transfers between devices: 650 us -> 259 us
  blocking collectives: 351 us -> 0 us
  Pallas kernels: 0 us -> 308 us
  local copies, waits for them, and re-layouts: 313 us -> 29.6 us
  other arithmetic: 163 us -> 68.2 us
  starting transfers between devices: 21.9 us -> 50.2 us
    dot_general x20 -> x0, matrix products: 456 us -> none  [the longest x1 107 us: on_device(): jnp.einsum('sjcf,sjcd->jfd', act_low, grad_arrived, preferred_element_typ...]
    all_gather x5 -> x0, blocking collectives: 311 us -> none  [the longest x1 164 us: on_device(): lax.all_gather(router.astype(jnp.bfloat16), ('rep', 'ep'), axis=0, tiled=...]
    pallas_call x0 -> x12, Pallas kernels: none -> 308 us  [the longest x2 114 us: expert_pass(): pl.pallas_call(functools.partial(expert_kernel, last), grid_spec=pltpu.Pr...]
    reduce_scatter x4 -> x0, waiting for transfers between devices: 261 us -> none  [the longest x1 132 us: on_device(): lax.psum_scatter(grad_out_matrix, ('rep', 'ep'), scatter_dimension=0, til...]
    unnamed x15 -> x2, waiting for transfers between devices: 258 us -> 0.03 us
    ppermute x0 -> x35, waiting for transfers between devices: none -> 209 us  [swap(): return lax.ppermute(array, AXES, [(d, d ^ bits) for d in range(devices)])]
    gather x7 -> x0, local copies, waits for them, and re-layouts: 113 us -> none  [the longest x1 25.8 us: on_device(): gate_list[pair_of_slot][:, None]]
    all_to_all x4 -> x0, waiting for transfers between devices: 93.5 us -> none  [the longest x1 60.9 us: on_device(): lax.all_to_all(grad_slots.reshape(groups, local, capacity, width), 'ep',...]
  transfers between devices with their start and end apart: 15 -> 37, of which waited for: 10 -> 26; matrix products, arithmetic and copies ran while one was open for 30% -> 8% of each run, Pallas kernels for 0% -> 42%
where the time goes in v1:
time: 744 us; the launch traced here: 734 us
  Pallas kernels  308 us (41%)
  waiting for transfers between devices  259 us (35%)
  other arithmetic  68.2 us (9%)
  starting transfers between devices  50.2 us (7%)
  local copies, waits for them, and re-layouts  29.6 us (4%)
  between operations  19.5 us (3%)
    ppermute x35, waiting for transfers between devices, swap(): return lax.ppermute(array, AXES, [(d, d ^ bits) for d in range(devices)])  209 us
    pallas_call x2, Pallas kernels, expert_pass(): pl.pallas_call(functools.partial(expert_kernel, last), grid_spec=pltpu.Pr...  114 us
    pallas_call x1, Pallas kernels, attention_back(): pl.pallas_call(attention_back_kernel, grid_spec=pltpu.PrefetchScalarGridS...  51 us
    pallas_call x1, Pallas kernels, combine(): pl.pallas_call(combine_kernel, grid_spec=pltpu.PrefetchScalarGridSpec(num...  50.4 us
    ppermute x35, starting transfers between devices, swap(): return lax.ppermute(array, AXES, [(d, d ^ bits) for d in range(devices)])  50.1 us
    all_gather x2, waiting for transfers between devices, replicate_plan(): lax.all_gather(piece[None], AXES, axis=0, tiled=True)  49.3 us
    pallas_call x1, Pallas kernels, attention(): pl.pallas_call(attention_kernel, grid=(images,), in_specs=[row(width), on...  27.9 us
    pallas_call x1, Pallas kernels, gather(): pl.pallas_call(gather_kernel, grid_spec=pltpu.PrefetchScalarGridSpec(num_...  27.6 us
  transfers between devices with their start and end apart: 37, of which 26 were waited for; matrix products, arithmetic and copies ran while one was open for 8% of the time, Pallas kernels for 42%

profile of v1, /device:TPU:0, one launch (start us, length us, event | category | flops | bytes accessed | tf_op | source)
XLA Modules:
  0.0 734.1 jit_solution(6480369757823850809)
XLA Ops:
  7.3 1.5 copy.157
  11.0 3.1 collective-permute-start
  14.1 2.6 collective-permute-start.1
  16.8 5.1 collective-permute-done.1
  23.0 1.6 collective-permute-start.3
  26.6 8.2 %collective-permute-done.3 = bf16[4,16,2304]{2,1,0:T(8,128)(2,1)S(1)} collective-permute-done((bf16[4,16,2304]{2,1,0:T(8,128)(2,1)S(1)}, bf16[4,16,2304]{2,1,0:T(8,128)(2,1)S(1)}, u32[]{:S(2)}, u32[]{:S(2)}) %collective-permute-start.3) | collective-permute-done | bytes 294944 | tf_op jit(solution)/shard_map/ppermute | solution.py:700
  34.8 1.8 collective-permute-done.4
  36.6 4.6 collective-permute-done.5
  41.2 1.6 fusion.51
  46.2 1.6 copy-done.7
  48.5 4.6 spread_rows.1
  54.8 9.5 %places.1 = (f32[10,8,208]{2,1,0:T(8,128)}, f32[2080,8]{1,0:T(8,128)}, s32[20,8]{1,0:T(8,128)}) custom-call(f32[8,2080]{1,0:T(8,128)} %pad.30.clone.rows_ref, f32[2080,8]{1,0:T(8,128)} %pad_bitcast_fusion.cols_ref), custom_call_target="tpu_custom_call" | custom-call | tf_op jit(solution)/shard_map/places/pallas_call | solution.py:207
  65.4 2.9 pad_maximum_fusion
  68.3 16.4 %assemble.1 = (bf16[512,1536]{1,0:T(8,128)(2,1)}, bf16[512,512]{1,0:T(8,128)(2,1)}, bf16[8,512]{1,0:T(8,128)(2,1)}, f32[8,512]{1,0:T(8,128)}, bf16[512,256]{1,0:T(8,128)(2,1)}) custom-call(s32[32]{0:T(128)} %broadcast_xor_fusion.place_ref, bf16[32,16,2304]{2,1,0:T(8,128)(2,1)} %bitcast.300), custom_call_target="tpu_custom_call" | custom-call | tf_op jit(solution)/shard_map/assemble/pallas_call | solution.py:148
  85.8 27.9 %attention.1 = (bf16[2080,1536]{1,0:T(8,128)(2,1)}, bf16[10,8,208,208]{3,2,1,0:T(8,128)(2,1)}, bf16[2080,512]{1,0:T(8,128)(2,1)}, f32[2080,512]{1,0:T(8,128)}, b...) custom-call(bf16[2080,512]{1,0:T(8,128)(2,1)} %get-tuple-element.79.tok_ref.tpad_ref, ...), custom_call_target="tpu_custom_call" | custom-call | tf_op jit(solution)/shard_map/attention/pallas_call | solution.py:297
  113.7 27.6 %gather.1 = (bf16[8,624,512]{2,1,0:T(8,128)(2,1)}, bf16[8,624,512]{2,1,0:T(8,128)(2,1)}, bf16[8,512,624]{2,1,0:T(8,128)(2,1)}, bf16[8,512,624]{2,1,0:T(8,128)(2,1)}) custom-call(s32[20,8]{1,0:T(8,128)} %get-tuple-element.78.meta_ref, bf16[2080,512]{1,0:T(8,128)(2,1)} %get-tuple-element.84.routed_ref, bf16[2080,512]{1,0:T(8,128)(2,1)} %get-tuple-element.85.cot_ref, ...), custom_call_target="tpu_custom_call" | custom-call | tf_op jit(solution)/shard_map/gather/pallas_call | solution.py:360
  142.5 56.7 %experts_first.1 = (f32[8,624,512]{2,1,0:T(8,128)}, f32[8,624,512]{2,1,0:T(8,128)}, bf16[2,8,2,512,256]{4,3,2,1,0:T(8,128)(2,1)}, bf16[2,8,2,512,256]{4,3,2,1,0:...) custom-call(s32[2]{0:T(128)} %pad_add_fusion.at_ref, bf16[8,624,512]{2,1,0:T(8,128)(2,1)} %get-tuple-element.88.refs_0_, ...), custom_call_target="tpu_custom_call" | custom-call | flops 31406948352 | bytes 60000000 | tf_op jit(solution)/shard_map/experts_first/pallas_call | solution.py:455
  199.7 49.3 %all-gather.5.cloned.1.call-done = bf16[64,512,256]{2,1,0:T(8,128)(2,1)} async-done(((bf16[2,512,256]{2,1,0:T(8,128)(2,1)}), bf16[64,512,256]{2,1,0:T(8,128)(2,1)}) %all-gather.5.cloned.1.call-update) | async-done | bytes 16777232 | tf_op jit(solution)/shard_map/all_gather | solution.py:833
  249.0 57.7 %experts_last.1 = (bf16[8,624,512]{2,1,0:T(8,128)(2,1)}, bf16[8,624,512]{2,1,0:T(8,128)(2,1)}, bf16[2,8,2,512,256]{4,3,2,1,0:T(8,128)(2,1)}, bf16[2,8,2,512,256]{4,3,2,1,0:T(8,128)(2,1)}, f32[8,4,256]{2,1,0:T(4,128)}) custom-call(s32[2]{0:T(128)} %pad_add_fusion.at_ref, bf16[8,624,512]{2,1,0:T(8,128)(2,1)} %get-tuple-element.88.refs_0_, ...), custom_call_target="tpu_custom_call" | custom-call | flops 31406948352 | bytes 60000000 | tf_op jit(solution)/shard_map/experts_last/pallas_call | solution.py:455
  307.9 50.4 %combine.1 = (f32[1970,512]{1,0:T(8,128)}, f32[2080,512]{1,0:T(8,128)}, bf16[2080,512]{1,0:T(8,128)(2,1)}, f32[512,512]{1,0:T(8,128)}, f32[8,512]{1,0:T(8,128)}, /*index=5*/f32[8,512]{1,0:T(8,128)}) custom-call(s32[20,8]{1,0:T(8,128)} %get-tuple-element.78.meta_ref, bf16[8,624,512]{2,1,0:T(8,128)(2,1)} %get-tuple-element.95.y_ref, ...), custom_call_target="tpu_custom_call" | custom-call | tf_op jit(solution)/shard_map/combine/pallas_call | solution.py:554
  361.0 51.0 %attention_back.1 = (f32[1970,512]{1,0:T(8,128)}, bf16[16,16,2176]{2,1,0:T(8,128)(2,1)}, bf16[16,16,2176]{2,1,0:T(8,128)(2,1)}) custom-call(s32[32]{0:T(128)} %broadcast_xor_fusion.place_ref, bf16[2080,1536]{1,0:T(8,128)(2,1)} %get-tuple-element.102.proj_ref, bf16[10,8,208,208]{3,2,1,0:T(8,128)(2,1)} %get-tuple-element.103.prob_ref, ...), custom_call_target="tpu_custom_call" | custom-call | tf_op jit(solution)/shard_map/attention_back/pallas_call | solution.py:668
  412.3 2.7 collective-permute-done.7.refs_1_
  416.0 2.6 block_sum.2
  418.7 1.5 collective-permute-start.10
  422.2 7.1 collective-permute-done.10.refs_3_
  429.3 5.2 collective-permute-done.8.refs_1_
  435.4 2.0 block_sum.3
  437.7 1.6 collective-permute-start.12
  439.3 2.5 collective-permute-start.13
  442.8 4.0 collective-permute-done.12.refs_2_
  447.4 1.7 last_sum.1
  449.1 2.0 multiply_reduce_fusion.14
  451.0 5.3 fusion.10
  457.6 5.1 fusion.13
  463.7 3.8 fusion.3
  468.9 3.5 fusion.6
  476.9 1.7 multiply_reduce_fusion.5
  478.6 26.6 %collective-permute-done.17 = bf16[4,2,512,256]{3,2,1,0:T(8,128)(2,1)} collective-permute-done((bf16[4,2,512,256]{3,2,1,0:T(8,128)(2,1)}, bf16[4,2,512,256]{3,2,1,0:T(8,128)(2,1)}, u32[]{:S(2)}, u32[]{:S(2)}) %collective-permute-start.17) | collective-permute-done | bytes 2097184 | tf_op jit(solution)/shard_map/ppermute | solution.py:700
  505.2 1.6 fusion.20
  506.9 1.5 collective-permute-start.18
  508.5 3.1 collective-permute-done.15
  515.3 34.9 %collective-permute-done.25 = bf16[4,2,512,256]{3,2,1,0:T(8,128)(2,1)} collective-permute-done((bf16[4,2,512,256]{3,2,1,0:T(8,128)(2,1)}, bf16[4,2,512,256]{3,2,1,0:T(8,128)(2,1)}, u32[]{:S(2)}, u32[]{:S(2)}) %collective-permute-start.25) | collective-permute-done | bytes 2097184 | tf_op jit(solution)/shard_map/ppermute | solution.py:700
  551.6 1.5 collective-permute-start.26
  553.1 3.4 collective-permute-done.23
  559.0 19.9 %collective-permute-done.18 = bf16[4,512,256]{2,1,0:T(8,128)(2,1)S(1)} collective-permute-done((bf16[4,512,256]{2,1,0:T(8,128)(2,1)S(1)}, bf16[4,512,256]{2,1,0:T(8,128)(2,1)S(1)}, u32[]{:S(2)}, u32[]{:S(2)}) %collective-permute-start.18) | collective-permute-done | bytes 1048608 | tf_op jit(solution)/shard_map/ppermute | solution.py:700
  584.5 2.0 collective-permute-start.21
  586.5 12.2 %collective-permute-done.26 = bf16[4,512,256]{2,1,0:T(8,128)(2,1)S(1)} collective-permute-done((bf16[4,512,256]{2,1,0:T(8,128)(2,1)S(1)}, bf16[4,512,256]{2,1,0:T(8,128)(2,1)S(1)}, u32[]{:S(2)}, u32[]{:S(2)}) %collective-permute-start.26) | collective-permute-done | bytes 1048608 | tf_op jit(solution)/shard_map/ppermute | solution.py:700
  601.6 2.4 collective-permute-start.27
  605.1 1.6 collective-permute-start.29
  606.7 15.0 %collective-permute-done.20 = bf16[2,512,256]{2,1,0:T(8,128)(2,1)S(1)} collective-permute-done((bf16[2,512,256]{2,1,0:T(8,128)(2,1)S(1)}, bf16[2,512,256]{2,1,0:T(8,128)(2,1)S(1)}, u32[]{:S(2)}, u32[]{:S(2)}) %collective-permute-start.20) | collective-permute-done | bytes 524320 | tf_op jit(solution)/shard_map/ppermute | solution.py:700
  622.8 6.7 collective-permute-done.27
  629.4 37.2 %collective-permute-done.28 = bf16[2,512,256]{2,1,0:T(8,128)(2,1)S(1)} collective-permute-done((bf16[2,512,256]{2,1,0:T(8,128)(2,1)S(1)}, bf16[2,512,256]{2,1,0:T(8,128)(2,1)S(1)}, u32[]{:S(2)}, u32[]{:S(2)}) %collective-permute-start.28) | collective-permute-done | bytes 524320 | tf_op jit(solution)/shard_map/ppermute | solution.py:700
  669.2 4.4 multiply_reduce_fusion.2
  673.6 2.7 multiply_reduce_fusion.3
  676.4 5.2 concatenate.77
  681.5 5.7 concatenate.80
  690.8 2.5 collective-permute-done.31
  695.1 2.5 collective-permute-done.32
  697.6 7.3 collective-permute-start.33
  704.9 1.5 collective-permute-done.33
  706.4 3.0 collective-permute-start.34
  709.5 1.5 collective-permute-done.34
  720.0 2.9 multiply_subtract_fusion
  722.9 1.5 multiply_subtract_fusion.1
  (245 shorter events, 66.0 us)
Async XLA Ops:
  7.2 135.3 %all-gather.7.cloned.1.call-start = ((), (), s32[]{:S(2)}) async-start(), calls=%async_computation.1 | async-start | bytes 17301504 | tf_op jit(solution)/shard_map/all_gather | solution.py:833
  9.9 239.1 %all-gather.5.cloned.1.call-start = ((), (), s32[]{:S(2)}) async-start(), calls=%async_computation | async-start | bytes 17301504 | tf_op jit(solution)/shard_map/all_gather | solution.py:833
  11.0 5.8 collective-permute-start
  14.1 7.8 %collective-permute-start.1 = (bf16[16,2304]{1,0:T(8,128)(2,1)S(1)}, bf16[16,2304]{1,0:T(8,128)(2,1)S(1)}, u32[]{:S(2)}, u32[]{:S(2)}) collective-permute-start(bf16[16,2304]{1,0:T(8,128)(2,1)S(1)} %pad_maximum_fusion.13), channel_id=1, source_target_pairs={{0,4},{1,5},{2,6},{3,7},{4,0},{5,1},{6,2},{7,3},{8,12},{9,13},{10,... | collective-permute-start | bytes 221192 | tf_op jit(solution)/shard_map/ppermute | solution.py:700
  16.7 6.3 collective-permute-start.2
  23.0 19.9 %copy-start.37 = (s32[1970,2]{0,1:T(2,128)S(1)}, s32[1970,2]{0,1:T(2,128)}, u32[]{:S(2)}) copy-start(s32[1970,2]{0,1:T(2,128)} %param.32) | copy-start | bytes 47284
  23.0 11.8 %collective-permute-start.3 = (bf16[4,16,2304]{2,1,0:T(8,128)(2,1)S(1)}, bf16[4,16,2304]{2,1,0:T(8,128)(2,1)S(1)}, u32[]{:S(2)}, u32[]{:S(2)}) collective-permute-start(bf16[4,16,2304]{2,1,0:T(8,128)(2,1)S(1)} %pad_maximum_fusion.12), channel_id=1, source_target_pairs={{0,1},{1,0},{2,3},{3,2},{4,5},{5,4},{6,7},{7,6},{8,9},{9,8},{10,11... | collective-permute-start | bytes 884744 | tf_op jit(solution)/shard_map/ppermute | solution.py:700
  24.6 12.0 %collective-permute-start.4 = (bf16[4,16,2304]{2,1,0:T(8,128)(2,1)S(1)}, bf16[4,16,2304]{2,1,0:T(8,128)(2,1)S(1)}, u32[]{:S(2)}, u32[]{:S(2)}) collective-permute-start(bf16[4,16,2304]{2,1,0:T(8,128)(2,1)S(1)} %pad_maximum_fusion.12), channel_id=1, source_target_pairs={{0,16},{1,17},{2,18},{3,19},{4,20},{5,21},{6,22},{7,23},{8,24},{9,... | collective-permute-start | bytes 884744 | tf_op jit(solution)/shard_map/ppermute | solution.py:700
  26.1 15.2 %collective-permute-start.5 = (bf16[4,16,2304]{2,1,0:T(8,128)(2,1)S(1)}, bf16[4,16,2304]{2,1,0:T(8,128)(2,1)S(1)}, u32[]{:S(2)}, u32[]{:S(2)}) collective-permute-start(bf16[4,16,2304]{2,1,0:T(8,128)(2,1)S(1)} %pad_maximum_fusion.12), channel_id=1, source_target_pairs={{0,17},{1,16},{2,19},{3,18},{4,21},{5,20},{6,23},{7,22},{8,25},{9,... | collective-permute-start | bytes 884744 | tf_op jit(solution)/shard_map/ppermute | solution.py:700
  42.8 22.6 %collective-permute-start.6 = (bf16[4,4,16,2304]{3,2,1,0:T(8,128)(2,1)}, bf16[4,4,16,2304]{3,2,1,0:T(8,128)(2,1)}, u32[]{:S(2)}, u32[]{:S(2)}) collective-permute-start(bf16[4,4,16,2304]{3,2,1,0:T(8,128)(2,1)} %get-tuple-element.186), channel_id=1, source_target_pairs={{0,8},{1,9},{2,10},{3,11},{4,12},{5,13},{6,14},{7,15},{8,0},{9,1},... | collective-permute-start | bytes 3538952 | tf_op jit(solution)/shard_map/ppermute | solution.py:700
  53.1 11.8 %copy-start.54 = (s32[32]{0:T(128)S(1)}, s32[32]{0:T(128)}, u32[]{:S(2)}) copy-start(s32[32]{0:T(128)} %constant.34.clone) | copy-start | bytes 388
  53.1 12.3 %copy-start.6 = (bf16[1,4,4,16,2304]{4,3,2,1,0:T(8,128)(2,1)S(1)}, bf16[1,4,4,16,2304]{4,3,2,1,0:T(8,128)(2,1)}, u32[]{:S(2)}) copy-start(bf16[1,4,4,16,2304]{4,3,2,1,0:T(8,128)(2,1)} %get-tuple-element.185) | copy-start | bytes 3538948
  199.2 251.8 %collective-permute-start.14 = (bf16[2,8,2,512,256]{4,3,2,1,0:T(8,128)(2,1)}, bf16[2,8,2,512,256]{4,3,2,1,0:T(8,128)(2,1)}, u32[]{:S(2)}, u32[]{:S(2)}) collective-permute-start(bf16[2,8,2,512,256]{4,3,2,1,0:T(8,128)(2,1)} %get-tuple-element.126), channel_id=1, source_target_pairs={{0,8},{1,9},{2,10},{3,11},{4,12},{5,13},{6,14},{7,15},{8,0},{9,1},... | collective-permute-start | bytes 25165832 | tf_op jit(solution)/shard_map/ppermute | solution.py:700
  249.0 58.1 %copy-start.34 = (f32[8,4,256]{2,1,0:T(4,128)S(1)}, f32[8,4,256]{2,1,0:T(4,128)}, u32[]{:S(2)}) copy-start(f32[8,4,256]{2,1,0:T(4,128)} %get-tuple-element.107) | copy-start | bytes 98308
  306.7 157.0 %collective-permute-start.22 = (bf16[2,8,2,512,256]{4,3,2,1,0:T(8,128)(2,1)}, bf16[2,8,2,512,256]{4,3,2,1,0:T(8,128)(2,1)}, u32[]{:S(2)}, u32[]{:S(2)}) collective-permute-start(bf16[2,8,2,512,256]{4,3,2,1,0:T(8,128)(2,1)} %get-tuple-element.128), channel_id=1, source_target_pairs={{0,8},{1,9},{2,10},{3,11},{4,12},{5,13},{6,14},{7,15},{8,0},{9,1},... | collective-permute-start | bytes 25165832 | tf_op jit(solution)/shard_map/ppermute | solution.py:700
  307.9 52.3 %copy-start.38 = (f32[8,1,512]{2,1,0:T(1,128)S(1)}, f32[8,1,512]{2,1,0:T(1,128)}, u32[]{:S(2)}) copy-start(f32[8,1,512]{2,1,0:T(1,128)} %get-tuple-element.109) | copy-start | bytes 49156
  412.0 37.1 %copy-start.52 = (f32[1,128]{1,0:T(1,128)S(1)}, f32[1,128]{1,0:T(1,128)}, u32[]{:S(2)}) copy-start(f32[1,128]{1,0:T(1,128)} %param.56) | copy-start | bytes 1540
  412.0 37.1 %copy-start.53 = (f32[1,128]{1,0:T(1,128)S(1)}, f32[1,128]{1,0:T(1,128)}, u32[]{:S(2)}) copy-start(f32[1,128]{1,0:T(1,128)} %param.57) | copy-start | bytes 1540
  412.0 3.0 collective-permute-start.7
  418.7 10.6 %collective-permute-start.10 = (bf16[4,16,2176]{2,1,0:T(8,128)(2,1)}, bf16[4,16,2176]{2,1,0:T(8,128)(2,1)S(1)}, u32[]{:S(2)}, u32[]{:S(2)}) collective-permute-start(bf16[4,16,2176]{2,1,0:T(8,128)(2,1)} %get-tuple-element.118), channel_id=1, source_target_pairs={{0,17},{1,16},{2,19},{3,18},{4,21},{5,20},{6,23},{7,22},{8,25},{9,... | collective-permute-start | bytes 835592 | tf_op jit(solution)/shard_map/ppermute | solution.py:700
  420.2 14.4 %collective-permute-start.8 = (bf16[4,16,2176]{2,1,0:T(8,128)(2,1)}, bf16[4,16,2176]{2,1,0:T(8,128)(2,1)S(1)}, u32[]{:S(2)}, u32[]{:S(2)}) collective-permute-start(bf16[4,16,2176]{2,1,0:T(8,128)(2,1)} %get-tuple-element.116), channel_id=1, source_target_pairs={{0,1},{1,0},{2,3},{3,2},{4,5},{5,4},{6,7},{7,6},{8,9},{9,8},{10,11... | collective-permute-start | bytes 835592 | tf_op jit(solution)/shard_map/ppermute | solution.py:700
  421.4 13.3 %collective-permute-start.9 = (bf16[4,16,2176]{2,1,0:T(8,128)(2,1)}, bf16[4,16,2176]{2,1,0:T(8,128)(2,1)S(1)}, u32[]{:S(2)}, u32[]{:S(2)}) collective-permute-start(bf16[4,16,2176]{2,1,0:T(8,128)(2,1)} %get-tuple-element.117), channel_id=1, source_target_pairs={{0,16},{1,17},{2,18},{3,19},{4,20},{5,21},{6,22},{7,23},{8,24},{9,... | collective-permute-start | bytes 835592 | tf_op jit(solution)/shard_map/ppermute | solution.py:700
  437.4 5.4 collective-permute-start.11
  437.7 9.0 %collective-permute-start.12 = (bf16[1,16,2176]{2,1,0:T(8,128)(2,1)}, bf16[1,16,2176]{2,1,0:T(8,128)(2,1)S(1)}, u32[]{:S(2)}, u32[]{:S(2)}) collective-permute-start(bf16[1,16,2176]{2,1,0:T(8,128)(2,1)} %get-tuple-element.121), channel_id=1, source_target_pairs={{0,4},{1,5},{2,6},{3,7},{4,0},{5,1},{6,2},{7,3},{8,12},{9,13},{10,... | collective-permute-start | bytes 208904 | tf_op jit(solution)/shard_map/ppermute | solution.py:700
  439.3 7.4 %collective-permute-start.13 = (bf16[1,16,2176]{2,1,0:T(8,128)(2,1)}, bf16[1,16,2176]{2,1,0:T(8,128)(2,1)S(1)}, u32[]{:S(2)}, u32[]{:S(2)}) collective-permute-start(bf16[1,16,2176]{2,1,0:T(8,128)(2,1)} %get-tuple-element.122), channel_id=1, source_target_pairs={{0,6},{1,7},{2,4},{3,5},{4,2},{5,3},{6,0},{7,1},{8,14},{9,15},{10,... | collective-permute-start | bytes 208904 | tf_op jit(solution)/shard_map/ppermute | solution.py:700
  451.0 12.7 %slice-start = ((s8[8388608]{0:T(1024)(128)(4,1)}), s8[4194304]{0:T(1024)(128)(4,1)S(1)}, s32[]{:S(2)}) async-start(s8[8388608]{0:T(1024)(128)(4,1)} %bitcast.301), calls=%async_computation.2 | async-start | bytes 8388608
  456.3 7.4 %slice-start.1 = ((s8[8388608]{0:T(1024)(128)(4,1)}), s8[4194304]{0:T(1024)(128)(4,1)S(1)}, s32[]{:S(2)}) async-start(s8[8388608]{0:T(1024)(128)(4,1)} %bitcast.301), calls=%async_computation.3 | async-start | bytes 8388608
  456.3 48.9 %collective-permute-start.17 = (bf16[4,2,512,256]{3,2,1,0:T(8,128)(2,1)}, bf16[4,2,512,256]{3,2,1,0:T(8,128)(2,1)}, u32[]{:S(2)}, u32[]{:S(2)}) collective-permute-start(bf16[4,2,512,256]{3,2,1,0:T(8,128)(2,1)} %get-tuple-element.164), channel_id=1, source_target_pairs={{0,16},{1,17},{2,18},{3,19},{4,20},{5,21},{6,22},{7,23},{8,24},{9,... | collective-permute-start | bytes 6291464 | tf_op jit(solution)/shard_map/ppermute | solution.py:700
  462.7 48.9 %collective-permute-start.15 = (bf16[2,4,512,256]{3,2,1,0:T(8,128)(2,1)}, bf16[2,4,512,256]{3,2,1,0:T(8,128)(2,1)}, u32[]{:S(2)}, u32[]{:S(2)}) collective-permute-start(bf16[2,4,512,256]{3,2,1,0:T(8,128)(2,1)} %get-tuple-element.162), channel_id=1, source_target_pairs={{0,1},{1,0},{2,3},{3,2},{4,5},{5,4},{6,7},{7,6},{8,9},{9,8},{10,11... | collective-permute-start | bytes 6291464 | tf_op jit(solution)/shard_map/ppermute | solution.py:700
  467.5 5.9 copy-start.46
  467.5 6.6 copy-start.47
  467.5 6.6 copy-start.48
  467.5 8.0 %copy-start.32 = (f32[16,512]{1,0:T(8,128)S(1)}, f32[16,512]{1,0:T(8,128)}, u32[]{:S(2)}) copy-start(f32[16,512]{1,0:T(8,128)} %param.38) | copy-start | bytes 98308
  467.5 7.9 %copy-start.33 = (f32[16,512]{1,0:T(8,128)S(1)}, f32[16,512]{1,0:T(8,128)}, u32[]{:S(2)}) copy-start(f32[16,512]{1,0:T(8,128)} %param.39) | copy-start | bytes 98308
  467.6 82.6 %collective-permute-start.25 = (bf16[4,2,512,256]{3,2,1,0:T(8,128)(2,1)}, bf16[4,2,512,256]{3,2,1,0:T(8,128)(2,1)}, u32[]{:S(2)}, u32[]{:S(2)}) collective-permute-start(bf16[4,2,512,256]{3,2,1,0:T(8,128)(2,1)} %get-tuple-element.168), channel_id=1, source_target_pairs={{0,16},{1,17},{2,18},{3,19},{4,20},{5,21},{6,22},{7,23},{8,24},{9,... | collective-permute-start | bytes 6291464 | tf_op jit(solution)/shard_map/ppermute | solution.py:700
  472.4 84.2 %collective-permute-start.23 = (bf16[2,4,512,256]{3,2,1,0:T(8,128)(2,1)}, bf16[2,4,512,256]{3,2,1,0:T(8,128)(2,1)}, u32[]{:S(2)}, u32[]{:S(2)}) collective-permute-start(bf16[2,4,512,256]{3,2,1,0:T(8,128)(2,1)} %get-tuple-element.166), channel_id=1, source_target_pairs={{0,1},{1,0},{2,3},{3,2},{4,5},{5,4},{6,7},{7,6},{8,9},{9,8},{10,11... | collective-permute-start | bytes 6291464 | tf_op jit(solution)/shard_map/ppermute | solution.py:700
  473.4 38.2 %copy-start.4 = (bf16[2,4,1,1,512,256]{5,4,1,0,3,2:T(8,128)(2,1)S(1)}, bf16[2,4,1,1,512,256]{5,4,1,0,3,2:T(8,128)(2,1)}, u32[]{:S(2)}) copy-start(bf16[2,4,1,1,512,256]{5,4,1,0,3,2:T(8,128)(2,1)} %get-tuple-element.161) | copy-start | bytes 6291460
  474.1 251.0 %copy-start.39 = (f32[16,8]{0,1:T(8,128)}, f32[16,8]{0,1:T(8,128)S(1)}, u32[]{:S(2)}) copy-start(f32[16,8]{0,1:T(8,128)S(1)} %get-tuple-element.155) | copy-start | bytes 1540
  474.1 251.0 %copy-start.40 = (f32[16,8]{0,1:T(8,128)}, f32[16,8]{0,1:T(8,128)S(1)}, u32[]{:S(2)}) copy-start(f32[16,8]{0,1:T(8,128)S(1)} %get-tuple-element.156) | copy-start | bytes 1540
  476.9 248.8 %copy-start.23 = (f32[16,512]{1,0:T(8,128)}, f32[16,512]{1,0:T(8,128)S(1)}, u32[]{:S(2)}) copy-start(f32[16,512]{1,0:T(8,128)S(1)} %get-tuple-element.157) | copy-start | bytes 98308
  476.9 248.8 %copy-start.24 = (f32[16,512]{1,0:T(8,128)}, f32[16,512]{1,0:T(8,128)S(1)}, u32[]{:S(2)}) copy-start(f32[16,512]{1,0:T(8,128)S(1)} %get-tuple-element.158) | copy-start | bytes 98308
  478.6 247.8 %copy-start.18 = (f32[16,1536]{1,0:T(8,128)}, f32[16,1536]{1,0:T(8,128)S(1)}, u32[]{:S(2)}) copy-start(f32[16,1536]{1,0:T(8,128)S(1)} %get-tuple-element.159) | copy-start | bytes 294916
  478.6 247.8 %copy-start.19 = (f32[16,1536]{1,0:T(8,128)}, f32[16,1536]{1,0:T(8,128)S(1)}, u32[]{:S(2)}) copy-start(f32[16,1536]{1,0:T(8,128)S(1)} %get-tuple-element.160) | copy-start | bytes 294916
  506.9 7.3 copy-start.36
  506.9 7.2 copy-start.50
  506.9 7.2 copy-start.51
  506.9 43.3 %copy-start.3 = (bf16[4,2,512,256]{3,2,1,0:T(8,128)(2,1)S(1)}, bf16[4,2,512,256]{3,2,1,0:T(8,128)(2,1)}, u32[]{:S(2)}) copy-start(bf16[4,2,512,256]{3,2,1,0:T(8,128)(2,1)} %get-tuple-element.167) | copy-start | bytes 6291460
  506.9 72.0 %collective-permute-start.18 = (bf16[4,512,256]{2,1,0:T(8,128)(2,1)S(1)}, bf16[4,512,256]{2,1,0:T(8,128)(2,1)S(1)}, u32[]{:S(2)}, u32[]{:S(2)}) collective-permute-start(bf16[4,512,256]{2,1,0:T(8,128)(2,1)S(1)} %fusion.20), channel_id=1, source_target_pairs={{0,1},{1,0},{2,3},{3,2},{4,5},{5,4},{6,7},{7,6},{8,9},{9,8},{10,11... | collective-permute-start | bytes 3145736 | tf_op jit(solution)/shard_map/ppermute | solution.py:700
  513.0 67.4 %collective-permute-start.16 = (bf16[4,512,256]{2,1,0:T(8,128)(2,1)S(1)}, bf16[4,512,256]{2,1,0:T(8,128)(2,1)S(1)}, u32[]{:S(2)}, u32[]{:S(2)}) collective-permute-start(bf16[4,512,256]{2,1,0:T(8,128)(2,1)S(1)} %fusion.21), channel_id=1, source_target_pairs={{0,16},{1,17},{2,18},{3,19},{4,20},{5,21},{6,22},{7,23},{8,24},{9,... | collective-permute-start | bytes 3145736 | tf_op jit(solution)/shard_map/ppermute | solution.py:700
  551.5 27.3 %copy-start.5 = (bf16[4,2,512,256]{3,2,1,0:T(8,128)(2,1)S(1)}, bf16[4,2,512,256]{3,2,1,0:T(8,128)(2,1)}, u32[]{:S(2)}) copy-start(bf16[4,2,512,256]{3,2,1,0:T(8,128)(2,1)} %get-tuple-element.163) | copy-start | bytes 6291460
  551.6 47.2 %collective-permute-start.26 = (bf16[4,512,256]{2,1,0:T(8,128)(2,1)S(1)}, bf16[4,512,256]{2,1,0:T(8,128)(2,1)S(1)}, u32[]{:S(2)}, u32[]{:S(2)}) collective-permute-start(bf16[4,512,256]{2,1,0:T(8,128)(2,1)S(1)} %fusion.18), channel_id=1, source_target_pairs={{0,1},{1,0},{2,3},{3,2},{4,5},{5,4},{6,7},{7,6},{8,9},{9,8},{10,11... | collective-permute-start | bytes 3145736 | tf_op jit(solution)/shard_map/ppermute | solution.py:700
  557.9 42.3 %collective-permute-start.24 = (bf16[4,512,256]{2,1,0:T(8,128)(2,1)S(1)}, bf16[4,512,256]{2,1,0:T(8,128)(2,1)S(1)}, u32[]{:S(2)}, u32[]{:S(2)}) collective-permute-start(bf16[4,512,256]{2,1,0:T(8,128)(2,1)S(1)} %fusion.19), channel_id=1, source_target_pairs={{0,16},{1,17},{2,18},{3,19},{4,20},{5,21},{6,22},{7,23},{8,24},{9,... | collective-permute-start | bytes 3145736 | tf_op jit(solution)/shard_map/ppermute | solution.py:700
  581.8 23.2 %collective-permute-start.19 = (bf16[2,512,256]{2,1,0:T(8,128)(2,1)S(1)}, bf16[2,512,256]{2,1,0:T(8,128)(2,1)S(1)}, u32[]{:S(2)}, u32[]{:S(2)}) collective-permute-start(bf16[2,512,256]{2,1,0:T(8,128)(2,1)S(1)} %pad_maximum_fusion.6), channel_id=1, source_target_pairs={{0,2},{1,3},{2,0},{3,1},{4,6},{5,7},{6,4},{7,5},{8,10},{9,11},{10,... | collective-permute-start | bytes 1572872 | tf_op jit(solution)/shard_map/ppermute | solution.py:700
  583.3 38.3 %collective-permute-start.20 = (bf16[2,512,256]{2,1,0:T(8,128)(2,1)S(1)}, bf16[2,512,256]{2,1,0:T(8,128)(2,1)S(1)}, u32[]{:S(2)}, u32[]{:S(2)}) collective-permute-start(bf16[2,512,256]{2,1,0:T(8,128)(2,1)S(1)} %pad_maximum_fusion.7), channel_id=1, source_target_pairs={{0,4},{1,5},{2,6},{3,7},{4,0},{5,1},{6,2},{7,3},{8,12},{9,13},{10,... | collective-permute-start | bytes 1572872 | tf_op jit(solution)/shard_map/ppermute | solution.py:700
  584.5 37.1 %collective-permute-start.21 = (bf16[2,512,256]{2,1,0:T(8,128)(2,1)S(1)}, bf16[2,512,256]{2,1,0:T(8,128)(2,1)S(1)}, u32[]{:S(2)}, u32[]{:S(2)}) collective-permute-start(bf16[2,512,256]{2,1,0:T(8,128)(2,1)S(1)} %pad_maximum_fusion.8), channel_id=1, source_target_pairs={{0,6},{1,7},{2,4},{3,5},{4,2},{5,3},{6,0},{7,1},{8,14},{9,15},{10,... | collective-permute-start | bytes 1572872 | tf_op jit(solution)/shard_map/ppermute | solution.py:700
  601.6 27.8 %collective-permute-start.27 = (bf16[2,512,256]{2,1,0:T(8,128)(2,1)S(1)}, bf16[2,512,256]{2,1,0:T(8,128)(2,1)S(1)}, u32[]{:S(2)}, u32[]{:S(2)}) collective-permute-start(bf16[2,512,256]{2,1,0:T(8,128)(2,1)S(1)} %pad_maximum_fusion.9), channel_id=1, source_target_pairs={{0,2},{1,3},{2,0},{3,1},{4,6},{5,7},{6,4},{7,5},{8,10},{9,11},{10,... | collective-permute-start | bytes 1572872 | tf_op jit(solution)/shard_map/ppermute | solution.py:700
  604.1 62.5 %collective-permute-start.28 = (bf16[2,512,256]{2,1,0:T(8,128)(2,1)S(1)}, bf16[2,512,256]{2,1,0:T(8,128)(2,1)S(1)}, u32[]{:S(2)}, u32[]{:S(2)}) collective-permute-start(bf16[2,512,256]{2,1,0:T(8,128)(2,1)S(1)} %pad_maximum_fusion.10), channel_id=1, source_target_pairs={{0,4},{1,5},{2,6},{3,7},{4,0},{5,1},{6,2},{7,3},{8,12},{9,13},{10,... | collective-permute-start | bytes 1572872 | tf_op jit(solution)/shard_map/ppermute | solution.py:700
  605.1 61.5 %collective-permute-start.29 = (bf16[2,512,256]{2,1,0:T(8,128)(2,1)S(1)}, bf16[2,512,256]{2,1,0:T(8,128)(2,1)S(1)}, u32[]{:S(2)}, u32[]{:S(2)}) collective-permute-start(bf16[2,512,256]{2,1,0:T(8,128)(2,1)S(1)} %pad_maximum_fusion.11), channel_id=1, source_target_pairs={{0,6},{1,7},{2,4},{3,5},{4,2},{5,3},{6,0},{7,1},{8,14},{9,15},{10,... | collective-permute-start | bytes 1572872 | tf_op jit(solution)/shard_map/ppermute | solution.py:700
  673.6 46.3 %copy-start.8 = (f32[1,512,512]{2,1,0:T(8,128)}, f32[1,512,512]{2,1,0:T(8,128)S(1)}, u32[]{:S(2)}) copy-start(f32[1,512,512]{2,1,0:T(8,128)S(1)} %get-tuple-element.145) | copy-start | bytes 3145732
  687.9 1.1 collective-permute-start.30
  689.8 3.6 collective-permute-start.31
  694.0 3.6 collective-permute-start.32
  697.6 8.9 %collective-permute-start.33 = (f32[2,12]{1,0:T(2,128)S(1)}, f32[2,12]{1,0:T(2,128)S(1)}, u32[]{:S(2)}, u32[]{:S(2)}) collective-permute-start(f32[2,12]{1,0:T(2,128)S(1)} %add.627), channel_id=1, source_target_pairs={{0,2},{1,3},{2,0},{3,1},{4,6},{5,7},{6,4},{7,5},{8,10},{9,11},{10,... | collective-permute-start | bytes 296 | tf_op jit(solution)/shard_map/ppermute | solution.py:700
  706.4 4.6 collective-permute-start.34
  (30 other events, 76.5 us)
Sparse Core Ops, SparseCore 0:
  11.7 120.4 all-gather.6
  135.8 113.1 all-gather.4

commit v2 on v1

--- a/solution.py
+++ b/solution.py
@@ -120,37 +120,49 @@
     return pl.BlockSpec(shape, lambda *_: (0,) * len(shape))
 
 
-def params(semantics=None, **kw):
+def cost(micros):
+    return pl.CostEstimate(flops=int(micros * 1e9), bytes_accessed=int(micros * 1e5), transcendentals=0)
+
+
+def params(**kw):
     return pltpu.CompilerParams(vmem_limit_bytes=VMEM, **kw)
 
 
-def assemble_kernel(place_ref, got_ref, in_ref, out_ref, router_ref, gains_ref, small_ref):
-    copies, rows = got_ref.shape[0], got_ref.shape[1]
+def behind(kernel, inputs, after):
+    def body(*refs):
+        return kernel(*refs[:inputs], *refs[inputs + len(after) :])
+
+    return body
+
+
+def unread(after):
+    return [pl.BlockSpec(memory_space=pl.ANY)] * len(after)
+
+
+def assemble_kernel(place_ref, near_ref, far_ref, in_ref, out_ref, router_ref, gains_ref, small_ref):
+    copies, rows = near_ref.shape[0], near_ref.shape[1]
     width = out_ref.shape[1]
-
-    def body(j, carry):
-        place = pl.multiple_of(place_ref[j] * rows, rows)
-        in_ref[pl.ds(place, rows), :] = got_ref[j, :, : 3 * width]
-        out_ref[pl.ds(place, rows), :] = got_ref[j, :, 3 * width : 4 * width]
-        small_ref[pl.ds(place, rows), :] = got_ref[j, :, 4 * width :]
-        return carry
-
-    lax.fori_loop(0, copies, body, 0)
+    for side, got_ref in enumerate((near_ref, far_ref)):
+        for j in range(copies):
+            place = pl.multiple_of(place_ref[side * copies + j] * rows, rows)
+            in_ref[pl.ds(place, rows), :] = got_ref[j, :, : 3 * width]
+            out_ref[pl.ds(place, rows), :] = got_ref[j, :, 3 * width : 4 * width]
+            small_ref[pl.ds(place, rows), :] = got_ref[j, :, 4 * width :]
     turned = small_ref[:, :128].astype(F32).T
     experts = router_ref.shape[0]
     router_ref[...] = turned[:experts].astype(BF)
     gains_ref[...] = turned[experts : experts + 8]
 
 
-def assemble(place, got, experts):
-    copies, rows, lanes = got.shape
-    width = copies * rows
+def assemble(place, near, far, experts):
+    copies, rows, lanes = near.shape
+    width = 2 * copies * rows
     return pl.pallas_call(
         assemble_kernel,
         grid_spec=pltpu.PrefetchScalarGridSpec(
             num_scalar_prefetch=1,
             grid=(1,),
-            in_specs=[whole(got.shape)],
+            in_specs=[whole(near.shape)] * 2,
             out_specs=[
                 whole((width, 3 * width)),
                 whole((width, width)),
@@ -167,8 +179,9 @@
             jax.ShapeDtypeStruct((width, lanes - 4 * width), BF),
         ],
         compiler_params=params(),
+        cost_estimate=cost(5),
         name="assemble",
-    )(place, got)
+    )(place, near, far)
 
 
 def places_kernel(capacity, rows_ref, cols_ref, lrow_ref, lcol_ref, meta_ref):
@@ -212,6 +225,7 @@
             jax.ShapeDtypeStruct((2 * images, experts), jnp.int32),
         ],
         compiler_params=params(),
+        cost_estimate=cost(9),
         name="places",
     )(rows, cols)
 
@@ -229,7 +243,7 @@
     count, width = tokens.shape
     shape = jax.ShapeDtypeStruct((count // SEQ * PAD, width), BF)
     return pl.pallas_call(
-        spread_kernel, out_shape=[shape, shape], compiler_params=params(), name="spread_rows"
+        spread_kernel, out_shape=[shape, shape], compiler_params=params(), cost_estimate=cost(5), name="spread_rows"
     )(tokens, cotangent)
 
 
@@ -288,16 +302,16 @@
     grow_ref[0] = gates.T
 
 
-def attention(tok_pad, in_matrix, out_matrix, router, gains, ids_col):
+def attention(tok_pad, in_matrix, out_matrix, router, gains, ids_col, after=()):
     padded, width = tok_pad.shape
     images = padded // PAD
     experts = router.shape[0]
     row = lambda lanes: pl.BlockSpec((PAD, lanes), lambda i: (i, 0))
     once = lambda a: pl.BlockSpec(a.shape, lambda i: (0, 0), pipeline_mode=pl.Buffered(1))
     return pl.pallas_call(
-        attention_kernel,
+        behind(attention_kernel, 6, after),
         grid=(images,),
-        in_specs=[row(width), once(in_matrix), once(out_matrix), once(router), once(gains), row(2)],
+        in_specs=[row(width), once(in_matrix), once(out_matrix), once(router), once(gains), row(2)] + unread(after),
         out_specs=[
             row(3 * width),
             pl.BlockSpec((1, HEADS, PAD, PAD), lambda i: (i, 0, 0, 0)),
@@ -315,8 +329,9 @@
         ],
         scratch_shapes=[pltpu.VMEM((PAD, width), BF)],
         compiler_params=params(),
+        cost_estimate=cost(28),
         name="attention",
-    )(tok_pad, in_matrix, out_matrix, router, gains, ids_col)
+    )(tok_pad, in_matrix, out_matrix, router, gains, ids_col, *after)
 
 
 def window_count():
@@ -351,26 +366,27 @@
     gt_ref[0] = g_all[0:listed, :].astype(BF).astype(F32).T.astype(BF)
 
 
-def gather(meta, routed, cot_pad, lrow, grow, listed):
+def gather(meta, routed, cot_pad, lrow, grow, listed, after=()):
     width = routed.shape[1]
     experts = lrow.shape[1]
     once = lambda a: pl.BlockSpec(a.shape, lambda e, m: (0,) * a.ndim, pipeline_mode=pl.Buffered(1))
     block = pl.BlockSpec((1, listed, width), lambda e, m: (e, 0, 0))
     turned = pl.BlockSpec((1, width, listed), lambda e, m: (e, 0, 0))
     return pl.pallas_call(
-        gather_kernel,
+        behind(gather_kernel, 5, after),
         grid_spec=pltpu.PrefetchScalarGridSpec(
             num_scalar_prefetch=1,
             grid=(experts,),
-            in_specs=[once(routed), once(cot_pad), once(lrow), once(grow)],
+            in_specs=[once(routed), once(cot_pad), once(lrow), once(grow)] + unread(after),
             out_specs=[block, block, turned, turned],
             scratch_shapes=[pltpu.VMEM((listed + WIN, width), F32)] * 2,
         ),
         out_shape=[jax.ShapeDtypeStruct((experts, listed, width), BF)] * 2
         + [jax.ShapeDtypeStruct((experts, width, listed), BF)] * 2,
         compiler_params=params(),
+        cost_estimate=cost(25),
         name="gather",
-    )(meta, routed, cot_pad, lrow, grow)
+    )(meta, routed, cot_pad, lrow, grow, *after)
 
 
 def gelu_both(pre):
@@ -382,90 +398,139 @@
     return pre * phi, phi + pre * bell * 0.3989422804014327
 
 
-def expert_kernel(last, at_ref, *refs):
-    if last:
-        (r_ref, g_ref, rt_ref, gt_ref, w_ref, b_ref, ob_ref, y_in, d_in,
-         y_ref, d_ref, near_ref, far_ref, db_ref, y_all, d_all) = refs
+def expert_kernel(first, last, half, at_ref, *refs):
+    rep = 4
+    if first:
+        (r_ref, g_ref, rt_ref, gt_ref, w_ref, b_ref), refs = refs[:6], refs[6 + 2 * (half > 0) :]
+        y_ref, d_ref, near_ref, far_ref, db_ref, obg_ref, y_all, d_all = refs
     else:
-        (r_ref, g_ref, rt_ref, gt_ref, w_ref, b_ref,
-         y_ref, d_ref, near_ref, far_ref, db_ref, obg_ref, y_all, d_all) = refs
-    rep = w_ref.shape[0]
-    rows, grads = r_ref[0], g_ref[0]
-    rows_t, grads_t = rt_ref[0], gt_ref[0]
-    if not last:
-        obg_ref[0] = jnp.sum(grads.astype(F32), axis=0, keepdims=True)
-    for r in range(rep):
-        place = lax.bitwise_xor(at_ref[0], r)
-        enter, leave = w_ref[place, 0, 0], w_ref[place, 0, 1]
-        pre = dot_nn(rows, enter) + b_ref[0, pl.ds(place, 1), :]
-        act, slope = gelu_both(pre)
-        act = act.astype(BF)
-        grad_pre = (dot_nn(grads, leave) * slope).astype(BF)
-        out = far_ref if r % 2 else near_ref
-        out[r // 2, 0, 0] = dot_nn(rows_t, grad_pre).astype(BF)
-        out[r // 2, 0, 1] = dot_nn(grads_t, act).astype(BF)
-        db_ref[0, pl.ds(place, 1), :] = jnp.sum(grad_pre.astype(F32), axis=0, keepdims=True)
-        y_part = dot_nt(act, leave)
-        d_part = dot_nt(grad_pre, enter)
-        if r == 0:
-            y_all[...] = y_part + y_in[0] if last else y_part
-            d_all[...] = d_part + d_in[0] if last else d_part
+        (r_ref, g_ref, rt_ref, gt_ref), w_refs, refs = refs[:4], refs[4:12], refs[12:]
+        (b_ref, ob_ref, y_in, d_in), refs = refs[:4], refs[4 + 2 * (half > 0) :]
+        y_ref, d_ref, near_ref, far_ref, db_ref, y_all, d_all = refs
+    listed = r_ref.shape[1]
+    step = pl.program_id(0)
+    count = at_ref[2 + lax.bitwise_xor(expert_rank(step, half), at_ref[1])]
+
+    def run(n):
+        rows_t, grads_t = rt_ref[0, :, :n], gt_ref[0, :, :n]
+
+        def weights(r):
+            place = lax.bitwise_xor(at_ref[0], r)
+            if first:
+                return place, w_ref[place, 0, 0], w_ref[place, 0, 1]
+            return place, w_refs[r][0], w_refs[rep + r][0]
+
+        def enter_part(r):
+            place, enter, leave = weights(r)
+            pre = dot_nn(r_ref[0, :n, :], enter) + b_ref[0, pl.ds(place, 1), :]
+            return pre, dot_nn(g_ref[0, :n, :], leave)
+
+        def middle_part(pre, grad_act):
+            act, slope = gelu_both(pre)
+            return act.astype(BF), (grad_act * slope).astype(BF)
+
+        def leave_part(r, act, grad_pre):
+            place, enter, leave = weights(r)
+            out = far_ref if r % 2 else near_ref
+            out[r // 2, 0, 0] = dot_nn(rows_t, grad_pre).astype(BF)
+            out[r // 2, 0, 1] = dot_nn(grads_t, act).astype(BF)
+            db_ref[0, pl.ds(place, 1), :] = jnp.sum(grad_pre.astype(F32), axis=0, keepdims=True)
+            y_part = dot_nt(act, leave)
+            d_part = dot_nt(grad_pre, enter)
+            if r == 0:
+                y_all[:n, :] = y_part if first else y_part + y_in[0, :n, :]
+                d_all[:n, :] = d_part if first else d_part + d_in[0, :n, :]
+            else:
+                y_all[:n, :] += y_part
+                d_all[:n, :] += d_part
+
+        held = enter_part(0)
+        ready = None
+        for r in range(rep):
+            now = middle_part(*held)
+            if r + 1 < rep:
+                held = enter_part(r + 1)
+            if ready is not None:
+                leave_part(r - 1, *ready)
+            ready = now
+        leave_part(rep - 1, *ready)
+        if last:
+            y_ref[0, :n, :] = (y_all[:n, :] + ob_ref[0]).astype(BF)
+            d_ref[0, :n, :] = d_all[:n, :].astype(BF)
         else:
-            y_all[...] += y_part
-            d_all[...] += d_part
-    if last:
-        y_ref[0] = (y_all[...] + ob_ref[0]).astype(BF)
-        d_ref[0] = d_all[...].astype(BF)
-    else:
-        y_ref[0] = y_all[...]
-        d_ref[0] = d_all[...]
-
-
-def expert_pass(at, lists, weights, bias, out_bias=None, carried=None):
-    last = carried is not None
+            y_ref[0, :n, :] = y_all[:n, :]
+            d_ref[0, :n, :] = d_all[:n, :]
+        if n < listed:
+            y_ref[0, n:, :] = jnp.zeros((listed - n, y_ref.shape[2]), y_ref.dtype)
+            d_ref[0, n:, :] = jnp.zeros((listed - n, y_ref.shape[2]), y_ref.dtype)
+
+    if first:
+        obg_ref[0] = jnp.sum(g_ref[0].astype(F32), axis=0, keepdims=True)
+    short = listed * 3 // 4 // 16 * 16
+    pl.when(count <= short)(lambda: run(short))
+    pl.when(count > short)(lambda: run(listed))
+
+
+def expert_rank(step, half):
+    return lax.shift_left(lax.bitwise_and(step, 3), 1) + lax.shift_right_logical(step, 2) + half
+
+
+def expert_pass(at, lists, weights, bias, out_bias=None, carried=None, half=0, done=None, after=()):
+    first = carried is None
     rows = lists[0]
     experts, listed, width = rows.shape
-    rep, _, _, _, cols = weights.shape
-    here = lambda e, at: lax.bitwise_xor(e, at[1])
+    rep, cols = bias.shape[1], bias.shape[2]
+    steps = experts // 2
+    here = lambda e, at: lax.bitwise_xor(expert_rank(e, half), at[1])
     block = pl.BlockSpec((1, listed, width), lambda e, at: (here(e, at), 0, 0))
     turned = pl.BlockSpec((1, width, listed), lambda e, at: (here(e, at), 0, 0))
     out_w = pl.BlockSpec((rep // 2, 1, 2, width, cols), lambda e, at: (0, e, 0, 0, 0))
     in_specs = [
         block, block, turned, turned,
-        pl.BlockSpec((rep, 1, 2, width, cols), lambda e, at: (0, here(e, at), 0, 0, 0)),
+        *(
+            [pl.BlockSpec((rep, 1, 2, width, cols), lambda e, at: (0, here(e, at), 0, 0, 0))]
+            if first
+            else [pl.BlockSpec((1, width, cols), lambda e, at: (e, 0, 0))] * len(weights)
+        ),
         pl.BlockSpec((1, rep, cols), lambda e, at: (here(e, at), 0, 0)),
     ]
-    args = list(lists) + [weights, bias]
-    kind = BF if last else F32
+    args = list(lists) + ([weights] if first else list(weights)) + [bias]
+    kind = F32 if first else BF
     out_specs = [block, block, out_w, out_w, pl.BlockSpec((1, rep, cols), lambda e, at: (here(e, at), 0, 0))]
     out_shape = [
         jax.ShapeDtypeStruct(rows.shape, kind),
         jax.ShapeDtypeStruct(rows.shape, kind),
-        jax.ShapeDtypeStruct((rep // 2, experts, 2, width, cols), BF),
-        jax.ShapeDtypeStruct((rep // 2, experts, 2, width, cols), BF),
+        jax.ShapeDtypeStruct((rep // 2, steps, 2, width, cols), BF),
+        jax.ShapeDtypeStruct((rep // 2, steps, 2, width, cols), BF),
         jax.ShapeDtypeStruct((experts, rep, cols), F32),
     ]
-    if last:
+    aliases = {}
+    if first:
+        out_specs.append(pl.BlockSpec((1, 1, width), lambda e, at: (here(e, at), 0, 0)))
+        out_shape.append(jax.ShapeDtypeStruct((experts, 1, width), F32))
+    else:
         in_specs += [pl.BlockSpec((1, 1, width), lambda e, at: (here(e, at), 0, 0)), block, block]
         args += [out_bias, *carried]
-    else:
-        out_specs.append(pl.BlockSpec((1, 1, width), lambda e, at: (here(e, at), 0, 0)))
-        out_shape.append(jax.ShapeDtypeStruct((experts, 1, width), F32))
-    flops = 12 * experts * listed * width * rep * cols
-    return pl.pallas_call(
-        functools.partial(expert_kernel, last),
+    if half:
+        aliases = {len(args) + 1: 0, len(args) + 2: 1}
+        in_specs += unread(done)
+        args += list(done)
+    kernel = behind(functools.partial(expert_kernel, first, not first, half), len(args) + 1, after)
+    return pl.pallas_call(
+        kernel,
         grid_spec=pltpu.PrefetchScalarGridSpec(
             num_scalar_prefetch=1,
-            grid=(experts,),
-            in_specs=in_specs,
+            grid=(steps,),
+            in_specs=in_specs + unread(after),
             out_specs=out_specs,
             scratch_shapes=[pltpu.VMEM((listed, width), F32)] * 2,
         ),
         out_shape=out_shape,
+        input_output_aliases=aliases,
         compiler_params=params(),
-        cost_estimate=pl.CostEstimate(flops=flops, bytes_accessed=60_000_000, transcendentals=0),
-        name="experts_last" if last else "experts_first",
-    )(at, *args)
+        cost_estimate=cost(6 * steps),
+        name=f"experts_{0 if first else 1}{half}",
+    )(at, *args, *after)
 
 
 def combine_kernel(
@@ -545,20 +610,20 @@
     dscale_ref[4:5, :] += jnp.sum(grad_hidden, axis=0, keepdims=True)
 
 
-def combine(meta, y, d, lcol, gcol, hidden, cot_pad, mixed, out_matrix, router, gains):
+def combine(meta, y, d, lcol, gcol, hidden, cot_pad, mixed, out_matrix, router, gains, after=()):
     padded, width = hidden.shape
     images = padded // PAD
     experts = y.shape[0]
     row = lambda lanes: pl.BlockSpec((PAD, lanes), lambda i, m: (i, 0))
     once = lambda a: pl.BlockSpec(a.shape, lambda i, m: (0,) * a.ndim, pipeline_mode=pl.Buffered(1))
     return pl.pallas_call(
-        combine_kernel,
+        behind(combine_kernel, 11, after),
         grid_spec=pltpu.PrefetchScalarGridSpec(
             num_scalar_prefetch=1,
             grid=(images,),
             in_specs=[
                 once(y), once(d), row(experts), row(experts), row(width), row(width), row(width),
-                once(out_matrix), once(router), once(gains),
+                once(out_matrix), once(router), once(gains), *unread(after),
             ],
             out_specs=[
                 whole((images * SEQ, width)), row(width), row(width), whole((width, width)), whole((experts, width)),
@@ -577,8 +642,9 @@
             jax.ShapeDtypeStruct((8, width), F32),
         ],
         compiler_params=params(),
+        cost_estimate=cost(40),
         name="combine",
-    )(meta, y, d, lcol, gcol, hidden, cot_pad, mixed, out_matrix, router, gains)
+    )(meta, y, d, lcol, gcol, hidden, cot_pad, mixed, out_matrix, router, gains, *after)
 
 
 def attention_back_kernel(
@@ -657,7 +723,7 @@
             lax.fori_loop(0, blocks // 2, body, 0)
 
 
-def attention_back(place, proj, probs, grad_mixed, grad_hidden, tok_pad, in_matrix, gains, grad_out, small):
+def attention_back(place, proj, probs, grad_mixed, grad_hidden, tok_pad, in_matrix, gains, grad_out, small, after=()):
     padded, width = grad_hidden.shape
     images = padded // PAD
     blocks = small.shape[0]
@@ -666,13 +732,14 @@
     once = lambda a: pl.BlockSpec(a.shape, lambda i, m: (0,) * a.ndim, pipeline_mode=pl.Buffered(1))
     half = (blocks // 2, rows, 4 * width + 128)
     return pl.pallas_call(
-        attention_back_kernel,
+        behind(attention_back_kernel, 10, after),
         grid_spec=pltpu.PrefetchScalarGridSpec(
             num_scalar_prefetch=1,
             grid=(images,),
             in_specs=[
                 row(3 * width), pl.BlockSpec((1, HEADS, PAD, PAD), lambda i, m: (i, 0, 0, 0)), row(width), row(width),
                 row(width), once(in_matrix), once(gains), once(grad_out), once(small),
+                *unread(after),
             ],
             out_specs=[whole((images * SEQ, width)), whole(half), whole(half)],
             scratch_shapes=[
@@ -686,8 +753,9 @@
             jax.ShapeDtypeStruct(half, BF),
         ],
         compiler_params=params(),
+        cost_estimate=cost(50),
         name="attention_back",
-    )(place, proj, probs, grad_mixed, grad_hidden, tok_pad, in_matrix, gains, grad_out, small)
+    )(place, proj, probs, grad_mixed, grad_hidden, tok_pad, in_matrix, gains, grad_out, small, *after)
 
 
 X_BIT, CORE_BIT, Y_BIT = 16, 8, 1
@@ -705,11 +773,39 @@
     return x * X_BIT + c * CORE_BIT + z * 2 + y * Y_BIT
 
 
-def gather_all(block):
-    zs = jnp.stack([block] + [swap(block, bits) for bits in Z_BITS])
-    others = [swap(zs, bits) for bits in (Y_BIT, X_BIT, X_BIT | Y_BIT)]
-    plane = jnp.stack([zs] + others)
-    return jnp.stack([plane, swap(plane, CORE_BIT)]).reshape((32,) + block.shape)
+def stack_kernel(count, *refs):
+    for j in range(count):
+        refs[count][j] = refs[j][...]
+
+
+def stack(arrays, after=()):
+    count = len(arrays)
+    return pl.pallas_call(
+        behind(functools.partial(stack_kernel, count), count, after),
+        in_specs=[pl.BlockSpec(memory_space=pltpu.VMEM)] * count + unread(after),
+        out_shape=jax.ShapeDtypeStruct((count,) + arrays[0].shape, arrays[0].dtype),
+        compiler_params=params(),
+        cost_estimate=cost(1),
+        name="stack",
+    )(*arrays, *after)
+
+
+def split_stack_kernel(*refs):
+    for j in range(4):
+        refs[4][j] = refs[j][0]
+        refs[5][j] = refs[j][1]
+
+
+def split_stack(arrays, after=()):
+    shape = jax.ShapeDtypeStruct((4,) + arrays[0].shape[1:], arrays[0].dtype)
+    return pl.pallas_call(
+        behind(split_stack_kernel, 4, after),
+        in_specs=[pl.BlockSpec(memory_space=pltpu.VMEM)] * 4 + unread(after),
+        out_shape=[shape, shape],
+        compiler_params=params(),
+        cost_estimate=cost(2),
+        name="split_stack",
+    )(*arrays, *after)
 
 
 def sum_everywhere(values):
@@ -754,51 +850,194 @@
     )(*terms)
 
 
-def last_sum_kernel(*refs):
-    ins, (big_ref, small_ref) = refs[:-2], refs[-2:]
-    lanes = ins[0].shape[2]
-    total = ins[0][0].astype(F32)
-    for t in ins[1:]:
-        total = total + t[0].astype(F32)
-    big_ref[...] = total[:, : lanes - 128]
-    small_ref[...] = unsplit(total[:, lanes - 128 :])
-
-
-def last_sum(terms):
-    lanes = terms[0].shape[2]
-    return pl.pallas_call(
-        last_sum_kernel,
-        out_shape=[jax.ShapeDtypeStruct((16, lanes - 128), F32), jax.ShapeDtypeStruct((8, 128), F32)],
-        compiler_params=params(),
-        name="last_sum",
-    )(*terms)
-
-
 def scatter_dense(near, far):
     parts = block_sum([near, swap(far, CORE_BIT)], 4)
     got = [swap(parts[1], Y_BIT), swap(parts[2], X_BIT), swap(parts[3], X_BIT | Y_BIT)]
     parts = block_sum([parts[0]] + got, 4)
-    return last_sum([parts[0]] + [swap(parts[z], Z_BITS[z - 1]) for z in (1, 2, 3)])
-
-
-def scatter_expert(near, far):
-    got = swap(far, CORE_BIT)
-    shape = (2, 4, 2) + near.shape[2:]
-    near, got = near.reshape(shape), got.reshape(shape)
-    add = lambda cut: near[cut] + got[cut]
-    every = slice(None)
-    a_keep, a_send = add((every, every, 0, 0)), add((every, every, 1, 0))
-    b_keep, b_send = add((0, every, every, 1)), add((1, every, every, 1))
-    a_got, b_got = swap(a_send, Y_BIT), swap(b_send, X_BIT)
-    a_far, b_far = a_keep[1] + a_got[1], b_keep[:, 1] + b_got[:, 1]
-    a_got2, b_got2 = swap(a_far, X_BIT), swap(b_far, Y_BIT)
-    total = lambda z: jnp.stack(
-        [a_keep[0, z] + a_got[0, z] + a_got2[z], b_keep[z, 0] + b_got[z, 0] + b_got2[z]]
-    )
-    result = total(0).astype(F32)
-    for z in (1, 2, 3):
-        result = result + swap(total(z), Z_BITS[z - 1]).astype(F32)
-    return result
+    return [parts[0]] + [swap(parts[z], Z_BITS[z - 1]) for z in (1, 2, 3)]
+
+
+def fold_cores_kernel(n0, n1, g0, g1, a_keep, b_keep, a_send, b_send):
+    for x in range(2):
+        a_keep[x, 0] = n0[x, 0, 0] + g0[x, 0, 0]
+        a_send[x, 0] = n1[x, 0, 0] + g1[x, 0, 0]
+        out = b_send if x else b_keep
+        out[0, 0] = n0[x, 0, 1] + g0[x, 0, 1]
+        out[1, 0] = n1[x, 0, 1] + g1[x, 0, 1]
+
+
+def fold_cores(near, got):
+    rows, cols = near[0].shape[3:]
+    out = jax.ShapeDtypeStruct((2, 4, rows, cols), BF)
+    return pl.pallas_call(
+        fold_cores_kernel,
+        grid=(4,),
+        in_specs=[pl.BlockSpec((2, 1, 2, rows, cols), lambda z: (0, z, 0, 0, 0))] * 4,
+        out_specs=[pl.BlockSpec((2, 1, rows, cols), lambda z: (0, z, 0, 0))] * 4,
+        out_shape=[out] * 4,
+        compiler_params=params(),
+        cost_estimate=cost(7),
+        name="fold_cores",
+    )(*near, *got)
+
+
+def fold_first_kernel(a_keep, b_keep, a_got, b_got, a_near, b_near, a_far, b_far):
+    a_near[0] = a_keep[0, 0] + a_got[0, 0]
+    b_near[0] = b_keep[0, 0] + b_got[0, 0]
+    a_far[0] = a_keep[1, 0] + a_got[1, 0]
+    b_far[0] = b_keep[1, 0] + b_got[1, 0]
+
+
+def fold_first(a_keep, b_keep, a_got, b_got, after=()):
+    rows, cols = a_keep.shape[2:]
+    return pl.pallas_call(
+        behind(fold_first_kernel, 4, after),
+        grid=(4,),
+        in_specs=[pl.BlockSpec((2, 1, rows, cols), lambda z: (0, z, 0, 0))] * 4 + unread(after),
+        out_specs=[pl.BlockSpec((1, rows, cols), lambda z: (z, 0, 0))] * 4,
+        out_shape=[jax.ShapeDtypeStruct((4, rows, cols), BF)] * 4,
+        compiler_params=params(),
+        cost_estimate=cost(4),
+        name="fold_first",
+    )(a_keep, b_keep, a_got, b_got, *after)
+
+
+def fold_second_kernel(a_keep, b_keep, a_got, b_got, *parts):
+    for z in range(4):
+        parts[z][0] = a_keep[z] + a_got[z]
+        parts[z][1] = b_keep[z] + b_got[z]
+
+
+def fold_second(a_keep, b_keep, a_got, b_got):
+    return pl.pallas_call(
+        fold_second_kernel,
+        out_shape=[jax.ShapeDtypeStruct((2,) + a_keep.shape[1:], BF)] * 4,
+        compiler_params=params(),
+        cost_estimate=cost(3),
+        name="fold_second",
+    )(a_keep, b_keep, a_got, b_got)
+
+
+def total_of(array):
+    return jnp.sum(jnp.sum(array, axis=1, keepdims=True), axis=0, keepdims=True)
+
+
+def expert_update_kernel(*refs):
+    parts, (wi, fi, si, wo, fo, so), outs = refs[:8], refs[8:14], refs[14:]
+    sums = outs[6]
+    lane = lane_iota(1, 128)
+    kept = jnp.zeros((1, 128), F32)
+    moved = jnp.zeros((1, 128), F32)
+    cols = parts[0].shape[2]
+    for m, (weight, first, second, new) in enumerate(((wi, fi, si, outs[0:3]), (wo, fo, so, outs[3:6]))):
+        for k in range(2):
+            grad = parts[4 * k][m].astype(F32)
+            for part in parts[4 * k + 1 : 4 * k + 4]:
+                grad = grad + part[m].astype(F32)
+            span = slice(k * cols, (k + 1) * cols)
+            if m == 0:
+                at = (0, slice(None), span)
+            else:
+                grad = grad.T
+                at = (0, span, slice(None))
+            state = moments(weight[at], grad, first[at], second[at])
+            for ref, value in zip(new, state):
+                ref[at] = value
+            slot = lane == (8 if m == 0 else 10)
+            kept += jnp.where(slot, total_of(weight[at] * weight[at]), 0.0)
+            moved += jnp.where(slot, total_of(state[2] * state[2]), 0.0)
+    sums[...] = jnp.zeros_like(sums)
+    sums[0:1, :] = kept
+    sums[1:2, :] = moved
+
+
+def expert_update(parts, arrays):
+    shape = jax.ShapeDtypeStruct(arrays[0].shape, F32)
+    return pl.pallas_call(
+        expert_update_kernel,
+        out_shape=[shape] * 6 + [jax.ShapeDtypeStruct((8, 128), F32)],
+        compiler_params=params(),
+        cost_estimate=cost(6),
+        name="expert_update",
+    )(*parts, *arrays)
+
+
+def narrow(row, columns, rows):
+    spread = jnp.where(lane_iota(rows, 128) % rows == row_iota(rows, 128), row, 0.0)
+    chosen = (row_iota(128, columns) // rows == lane_iota(128, columns)).astype(F32)
+    return lax.dot_general(
+        spread, chosen, (((1,), (0,)), ((), ())), preferred_element_type=F32, precision=lax.Precision.HIGHEST
+    )
+
+
+def dense_update_kernel(*refs):
+    ins, sums, states, outs = refs[:4], refs[4], refs[5:23], refs[23:]
+    width = ins[0].shape[2] - 128
+    total = ins[0][0].astype(F32)
+    for t in ins[1:]:
+        total = total + t[0].astype(F32)
+    small = unsplit(total[:, width:])
+    experts, rows = states[6].shape[1], states[6].shape[0]
+    bias_rows = states[12].shape[1] // 128
+    grads = (
+        total[:, : width * 3 // 4],
+        total[:, width * 3 // 4 : width],
+        narrow(small[bias_rows + 1 : bias_rows + 2], experts, rows),
+        narrow(small[bias_rows + 2 : bias_rows + 3], 5, rows),
+        jnp.concatenate([small[j : j + 1] for j in range(bias_rows)], axis=1),
+        small[bias_rows : bias_rows + 1],
+    )
+    lane = lane_iota(1, 128)
+    kept, moved = sums[0:1, :], sums[1:2, :]
+    for j, grad in enumerate(grads):
+        weight, first, second = (states[3 * j + k][...] for k in range(3))
+        state = moments(weight, grad, first, second)
+        for k in range(3):
+            outs[3 * j + k][...] = state[k]
+        for c, slot in enumerate({0: (0,), 1: (1,), 2: (2,), 3: (3, 4, 5, 6, 7), 4: (9,), 5: (11,)}[j]):
+            cut = (slice(None), slice(c, c + 1)) if j == 3 else (slice(None), slice(None))
+            kept += jnp.where(lane == slot, total_of(weight[cut] * weight[cut]), 0.0)
+            moved += jnp.where(lane == slot, total_of(state[2][cut] * state[2][cut]), 0.0)
+    outs[18][...] = jnp.zeros_like(outs[18])
+    outs[18][0:1, :] = kept
+    outs[18][1:2, :] = moved
+
+
+def dense_update(terms, sums, states):
+    return pl.pallas_call(
+        dense_update_kernel,
+        out_shape=[jax.ShapeDtypeStruct(a.shape, F32) for a in states] + [jax.ShapeDtypeStruct((8, 128), F32)],
+        compiler_params=params(),
+        cost_estimate=cost(3),
+        name="dense_update",
+    )(*terms, sums, *states)
+
+
+def new_weights_kernel(sums, counts, *refs):
+    weights, steps, outs, norms = refs[:8], refs[8:16], refs[16:24], refs[24]
+    weight_rms = jnp.sqrt(sums[0:1, :] / counts[...])
+    step_rms = jnp.sqrt(sums[1:2, :] / counts[...])
+    trust = weight_rms / step_rms
+    norms[...] = jnp.zeros_like(norms)
+    norms[0:1, :] = weight_rms
+    norms[1:2, :] = step_rms
+    norms[2:3, :] = trust
+    for j, begin in enumerate((0, 1, 2, 3, 8, 9, 10, 11)):
+        scale = trust[:, 3:8] if j == 3 else trust[:, begin : begin + 1]
+        if len(outs[j].shape) == 3:
+            outs[j][0] = weights[j][0] - RATE * scale * steps[j][0]
+        else:
+            outs[j][...] = weights[j][...] - RATE * scale * steps[j][...]
+
+
+def new_weights(sums, counts, weights, steps):
+    return pl.pallas_call(
+        new_weights_kernel,
+        out_shape=[jax.ShapeDtypeStruct(a.shape, F32) for a in weights] + [jax.ShapeDtypeStruct((8, 128), F32)],
+        compiler_params=params(),
+        cost_estimate=cost(5),
+        name="new_weights",
+    )(sums, counts, *weights, *steps)
 
 
 CHUNKS = 2
@@ -829,9 +1068,7 @@
         jnp.stack([enter_low[:, k * cols : (k + 1) * cols], leave_low[:, k * cols : (k + 1) * cols]])
         for k in range(CHUNKS)
     ]
-    wide = [
-        lax.all_gather(piece[None], AXES, axis=0, tiled=True).reshape(rep, ep, 2, width, cols) for piece in pieces
-    ]
+    wide = lax.all_gather(pieces[0][None], AXES, axis=0, tiled=True).reshape(rep, ep, 2, width, cols)
 
     rows_here = heads_in.shape[0]
     small = jnp.concatenate([router, scales], axis=1)
@@ -841,37 +1078,76 @@
     dense = jnp.concatenate([heads_in, heads_out, small, biases], axis=1).astype(BF)
     order = jnp.array([relative(p) for p in range(rep * ep)], jnp.int32)
     place = jnp.bitwise_xor(order, me)
-    in_matrix, out_matrix, router_matrix, gains, small_all = assemble(place, gather_all(dense), experts)
-    bias_all = small_all[:, 128:].reshape(rep, ep, rows_here, 128)
-    in_rows = hidden_part // 128
-    enter_bias = bias_all[:, :, :in_rows].reshape(rep, ep, hidden_part).astype(F32).transpose(1, 0, 2)
-    leave_bias = bias_all[:, :, in_rows].astype(F32).transpose(1, 0, 2).reshape(ep, 1, width)
-
     spread = lambda a, fill: jnp.pad(
         a.reshape(-1, images, SEQ), ((0, 0), (0, 0), (0, PAD - SEQ)), constant_values=fill
     ).reshape(-1, images * PAD)
     ids_rows = spread(expert_ids.T, -1)
     rows = jnp.concatenate([spread(priority, count), ids_rows], axis=0).astype(F32)
     rows = jnp.pad(rows, ((0, 5), (0, 0)))
+
+    zs_got = [swap(dense, bits) for bits in Z_BITS]
+    tok_pad, cot_pad = spread_rows(tokens, cotangent)
+    zs = stack([dense] + zs_got, after=(tok_pad,))
+    others = [swap(zs, bits) for bits in (Y_BIT, X_BIT, X_BIT | Y_BIT)]
     lrow, lcol, meta = find_places(rows, rows.T, capacity, experts)
-
-    tok_pad, cot_pad = spread_rows(tokens, cotangent)
+    plane = stack([zs] + others, after=(lrow,))
+    in_matrix, out_matrix, router_matrix, gains, small_all = assemble(
+        place, plane.reshape((16,) + dense.shape), swap(plane, CORE_BIT).reshape((16,) + dense.shape), experts
+    )
+    bias_all = small_all[:, 128:].reshape(rep, ep, rows_here, 128)
+    in_rows = hidden_part // 128
+    enter_bias = bias_all[:, :, :in_rows].reshape(rep, ep, hidden_part).astype(F32).transpose(1, 0, 2)
+    leave_bias = bias_all[:, :, in_rows].astype(F32).transpose(1, 0, 2).reshape(ep, 1, width)
+
+    piece_got = [swap(pieces[1], bits) for bits in Z_BITS]
     proj, probs, mixed, hidden, routed, gcol, grow = attention(
         tok_pad, in_matrix, out_matrix, router_matrix, gains, ids_rows.T
     )
-    lists = gather(meta, routed, cot_pad, lrow, grow, listed)
-
+    halves = split_stack([pieces[1]] + piece_got, after=(gcol,))
+    far_x = [swap(h, X_BIT) for h in halves]
+    far_y = [swap(h, Y_BIT) for h in halves]
+    lists = gather(meta, routed, cot_pad, lrow, grow, listed, after=halves)
+
+    totals_here = meta[images - 1] + meta[2 * images - 1]
+    at = jnp.concatenate([at, totals_here])
     bias_cut = lambda k: enter_bias[:, :, k * cols : (k + 1) * cols]
-    near, far, grad_bias = [], [], []
-    y, d, n, f, b, grad_leave_bias = expert_pass(at, lists, wide[0], bias_cut(0))
-    near.append(n), far.append(f), grad_bias.append(b)
-    y, d, n, f, b = expert_pass(at, lists, wide[1], bias_cut(1), leave_bias, (y, d))
-    near.append(n), far.append(f), grad_bias.append(b)
-    expert_sums = [scatter_expert(n, f) for n, f in zip(near, far)]
-
+    cross = lambda arrays: [swap(a, CORE_BIT) for a in arrays]
+    mingle = lambda near, far: [a for pair in zip(near, far) for a in pair]
+    far_xy = swap(far_x[0], Y_BIT), swap(far_y[1], X_BIT)
+    y_part, d_part, near_a, far_a, bias_a, leave_a = expert_pass(
+        at, lists, wide, bias_cut(0), after=far_x + far_y
+    )
+    near_half = [halves[0], far_x[0], halves[1], far_x[1]]
+    far_half = [far_y[0], far_xy[0], far_y[1], far_xy[1]]
+    crossed = cross(near_half)
+    got_a = swap(far_a, CORE_BIT)
+    y_half, d_half, near_b, far_b, bias_b, leave_b = expert_pass(
+        at, lists, wide, bias_cut(0), half=1, done=(y_part, d_part), after=list(far_xy) + crossed
+    )
+    got_b = swap(far_b, CORE_BIT)
+    one = fold_cores((near_a, near_b), (got_a, got_b))
+    even = lax.bitwise_xor(jnp.arange(ep, dtype=jnp.int32), ep_me)[:, None, None] % 2 == 0
+    grad_bias = [jnp.where(even, bias_a, bias_b)]
+    grad_leave_bias = jnp.where(even, leave_a, leave_b)
+    one_got = swap(one[2], Y_BIT), swap(one[3], X_BIT)
+    crossed_far = cross(far_half)
+    y_part, d_part, near_a, far_a, bias_a = expert_pass(
+        at, lists, mingle(near_half, crossed), bias_cut(1), leave_bias, (y_half, d_half)
+    )
+    got_a = swap(far_a, CORE_BIT)
+    y, d, near_b, far_b, bias_b = expert_pass(
+        at, lists, mingle(far_half, crossed_far), bias_cut(1), leave_bias, (y_half, d_half), half=1,
+        done=(y_part, d_part), after=list(one_got),
+    )
+    one = fold_first(*one[:2], *one_got)
+    one_got = swap(one[2], X_BIT), swap(one[3], Y_BIT)
+    got_b = swap(far_b, CORE_BIT)
     output, grad_hidden, grad_mixed, grad_out, grad_router, grad_scale = combine(
         meta, y, d, lcol, gcol, hidden, cot_pad, mixed, out_matrix, router_matrix, gains
     )
+    one = fold_second(*one[:2], *one_got)
+    two = fold_cores((near_a, near_b), (got_a, got_b))
+    grad_bias.append(jnp.where(even, bias_a, bias_b))
     devices = rep * ep
     by_device = lambda a: jnp.pad(
         a.reshape(a.shape[0], devices, rows_here).transpose(1, 0, 2).reshape(devices, 1, -1),
@@ -887,34 +1163,47 @@
         axis=1,
     )
     small_grads = jnp.pad(small_grads, ((0, 0), (0, 8 - small_grads.shape[1]), (0, 0)))
+    one_got = [swap(one[z], Z_BITS[z - 1]) for z in (1, 2, 3)]
+    two_got = swap(two[2], Y_BIT), swap(two[3], X_BIT)
     input_grad, near_dense, far_dense = attention_back(
-        place, proj, probs, grad_mixed, grad_hidden, tok_pad, in_matrix, gains, grad_out, small_grads
-    )
-    big, small = scatter_dense(near_dense, far_dense)
-    grads_now = (
-        big[:, : 3 * width],
-        big[:, 3 * width :],
-        small[in_rows + 1].reshape(experts, rows_here).T,
-        small[in_rows + 2, : 5 * rows_here].reshape(5, rows_here).T,
-        jnp.concatenate([total[0] for total in expert_sums], axis=1)[None],
-        small[:in_rows].reshape(1, hidden_part),
-        jnp.concatenate([total[1] for total in expert_sums], axis=1).T[None],
-        small[in_rows][None],
-    )
+        place, proj, probs, grad_mixed, grad_hidden, tok_pad, in_matrix, gains, grad_out, small_grads,
+        after=list(one[1:]) + list(two[2:]),
+    )
+    two = fold_first(*two[:2], *two_got, after=one_got)
+    two_got = swap(two[2], X_BIT), swap(two[3], Y_BIT)
+    dense_terms = scatter_dense(near_dense, far_dense)
+    two = fold_second(*two[:2], *two_got)
+    two_got = [swap(two[z], Z_BITS[z - 1]) for z in (1, 2, 3)]
+    parts = [one[0]] + one_got + [two[0]] + two_got
+    (in_first, in_second, in_step, out_first, out_second, out_step, sums) = expert_update(
+        parts, (expert_in, expert_in_first, expert_in_second, expert_out, expert_out_first, expert_out_second)
+    )
+    dense_states = (
+        heads_in, heads_in_first, heads_in_second, heads_out, heads_out_first, heads_out_second,
+        router, router_first, router_second, scales, scales_first, scales_second,
+        bias_in, bias_in_first, bias_in_second, bias_out, bias_out_first, bias_out_second,
+    )
+    *dense_new, sums = dense_update(dense_terms, sums, dense_states)
+    sums = sum_everywhere(sums)
+    counts = jnp.array(
+        [3 * width * width, width * width, width * experts]
+        + [width] * 5
+        + [experts * width * FF, experts * FF, experts * FF * width, experts * width]
+        + [1] * (128 - 12),
+        jnp.float32,
+    )[None]
+    trio = lambda j: tuple(dense_new[3 * j : 3 * j + 3])
+    states = [
+        trio(0), trio(1), trio(2), trio(3), (in_first, in_second, in_step), trio(4),
+        (out_first, out_second, out_step), trio(5),
+    ]
     weights_now = (heads_in, heads_out, router, scales, expert_in, bias_in, expert_out, bias_out)
-    firsts = (
-        heads_in_first, heads_out_first, router_first, scales_first,
-        expert_in_first, bias_in_first, expert_out_first, bias_out_first,
-    )
-    seconds = (
-        heads_in_second, heads_out_second, router_second, scales_second,
-        expert_in_second, bias_in_second, expert_out_second, bias_out_second,
-    )
-    states = [moments(w, g, f, s) for w, g, f, s in zip(weights_now, grads_now, firsts, seconds)]
-    weight_terms = jnp.concatenate([squares(w, index == 3) for index, w in enumerate(weights_now)])
-    step_terms = jnp.concatenate([squares(state[2], index == 3) for index, state in enumerate(states)])
-    totals = sum_everywhere(jnp.stack([weight_terms, step_terms]))
-    return (output, input_grad) + finish(totals, weights_now, states, width, experts)
+    *fresh, norms = new_weights(sums, counts, weights_now, [state[2] for state in states])
+    results = [output, input_grad]
+    for state, weight in zip(states, fresh):
+        results.extend([state[0], state[1], weight])
+    results.append(norms[:3, :12])
+    return tuple(results)
 
 
 def expert_front(rows, enter_weight, enter_bias):

time: 744 us -> 623 us (0.84)
  waiting for transfers between devices: 259 us -> 137 us
  other arithmetic: 68.2 us -> 6.13 us
  starting transfers between devices: 50.2 us -> 86.7 us
  Pallas kernels: 308 us -> 335 us
    ppermute x35 -> x54, waiting for transfers between devices: 209 us -> 137 us  [swap(): return lax.ppermute(array, AXES, [(d, d ^ bits) for d in range(devices)])]
    all_gather x2 -> x1, waiting for transfers between devices: 49.3 us -> 0.01 us  [replicate_plan(): lax.all_gather(pieces[0][None], AXES, axis=0, tiled=True)]
    pallas_call x7 -> x20, Pallas kernels: 273 us -> 312 us  [the longest x4 96.7 us: expert_pass(): pl.pallas_call(kernel, grid_spec=pltpu.PrefetchScalarGridSpec(num_scalar_...]
    ppermute x35 -> x54, starting transfers between devices: 50.1 us -> 86.7 us  [swap(): return lax.ppermute(array, AXES, [(d, d ^ bits) for d in range(devices)])]
    add x14 -> x1, other arithmetic: 29.6 us -> 0.69 us  [replicate_plan(): totals_here = meta[images - 1] + meta[2 * images - 1]]
    unnamed x118 -> x130, local copies, waits for them, and re-layouts: 6.96 us -> 25.7 us
    reduce_sum x8 -> x0, other arithmetic: 15.5 us -> none  [the longest x7 14.1 us: squares(): return jnp.sum(array * array)[None]]
    pallas_call x1, Pallas kernels: 16.4 us -> 3.87 us  [assemble(): pl.pallas_call(assemble_kernel, grid_spec=pltpu.PrefetchScalarGridSpec(nu...]
  transfers between devices with their start and end apart: 37 -> 55, of which waited for: 26 -> 21; matrix products, arithmetic and copies ran while one was open for 8% -> 3% of each run, Pallas kernels for 42% -> 50%
where the time goes in v2:
time: 623 us; the launch traced here: 613 us
  Pallas kernels  335 us (54%)
  waiting for transfers between devices  137 us (22%)
  starting transfers between devices  86.7 us (14%)
  local copies, waits for them, and re-layouts  33.7 us (5%)
  between operations  15.1 us (2%)
    ppermute x54, waiting for transfers between devices, swap(): return lax.ppermute(array, AXES, [(d, d ^ bits) for d in range(devices)])  137 us
    pallas_call x4, Pallas kernels, expert_pass(): pl.pallas_call(kernel, grid_spec=pltpu.PrefetchScalarGridSpec(num_scalar_...  96.7 us
    ppermute x54, starting transfers between devices, swap(): return lax.ppermute(array, AXES, [(d, d ^ bits) for d in range(devices)])  86.7 us
    pallas_call x1, Pallas kernels, attention_back(): pl.pallas_call(behind(attention_back_kernel, 10, after), grid_spec=pltpu....  51 us
    pallas_call x1, Pallas kernels, combine(): pl.pallas_call(behind(combine_kernel, 11, after), grid_spec=pltpu.Prefetc...  50.3 us
    pallas_call x1, Pallas kernels, attention(): pl.pallas_call(behind(attention_kernel, 6, after), grid=(images,), in_spe...  28.1 us
    pallas_call x1, Pallas kernels, gather(): pl.pallas_call(behind(gather_kernel, 5, after), grid_spec=pltpu.PrefetchS...  27.8 us
    unnamed x130, local copies, waits for them, and re-layouts  25.7 us
  transfers between devices with their start and end apart: 55, of which 21 were waited for; matrix products, arithmetic and copies ran while one was open for 3% of the time, Pallas kernels for 50%

profile of v2, /device:TPU:0, one launch (start us, length us, event | category | flops | bytes accessed | tf_op | source)
XLA Modules:
  0.0 613.0 jit_solution(15353982349304389409)
XLA Ops:
  7.3 1.5 copy.176
  11.0 3.1 collective-permute-start
  14.1 2.6 collective-permute-start.1
  19.4 4.7 spread_rows.1
  26.1 1.7 stack.34.refs_0_
  27.8 1.7 collective-permute-start.3
  29.6 1.5 collective-permute-start.4
  31.3 9.6 %places.1 = (f32[10,8,208]{2,1,0:T(8,128)}, f32[2080,8]{1,0:T(8,128)}, s32[20,8]{1,0:T(8,128)}) custom-call(f32[8,2080]{1,0:T(8,128)} %pad.32.clone.rows_ref, f32[2080,8]{1,0:T(8,128)} %pad_bitcast_fusion.cols_ref), custom_call_target="tpu_custom_call" | custom-call | flops 8999999488 | bytes 900000 | tf_op jit(solution)/shard_map/places/pallas_call | solution.py:220
  40.9 2.8 collective-permute-done.5.refs_3_
  44.4 2.3 stack.35
  47.6 3.4 collective-permute-start.8
  54.1 3.9 assemble.1
  58.0 28.1 %attention.1 = (bf16[2080,1536]{1,0:T(8,128)(2,1)}, bf16[10,8,208,208]{3,2,1,0:T(8,128)(2,1)}, bf16[2080,512]{1,0:T(8,128)(2,1)}, f32[2080,512]{1,0:T(8,128)}, b...) custom-call(bf16[2080,512]{1,0:T(8,128)(2,1)} %get-tuple-element.149.refs_4_.refs_0_.refs_5_, ...), custom_call_target="tpu_custom_call" | custom-call | flops 28000000000 | bytes 2800000 | tf_op jit(solution)/shard_map/attention/pallas_call | solution.py:311
  86.1 4.1 collective-permute-done.7.refs_1_
  90.2 19.0 %collective-permute-done.9.refs_3_ = bf16[2,512,256]{2,1,0:T(8,128)(2,1)S(1)} collective-permute-done((bf16[2,512,256]{2,1,0:T(8,128)(2,1)S(1)}, bf16[2,512,256]{2,1,0:T(8,128)(2,1)S(1)}, u32[]{:S(2)}, u32[]{:S(2)}) %collective-permute-start.9) | collective-permute-done | bytes 524320 | tf_op jit(solution)/shard_map/ppermute | solution.py:768
  110.1 2.9 split_stack.1
  113.0 1.5 collective-permute-start.10
  117.1 27.8 %gather.1 = (bf16[8,624,512]{2,1,0:T(8,128)(2,1)}, bf16[8,624,512]{2,1,0:T(8,128)(2,1)}, bf16[8,512,624]{2,1,0:T(8,128)(2,1)}, bf16[8,512,624]{2,1,0:T(8,128)(2,1)}) custom-call(s32[20,8]{1,0:T(8,128)} %get-tuple-element.148.refs_0_, bf16[2080,512]{1,0:T(8,128)(2,1)} %get-tuple-element.155.refs_1_, bf16[2080,512]{1,0:T(8,128)(2,1)} %get-tuple-element.156.refs_2_.refs_6_, ...), custom_call_target="tpu_custom_call" | custom-call | flops 24999999488 | bytes 2500000 | tf_op jit(solution)/shard_map/gather/pallas_call | solution.py:375
  145.6 2.5 collective-permute-done.10.refs_9_.refs_5_
  148.4 1.5 collective-permute-start.13
  149.9 20.9 %collective-permute-done.15.refs_10_.refs_9_ = bf16[4,512,256]{2,1,0:T(8,128)(2,1)} collective-permute-done((bf16[4,512,256]{2,1,0:T(8,128)(2,1)}, bf16[4,512,256]{2,1,0:T(8,128)(2,1)}, u32[]{:S(2)}, u32[]{:S(2)}) %collective-permute-start.15) | collective-permute-done | bytes 1048608 | tf_op jit(solution)/shard_map/ppermute | solution.py:768
  170.7 1.5 collective-permute-start.17
  172.4 24.8 %experts_00.1 = (f32[8,624,512]{2,1,0:T(8,128)}, f32[8,624,512]{2,1,0:T(8,128)}, bf16[2,4,2,512,256]{4,3,2,1,0:T(8,128)(2,1)}, bf16[2,4,2,512,256]{4,3,2,1,0:T(8...) custom-call(s32[10]{0:T(128)} %pad_add_fusion.refs_0_, bf16[8,624,512]{2,1,0:T(8,128)(2,1)} %get-tuple-element.161.refs_1_, ...), custom_call_target="tpu_custom_call" | custom-call | flops 24000000000 | bytes 2400000 | tf_op jit(solution)/shard_map/experts_00/pallas_call | solution.py:519
  197.3 23.4 %experts_01.1 = (f32[8,624,512]{2,1,0:T(8,128)}, f32[8,624,512]{2,1,0:T(8,128)}, bf16[2,4,2,512,256]{4,3,2,1,0:T(8,128)(2,1)}, bf16[2,4,2,512,256]{4,3,2,1,0:T(8...) custom-call(s32[10]{0:T(128)} %pad_add_fusion.refs_0_, ...), custom_call_target="tpu_custom_call", output_to_operand_aliasing={{0}: (7, {}), {1}: (8, {})} | custom-call | flops 24000000000 | bytes 2400000 | tf_op jit(solution)/shard_map/experts_01/pallas_call | solution.py:519
  220.7 1.7 collective-permute-start.25
  224.1 6.3 %collective-permute-done.25.g1 = bf16[2,4,2,512,256]{4,3,2,1,0:T(8,128)(2,1)} collective-permute-done((bf16[2,4,2,512,256]{4,3,2,1,0:T(8,128)(2,1)}, bf16[2,4,2,512,256]{4,3,2,1,0:T(8,128)(2,1)}, u32[]{:S(2)}, u32[]{:S(2)}) %collective-permute-start.25) | collective-permute-done | bytes 4194336 | tf_op jit(solution)/shard_map/ppermute | solution.py:768
  230.8 6.3 %collective-permute-done.24.g0 = bf16[2,4,2,512,256]{4,3,2,1,0:T(8,128)(2,1)} collective-permute-done((bf16[2,4,2,512,256]{4,3,2,1,0:T(8,128)(2,1)}, bf16[2,4,2,512,256]{4,3,2,1,0:T(8,128)(2,1)}, u32[]{:S(2)}, u32[]{:S(2)}) %collective-permute-start.24) | collective-permute-done | bytes 4194336 | tf_op jit(solution)/shard_map/ppermute | solution.py:768
  237.1 9.0 %fold_cores.2 = (bf16[2,4,512,256]{3,2,1,0:T(8,128)(2,1)}, bf16[2,4,512,256]{3,2,1,0:T(8,128)(2,1)}, bf16[2,4,512,256]{3,2,1,0:T(8,128)(2,1)}, bf16[2,4,512,256]{3,2,1,0:T(8,128)(2,1)}) custom-call(bf16[2,4,2,512,256]{4,3,2,1,0:T(8,128)(2,1)} %get-tuple-element.172.n0, bf16[2,4,2,512,256]{4,3,2,1,0:T(8,128)(2,1)} %get-tuple-element.173.n1, ...), custom_call_target="tpu_custom_call" | custom-call | flops 7000000000 | bytes 700000 | tf_op jit(solution)/shard_map/fold_cores/pallas_call | solution.py:872
  246.0 1.8 collective-permute-start.27
  247.8 25.0 %experts_10.1 = (bf16[8,624,512]{2,1,0:T(8,128)(2,1)}, bf16[8,624,512]{2,1,0:T(8,128)(2,1)}, bf16[2,4,2,512,256]{4,3,2,1,0:T(8,128)(2,1)}, bf16[2,4,2,512,256]{4,3,2,1,0:T(8,128)(2,1)}, f32[8,4,256]{2,1,0:T(4,128)}) custom-call(s32[10]{0:T(128)} %pad_add_fusion.refs_0_, bf16[8,624,512]{2,1,0:T(8,128)(2,1)} %get-tuple-element.161.refs_1_, ...), custom_call_target="tpu_custom_call" | custom-call | flops 24000000000 | bytes 2400000 | tf_op jit(solution)/shard_map/experts_10/pallas_call | solution.py:519
  273.0 21.1 %collective-permute-done.26.refs_19_.refs_2_ = bf16[2,4,512,256]{3,2,1,0:T(8,128)(2,1)S(1)} collective-permute-done((bf16[2,4,512,256]{3,2,1,0:T(8,128)(2,1)}, bf16[2,4,512,256]{3,2,1,0:T(8,128)(2,1)S(1)}, u32[]{:S(2)}, u32[]{:S(2)}) %collective-permute-start.26) | collective-permute-done | bytes 2097184 | tf_op jit(solution)/shard_map/ppermute | solution.py:768
  295.4 23.6 %experts_11.1 = (bf16[8,624,512]{2,1,0:T(8,128)(2,1)}, bf16[8,624,512]{2,1,0:T(8,128)(2,1)}, bf16[2,4,2,512,256]{4,3,2,1,0:T(8,128)(2,1)}, bf16[2,4,2,512,256]{4,3,2,1,0:T(8,128)(2,1)}, f32[8,4,256]{2,1,0:T(4,128)}) custom-call(s32[10]{0:T(128)} %pad_add_fusion.refs_0_, ...), custom_call_target="tpu_custom_call", output_to_operand_aliasing={{0}: (17, {}), {1}: (18, {})} | custom-call | flops 24000000000 | bytes 2400000 | tf_op jit(solution)/shard_map/experts_11/pallas_call | solution.py:519
  320.2 5.7 fold_first.2
  325.9 2.0 collective-permute-start.29
  327.9 50.3 %combine.1 = (f32[1970,512]{1,0:T(8,128)}, f32[2080,512]{1,0:T(8,128)}, bf16[2080,512]{1,0:T(8,128)(2,1)}, f32[512,512]{1,0:T(8,128)}, f32[8,512]{1,0:T(8,128)}, /*index=5*/f32[8,512]{1,0:T(8,128)}) custom-call(s32[20,8]{1,0:T(8,128)} %get-tuple-element.148.refs_0_, bf16[8,624,512]{2,1,0:T(8,128)(2,1)} %get-tuple-element.178.refs_1_, ...), custom_call_target="tpu_custom_call" | custom-call | flops 40000000000 | bytes 4000000 | tf_op jit(solution)/shard_map/combine/pallas_call | solution.py:619
  382.4 3.5 fold_second.2
  386.0 22.6 %collective-permute-start.39 = (bf16[2,512,256]{2,1,0:T(8,128)(2,1)}, bf16[2,512,256]{2,1,0:T(8,128)(2,1)S(1)}, u32[]{:S(2)}, u32[]{:S(2)}) collective-permute-start(bf16[2,512,256]{2,1,0:T(8,128)(2,1)} %get-tuple-element.203.refs_10_), channel_id=1, source_target_pairs={{0,2},{1,3},{2,0},{3,1},{4,6},{5,7},{6,4},{7,5},{8,10},{9,11},{10,... | collective-permute-start | bytes 1572872 | tf_op jit(solution)/shard_map/ppermute | solution.py:768
  408.5 2.2 collective-permute-start.40
  412.2 9.0 %fold_cores.3 = (bf16[2,4,512,256]{3,2,1,0:T(8,128)(2,1)}, bf16[2,4,512,256]{3,2,1,0:T(8,128)(2,1)}, bf16[2,4,512,256]{3,2,1,0:T(8,128)(2,1)}, bf16[2,4,512,256]{3,2,1,0:T(8,128)(2,1)}) custom-call(bf16[2,4,2,512,256]{4,3,2,1,0:T(8,128)(2,1)} %get-tuple-element.206.n0, bf16[2,4,2,512,256]{4,3,2,1,0:T(8,128)(2,1)} %get-tuple-element.207.n1, ...), custom_call_target="tpu_custom_call" | custom-call | flops 7000000000 | bytes 700000 | tf_op jit(solution)/shard_map/fold_cores/pallas_call | solution.py:872
  421.8 51.0 %attention_back.1 = (f32[1970,512]{1,0:T(8,128)}, bf16[16,16,2176]{2,1,0:T(8,128)(2,1)}, bf16[16,16,2176]{2,1,0:T(8,128)(2,1)}) custom-call(s32[32]{0:T(128)} %broadcast_xor_fusion.place_ref.refs_0_, bf16[2080,1536]{1,0:T(8,128)(2,1)} %get-tuple-element.184.refs_1_, bf16[10,8,208,208]{3,2,1,0:T(8,128)(2,1)} %get-tuple-element.185.refs_2_, ...), custom_call_target="tpu_custom_call" | custom-call | flops 49999998976 | bytes 5000000 | tf_op jit(solution)/shard_map/attention_back/pallas_call | solution.py:734
  474.3 5.7 fold_first.3
  481.4 1.9 collective-permute-start.45
  484.4 2.7 block_sum.2
  487.1 18.6 %collective-permute-done.44.a_got = bf16[4,512,256]{2,1,0:T(8,128)(2,1)S(1)} collective-permute-done((bf16[4,512,256]{2,1,0:T(8,128)(2,1)}, bf16[4,512,256]{2,1,0:T(8,128)(2,1)S(1)}, u32[]{:S(2)}, u32[]{:S(2)}) %collective-permute-start.44) | collective-permute-done | bytes 1048608 | tf_op jit(solution)/shard_map/ppermute | solution.py:768
  505.7 1.9 collective-permute-done.45.b_got
  508.7 3.6 fold_second.3
  512.9 2.4 collective-permute-start.47
  517.3 2.9 collective-permute-start.35
  524.2 2.0 collective-permute-done.34.refs_2_
  526.3 4.1 collective-permute-done.35.refs_3_
  531.1 2.0 block_sum.3
  533.0 2.9 collective-permute-start.37
  536.6 1.8 collective-permute-start.38
  538.4 15.8 %collective-permute-done.47.refs_6_ = bf16[2,512,256]{2,1,0:T(8,128)(2,1)S(1)} collective-permute-done((bf16[2,512,256]{2,1,0:T(8,128)(2,1)}, bf16[2,512,256]{2,1,0:T(8,128)(2,1)S(1)}, u32[]{:S(2)}, u32[]{:S(2)}) %collective-permute-start.47) | collective-permute-done | bytes 524320 | tf_op jit(solution)/shard_map/ppermute | solution.py:768
  555.3 8.3 %expert_update.1 = (f32[1,512,512]{2,1,0:T(8,128)}, f32[1,512,512]{2,1,0:T(8,128)}, f32[1,512,512]{2,1,0:T(8,128)}, f32[1,512,512]{2,1,0:T(8,128)}, f32[1,512,51...) custom-call(bf16[2,512,256]{2,1,0:T(8,128)(2,1)} %get-tuple-element.223.refs_0_, ...), custom_call_target="tpu_custom_call" | custom-call | flops 6000000000 | bytes 600000 | tf_op jit(solution)/shard_map/expert_update/pallas_call | solution.py:956
  563.7 1.9 collective-permute-done.37.refs_2_
  566.2 2.2 dense_update.1
  570.5 1.5 collective-permute-start.50
  572.0 2.1 collective-permute-done.50
  574.7 3.0 collective-permute-done.51
  577.7 9.0 %collective-permute-start.52 = (f32[8,128]{1,0:T(8,128)S(1)}, f32[8,128]{1,0:T(8,128)S(1)}, u32[]{:S(2)}, u32[]{:S(2)}) collective-permute-start(f32[8,128]{1,0:T(8,128)S(1)} %add.55), channel_id=1, source_target_pairs={{0,2},{1,3},{2,0},{3,1},{4,6},{5,7},{6,4},{7,5},{8,10},{9,11},{10,... | collective-permute-start | bytes 12296 | tf_op jit(solution)/shard_map/ppermute | solution.py:768
  586.8 1.6 collective-permute-done.52
  588.4 3.5 collective-permute-start.53
  597.9 4.1 new_weights.1
  (255 shorter events, 54.6 us)
Async XLA Ops:
  7.2 165.2 %all-gather.3.cloned.1.call-start = ((), (), s32[]{:S(2)}) async-start(), calls=%async_computation | async-start | bytes 17301504 | tf_op jit(solution)/shard_map/all_gather | solution.py:1071
  11.0 15.1 %collective-permute-start = (bf16[16,2304]{1,0:T(8,128)(2,1)S(1)}, bf16[16,2304]{1,0:T(8,128)(2,1)}, u32[]{:S(2)}, u32[]{:S(2)}) collective-permute-start(bf16[16,2304]{1,0:T(8,128)(2,1)S(1)} %pad_maximum_fusion.2.refs_0_), channel_id=1, source_target_pairs={{0,2},{1,3},{2,0},{3,1},{4,6},{5,7},{6,4},{7,5},{8,10},{9,11},{10,... | collective-permute-start | bytes 221192 | tf_op jit(solution)/shard_map/ppermute | solution.py:768
  14.1 12.0 %collective-permute-start.1 = (bf16[16,2304]{1,0:T(8,128)(2,1)S(1)}, bf16[16,2304]{1,0:T(8,128)(2,1)}, u32[]{:S(2)}, u32[]{:S(2)}) collective-permute-start(bf16[16,2304]{1,0:T(8,128)(2,1)S(1)} %pad_maximum_fusion.2.refs_0_), channel_id=1, source_target_pairs={{0,4},{1,5},{2,6},{3,7},{4,0},{5,1},{6,2},{7,3},{8,12},{9,13},{10,... | collective-permute-start | bytes 221192 | tf_op jit(solution)/shard_map/ppermute | solution.py:768
  16.7 9.4 %collective-permute-start.2 = (bf16[16,2304]{1,0:T(8,128)(2,1)S(1)}, bf16[16,2304]{1,0:T(8,128)(2,1)}, u32[]{:S(2)}, u32[]{:S(2)}) collective-permute-start(bf16[16,2304]{1,0:T(8,128)(2,1)S(1)} %pad_maximum_fusion.2.refs_0_), channel_id=1, source_target_pairs={{0,6},{1,7},{2,4},{3,5},{4,2},{5,3},{6,0},{7,1},{8,14},{9,15},{10,... | collective-permute-start | bytes 221192 | tf_op jit(solution)/shard_map/ppermute | solution.py:768
  27.8 13.1 %collective-permute-start.3 = (bf16[4,16,2304]{2,1,0:T(8,128)(2,1)}, bf16[4,16,2304]{2,1,0:T(8,128)(2,1)S(1)}, u32[]{:S(2)}, u32[]{:S(2)}) collective-permute-start(bf16[4,16,2304]{2,1,0:T(8,128)(2,1)} %stack.34.refs_0_), channel_id=1, source_target_pairs={{0,1},{1,0},{2,3},{3,2},{4,5},{5,4},{6,7},{7,6},{8,9},{9,8},{10,11... | collective-permute-start | bytes 884744 | tf_op jit(solution)/shard_map/ppermute | solution.py:768
  29.6 11.4 %collective-permute-start.4 = (bf16[4,16,2304]{2,1,0:T(8,128)(2,1)}, bf16[4,16,2304]{2,1,0:T(8,128)(2,1)S(1)}, u32[]{:S(2)}, u32[]{:S(2)}) collective-permute-start(bf16[4,16,2304]{2,1,0:T(8,128)(2,1)} %stack.34.refs_0_), channel_id=1, source_target_pairs={{0,16},{1,17},{2,18},{3,19},{4,20},{5,21},{6,22},{7,23},{8,24},{9,... | collective-permute-start | bytes 884744 | tf_op jit(solution)/shard_map/ppermute | solution.py:768
  31.1 12.7 %collective-permute-start.5 = (bf16[4,16,2304]{2,1,0:T(8,128)(2,1)}, bf16[4,16,2304]{2,1,0:T(8,128)(2,1)S(1)}, u32[]{:S(2)}, u32[]{:S(2)}) collective-permute-start(bf16[4,16,2304]{2,1,0:T(8,128)(2,1)} %stack.34.refs_0_), channel_id=1, source_target_pairs={{0,17},{1,16},{2,19},{3,18},{4,21},{5,20},{6,23},{7,22},{8,25},{9,... | collective-permute-start | bytes 884744 | tf_op jit(solution)/shard_map/ppermute | solution.py:768
  46.8 6.3 %collective-permute-start.6 = (bf16[4,4,16,2304]{3,2,1,0:T(8,128)(2,1)}, bf16[4,4,16,2304]{3,2,1,0:T(8,128)(2,1)S(1)}, u32[]{:S(2)}, u32[]{:S(2)}) collective-permute-start(bf16[4,4,16,2304]{3,2,1,0:T(8,128)(2,1)} %stack.35), channel_id=1, source_target_pairs={{0,8},{1,9},{2,10},{3,11},{4,12},{5,13},{6,14},{7,15},{8,0},{9,1},... | collective-permute-start | bytes 3538952 | tf_op jit(solution)/shard_map/ppermute | solution.py:768
  46.8 43.4 %collective-permute-start.7 = (bf16[2,512,256]{2,1,0:T(8,128)(2,1)S(1)}, bf16[2,512,256]{2,1,0:T(8,128)(2,1)S(1)}, u32[]{:S(2)}, u32[]{:S(2)}) collective-permute-start(bf16[2,512,256]{2,1,0:T(8,128)(2,1)S(1)} %pad_maximum_fusion.refs_0_), channel_id=1, source_target_pairs={{0,2},{1,3},{2,0},{3,1},{4,6},{5,7},{6,4},{7,5},{8,10},{9,11},{10,... | collective-permute-start | bytes 1572872 | tf_op jit(solution)/shard_map/ppermute | solution.py:768
  47.6 42.6 %collective-permute-start.8 = (bf16[2,512,256]{2,1,0:T(8,128)(2,1)S(1)}, bf16[2,512,256]{2,1,0:T(8,128)(2,1)S(1)}, u32[]{:S(2)}, u32[]{:S(2)}) collective-permute-start(bf16[2,512,256]{2,1,0:T(8,128)(2,1)S(1)} %pad_maximum_fusion.refs_0_), channel_id=1, source_target_pairs={{0,4},{1,5},{2,6},{3,7},{4,0},{5,1},{6,2},{7,3},{8,12},{9,13},{10,... | collective-permute-start | bytes 1572872 | tf_op jit(solution)/shard_map/ppermute | solution.py:768
  51.0 58.2 %collective-permute-start.9 = (bf16[2,512,256]{2,1,0:T(8,128)(2,1)S(1)}, bf16[2,512,256]{2,1,0:T(8,128)(2,1)S(1)}, u32[]{:S(2)}, u32[]{:S(2)}) collective-permute-start(bf16[2,512,256]{2,1,0:T(8,128)(2,1)S(1)} %pad_maximum_fusion.refs_0_), channel_id=1, source_target_pairs={{0,6},{1,7},{2,4},{3,5},{4,2},{5,3},{6,0},{7,1},{8,14},{9,15},{10,... | collective-permute-start | bytes 1572872 | tf_op jit(solution)/shard_map/ppermute | solution.py:768
  113.0 35.1 %collective-permute-start.10 = (bf16[4,512,256]{2,1,0:T(8,128)(2,1)}, bf16[4,512,256]{2,1,0:T(8,128)(2,1)S(1)}, u32[]{:S(2)}, u32[]{:S(2)}) collective-permute-start(bf16[4,512,256]{2,1,0:T(8,128)(2,1)} %get-tuple-element.159.refs_5_), channel_id=1, source_target_pairs={{0,1},{1,0},{2,3},{3,2},{4,5},{5,4},{6,7},{7,6},{8,9},{9,8},{10,11... | collective-permute-start | bytes 3145736 | tf_op jit(solution)/shard_map/ppermute | solution.py:768
  114.5 33.9 %collective-permute-start.12 = (bf16[4,512,256]{2,1,0:T(8,128)(2,1)}, bf16[4,512,256]{2,1,0:T(8,128)(2,1)S(1)}, u32[]{:S(2)}, u32[]{:S(2)}) collective-permute-start(bf16[4,512,256]{2,1,0:T(8,128)(2,1)} %get-tuple-element.159.refs_5_), channel_id=1, source_target_pairs={{0,16},{1,17},{2,18},{3,19},{4,20},{5,21},{6,22},{7,23},{8,24},{9,... | collective-permute-start | bytes 3145736 | tf_op jit(solution)/shard_map/ppermute | solution.py:768
  115.9 54.8 %collective-permute-start.15 = (bf16[4,512,256]{2,1,0:T(8,128)(2,1)}, bf16[4,512,256]{2,1,0:T(8,128)(2,1)}, u32[]{:S(2)}, u32[]{:S(2)}) collective-permute-start(bf16[4,512,256]{2,1,0:T(8,128)(2,1)} %get-tuple-element.160.refs_6_.refs_9_), channel_id=1, source_target_pairs={{0,1},{1,0},{2,3},{3,2},{4,5},{5,4},{6,7},{7,6},{8,9},{9,8},{10,11... | collective-permute-start | bytes 3145736 | tf_op jit(solution)/shard_map/ppermute | solution.py:768
  116.5 54.2 %collective-permute-start.19 = (bf16[4,512,256]{2,1,0:T(8,128)(2,1)}, bf16[4,512,256]{2,1,0:T(8,128)(2,1)}, u32[]{:S(2)}, u32[]{:S(2)}) collective-permute-start(bf16[4,512,256]{2,1,0:T(8,128)(2,1)} %get-tuple-element.160.refs_6_.refs_9_), channel_id=1, source_target_pairs={{0,16},{1,17},{2,18},{3,19},{4,20},{5,21},{6,22},{7,23},{8,24},{9,... | collective-permute-start | bytes 3145736 | tf_op jit(solution)/shard_map/ppermute | solution.py:768
  117.1 55.1 %collective-permute-start.20 = (bf16[4,512,256]{2,1,0:T(8,128)(2,1)}, bf16[4,512,256]{2,1,0:T(8,128)(2,1)}, u32[]{:S(2)}, u32[]{:S(2)}) collective-permute-start(bf16[4,512,256]{2,1,0:T(8,128)(2,1)} %get-tuple-element.159.refs_5_), channel_id=1, source_target_pairs={{0,8},{1,9},{2,10},{3,11},{4,12},{5,13},{6,14},{7,15},{8,0},{9,1},... | collective-permute-start | bytes 3145736 | tf_op jit(solution)/shard_map/ppermute | solution.py:768
  117.1 27.9 %copy-start.10 = (bf16[512,256]{1,0:T(8,128)(2,1)S(1)}, bf16[512,256]{1,0:T(8,128)(2,1)}, u32[]{:S(2)}) copy-start(bf16[512,256]{1,0:T(8,128)(2,1)} %get-tuple-element.165) | copy-start | bytes 786436
  117.1 31.1 %copy-start.34 = (bf16[4,512,256]{2,1,0:T(8,128)(2,1)S(1)}, bf16[4,512,256]{2,1,0:T(8,128)(2,1)}, u32[]{:S(2)}) copy-start(bf16[4,512,256]{2,1,0:T(8,128)(2,1)} %get-tuple-element.160.refs_6_.refs_9_) | copy-start | bytes 3145732
  148.1 49.1 %collective-permute-start.22 = (bf16[4,512,256]{2,1,0:T(8,128)(2,1)S(1)}, bf16[4,512,256]{2,1,0:T(8,128)(2,1)}, u32[]{:S(2)}, u32[]{:S(2)}) collective-permute-start(bf16[4,512,256]{2,1,0:T(8,128)(2,1)S(1)} %copy-done.34), channel_id=1, source_target_pairs={{0,8},{1,9},{2,10},{3,11},{4,12},{5,13},{6,14},{7,15},{8,0},{9,1},... | collective-permute-start | bytes 3145736 | tf_op jit(solution)/shard_map/ppermute | solution.py:768
  148.4 48.9 %collective-permute-start.13 = (bf16[4,512,256]{2,1,0:T(8,128)(2,1)S(1)}, bf16[4,512,256]{2,1,0:T(8,128)(2,1)}, u32[]{:S(2)}, u32[]{:S(2)}) collective-permute-start(bf16[4,512,256]{2,1,0:T(8,128)(2,1)S(1)} %collective-permute-done.12.refs_7_), channel_id=1, source_target_pairs={{0,1},{1,0},{2,3},{3,2},{4,5},{5,4},{6,7},{7,6},{8,9},{9,8},{10,11... | collective-permute-start | bytes 3145736 | tf_op jit(solution)/shard_map/ppermute | solution.py:768
  170.7 26.6 %collective-permute-start.21 = (bf16[4,512,256]{2,1,0:T(8,128)(2,1)S(1)}, bf16[4,512,256]{2,1,0:T(8,128)(2,1)}, u32[]{:S(2)}, u32[]{:S(2)}) collective-permute-start(bf16[4,512,256]{2,1,0:T(8,128)(2,1)S(1)} %collective-permute-done.12.refs_7_), channel_id=1, source_target_pairs={{0,8},{1,9},{2,10},{3,11},{4,12},{5,13},{6,14},{7,15},{8,0},{9,1},... | collective-permute-start | bytes 3145736 | tf_op jit(solution)/shard_map/ppermute | solution.py:768
  170.7 26.6 %collective-permute-start.17 = (bf16[4,512,256]{2,1,0:T(8,128)(2,1)}, bf16[4,512,256]{2,1,0:T(8,128)(2,1)}, u32[]{:S(2)}, u32[]{:S(2)}) collective-permute-start(bf16[4,512,256]{2,1,0:T(8,128)(2,1)} %collective-permute-done.15.refs_10_.refs_9_), channel_id=1, source_target_pairs={{0,16},{1,17},{2,18},{3,19},{4,20},{5,21},{6,22},{7,23},{8,24},{9,... | collective-permute-start | bytes 3145736 | tf_op jit(solution)/shard_map/ppermute | solution.py:768
  172.2 25.1 %collective-permute-start.23 = (bf16[4,512,256]{2,1,0:T(8,128)(2,1)}, bf16[4,512,256]{2,1,0:T(8,128)(2,1)}, u32[]{:S(2)}, u32[]{:S(2)}) collective-permute-start(bf16[4,512,256]{2,1,0:T(8,128)(2,1)} %collective-permute-done.19.refs_8_.refs_11_), channel_id=1, source_target_pairs={{0,8},{1,9},{2,10},{3,11},{4,12},{5,13},{6,14},{7,15},{8,0},{9,1},... | collective-permute-start | bytes 3145736 | tf_op jit(solution)/shard_map/ppermute | solution.py:768
  197.3 25.2 %copy-start.33 = (bf16[4,512,256]{2,1,0:T(8,128)(2,1)S(1)}, bf16[4,512,256]{2,1,0:T(8,128)(2,1)}, u32[]{:S(2)}) copy-start(bf16[4,512,256]{2,1,0:T(8,128)(2,1)} %copy-done.32) | copy-start | bytes 3145732
  220.7 9.7 %collective-permute-start.25 = (bf16[2,4,2,512,256]{4,3,2,1,0:T(8,128)(2,1)}, bf16[2,4,2,512,256]{4,3,2,1,0:T(8,128)(2,1)}, u32[]{:S(2)}, u32[]{:S(2)}) collective-permute-start(bf16[2,4,2,512,256]{4,3,2,1,0:T(8,128)(2,1)} %get-tuple-element.175), channel_id=1, source_target_pairs={{0,8},{1,9},{2,10},{3,11},{4,12},{5,13},{6,14},{7,15},{8,0},{9,1},... | collective-permute-start | bytes 12582920 | tf_op jit(solution)/shard_map/ppermute | solution.py:768
  222.4 14.6 %collective-permute-start.24 = (bf16[2,4,2,512,256]{4,3,2,1,0:T(8,128)(2,1)}, bf16[2,4,2,512,256]{4,3,2,1,0:T(8,128)(2,1)}, u32[]{:S(2)}, u32[]{:S(2)}) collective-permute-start(bf16[2,4,2,512,256]{4,3,2,1,0:T(8,128)(2,1)} %get-tuple-element.174), channel_id=1, source_target_pairs={{0,8},{1,9},{2,10},{3,11},{4,12},{5,13},{6,14},{7,15},{8,0},{9,1},... | collective-permute-start | bytes 12582920 | tf_op jit(solution)/shard_map/ppermute | solution.py:768
  222.5 23.5 %collective-permute-start.11 = (bf16[4,512,256]{2,1,0:T(8,128)(2,1)S(1)}, bf16[4,512,256]{2,1,0:T(8,128)(2,1)}, u32[]{:S(2)}, u32[]{:S(2)}) collective-permute-start(bf16[4,512,256]{2,1,0:T(8,128)(2,1)S(1)} %copy-done.33), channel_id=1, source_target_pairs={{0,8},{1,9},{2,10},{3,11},{4,12},{5,13},{6,14},{7,15},{8,0},{9,1},... | collective-permute-start | bytes 3145736 | tf_op jit(solution)/shard_map/ppermute | solution.py:768
  223.6 49.3 %collective-permute-start.16 = (bf16[4,512,256]{2,1,0:T(8,128)(2,1)}, bf16[4,512,256]{2,1,0:T(8,128)(2,1)}, u32[]{:S(2)}, u32[]{:S(2)}) collective-permute-start(bf16[4,512,256]{2,1,0:T(8,128)(2,1)} %collective-permute-done.15.refs_10_.refs_9_), channel_id=1, source_target_pairs={{0,8},{1,9},{2,10},{3,11},{4,12},{5,13},{6,14},{7,15},{8,0},{9,1},... | collective-permute-start | bytes 3145736 | tf_op jit(solution)/shard_map/ppermute | solution.py:768
  223.7 49.3 %collective-permute-start.14 = (bf16[4,512,256]{2,1,0:T(8,128)(2,1)}, bf16[4,512,256]{2,1,0:T(8,128)(2,1)}, u32[]{:S(2)}, u32[]{:S(2)}) collective-permute-start(bf16[4,512,256]{2,1,0:T(8,128)(2,1)} %collective-permute-done.13.refs_9_.refs_7_), channel_id=1, source_target_pairs={{0,8},{1,9},{2,10},{3,11},{4,12},{5,13},{6,14},{7,15},{8,0},{9,1},... | collective-permute-start | bytes 3145736 | tf_op jit(solution)/shard_map/ppermute | solution.py:768
  230.4 42.6 %collective-permute-start.18 = (bf16[4,512,256]{2,1,0:T(8,128)(2,1)}, bf16[4,512,256]{2,1,0:T(8,128)(2,1)}, u32[]{:S(2)}, u32[]{:S(2)}) collective-permute-start(bf16[4,512,256]{2,1,0:T(8,128)(2,1)} %collective-permute-done.17.refs_10_.refs_11_), channel_id=1, source_target_pairs={{0,8},{1,9},{2,10},{3,11},{4,12},{5,13},{6,14},{7,15},{8,0},{9,1},... | collective-permute-start | bytes 3145736 | tf_op jit(solution)/shard_map/ppermute | solution.py:768
  246.0 48.1 %collective-permute-start.26 = (bf16[2,4,512,256]{3,2,1,0:T(8,128)(2,1)}, bf16[2,4,512,256]{3,2,1,0:T(8,128)(2,1)S(1)}, u32[]{:S(2)}, u32[]{:S(2)}) collective-permute-start(bf16[2,4,512,256]{3,2,1,0:T(8,128)(2,1)} %get-tuple-element.176), channel_id=1, source_target_pairs={{0,1},{1,0},{2,3},{3,2},{4,5},{5,4},{6,7},{7,6},{8,9},{9,8},{10,11... | collective-permute-start | bytes 6291464 | tf_op jit(solution)/shard_map/ppermute | solution.py:768
  246.0 48.3 %collective-permute-start.27 = (bf16[2,4,512,256]{3,2,1,0:T(8,128)(2,1)}, bf16[2,4,512,256]{3,2,1,0:T(8,128)(2,1)}, u32[]{:S(2)}, u32[]{:S(2)}) collective-permute-start(bf16[2,4,512,256]{3,2,1,0:T(8,128)(2,1)} %get-tuple-element.177), channel_id=1, source_target_pairs={{0,16},{1,17},{2,18},{3,19},{4,20},{5,21},{6,22},{7,23},{8,24},{9,... | collective-permute-start | bytes 6291464 | tf_op jit(solution)/shard_map/ppermute | solution.py:768
  247.8 25.0 %copy-start.17 = (f32[8,1,512]{2,1,0:T(1,128)S(1)}, f32[8,1,512]{2,1,0:T(1,128)}, u32[]{:S(2)}) copy-start(f32[8,1,512]{2,1,0:T(1,128)} %get-tuple-element.193) | copy-start | bytes 49156
  247.8 25.0 %copy-start.18 = (f32[8,1,512]{2,1,0:T(1,128)S(1)}, f32[8,1,512]{2,1,0:T(1,128)}, u32[]{:S(2)}) copy-start(f32[8,1,512]{2,1,0:T(1,128)} %get-tuple-element.194) | copy-start | bytes 49156
  272.9 139.2 %collective-permute-start.30 = (bf16[2,4,2,512,256]{4,3,2,1,0:T(8,128)(2,1)}, bf16[2,4,2,512,256]{4,3,2,1,0:T(8,128)(2,1)}, u32[]{:S(2)}, u32[]{:S(2)}) collective-permute-start(bf16[2,4,2,512,256]{4,3,2,1,0:T(8,128)(2,1)} %get-tuple-element.208), channel_id=1, source_target_pairs={{0,8},{1,9},{2,10},{3,11},{4,12},{5,13},{6,14},{7,15},{8,0},{9,1},... | collective-permute-start | bytes 12582920 | tf_op jit(solution)/shard_map/ppermute | solution.py:768
  319.0 93.1 %collective-permute-start.31 = (bf16[2,4,2,512,256]{4,3,2,1,0:T(8,128)(2,1)}, bf16[2,4,2,512,256]{4,3,2,1,0:T(8,128)(2,1)}, u32[]{:S(2)}, u32[]{:S(2)}) collective-permute-start(bf16[2,4,2,512,256]{4,3,2,1,0:T(8,128)(2,1)} %get-tuple-element.209), channel_id=1, source_target_pairs={{0,8},{1,9},{2,10},{3,11},{4,12},{5,13},{6,14},{7,15},{8,0},{9,1},... | collective-permute-start | bytes 12582920 | tf_op jit(solution)/shard_map/ppermute | solution.py:768
  325.9 55.2 %collective-permute-start.28 = (bf16[4,512,256]{2,1,0:T(8,128)(2,1)}, bf16[4,512,256]{2,1,0:T(8,128)(2,1)S(1)}, u32[]{:S(2)}, u32[]{:S(2)}) collective-permute-start(bf16[4,512,256]{2,1,0:T(8,128)(2,1)} %get-tuple-element.201), channel_id=1, source_target_pairs={{0,16},{1,17},{2,18},{3,19},{4,20},{5,21},{6,22},{7,23},{8,24},{9,... | collective-permute-start | bytes 3145736 | tf_op jit(solution)/shard_map/ppermute | solution.py:768
  325.9 55.2 %collective-permute-start.29 = (bf16[4,512,256]{2,1,0:T(8,128)(2,1)}, bf16[4,512,256]{2,1,0:T(8,128)(2,1)S(1)}, u32[]{:S(2)}, u32[]{:S(2)}) collective-permute-start(bf16[4,512,256]{2,1,0:T(8,128)(2,1)} %get-tuple-element.202), channel_id=1, source_target_pairs={{0,1},{1,0},{2,3},{3,2},{4,5},{5,4},{6,7},{7,6},{8,9},{9,8},{10,11... | collective-permute-start | bytes 3145736 | tf_op jit(solution)/shard_map/ppermute | solution.py:768
  327.9 50.3 %copy-start.12 = (f32[8,4,256]{2,1,0:T(4,128)S(1)}, f32[8,4,256]{2,1,0:T(4,128)}, u32[]{:S(2)}) copy-start(f32[8,4,256]{2,1,0:T(4,128)} %get-tuple-element.189) | copy-start | bytes 98308
  327.9 50.3 %copy-start.13 = (f32[8,4,256]{2,1,0:T(4,128)S(1)}, f32[8,4,256]{2,1,0:T(4,128)}, u32[]{:S(2)}) copy-start(f32[8,4,256]{2,1,0:T(4,128)} %get-tuple-element.190) | copy-start | bytes 98308
  327.9 50.3 %copy-start.14 = (f32[8,4,256]{2,1,0:T(4,128)S(1)}, f32[8,4,256]{2,1,0:T(4,128)}, u32[]{:S(2)}) copy-start(f32[8,4,256]{2,1,0:T(4,128)} %get-tuple-element.191) | copy-start | bytes 98308
  327.9 50.3 %copy-start.15 = (f32[8,4,256]{2,1,0:T(4,128)S(1)}, f32[8,4,256]{2,1,0:T(4,128)}, u32[]{:S(2)}) copy-start(f32[8,4,256]{2,1,0:T(4,128)} %get-tuple-element.192) | copy-start | bytes 98308
  386.0 86.9 %collective-permute-start.39 = (bf16[2,512,256]{2,1,0:T(8,128)(2,1)}, bf16[2,512,256]{2,1,0:T(8,128)(2,1)S(1)}, u32[]{:S(2)}, u32[]{:S(2)}) collective-permute-start(bf16[2,512,256]{2,1,0:T(8,128)(2,1)} %get-tuple-element.203.refs_10_), channel_id=1, source_target_pairs={{0,2},{1,3},{2,0},{3,1},{4,6},{5,7},{6,4},{7,5},{8,10},{9,11},{10,... | collective-permute-start | bytes 1572872 | tf_op jit(solution)/shard_map/ppermute | solution.py:768
  408.5 64.4 %collective-permute-start.40 = (bf16[2,512,256]{2,1,0:T(8,128)(2,1)}, bf16[2,512,256]{2,1,0:T(8,128)(2,1)}, u32[]{:S(2)}, u32[]{:S(2)}) collective-permute-start(bf16[2,512,256]{2,1,0:T(8,128)(2,1)} %get-tuple-element.204.refs_11_), channel_id=1, source_target_pairs={{0,4},{1,5},{2,6},{3,7},{4,0},{5,1},{6,2},{7,3},{8,12},{9,13},{10,... | collective-permute-start | bytes 1572872 | tf_op jit(solution)/shard_map/ppermute | solution.py:768
  410.7 62.3 %collective-permute-start.41 = (bf16[2,512,256]{2,1,0:T(8,128)(2,1)}, bf16[2,512,256]{2,1,0:T(8,128)(2,1)}, u32[]{:S(2)}, u32[]{:S(2)}) collective-permute-start(bf16[2,512,256]{2,1,0:T(8,128)(2,1)} %get-tuple-element.205.refs_12_), channel_id=1, source_target_pairs={{0,6},{1,7},{2,4},{3,5},{4,2},{5,3},{6,0},{7,1},{8,14},{9,15},{10,... | collective-permute-start | bytes 1572872 | tf_op jit(solution)/shard_map/ppermute | solution.py:768
  421.2 51.8 %collective-permute-start.42 = (bf16[2,4,512,256]{3,2,1,0:T(8,128)(2,1)}, bf16[2,4,512,256]{3,2,1,0:T(8,128)(2,1)S(1)}, u32[]{:S(2)}, u32[]{:S(2)}) collective-permute-start(bf16[2,4,512,256]{3,2,1,0:T(8,128)(2,1)} %get-tuple-element.210.refs_13_), channel_id=1, source_target_pairs={{0,1},{1,0},{2,3},{3,2},{4,5},{5,4},{6,7},{7,6},{8,9},{9,8},{10,11... | collective-permute-start | bytes 6291464 | tf_op jit(solution)/shard_map/ppermute | solution.py:768
  421.2 51.8 %collective-permute-start.43 = (bf16[2,4,512,256]{3,2,1,0:T(8,128)(2,1)}, bf16[2,4,512,256]{3,2,1,0:T(8,128)(2,1)}, u32[]{:S(2)}, u32[]{:S(2)}) collective-permute-start(bf16[2,4,512,256]{3,2,1,0:T(8,128)(2,1)} %get-tuple-element.211.refs_14_), channel_id=1, source_target_pairs={{0,16},{1,17},{2,18},{3,19},{4,20},{5,21},{6,22},{7,23},{8,24},{9,... | collective-permute-start | bytes 6291464 | tf_op jit(solution)/shard_map/ppermute | solution.py:768
  472.9 10.5 %collective-permute-start.32 = (bf16[16,16,2176]{2,1,0:T(8,128)(2,1)}, bf16[16,16,2176]{2,1,0:T(8,128)(2,1)S(1)}, u32[]{:S(2)}, u32[]{:S(2)}) collective-permute-start(bf16[16,16,2176]{2,1,0:T(8,128)(2,1)} %get-tuple-element.214), channel_id=1, source_target_pairs={{0,8},{1,9},{2,10},{3,11},{4,12},{5,13},{6,14},{7,15},{8,0},{9,1},... | collective-permute-start | bytes 3342344 | tf_op jit(solution)/shard_map/ppermute | solution.py:768
  480.0 25.7 %collective-permute-start.44 = (bf16[4,512,256]{2,1,0:T(8,128)(2,1)}, bf16[4,512,256]{2,1,0:T(8,128)(2,1)S(1)}, u32[]{:S(2)}, u32[]{:S(2)}) collective-permute-start(bf16[4,512,256]{2,1,0:T(8,128)(2,1)} %get-tuple-element.228), channel_id=1, source_target_pairs={{0,16},{1,17},{2,18},{3,19},{4,20},{5,21},{6,22},{7,23},{8,24},{9,... | collective-permute-start | bytes 3145736 | tf_op jit(solution)/shard_map/ppermute | solution.py:768
  481.4 26.2 %collective-permute-start.45 = (bf16[4,512,256]{2,1,0:T(8,128)(2,1)}, bf16[4,512,256]{2,1,0:T(8,128)(2,1)S(1)}, u32[]{:S(2)}, u32[]{:S(2)}) collective-permute-start(bf16[4,512,256]{2,1,0:T(8,128)(2,1)} %get-tuple-element.229), channel_id=1, source_target_pairs={{0,1},{1,0},{2,3},{3,2},{4,5},{5,4},{6,7},{7,6},{8,9},{9,8},{10,11... | collective-permute-start | bytes 3145736 | tf_op jit(solution)/shard_map/ppermute | solution.py:768
  487.1 30.2 %collective-permute-start.33 = (bf16[4,16,2176]{2,1,0:T(8,128)(2,1)}, bf16[4,16,2176]{2,1,0:T(8,128)(2,1)S(1)}, u32[]{:S(2)}, u32[]{:S(2)}) collective-permute-start(bf16[4,16,2176]{2,1,0:T(8,128)(2,1)} %get-tuple-element.216), channel_id=1, source_target_pairs={{0,1},{1,0},{2,3},{3,2},{4,5},{5,4},{6,7},{7,6},{8,9},{9,8},{10,11... | collective-permute-start | bytes 835592 | tf_op jit(solution)/shard_map/ppermute | solution.py:768
  512.3 24.3 %collective-permute-start.46 = (bf16[2,512,256]{2,1,0:T(8,128)(2,1)}, bf16[2,512,256]{2,1,0:T(8,128)(2,1)S(1)}, u32[]{:S(2)}, u32[]{:S(2)}) collective-permute-start(bf16[2,512,256]{2,1,0:T(8,128)(2,1)} %get-tuple-element.231), channel_id=1, source_target_pairs={{0,2},{1,3},{2,0},{3,1},{4,6},{5,7},{6,4},{7,5},{8,10},{9,11},{10,... | collective-permute-start | bytes 1572872 | tf_op jit(solution)/shard_map/ppermute | solution.py:768
  512.9 41.4 %collective-permute-start.47 = (bf16[2,512,256]{2,1,0:T(8,128)(2,1)}, bf16[2,512,256]{2,1,0:T(8,128)(2,1)S(1)}, u32[]{:S(2)}, u32[]{:S(2)}) collective-permute-start(bf16[2,512,256]{2,1,0:T(8,128)(2,1)} %get-tuple-element.232), channel_id=1, source_target_pairs={{0,4},{1,5},{2,6},{3,7},{4,0},{5,1},{6,2},{7,3},{8,12},{9,13},{10,... | collective-permute-start | bytes 1572872 | tf_op jit(solution)/shard_map/ppermute | solution.py:768
  515.2 39.1 %collective-permute-start.48 = (bf16[2,512,256]{2,1,0:T(8,128)(2,1)}, bf16[2,512,256]{2,1,0:T(8,128)(2,1)S(1)}, u32[]{:S(2)}, u32[]{:S(2)}) collective-permute-start(bf16[2,512,256]{2,1,0:T(8,128)(2,1)} %get-tuple-element.233), channel_id=1, source_target_pairs={{0,6},{1,7},{2,4},{3,5},{4,2},{5,3},{6,0},{7,1},{8,14},{9,15},{10,... | collective-permute-start | bytes 1572872 | tf_op jit(solution)/shard_map/ppermute | solution.py:768
  516.7 9.6 %collective-permute-start.34 = (bf16[4,16,2176]{2,1,0:T(8,128)(2,1)S(1)}, bf16[4,16,2176]{2,1,0:T(8,128)(2,1)S(1)}, u32[]{:S(2)}, u32[]{:S(2)}) collective-permute-start(bf16[4,16,2176]{2,1,0:T(8,128)(2,1)S(1)} %copy-done.51), channel_id=1, source_target_pairs={{0,16},{1,17},{2,18},{3,19},{4,20},{5,21},{6,22},{7,23},{8,24},{9,... | collective-permute-start | bytes 835592 | tf_op jit(solution)/shard_map/ppermute | solution.py:768
  517.3 13.1 %collective-permute-start.35 = (bf16[4,16,2176]{2,1,0:T(8,128)(2,1)S(1)}, bf16[4,16,2176]{2,1,0:T(8,128)(2,1)S(1)}, u32[]{:S(2)}, u32[]{:S(2)}) collective-permute-start(bf16[4,16,2176]{2,1,0:T(8,128)(2,1)S(1)} %copy-done.50), channel_id=1, source_target_pairs={{0,17},{1,16},{2,19},{3,18},{4,21},{5,20},{6,23},{7,22},{8,25},{9,... | collective-permute-start | bytes 835592 | tf_op jit(solution)/shard_map/ppermute | solution.py:768
  533.0 30.6 %collective-permute-start.36 = (bf16[1,16,2176]{2,1,0:T(8,128)(2,1)}, bf16[1,16,2176]{2,1,0:T(8,128)(2,1)S(1)}, u32[]{:S(2)}, u32[]{:S(2)}) collective-permute-start(bf16[1,16,2176]{2,1,0:T(8,128)(2,1)} %get-tuple-element.220), channel_id=1, source_target_pairs={{0,2},{1,3},{2,0},{3,1},{4,6},{5,7},{6,4},{7,5},{8,10},{9,11},{10,... | collective-permute-start | bytes 208904 | tf_op jit(solution)/shard_map/ppermute | solution.py:768
  533.0 32.5 %collective-permute-start.37 = (bf16[1,16,2176]{2,1,0:T(8,128)(2,1)}, bf16[1,16,2176]{2,1,0:T(8,128)(2,1)S(1)}, u32[]{:S(2)}, u32[]{:S(2)}) collective-permute-start(bf16[1,16,2176]{2,1,0:T(8,128)(2,1)} %get-tuple-element.221), channel_id=1, source_target_pairs={{0,4},{1,5},{2,6},{3,7},{4,0},{5,1},{6,2},{7,3},{8,12},{9,13},{10,... | collective-permute-start | bytes 208904 | tf_op jit(solution)/shard_map/ppermute | solution.py:768
  536.6 28.9 %collective-permute-start.38 = (bf16[1,16,2176]{2,1,0:T(8,128)(2,1)}, bf16[1,16,2176]{2,1,0:T(8,128)(2,1)S(1)}, u32[]{:S(2)}, u32[]{:S(2)}) collective-permute-start(bf16[1,16,2176]{2,1,0:T(8,128)(2,1)} %get-tuple-element.222), channel_id=1, source_target_pairs={{0,6},{1,7},{2,4},{3,5},{4,2},{5,3},{6,0},{7,1},{8,14},{9,15},{10,... | collective-permute-start | bytes 208904 | tf_op jit(solution)/shard_map/ppermute | solution.py:768
  568.4 1.4 collective-permute-start.49
  570.5 3.6 collective-permute-start.50
  574.1 3.6 collective-permute-start.51
  577.7 10.6 %collective-permute-start.52 = (f32[8,128]{1,0:T(8,128)S(1)}, f32[8,128]{1,0:T(8,128)S(1)}, u32[]{:S(2)}, u32[]{:S(2)}) collective-permute-start(f32[8,128]{1,0:T(8,128)S(1)} %add.55), channel_id=1, source_target_pairs={{0,2},{1,3},{2,0},{3,1},{4,6},{5,7},{6,4},{7,5},{8,10},{9,11},{10,... | collective-permute-start | bytes 12296 | tf_op jit(solution)/shard_map/ppermute | solution.py:768
  588.4 8.9 %collective-permute-start.53 = (f32[8,128]{1,0:T(8,128)S(1)}, f32[8,128]{1,0:T(8,128)S(1)}, u32[]{:S(2)}, u32[]{:S(2)}) collective-permute-start(f32[8,128]{1,0:T(8,128)S(1)} %add.56), channel_id=1, source_target_pairs={{0,4},{1,5},{2,6},{3,7},{4,0},{5,1},{6,2},{7,3},{8,12},{9,13},{10,... | collective-permute-start | bytes 12296 | tf_op jit(solution)/shard_map/ppermute | solution.py:768
  (48 other events, 308.7 us)
Sparse Core Ops, SparseCore 0:
  11.1 150.0 all-gather.2

commit v3 on v2

--- a/solution.py
+++ b/solution.py
@@ -179,7 +179,7 @@
             jax.ShapeDtypeStruct((width, lanes - 4 * width), BF),
         ],
         compiler_params=params(),
-        cost_estimate=cost(5),
+        cost_estimate=cost(1),
         name="assemble",
     )(place, near, far)
 
@@ -225,7 +225,7 @@
             jax.ShapeDtypeStruct((2 * images, experts), jnp.int32),
         ],
         compiler_params=params(),
-        cost_estimate=cost(9),
+        cost_estimate=cost(2),
         name="places",
     )(rows, cols)
 
@@ -253,6 +253,11 @@
         @pl.when(i == image)
         def _(image=image):
             target[SEQ * image : SEQ * (image + 1), :] = values[0:SEQ, :]
+
+
+def split_halves(block, halves):
+    zero = jnp.zeros_like(block)
+    return jnp.concatenate([jnp.where(halves, block, zero), jnp.where(halves, zero, block)], axis=0)
 
 
 def attention_kernel(
@@ -266,23 +271,21 @@
     proj_ref[...] = dot_nn(entry, in_ref[...]).astype(BF)
     pair = 2 * HEAD
     halves = lane_iota(PAD, pair) < HEAD
-    key_there = lane_iota(PAD, PAD) < SEQ
+    key_there = lane_iota(2 * PAD, PAD) < SEQ
     for p in range(HEADS // 2):
         q = proj_ref[:, pair * p : pair * (p + 1)] * jnp.asarray(HEAD ** -0.5, BF)
         k = proj_ref[:, width + pair * p : width + pair * (p + 1)]
         v = proj_ref[:, 2 * width + pair * p : 2 * width + pair * (p + 1)]
-        sides = []
-        for s in range(2):
-            mine = halves if s == 0 else jnp.logical_not(halves)
-            scores = dot_nt(jnp.where(mine, q, jnp.zeros_like(q)), k)
-            scores = jnp.where(key_there, scores, -1e30)
-            peak = jnp.max(scores, axis=1, keepdims=True)
-            raised = jnp.exp(scores - peak)
-            total = jnp.sum(raised, axis=1, keepdims=True)
-            weights = (raised * (1.0 / total)).astype(BF)
-            prob_ref[0, 2 * p + s] = weights
-            sides.append(dot_nn(weights, v))
-        mixed_all[:, pair * p : pair * (p + 1)] = jnp.where(halves, sides[0], sides[1]).astype(BF)
+        scores = dot_nt(split_halves(q, halves), k)
+        scores = jnp.where(key_there, scores, -1e30)
+        peak = jnp.max(scores, axis=1, keepdims=True)
+        raised = jnp.exp(scores - peak)
+        total = jnp.sum(raised, axis=1, keepdims=True)
+        weights = (raised * (1.0 / total)).astype(BF)
+        prob_ref[0, 2 * p] = weights[:PAD]
+        prob_ref[0, 2 * p + 1] = weights[PAD:]
+        out = dot_nn(weights, v)
+        mixed_all[:, pair * p : pair * (p + 1)] = jnp.where(halves, out[:PAD], out[PAD:]).astype(BF)
     mixed = mixed_all[...]
     mixed_ref[...] = mixed
     hidden = x + dot_nn(mixed, out_ref[...]) + gains_ref[4:5, :]
@@ -329,7 +332,7 @@
         ],
         scratch_shapes=[pltpu.VMEM((PAD, width), BF)],
         compiler_params=params(),
-        cost_estimate=cost(28),
+        cost_estimate=cost(8),
         name="attention",
     )(tok_pad, in_matrix, out_matrix, router, gains, ids_col, *after)
 
@@ -384,7 +387,7 @@
         out_shape=[jax.ShapeDtypeStruct((experts, listed, width), BF)] * 2
         + [jax.ShapeDtypeStruct((experts, width, listed), BF)] * 2,
         compiler_params=params(),
-        cost_estimate=cost(25),
+        cost_estimate=cost(8),
         name="gather",
     )(meta, routed, cot_pad, lrow, grow, *after)
 
@@ -398,14 +401,14 @@
     return pre * phi, phi + pre * bell * 0.3989422804014327
 
 
-def expert_kernel(first, last, half, at_ref, *refs):
+def expert_kernel(first, half, at_ref, *refs):
     rep = 4
+    (r_ref, g_ref, rt_ref, gt_ref), w_refs, b_ref, refs = refs[:4], refs[4:12], refs[12], refs[13:]
     if first:
-        (r_ref, g_ref, rt_ref, gt_ref, w_ref, b_ref), refs = refs[:6], refs[6 + 2 * (half > 0) :]
+        refs = refs[2 * (half > 0) :]
         y_ref, d_ref, near_ref, far_ref, db_ref, obg_ref, y_all, d_all = refs
     else:
-        (r_ref, g_ref, rt_ref, gt_ref), w_refs, refs = refs[:4], refs[4:12], refs[12:]
-        (b_ref, ob_ref, y_in, d_in), refs = refs[:4], refs[4 + 2 * (half > 0) :]
+        (ob_ref, y_in, d_in), refs = refs[:3], refs[3 + 2 * (half > 0) :]
         y_ref, d_ref, near_ref, far_ref, db_ref, y_all, d_all = refs
     listed = r_ref.shape[1]
     step = pl.program_id(0)
@@ -416,9 +419,7 @@
 
         def weights(r):
             place = lax.bitwise_xor(at_ref[0], r)
-            if first:
-                return place, w_ref[place, 0, 0], w_ref[place, 0, 1]
-            return place, w_refs[r][0], w_refs[rep + r][0]
+            return place, w_refs[r][0, 0], w_refs[rep + r][0, 0]
 
         def enter_part(r):
             place, enter, leave = weights(r)
@@ -454,7 +455,7 @@
                 leave_part(r - 1, *ready)
             ready = now
         leave_part(rep - 1, *ready)
-        if last:
+        if not first:
             y_ref[0, :n, :] = (y_all[:n, :] + ob_ref[0]).astype(BF)
             d_ref[0, :n, :] = d_all[:n, :].astype(BF)
         else:
@@ -487,14 +488,10 @@
     out_w = pl.BlockSpec((rep // 2, 1, 2, width, cols), lambda e, at: (0, e, 0, 0, 0))
     in_specs = [
         block, block, turned, turned,
-        *(
-            [pl.BlockSpec((rep, 1, 2, width, cols), lambda e, at: (0, here(e, at), 0, 0, 0))]
-            if first
-            else [pl.BlockSpec((1, width, cols), lambda e, at: (e, 0, 0))] * len(weights)
-        ),
+        *[pl.BlockSpec((1, 1, width, cols), lambda e, at, m=m: (m, e, 0, 0)) for _, m in weights],
         pl.BlockSpec((1, rep, cols), lambda e, at: (here(e, at), 0, 0)),
     ]
-    args = list(lists) + ([weights] if first else list(weights)) + [bias]
+    args = list(lists) + [a for a, _ in weights] + [bias]
     kind = F32 if first else BF
     out_specs = [block, block, out_w, out_w, pl.BlockSpec((1, rep, cols), lambda e, at: (here(e, at), 0, 0))]
     out_shape = [
@@ -515,7 +512,7 @@
         aliases = {len(args) + 1: 0, len(args) + 2: 1}
         in_specs += unread(done)
         args += list(done)
-    kernel = behind(functools.partial(expert_kernel, first, not first, half), len(args) + 1, after)
+    kernel = behind(functools.partial(expert_kernel, first, half), len(args) + 1, after)
     return pl.pallas_call(
         kernel,
         grid_spec=pltpu.PrefetchScalarGridSpec(
@@ -528,7 +525,7 @@
         out_shape=out_shape,
         input_output_aliases=aliases,
         compiler_params=params(),
-        cost_estimate=cost(6 * steps),
+        cost_estimate=cost(10),
         name=f"experts_{0 if first else 1}{half}",
     )(at, *args, *after)
 
@@ -662,22 +659,18 @@
         k = proj_ref[:, width + pair * p : width + pair * (p + 1)]
         v = proj_ref[:, 2 * width + pair * p : 2 * width + pair * (p + 1)]
         gm = gm_ref[:, cut]
-        both = []
-        for s in range(2):
-            mine = halves if s == 0 else jnp.logical_not(halves)
-            low = prob_ref[0, 2 * p + s]
-            probs = low.astype(F32)
-            grad_probs = dot_nt(jnp.where(mine, gm, jnp.zeros_like(gm)), v)
-            middle = jnp.sum(probs * grad_probs, axis=1, keepdims=True)
-            grad_scores = (probs * (grad_probs - middle)).astype(BF)
-            both.append((dot_nn(grad_scores, k), dot_tn(grad_scores, q), dot_tn(low, gm)))
-        dproj[:, cut] = (jnp.where(halves, both[0][0], both[1][0]) * factor).astype(BF)
+        gms = split_halves(gm, halves)
+        low = jnp.concatenate([prob_ref[0, 2 * p], prob_ref[0, 2 * p + 1]], axis=0)
+        probs = low.astype(F32)
+        grad_probs = dot_nt(gms, v)
+        middle = jnp.sum(probs * grad_probs, axis=1, keepdims=True)
+        grad_scores = (probs * (grad_probs - middle)).astype(BF)
+        grad_q = dot_nn(grad_scores, k)
+        dproj[:, cut] = (jnp.where(halves, grad_q[:PAD], grad_q[PAD:]) * factor).astype(BF)
         dproj[:, width + pair * p : width + pair * (p + 1)] = (
-            jnp.where(halves, both[0][1], both[1][1]) * factor
+            dot_tn(grad_scores, split_halves(q, halves)) * factor
         ).astype(BF)
-        dproj[:, 2 * width + pair * p : 2 * width + pair * (p + 1)] = jnp.where(
-            halves, both[0][2], both[1][2]
-        ).astype(BF)
+        dproj[:, 2 * width + pair * p : 2 * width + pair * (p + 1)] = dot_tn(low, gms).astype(BF)
     normed, inverse = normalize(tpad_ref[...].astype(F32))
     entry = (normed * gains_ref[0:1, :] + gains_ref[1:2, :]).astype(BF)
     grads = dproj[...]
@@ -790,22 +783,40 @@
     )(*arrays, *after)
 
 
-def split_stack_kernel(*refs):
-    for j in range(4):
-        refs[4][j] = refs[j][0]
-        refs[5][j] = refs[j][1]
-
-
-def split_stack(arrays, after=()):
-    shape = jax.ShapeDtypeStruct((4,) + arrays[0].shape[1:], arrays[0].dtype)
-    return pl.pallas_call(
-        behind(split_stack_kernel, 4, after),
+def turn_stack_kernel(*refs):
+    for m in range(2):
+        for j in range(4):
+            refs[4][m, j] = refs[j][m]
+
+
+def turn_stack(arrays, after=()):
+    piece = arrays[0].shape
+    return pl.pallas_call(
+        behind(turn_stack_kernel, 4, after),
         in_specs=[pl.BlockSpec(memory_space=pltpu.VMEM)] * 4 + unread(after),
-        out_shape=[shape, shape],
+        out_shape=jax.ShapeDtypeStruct((2, 4) + piece[1:], arrays[0].dtype),
         compiler_params=params(),
         cost_estimate=cost(2),
-        name="split_stack",
+        name="turn_stack",
     )(*arrays, *after)
+
+
+def pick_kernel(far_x, far_y, x_in, x_out, y_out):
+    x_in[0] = far_x[0]
+    x_out[0] = far_x[1]
+    y_out[0] = far_y[1]
+
+
+def pick(far_x, far_y, after=()):
+    shape = (1,) + far_x.shape[1:]
+    return pl.pallas_call(
+        behind(pick_kernel, 2, after),
+        in_specs=[pl.BlockSpec(memory_space=pltpu.VMEM)] * 2 + unread(after),
+        out_shape=[jax.ShapeDtypeStruct(shape, far_x.dtype)] * 3,
+        compiler_params=params(),
+        cost_estimate=cost(3),
+        name="pick",
+    )(far_x, far_y, *after)
 
 
 def sum_everywhere(values):
@@ -1068,7 +1079,6 @@
         jnp.stack([enter_low[:, k * cols : (k + 1) * cols], leave_low[:, k * cols : (k + 1) * cols]])
         for k in range(CHUNKS)
     ]
-    wide = lax.all_gather(pieces[0][None], AXES, axis=0, tiled=True).reshape(rep, ep, 2, width, cols)
 
     rows_here = heads_in.shape[0]
     small = jnp.concatenate([router, scales], axis=1)
@@ -1088,9 +1098,11 @@
     zs_got = [swap(dense, bits) for bits in Z_BITS]
     tok_pad, cot_pad = spread_rows(tokens, cotangent)
     zs = stack([dense] + zs_got, after=(tok_pad,))
+    zs, pieces[0] = lax.optimization_barrier((zs, pieces[0]))
     others = [swap(zs, bits) for bits in (Y_BIT, X_BIT, X_BIT | Y_BIT)]
     lrow, lcol, meta = find_places(rows, rows.T, capacity, experts)
-    plane = stack([zs] + others, after=(lrow,))
+    piece_got = [swap(pieces[0], bits) for bits in Z_BITS]
+    plane = stack([zs] + others, after=(lrow, piece_got[0]))
     in_matrix, out_matrix, router_matrix, gains, small_all = assemble(
         place, plane.reshape((16,) + dense.shape), swap(plane, CORE_BIT).reshape((16,) + dense.shape), experts
     )
@@ -1099,51 +1111,76 @@
     enter_bias = bias_all[:, :, :in_rows].reshape(rep, ep, hidden_part).astype(F32).transpose(1, 0, 2)
     leave_bias = bias_all[:, :, in_rows].astype(F32).transpose(1, 0, 2).reshape(ep, 1, width)
 
-    piece_got = [swap(pieces[1], bits) for bits in Z_BITS]
     proj, probs, mixed, hidden, routed, gcol, grow = attention(
         tok_pad, in_matrix, out_matrix, router_matrix, gains, ids_rows.T
     )
-    halves = split_stack([pieces[1]] + piece_got, after=(gcol,))
-    far_x = [swap(h, X_BIT) for h in halves]
-    far_y = [swap(h, Y_BIT) for h in halves]
-    lists = gather(meta, routed, cot_pad, lrow, grow, listed, after=halves)
+    near = turn_stack([pieces[0]] + piece_got, after=(gcol,))
+    far_x, far_y = swap(near, X_BIT), swap(near, Y_BIT)
+    near, pieces[1] = lax.optimization_barrier((near, pieces[1]))
+    lists = gather(meta, routed, cot_pad, lrow, grow, listed, after=(near,))
+    near_two = turn_stack([pieces[1]] + [swap(pieces[1], bits) for bits in Z_BITS], after=(lists[0],))
 
     totals_here = meta[images - 1] + meta[2 * images - 1]
     at = jnp.concatenate([at, totals_here])
     bias_cut = lambda k: enter_bias[:, :, k * cols : (k + 1) * cols]
-    cross = lambda arrays: [swap(a, CORE_BIT) for a in arrays]
-    mingle = lambda near, far: [a for pair in zip(near, far) for a in pair]
-    far_xy = swap(far_x[0], Y_BIT), swap(far_y[1], X_BIT)
+    cross = lambda a: swap(a, CORE_BIT)
+
+    def first_half(near, far_x, crossed):
+        pairs = []
+        for m in range(2):
+            other = (crossed[1][m], 0) if isinstance(crossed[1], tuple) else (crossed[1], m)
+            pairs += [(near, m), (crossed[0], m), (far_x, m), other]
+        return pairs
+
+    def other_half(far_y, far_xy, crossed):
+        return [
+            pair
+            for m in range(2)
+            for pair in ((far_y, m), (crossed[0], m), (far_xy[m], 0), (crossed[1 + m], 0))
+        ]
+
+    x_in, x_out, y_out = pick(far_x, far_y, after=(near_two,))
+    far_xy = swap(x_in, Y_BIT), swap(y_out, X_BIT)
+    near, x_in = lax.optimization_barrier((near, x_in))
+    crossed = cross(near), (cross(x_in), cross(x_out))
     y_part, d_part, near_a, far_a, bias_a, leave_a = expert_pass(
-        at, lists, wide, bias_cut(0), after=far_x + far_y
-    )
-    near_half = [halves[0], far_x[0], halves[1], far_x[1]]
-    far_half = [far_y[0], far_xy[0], far_y[1], far_xy[1]]
-    crossed = cross(near_half)
+        at, lists, first_half(near, far_x, crossed), bias_cut(0), after=far_xy
+    )
+    near_two, *far_xy = lax.optimization_barrier((near_two, *far_xy))
+    far_x_two, far_y_two = swap(near_two, X_BIT), swap(near_two, Y_BIT)
+    crossed = cross(far_y), cross(far_xy[0]), cross(far_xy[1])
+    y_half, d_half, near_b, far_b, bias_b, leave_b = expert_pass(
+        at, lists, other_half(far_y, far_xy, crossed), bias_cut(0), half=1, done=(y_part, d_part),
+    )
     got_a = swap(far_a, CORE_BIT)
-    y_half, d_half, near_b, far_b, bias_b, leave_b = expert_pass(
-        at, lists, wide, bias_cut(0), half=1, done=(y_part, d_part), after=list(far_xy) + crossed
-    )
+    far_b, far_x_two, far_y_two = lax.optimization_barrier((far_b, far_x_two, far_y_two))
+    crossed = cross(near_two), cross(far_x_two)
     got_b = swap(far_b, CORE_BIT)
     one = fold_cores((near_a, near_b), (got_a, got_b))
+    a_send, far_x_two, far_y_two = lax.optimization_barrier((one[2], far_x_two, far_y_two))
+    one = (*one[:2], a_send, one[3])
+    far_xy_two = swap(far_x_two[0:1], Y_BIT), swap(far_y_two[1:2], X_BIT)
     even = lax.bitwise_xor(jnp.arange(ep, dtype=jnp.int32), ep_me)[:, None, None] % 2 == 0
     grad_bias = [jnp.where(even, bias_a, bias_b)]
     grad_leave_bias = jnp.where(even, leave_a, leave_b)
     one_got = swap(one[2], Y_BIT), swap(one[3], X_BIT)
-    crossed_far = cross(far_half)
     y_part, d_part, near_a, far_a, bias_a = expert_pass(
-        at, lists, mingle(near_half, crossed), bias_cut(1), leave_bias, (y_half, d_half)
-    )
+        at, lists, first_half(near_two, far_x_two, crossed), bias_cut(1), leave_bias, (y_half, d_half),
+        after=one[2:],
+    )
+    y_part, *far_xy_two = lax.optimization_barrier((y_part, *far_xy_two))
+    crossed = cross(far_y_two), cross(far_xy_two[0]), cross(far_xy_two[1])
     got_a = swap(far_a, CORE_BIT)
     y, d, near_b, far_b, bias_b = expert_pass(
-        at, lists, mingle(far_half, crossed_far), bias_cut(1), leave_bias, (y_half, d_half), half=1,
-        done=(y_part, d_part), after=list(one_got),
+        at, lists, other_half(far_y_two, far_xy_two, crossed), bias_cut(1), leave_bias, (y_half, d_half), half=1,
+        done=(y_part, d_part),
     )
     one = fold_first(*one[:2], *one_got)
     one_got = swap(one[2], X_BIT), swap(one[3], Y_BIT)
     got_b = swap(far_b, CORE_BIT)
     output, grad_hidden, grad_mixed, grad_out, grad_router, grad_scale = combine(
-        meta, y, d, lcol, gcol, hidden, cot_pad, mixed, out_matrix, router_matrix, gains
+        meta, y, d, lcol, gcol, hidden, cot_pad, mixed, out_matrix, router_matrix, gains,
+        after=one,
     )
     one = fold_second(*one[:2], *one_got)
     two = fold_cores((near_a, near_b), (got_a, got_b))

time: 623 us -> 593 us (0.952)
  waiting for transfers between devices: 137 us -> 117 us
  between operations: 15.1 us -> 1.64 us
    ppermute x54 -> x62, waiting for transfers between devices: 137 us -> 117 us  [swap(): return lax.ppermute(array, AXES, [(d, d ^ bits) for d in range(devices)])]
    pallas_call x1, Pallas kernels: 51 us -> 40.8 us  [attention_back(): pl.pallas_call(behind(attention_back_kernel, 10, after), grid_spec=pltpu....]
    pallas_call x1 -> x3, Pallas kernels: 2.95 us -> 10.1 us  [the longest x2 6.03 us: turn_stack(): pl.pallas_call(behind(turn_stack_kernel, 4, after), in_specs=[pl.BlockSpe...]
    ppermute x54 -> x62, starting transfers between devices: 86.7 us -> 82.7 us  [swap(): return lax.ppermute(array, AXES, [(d, d ^ bits) for d in range(devices)])]
    unnamed x130 -> x124, local copies, waits for them, and re-layouts: 25.7 us -> 26.8 us
  transfers between devices with their start and end apart: 55 -> 62, of which waited for: 21 -> 19; matrix products, arithmetic and copies ran while one was open for 3% -> 5% of each run, Pallas kernels for 50% -> 54%
where the time goes in v3:
time: 593 us; the launch traced here: 583 us
  Pallas kernels  332 us (56%)
  waiting for transfers between devices  117 us (20%)
  starting transfers between devices  82.7 us (14%)
  local copies, waits for them, and re-layouts  39.3 us (7%)
  other arithmetic  9.75 us (2%)
    ppermute x62, waiting for transfers between devices, swap(): return lax.ppermute(array, AXES, [(d, d ^ bits) for d in range(devices)])  117 us
    pallas_call x4, Pallas kernels, expert_pass(): pl.pallas_call(kernel, grid_spec=pltpu.PrefetchScalarGridSpec(num_scalar_...  96.9 us
    ppermute x62, starting transfers between devices, swap(): return lax.ppermute(array, AXES, [(d, d ^ bits) for d in range(devices)])  82.7 us
    pallas_call x1, Pallas kernels, combine(): pl.pallas_call(behind(combine_kernel, 11, after), grid_spec=pltpu.Prefetc...  50.4 us
    pallas_call x1, Pallas kernels, attention_back(): pl.pallas_call(behind(attention_back_kernel, 10, after), grid_spec=pltpu....  40.8 us
    pallas_call x1, Pallas kernels, attention(): pl.pallas_call(behind(attention_kernel, 6, after), grid=(images,), in_spe...  28.1 us
    pallas_call x1, Pallas kernels, gather(): pl.pallas_call(behind(gather_kernel, 5, after), grid_spec=pltpu.PrefetchS...  27.6 us
    unnamed x124, local copies, waits for them, and re-layouts  26.8 us
  transfers between devices with their start and end apart: 62, of which 19 were waited for; matrix products, arithmetic and copies ran while one was open for 5% of the time, Pallas kernels for 54%

profile of v3, /device:TPU:0, one launch (start us, length us, event | category | flops | bytes accessed | tf_op | source)
XLA Modules:
  0.0 582.9 jit_solution(2417577541430760642)
XLA Ops:
  5.5 3.1 collective-permute-start
  8.6 2.6 collective-permute-start.1
  14.9 4.6 spread_rows.1
  21.4 1.9 stack.34.refs_0_
  23.4 1.7 collective-permute-start.3
  25.1 1.5 collective-permute-start.4
  29.8 9.5 %places.1 = (f32[10,8,208]{2,1,0:T(8,128)}, f32[2080,8]{1,0:T(8,128)}, s32[20,8]{1,0:T(8,128)}) custom-call(f32[8,2080]{1,0:T(8,128)} %pad.32.clone.rows_ref, f32[2080,8]{1,0:T(8,128)} %pad_bitcast_fusion.cols_ref), custom_call_target="tpu_custom_call" | custom-call | flops 2000000000 | bytes 200000 | tf_op jit(solution)/shard_map/places/pallas_call | solution.py:220
  40.3 2.3 stack.35
  43.2 3.5 collective-permute-start.8
  47.7 3.9 assemble.1
  51.6 28.1 %attention.1 = (bf16[2080,1536]{1,0:T(8,128)(2,1)}, bf16[10,8,208,208]{3,2,1,0:T(8,128)(2,1)}, bf16[2080,512]{1,0:T(8,128)(2,1)}, f32[2080,512]{1,0:T(8,128)}, b...) custom-call(bf16[2080,512]{1,0:T(8,128)(2,1)} %get-tuple-element.168.refs_4_.refs_0_.refs_5_, ...), custom_call_target="tpu_custom_call" | custom-call | flops 8000000000 | bytes 800000 | tf_op jit(solution)/shard_map/attention/pallas_call | solution.py:314
  79.7 1.9 collective-permute-done.8.refs_2_
  82.6 3.1 turn_stack.2.refs_5_.refs_9_
  85.6 1.6 collective-permute-start.10
  87.2 1.5 collective-permute-start.11
  88.8 11.7 %collective-permute-start.12 = (bf16[2,512,256]{2,1,0:T(8,128)(2,1)S(1)}, bf16[2,512,256]{2,1,0:T(8,128)(2,1)S(1)}, u32[]{:S(2)}, u32[]{:S(2)}) collective-permute-start(bf16[2,512,256]{2,1,0:T(8,128)(2,1)S(1)} %pad_maximum_fusion.1.refs_0_), channel_id=1, source_target_pairs={{0,2},{1,3},{2,0},{3,1},{4,6},{5,7},{6,4},{7,5},{8,10},{9,11},{10,... | collective-permute-start | bytes 1572872 | tf_op jit(solution)/shard_map/ppermute | solution.py:761
  103.0 27.6 %gather.1 = (bf16[8,624,512]{2,1,0:T(8,128)(2,1)}, bf16[8,624,512]{2,1,0:T(8,128)(2,1)}, bf16[8,512,624]{2,1,0:T(8,128)(2,1)}, bf16[8,512,624]{2,1,0:T(8,128)(2,1)}) custom-call(s32[20,8]{1,0:T(8,128)} %get-tuple-element.167.refs_0_, bf16[2080,512]{1,0:T(8,128)(2,1)} %get-tuple-element.176.refs_1_, bf16[2080,512]{1,0:T(8,128)(2,1)} %get-tuple-element.177.refs_2_.refs_6_, ...), custom_call_target="tpu_custom_call" | custom-call | flops 8000000000 | bytes 800000 | tf_op jit(solution)/shard_map/gather/pallas_call | solution.py:378
  130.7 8.0 %collective-permute-done.13.refs_2_ = bf16[2,512,256]{2,1,0:T(8,128)(2,1)S(1)} collective-permute-done((bf16[2,512,256]{2,1,0:T(8,128)(2,1)S(1)}, bf16[2,512,256]{2,1,0:T(8,128)(2,1)S(1)}, u32[]{:S(2)}, u32[]{:S(2)}) %collective-permute-start.13) | collective-permute-done | bytes 524320 | tf_op jit(solution)/shard_map/ppermute | solution.py:761
  139.7 3.0 turn_stack.3.refs_2_.refs_5_.refs_9_
  142.7 4.1 pick.1
  148.2 24.3 %collective-permute-done.18.refs_14_.refs_7_ = bf16[1,4,512,256]{3,2,1,0:T(8,128)(2,1)S(1)} collective-permute-done((bf16[1,4,512,256]{3,2,1,0:T(8,128)(2,1)}, bf16[1,4,512,256]{3,2,1,0:T(8,128)(2,1)S(1)}, u32[]{:S(2)}, u32[]{:S(2)}) %collective-permute-start.18) | collective-permute-done | bytes 1048608 | tf_op jit(solution)/shard_map/ppermute | solution.py:761
  176.1 23.6 %experts_00.1 = (f32[8,624,512]{2,1,0:T(8,128)}, f32[8,624,512]{2,1,0:T(8,128)}, bf16[2,4,2,512,256]{4,3,2,1,0:T(8,128)(2,1)}, bf16[2,4,2,512,256]{4,3,2,1,0:T(8...) custom-call(s32[10]{0:T(128)} %pad_add_fusion.refs_0_, bf16[8,624,512]{2,1,0:T(8,128)(2,1)} %get-tuple-element.181.refs_4_.refs_1_, ...), custom_call_target="tpu_custom_call" | custom-call | flops 10000000000 | bytes 1000000 | tf_op jit(solution)/shard_map/experts_00/pallas_call | solution.py:516
  199.9 24.7 %experts_01.1 = (f32[8,624,512]{2,1,0:T(8,128)}, f32[8,624,512]{2,1,0:T(8,128)}, bf16[2,4,2,512,256]{4,3,2,1,0:T(8,128)(2,1)}, bf16[2,4,2,512,256]{4,3,2,1,0:T(8...) custom-call(s32[10]{0:T(128)} %pad_add_fusion.refs_0_, ...), custom_call_target="tpu_custom_call", output_to_operand_aliasing={{0}: (14, {}), {1}: (15, {})} | custom-call | flops 10000000000 | bytes 1000000 | tf_op jit(solution)/shard_map/experts_01/pallas_call | solution.py:516
  225.7 9.6 %collective-permute-done.26.g1 = bf16[2,4,2,512,256]{4,3,2,1,0:T(8,128)(2,1)} collective-permute-done((bf16[2,4,2,512,256]{4,3,2,1,0:T(8,128)(2,1)}, bf16[2,4,2,512,256]{4,3,2,1,0:T(8,128)(2,1)}, u32[]{:S(2)}, u32[]{:S(2)}) %collective-permute-start.26) | collective-permute-done | bytes 4194336 | tf_op jit(solution)/shard_map/ppermute | solution.py:761
  235.3 9.0 %fold_cores.2 = (bf16[2,4,512,256]{3,2,1,0:T(8,128)(2,1)}, bf16[2,4,512,256]{3,2,1,0:T(8,128)(2,1)}, bf16[2,4,512,256]{3,2,1,0:T(8,128)(2,1)}, bf16[2,4,512,256]{3,2,1,0:T(8,128)(2,1)}) custom-call(bf16[2,4,2,512,256]{4,3,2,1,0:T(8,128)(2,1)} %get-tuple-element.192.n0, bf16[2,4,2,512,256]{4,3,2,1,0:T(8,128)(2,1)} %get-tuple-element.197.n1, ...), custom_call_target="tpu_custom_call" | custom-call | flops 7000000000 | bytes 700000 | tf_op jit(solution)/shard_map/fold_cores/pallas_call | solution.py:883
  244.3 2.3 slice.59
  247.0 2.3 slice.58
  249.2 1.4 collective-permute-start.30
  250.7 1.5 collective-permute-start.31
  253.9 23.5 %experts_10.1 = (bf16[8,624,512]{2,1,0:T(8,128)(2,1)}, bf16[8,624,512]{2,1,0:T(8,128)(2,1)}, bf16[2,4,2,512,256]{4,3,2,1,0:T(8,128)(2,1)}, bf16[2,4,2,512,256]{4,3,2,1,0:T(8,128)(2,1)}, f32[8,4,256]{2,1,0:T(4,128)}) custom-call(s32[10]{0:T(128)} %pad_add_fusion.refs_0_, bf16[8,624,512]{2,1,0:T(8,128)(2,1)} %get-tuple-element.181.refs_4_.refs_1_, ...), custom_call_target="tpu_custom_call" | custom-call | flops 10000000000 | bytes 1000000 | tf_op jit(solution)/shard_map/experts_10/pallas_call | solution.py:516
  278.1 2.7 collective-permute-done.32.refs_8_
  282.8 25.1 %experts_11.1 = (bf16[8,624,512]{2,1,0:T(8,128)(2,1)}, bf16[8,624,512]{2,1,0:T(8,128)(2,1)}, bf16[2,4,2,512,256]{4,3,2,1,0:T(8,128)(2,1)}, bf16[2,4,2,512,256]{4,3,2,1,0:T(8,128)(2,1)}, f32[8,4,256]{2,1,0:T(4,128)}) custom-call(s32[10]{0:T(128)} %pad_add_fusion.refs_0_, ...), custom_call_target="tpu_custom_call", output_to_operand_aliasing={{0}: (17, {}), {1}: (18, {})} | custom-call | flops 10000000000 | bytes 1000000 | tf_op jit(solution)/shard_map/experts_11/pallas_call | solution.py:516
  308.1 11.6 %collective-permute-done.34.refs_2_ = bf16[2,4,512,256]{3,2,1,0:T(8,128)(2,1)} collective-permute-done((bf16[2,4,512,256]{3,2,1,0:T(8,128)(2,1)}, bf16[2,4,512,256]{3,2,1,0:T(8,128)(2,1)}, u32[]{:S(2)}, u32[]{:S(2)}) %collective-permute-start.34) | collective-permute-done | bytes 2097184 | tf_op jit(solution)/shard_map/ppermute | solution.py:761
  320.8 5.7 fold_first.2
  326.5 1.5 collective-permute-start.36
  328.7 50.4 %combine.1 = (f32[1970,512]{1,0:T(8,128)}, f32[2080,512]{1,0:T(8,128)}, bf16[2080,512]{1,0:T(8,128)(2,1)}, f32[512,512]{1,0:T(8,128)}, f32[8,512]{1,0:T(8,128)}, /*index=5*/f32[8,512]{1,0:T(8,128)}) custom-call(s32[20,8]{1,0:T(8,128)} %get-tuple-element.167.refs_0_, bf16[8,624,512]{2,1,0:T(8,128)(2,1)} %get-tuple-element.216.refs_1_, ...), custom_call_target="tpu_custom_call" | custom-call | flops 40000000000 | bytes 4000000 | tf_op jit(solution)/shard_map/combine/pallas_call | solution.py:616
  384.0 3.6 fold_second.2
  387.5 9.8 %collective-permute-start.47 = (bf16[2,512,256]{2,1,0:T(8,128)(2,1)}, bf16[2,512,256]{2,1,0:T(8,128)(2,1)S(1)}, u32[]{:S(2)}, u32[]{:S(2)}) collective-permute-start(bf16[2,512,256]{2,1,0:T(8,128)(2,1)} %get-tuple-element.241.refs_10_), channel_id=1, source_target_pairs={{0,2},{1,3},{2,0},{3,1},{4,6},{5,7},{6,4},{7,5},{8,10},{9,11},{10,... | collective-permute-start | bytes 1572872 | tf_op jit(solution)/shard_map/ppermute | solution.py:761
  398.2 1.6 collective-permute-start.49
  399.7 9.0 %fold_cores.3 = (bf16[2,4,512,256]{3,2,1,0:T(8,128)(2,1)}, bf16[2,4,512,256]{3,2,1,0:T(8,128)(2,1)}, bf16[2,4,512,256]{3,2,1,0:T(8,128)(2,1)}, bf16[2,4,512,256]{3,2,1,0:T(8,128)(2,1)}) custom-call(bf16[2,4,2,512,256]{4,3,2,1,0:T(8,128)(2,1)} %get-tuple-element.244.n0, bf16[2,4,2,512,256]{4,3,2,1,0:T(8,128)(2,1)} %get-tuple-element.245.n1, ...), custom_call_target="tpu_custom_call" | custom-call | flops 7000000000 | bytes 700000 | tf_op jit(solution)/shard_map/fold_cores/pallas_call | solution.py:883
  408.7 1.5 collective-permute-start.50
  410.8 40.8 %attention_back.1 = (f32[1970,512]{1,0:T(8,128)}, bf16[16,16,2176]{2,1,0:T(8,128)(2,1)}, bf16[16,16,2176]{2,1,0:T(8,128)(2,1)}) custom-call(s32[32]{0:T(128)} %broadcast_xor_fusion.place_ref.refs_0_, bf16[2080,1536]{1,0:T(8,128)(2,1)} %get-tuple-element.228.refs_1_, bf16[10,8,208,208]{3,2,1,0:T(8,128)(2,1)} %get-tuple-element.229.refs_2_, ...), custom_call_target="tpu_custom_call" | custom-call | flops 49999998976 | bytes 5000000 | tf_op jit(solution)/shard_map/attention_back/pallas_call | solution.py:727
  451.7 2.8 collective-permute-done.50.refs_2_
  455.8 5.9 %fold_first.3 = (bf16[4,512,256]{2,1,0:T(8,128)(2,1)}, bf16[4,512,256]{2,1,0:T(8,128)(2,1)}, bf16[4,512,256]{2,1,0:T(8,128)(2,1)}, bf16[4,512,256]{2,1,0:T(8,128)(2,1)}) custom-call(bf16[2,4,512,256]{3,2,1,0:T(8,128)(2,1)} %get-tuple-element.262.refs_0_, bf16[2,4,512,256]{3,2,1,0:T(8,128)(2,1)} %get-tuple-element.263.refs_1_, ...), custom_call_target="tpu_custom_call" | custom-call | flops 4000000000 | bytes 400000 | tf_op jit(solution)/shard_map/fold_first/pallas_call | solution.py:904
  464.6 2.6 block_sum.2
  467.9 16.8 %collective-permute-done.52.a_got = bf16[4,512,256]{2,1,0:T(8,128)(2,1)S(1)} collective-permute-done((bf16[4,512,256]{2,1,0:T(8,128)(2,1)}, bf16[4,512,256]{2,1,0:T(8,128)(2,1)S(1)}, u32[]{:S(2)}, u32[]{:S(2)}) %collective-permute-start.52) | collective-permute-done | bytes 1048608 | tf_op jit(solution)/shard_map/ppermute | solution.py:761
  484.7 3.9 collective-permute-done.53.b_got
  489.6 3.6 fold_second.3
  494.0 1.9 collective-permute-start.55
  495.9 1.6 collective-permute-start.56
  498.4 1.5 collective-permute-start.43
  504.1 3.3 collective-permute-done.43.refs_3_
  508.1 2.0 block_sum.3
  510.3 2.6 collective-permute-start.45
  512.9 2.4 collective-permute-start.46
  515.3 19.8 %collective-permute-done.55.refs_6_ = bf16[2,512,256]{2,1,0:T(8,128)(2,1)S(1)} collective-permute-done((bf16[2,512,256]{2,1,0:T(8,128)(2,1)}, bf16[2,512,256]{2,1,0:T(8,128)(2,1)S(1)}, u32[]{:S(2)}, u32[]{:S(2)}) %collective-permute-start.55) | collective-permute-done | bytes 524320 | tf_op jit(solution)/shard_map/ppermute | solution.py:761
  536.1 8.3 %expert_update.1 = (f32[1,512,512]{2,1,0:T(8,128)}, f32[1,512,512]{2,1,0:T(8,128)}, f32[1,512,512]{2,1,0:T(8,128)}, f32[1,512,512]{2,1,0:T(8,128)}, f32[1,512,51...) custom-call(bf16[2,512,256]{2,1,0:T(8,128)(2,1)} %get-tuple-element.261.refs_0_, ...), custom_call_target="tpu_custom_call" | custom-call | flops 6000000000 | bytes 600000 | tf_op jit(solution)/shard_map/expert_update/pallas_call | solution.py:967
  545.1 2.2 dense_update.1
  549.4 3.6 collective-permute-done.58
  554.0 2.7 collective-permute-done.59
  556.7 7.6 %collective-permute-start.60 = (f32[8,128]{1,0:T(8,128)S(1)}, f32[8,128]{1,0:T(8,128)S(1)}, u32[]{:S(2)}, u32[]{:S(2)}) collective-permute-start(f32[8,128]{1,0:T(8,128)S(1)} %add.55), channel_id=1, source_target_pairs={{0,2},{1,3},{2,0},{3,1},{4,6},{5,7},{6,4},{7,5},{8,10},{9,11},{10,... | collective-permute-start | bytes 12296 | tf_op jit(solution)/shard_map/ppermute | solution.py:761
  564.3 1.6 collective-permute-done.60
  565.9 2.7 collective-permute-start.61
  574.6 4.1 new_weights.1
  (266 shorter events, 67.3 us)
Async XLA Ops:
  5.5 16.0 %collective-permute-start = (bf16[16,2304]{1,0:T(8,128)(2,1)S(1)}, bf16[16,2304]{1,0:T(8,128)(2,1)}, u32[]{:S(2)}, u32[]{:S(2)}) collective-permute-start(bf16[16,2304]{1,0:T(8,128)(2,1)S(1)} %pad_maximum_fusion.2.refs_0_), channel_id=1, source_target_pairs={{0,2},{1,3},{2,0},{3,1},{4,6},{5,7},{6,4},{7,5},{8,10},{9,11},{10,... | collective-permute-start | bytes 221192 | tf_op jit(solution)/shard_map/ppermute | solution.py:761
  8.6 12.9 %collective-permute-start.1 = (bf16[16,2304]{1,0:T(8,128)(2,1)S(1)}, bf16[16,2304]{1,0:T(8,128)(2,1)}, u32[]{:S(2)}, u32[]{:S(2)}) collective-permute-start(bf16[16,2304]{1,0:T(8,128)(2,1)S(1)} %pad_maximum_fusion.2.refs_0_), channel_id=1, source_target_pairs={{0,4},{1,5},{2,6},{3,7},{4,0},{5,1},{6,2},{7,3},{8,12},{9,13},{10,... | collective-permute-start | bytes 221192 | tf_op jit(solution)/shard_map/ppermute | solution.py:761
  11.2 10.3 %collective-permute-start.2 = (bf16[16,2304]{1,0:T(8,128)(2,1)S(1)}, bf16[16,2304]{1,0:T(8,128)(2,1)}, u32[]{:S(2)}, u32[]{:S(2)}) collective-permute-start(bf16[16,2304]{1,0:T(8,128)(2,1)S(1)} %pad_maximum_fusion.2.refs_0_), channel_id=1, source_target_pairs={{0,6},{1,7},{2,4},{3,5},{4,2},{5,3},{6,0},{7,1},{8,14},{9,15},{10,... | collective-permute-start | bytes 221192 | tf_op jit(solution)/shard_map/ppermute | solution.py:761
  23.4 16.0 %collective-permute-start.3 = (bf16[4,16,2304]{2,1,0:T(8,128)(2,1)}, bf16[4,16,2304]{2,1,0:T(8,128)(2,1)S(1)}, u32[]{:S(2)}, u32[]{:S(2)}) collective-permute-start(bf16[4,16,2304]{2,1,0:T(8,128)(2,1)} %stack.34.refs_0_), channel_id=1, source_target_pairs={{0,1},{1,0},{2,3},{3,2},{4,5},{5,4},{6,7},{7,6},{8,9},{9,8},{10,11... | collective-permute-start | bytes 884744 | tf_op jit(solution)/shard_map/ppermute | solution.py:761
  25.1 14.3 %collective-permute-start.4 = (bf16[4,16,2304]{2,1,0:T(8,128)(2,1)}, bf16[4,16,2304]{2,1,0:T(8,128)(2,1)S(1)}, u32[]{:S(2)}, u32[]{:S(2)}) collective-permute-start(bf16[4,16,2304]{2,1,0:T(8,128)(2,1)} %stack.34.refs_0_), channel_id=1, source_target_pairs={{0,16},{1,17},{2,18},{3,19},{4,20},{5,21},{6,22},{7,23},{8,24},{9,... | collective-permute-start | bytes 884744 | tf_op jit(solution)/shard_map/ppermute | solution.py:761
  26.6 12.8 %collective-permute-start.5 = (bf16[4,16,2304]{2,1,0:T(8,128)(2,1)}, bf16[4,16,2304]{2,1,0:T(8,128)(2,1)}, u32[]{:S(2)}, u32[]{:S(2)}) collective-permute-start(bf16[4,16,2304]{2,1,0:T(8,128)(2,1)} %stack.34.refs_0_), channel_id=1, source_target_pairs={{0,17},{1,16},{2,19},{3,18},{4,21},{5,20},{6,23},{7,22},{8,25},{9,... | collective-permute-start | bytes 884744 | tf_op jit(solution)/shard_map/ppermute | solution.py:761
  26.8 12.5 %collective-permute-start.6 = (bf16[2,512,256]{2,1,0:T(8,128)(2,1)S(1)}, bf16[2,512,256]{2,1,0:T(8,128)(2,1)S(1)}, u32[]{:S(2)}, u32[]{:S(2)}) collective-permute-start(bf16[2,512,256]{2,1,0:T(8,128)(2,1)S(1)} %pad_maximum_fusion.refs_0_), channel_id=1, source_target_pairs={{0,2},{1,3},{2,0},{3,1},{4,6},{5,7},{6,4},{7,5},{8,10},{9,11},{10,... | collective-permute-start | bytes 1572872 | tf_op jit(solution)/shard_map/ppermute | solution.py:761
  42.7 4.0 collective-permute-start.7
  43.2 38.4 %collective-permute-start.8 = (bf16[2,512,256]{2,1,0:T(8,128)(2,1)S(1)}, bf16[2,512,256]{2,1,0:T(8,128)(2,1)S(1)}, u32[]{:S(2)}, u32[]{:S(2)}) collective-permute-start(bf16[2,512,256]{2,1,0:T(8,128)(2,1)S(1)} %pad_maximum_fusion.refs_0_), channel_id=1, source_target_pairs={{0,4},{1,5},{2,6},{3,7},{4,0},{5,1},{6,2},{7,3},{8,12},{9,13},{10,... | collective-permute-start | bytes 1572872 | tf_op jit(solution)/shard_map/ppermute | solution.py:761
  46.7 34.9 %collective-permute-start.9 = (bf16[2,512,256]{2,1,0:T(8,128)(2,1)S(1)}, bf16[2,512,256]{2,1,0:T(8,128)(2,1)S(1)}, u32[]{:S(2)}, u32[]{:S(2)}) collective-permute-start(bf16[2,512,256]{2,1,0:T(8,128)(2,1)S(1)} %pad_maximum_fusion.refs_0_), channel_id=1, source_target_pairs={{0,6},{1,7},{2,4},{3,5},{4,2},{5,3},{6,0},{7,1},{8,14},{9,15},{10,... | collective-permute-start | bytes 1572872 | tf_op jit(solution)/shard_map/ppermute | solution.py:761
  85.6 57.0 %collective-permute-start.10 = (bf16[2,4,512,256]{3,2,1,0:T(8,128)(2,1)}, bf16[2,4,512,256]{3,2,1,0:T(8,128)(2,1)}, u32[]{:S(2)}, u32[]{:S(2)}) collective-permute-start(bf16[2,4,512,256]{3,2,1,0:T(8,128)(2,1)} %turn_stack.2.refs_5_.refs_9_), channel_id=1, source_target_pairs={{0,16},{1,17},{2,18},{3,19},{4,20},{5,21},{6,22},{7,23},{8,24},{9,... | collective-permute-start | bytes 6291464 | tf_op jit(solution)/shard_map/ppermute | solution.py:761
  87.2 55.5 %collective-permute-start.11 = (bf16[2,4,512,256]{3,2,1,0:T(8,128)(2,1)}, bf16[2,4,512,256]{3,2,1,0:T(8,128)(2,1)}, u32[]{:S(2)}, u32[]{:S(2)}) collective-permute-start(bf16[2,4,512,256]{3,2,1,0:T(8,128)(2,1)} %turn_stack.2.refs_5_.refs_9_), channel_id=1, source_target_pairs={{0,1},{1,0},{2,3},{3,2},{4,5},{5,4},{6,7},{7,6},{8,9},{9,8},{10,11... | collective-permute-start | bytes 6291464 | tf_op jit(solution)/shard_map/ppermute | solution.py:761
  88.8 41.9 %collective-permute-start.12 = (bf16[2,512,256]{2,1,0:T(8,128)(2,1)S(1)}, bf16[2,512,256]{2,1,0:T(8,128)(2,1)S(1)}, u32[]{:S(2)}, u32[]{:S(2)}) collective-permute-start(bf16[2,512,256]{2,1,0:T(8,128)(2,1)S(1)} %pad_maximum_fusion.1.refs_0_), channel_id=1, source_target_pairs={{0,2},{1,3},{2,0},{3,1},{4,6},{5,7},{6,4},{7,5},{8,10},{9,11},{10,... | collective-permute-start | bytes 1572872 | tf_op jit(solution)/shard_map/ppermute | solution.py:761
  100.5 38.2 %collective-permute-start.13 = (bf16[2,512,256]{2,1,0:T(8,128)(2,1)S(1)}, bf16[2,512,256]{2,1,0:T(8,128)(2,1)S(1)}, u32[]{:S(2)}, u32[]{:S(2)}) collective-permute-start(bf16[2,512,256]{2,1,0:T(8,128)(2,1)S(1)} %pad_maximum_fusion.1.refs_0_), channel_id=1, source_target_pairs={{0,4},{1,5},{2,6},{3,7},{4,0},{5,1},{6,2},{7,3},{8,12},{9,13},{10,... | collective-permute-start | bytes 1572872 | tf_op jit(solution)/shard_map/ppermute | solution.py:761
  101.7 37.0 %collective-permute-start.14 = (bf16[2,512,256]{2,1,0:T(8,128)(2,1)S(1)}, bf16[2,512,256]{2,1,0:T(8,128)(2,1)S(1)}, u32[]{:S(2)}, u32[]{:S(2)}) collective-permute-start(bf16[2,512,256]{2,1,0:T(8,128)(2,1)S(1)} %pad_maximum_fusion.1.refs_0_), channel_id=1, source_target_pairs={{0,6},{1,7},{2,4},{3,5},{4,2},{5,3},{6,0},{7,1},{8,14},{9,15},{10,... | collective-permute-start | bytes 1572872 | tf_op jit(solution)/shard_map/ppermute | solution.py:761
  146.8 28.2 %collective-permute-start.15 = (bf16[2,4,512,256]{3,2,1,0:T(8,128)(2,1)}, bf16[2,4,512,256]{3,2,1,0:T(8,128)(2,1)}, u32[]{:S(2)}, u32[]{:S(2)}) collective-permute-start(bf16[2,4,512,256]{3,2,1,0:T(8,128)(2,1)} %turn_stack.2.refs_5_.refs_9_), channel_id=1, source_target_pairs={{0,8},{1,9},{2,10},{3,11},{4,12},{5,13},{6,14},{7,15},{8,0},{9,1},... | collective-permute-start | bytes 6291464 | tf_op jit(solution)/shard_map/ppermute | solution.py:761
  146.8 25.8 %collective-permute-start.18 = (bf16[1,4,512,256]{3,2,1,0:T(8,128)(2,1)}, bf16[1,4,512,256]{3,2,1,0:T(8,128)(2,1)S(1)}, u32[]{:S(2)}, u32[]{:S(2)}) collective-permute-start(bf16[1,4,512,256]{3,2,1,0:T(8,128)(2,1)} %get-tuple-element.188), channel_id=1, source_target_pairs={{0,1},{1,0},{2,3},{3,2},{4,5},{5,4},{6,7},{7,6},{8,9},{9,8},{10,11... | collective-permute-start | bytes 3145736 | tf_op jit(solution)/shard_map/ppermute | solution.py:761
  147.3 26.7 %collective-permute-start.19 = (bf16[1,4,512,256]{3,2,1,0:T(8,128)(2,1)}, bf16[1,4,512,256]{3,2,1,0:T(8,128)(2,1)}, u32[]{:S(2)}, u32[]{:S(2)}) collective-permute-start(bf16[1,4,512,256]{3,2,1,0:T(8,128)(2,1)} %get-tuple-element.191), channel_id=1, source_target_pairs={{0,16},{1,17},{2,18},{3,19},{4,20},{5,21},{6,22},{7,23},{8,24},{9,... | collective-permute-start | bytes 3145736 | tf_op jit(solution)/shard_map/ppermute | solution.py:761
  147.7 26.8 %collective-permute-start.16 = (bf16[1,4,512,256]{3,2,1,0:T(8,128)(2,1)}, bf16[1,4,512,256]{3,2,1,0:T(8,128)(2,1)}, u32[]{:S(2)}, u32[]{:S(2)}) collective-permute-start(bf16[1,4,512,256]{3,2,1,0:T(8,128)(2,1)} %get-tuple-element.188), channel_id=1, source_target_pairs={{0,8},{1,9},{2,10},{3,11},{4,12},{5,13},{6,14},{7,15},{8,0},{9,1},... | collective-permute-start | bytes 3145736 | tf_op jit(solution)/shard_map/ppermute | solution.py:761
  147.7 27.2 %collective-permute-start.17 = (bf16[1,4,512,256]{3,2,1,0:T(8,128)(2,1)}, bf16[1,4,512,256]{3,2,1,0:T(8,128)(2,1)}, u32[]{:S(2)}, u32[]{:S(2)}) collective-permute-start(bf16[1,4,512,256]{3,2,1,0:T(8,128)(2,1)} %get-tuple-element.189), channel_id=1, source_target_pairs={{0,8},{1,9},{2,10},{3,11},{4,12},{5,13},{6,14},{7,15},{8,0},{9,1},... | collective-permute-start | bytes 3145736 | tf_op jit(solution)/shard_map/ppermute | solution.py:761
  172.5 27.4 %collective-permute-start.20 = (bf16[2,4,512,256]{3,2,1,0:T(8,128)(2,1)}, bf16[2,4,512,256]{3,2,1,0:T(8,128)(2,1)}, u32[]{:S(2)}, u32[]{:S(2)}) collective-permute-start(bf16[2,4,512,256]{3,2,1,0:T(8,128)(2,1)} %collective-permute-done.11.refs_1_.refs_5_.refs_9_), channel_id=1, source_target_pairs={{0,8},{1,9},{2,10},{3,11},{4,12},{5,13},{6,14},{7,15},{8,0},{9,1},... | collective-permute-start | bytes 6291464 | tf_op jit(solution)/shard_map/ppermute | solution.py:761
  173.9 50.7 %collective-permute-start.24 = (bf16[2,4,512,256]{3,2,1,0:T(8,128)(2,1)S(1)}, bf16[2,4,512,256]{3,2,1,0:T(8,128)(2,1)}, u32[]{:S(2)}, u32[]{:S(2)}) collective-permute-start(bf16[2,4,512,256]{3,2,1,0:T(8,128)(2,1)S(1)} %copy-done), channel_id=1, source_target_pairs={{0,16},{1,17},{2,18},{3,19},{4,20},{5,21},{6,22},{7,23},{8,24},{9,... | collective-permute-start | bytes 6291464 | tf_op jit(solution)/shard_map/ppermute | solution.py:761
  174.5 50.1 %collective-permute-start.25 = (bf16[2,4,512,256]{3,2,1,0:T(8,128)(2,1)S(1)}, bf16[2,4,512,256]{3,2,1,0:T(8,128)(2,1)}, u32[]{:S(2)}, u32[]{:S(2)}) collective-permute-start(bf16[2,4,512,256]{3,2,1,0:T(8,128)(2,1)S(1)} %copy-done), channel_id=1, source_target_pairs={{0,1},{1,0},{2,3},{3,2},{4,5},{5,4},{6,7},{7,6},{8,9},{9,8},{10,11... | collective-permute-start | bytes 6291464 | tf_op jit(solution)/shard_map/ppermute | solution.py:761
  175.0 24.8 %collective-permute-start.21 = (bf16[1,4,512,256]{3,2,1,0:T(8,128)(2,1)S(1)}, bf16[1,4,512,256]{3,2,1,0:T(8,128)(2,1)}, u32[]{:S(2)}, u32[]{:S(2)}) collective-permute-start(bf16[1,4,512,256]{3,2,1,0:T(8,128)(2,1)S(1)} %collective-permute-done.18.refs_14_.refs_7_), channel_id=1, source_target_pairs={{0,8},{1,9},{2,10},{3,11},{4,12},{5,13},{6,14},{7,15},{8,0},{9,1},... | collective-permute-start | bytes 3145736 | tf_op jit(solution)/shard_map/ppermute | solution.py:761
  175.0 24.9 %collective-permute-start.22 = (bf16[1,4,512,256]{3,2,1,0:T(8,128)(2,1)}, bf16[1,4,512,256]{3,2,1,0:T(8,128)(2,1)}, u32[]{:S(2)}, u32[]{:S(2)}) collective-permute-start(bf16[1,4,512,256]{3,2,1,0:T(8,128)(2,1)} %collective-permute-done.19.refs_15_.refs_11_), channel_id=1, source_target_pairs={{0,8},{1,9},{2,10},{3,11},{4,12},{5,13},{6,14},{7,15},{8,0},{9,1},... | collective-permute-start | bytes 3145736 | tf_op jit(solution)/shard_map/ppermute | solution.py:761
  199.8 26.0 %collective-permute-start.23 = (bf16[2,4,2,512,256]{4,3,2,1,0:T(8,128)(2,1)}, bf16[2,4,2,512,256]{4,3,2,1,0:T(8,128)(2,1)}, u32[]{:S(2)}, u32[]{:S(2)}) collective-permute-start(bf16[2,4,2,512,256]{4,3,2,1,0:T(8,128)(2,1)} %get-tuple-element.198), channel_id=1, source_target_pairs={{0,8},{1,9},{2,10},{3,11},{4,12},{5,13},{6,14},{7,15},{8,0},{9,1},... | collective-permute-start | bytes 12582920 | tf_op jit(solution)/shard_map/ppermute | solution.py:761
  224.7 10.6 %collective-permute-start.26 = (bf16[2,4,2,512,256]{4,3,2,1,0:T(8,128)(2,1)}, bf16[2,4,2,512,256]{4,3,2,1,0:T(8,128)(2,1)}, u32[]{:S(2)}, u32[]{:S(2)}) collective-permute-start(bf16[2,4,2,512,256]{4,3,2,1,0:T(8,128)(2,1)} %get-tuple-element.201), channel_id=1, source_target_pairs={{0,8},{1,9},{2,10},{3,11},{4,12},{5,13},{6,14},{7,15},{8,0},{9,1},... | collective-permute-start | bytes 12582920 | tf_op jit(solution)/shard_map/ppermute | solution.py:761
  225.2 27.5 %collective-permute-start.28 = (bf16[2,4,512,256]{3,2,1,0:T(8,128)(2,1)S(1)}, bf16[2,4,512,256]{3,2,1,0:T(8,128)(2,1)}, u32[]{:S(2)}, u32[]{:S(2)}) collective-permute-start(bf16[2,4,512,256]{3,2,1,0:T(8,128)(2,1)S(1)} %copy-done), channel_id=1, source_target_pairs={{0,8},{1,9},{2,10},{3,11},{4,12},{5,13},{6,14},{7,15},{8,0},{9,1},... | collective-permute-start | bytes 6291464 | tf_op jit(solution)/shard_map/ppermute | solution.py:761
  225.3 28.1 %collective-permute-start.29 = (bf16[2,4,512,256]{3,2,1,0:T(8,128)(2,1)}, bf16[2,4,512,256]{3,2,1,0:T(8,128)(2,1)}, u32[]{:S(2)}, u32[]{:S(2)}) collective-permute-start(bf16[2,4,512,256]{3,2,1,0:T(8,128)(2,1)} %collective-permute-done.24.refs_7_.refs_11_), channel_id=1, source_target_pairs={{0,8},{1,9},{2,10},{3,11},{4,12},{5,13},{6,14},{7,15},{8,0},{9,1},... | collective-permute-start | bytes 6291464 | tf_op jit(solution)/shard_map/ppermute | solution.py:761
  246.6 35.2 %collective-permute-start.27 = (bf16[2,4,512,256]{3,2,1,0:T(8,128)(2,1)}, bf16[2,4,512,256]{3,2,1,0:T(8,128)(2,1)}, u32[]{:S(2)}, u32[]{:S(2)}) collective-permute-start(bf16[2,4,512,256]{3,2,1,0:T(8,128)(2,1)} %collective-permute-done.25.refs_5_.refs_9_), channel_id=1, source_target_pairs={{0,8},{1,9},{2,10},{3,11},{4,12},{5,13},{6,14},{7,15},{8,0},{9,1},... | collective-permute-start | bytes 6291464 | tf_op jit(solution)/shard_map/ppermute | solution.py:761
  249.2 28.1 %collective-permute-start.30 = (bf16[1,4,512,256]{3,2,1,0:T(8,128)(2,1)}, bf16[1,4,512,256]{3,2,1,0:T(8,128)(2,1)S(1)}, u32[]{:S(2)}, u32[]{:S(2)}) collective-permute-start(bf16[1,4,512,256]{3,2,1,0:T(8,128)(2,1)} %slice.58), channel_id=1, source_target_pairs={{0,1},{1,0},{2,3},{3,2},{4,5},{5,4},{6,7},{7,6},{8,9},{9,8},{10,11... | collective-permute-start | bytes 3145736 | tf_op jit(solution)/shard_map/ppermute | solution.py:761
  250.7 26.7 %collective-permute-start.31 = (bf16[1,4,512,256]{3,2,1,0:T(8,128)(2,1)}, bf16[1,4,512,256]{3,2,1,0:T(8,128)(2,1)}, u32[]{:S(2)}, u32[]{:S(2)}) collective-permute-start(bf16[1,4,512,256]{3,2,1,0:T(8,128)(2,1)} %slice.59), channel_id=1, source_target_pairs={{0,16},{1,17},{2,18},{3,19},{4,20},{5,21},{6,22},{7,23},{8,24},{9,... | collective-permute-start | bytes 3145736 | tf_op jit(solution)/shard_map/ppermute | solution.py:761
  252.7 66.9 %collective-permute-start.34 = (bf16[2,4,512,256]{3,2,1,0:T(8,128)(2,1)}, bf16[2,4,512,256]{3,2,1,0:T(8,128)(2,1)}, u32[]{:S(2)}, u32[]{:S(2)}) collective-permute-start(bf16[2,4,512,256]{3,2,1,0:T(8,128)(2,1)} %get-tuple-element.209.refs_17_), channel_id=1, source_target_pairs={{0,1},{1,0},{2,3},{3,2},{4,5},{5,4},{6,7},{7,6},{8,9},{9,8},{10,11... | collective-permute-start | bytes 6291464 | tf_op jit(solution)/shard_map/ppermute | solution.py:761
  253.4 67.4 %collective-permute-start.35 = (bf16[2,4,512,256]{3,2,1,0:T(8,128)(2,1)}, bf16[2,4,512,256]{3,2,1,0:T(8,128)(2,1)}, u32[]{:S(2)}, u32[]{:S(2)}) collective-permute-start(bf16[2,4,512,256]{3,2,1,0:T(8,128)(2,1)} %get-tuple-element.210.refs_18_), channel_id=1, source_target_pairs={{0,16},{1,17},{2,18},{3,19},{4,20},{5,21},{6,22},{7,23},{8,24},{9,... | collective-permute-start | bytes 6291464 | tf_op jit(solution)/shard_map/ppermute | solution.py:761
  277.4 3.4 collective-permute-start.32
  277.5 4.4 collective-permute-start.33
  280.8 118.9 %collective-permute-start.38 = (bf16[2,4,2,512,256]{4,3,2,1,0:T(8,128)(2,1)}, bf16[2,4,2,512,256]{4,3,2,1,0:T(8,128)(2,1)}, u32[]{:S(2)}, u32[]{:S(2)}) collective-permute-start(bf16[2,4,2,512,256]{4,3,2,1,0:T(8,128)(2,1)} %get-tuple-element.246), channel_id=1, source_target_pairs={{0,8},{1,9},{2,10},{3,11},{4,12},{5,13},{6,14},{7,15},{8,0},{9,1},... | collective-permute-start | bytes 12582920 | tf_op jit(solution)/shard_map/ppermute | solution.py:761
  307.9 91.8 %collective-permute-start.39 = (bf16[2,4,2,512,256]{4,3,2,1,0:T(8,128)(2,1)}, bf16[2,4,2,512,256]{4,3,2,1,0:T(8,128)(2,1)}, u32[]{:S(2)}, u32[]{:S(2)}) collective-permute-start(bf16[2,4,2,512,256]{4,3,2,1,0:T(8,128)(2,1)} %get-tuple-element.247), channel_id=1, source_target_pairs={{0,8},{1,9},{2,10},{3,11},{4,12},{5,13},{6,14},{7,15},{8,0},{9,1},... | collective-permute-start | bytes 12582920 | tf_op jit(solution)/shard_map/ppermute | solution.py:761
  326.5 55.5 %collective-permute-start.36 = (bf16[4,512,256]{2,1,0:T(8,128)(2,1)}, bf16[4,512,256]{2,1,0:T(8,128)(2,1)S(1)}, u32[]{:S(2)}, u32[]{:S(2)}) collective-permute-start(bf16[4,512,256]{2,1,0:T(8,128)(2,1)} %get-tuple-element.225.refs_13_), channel_id=1, source_target_pairs={{0,16},{1,17},{2,18},{3,19},{4,20},{5,21},{6,22},{7,23},{8,24},{9,... | collective-permute-start | bytes 3145736 | tf_op jit(solution)/shard_map/ppermute | solution.py:761
  328.0 54.0 %collective-permute-start.37 = (bf16[4,512,256]{2,1,0:T(8,128)(2,1)}, bf16[4,512,256]{2,1,0:T(8,128)(2,1)S(1)}, u32[]{:S(2)}, u32[]{:S(2)}) collective-permute-start(bf16[4,512,256]{2,1,0:T(8,128)(2,1)} %get-tuple-element.226.refs_14_), channel_id=1, source_target_pairs={{0,1},{1,0},{2,3},{3,2},{4,5},{5,4},{6,7},{7,6},{8,9},{9,8},{10,11... | collective-permute-start | bytes 3145736 | tf_op jit(solution)/shard_map/ppermute | solution.py:761
  328.7 50.4 %copy-start.21 = (f32[8,4,256]{2,1,0:T(4,128)S(1)}, f32[8,4,256]{2,1,0:T(4,128)}, u32[]{:S(2)}) copy-start(f32[8,4,256]{2,1,0:T(4,128)} %get-tuple-element.235) | copy-start | bytes 98308
  328.7 50.4 %copy-start.22 = (f32[8,4,256]{2,1,0:T(4,128)S(1)}, f32[8,4,256]{2,1,0:T(4,128)}, u32[]{:S(2)}) copy-start(f32[8,4,256]{2,1,0:T(4,128)} %get-tuple-element.236) | copy-start | bytes 98308
  387.5 64.0 %collective-permute-start.47 = (bf16[2,512,256]{2,1,0:T(8,128)(2,1)}, bf16[2,512,256]{2,1,0:T(8,128)(2,1)S(1)}, u32[]{:S(2)}, u32[]{:S(2)}) collective-permute-start(bf16[2,512,256]{2,1,0:T(8,128)(2,1)} %get-tuple-element.241.refs_10_), channel_id=1, source_target_pairs={{0,2},{1,3},{2,0},{3,1},{4,6},{5,7},{6,4},{7,5},{8,10},{9,11},{10,... | collective-permute-start | bytes 1572872 | tf_op jit(solution)/shard_map/ppermute | solution.py:761
  397.4 54.3 %collective-permute-start.48 = (bf16[2,512,256]{2,1,0:T(8,128)(2,1)}, bf16[2,512,256]{2,1,0:T(8,128)(2,1)}, u32[]{:S(2)}, u32[]{:S(2)}) collective-permute-start(bf16[2,512,256]{2,1,0:T(8,128)(2,1)} %get-tuple-element.242.refs_11_), channel_id=1, source_target_pairs={{0,4},{1,5},{2,6},{3,7},{4,0},{5,1},{6,2},{7,3},{8,12},{9,13},{10,... | collective-permute-start | bytes 1572872 | tf_op jit(solution)/shard_map/ppermute | solution.py:761
  398.2 53.5 %collective-permute-start.49 = (bf16[2,512,256]{2,1,0:T(8,128)(2,1)}, bf16[2,512,256]{2,1,0:T(8,128)(2,1)}, u32[]{:S(2)}, u32[]{:S(2)}) collective-permute-start(bf16[2,512,256]{2,1,0:T(8,128)(2,1)} %get-tuple-element.243.refs_12_), channel_id=1, source_target_pairs={{0,6},{1,7},{2,4},{3,5},{4,2},{5,3},{6,0},{7,1},{8,14},{9,15},{10,... | collective-permute-start | bytes 1572872 | tf_op jit(solution)/shard_map/ppermute | solution.py:761
  408.7 45.7 %collective-permute-start.50 = (bf16[2,4,512,256]{3,2,1,0:T(8,128)(2,1)}, bf16[2,4,512,256]{3,2,1,0:T(8,128)(2,1)S(1)}, u32[]{:S(2)}, u32[]{:S(2)}) collective-permute-start(bf16[2,4,512,256]{3,2,1,0:T(8,128)(2,1)} %get-tuple-element.248.refs_13_), channel_id=1, source_target_pairs={{0,1},{1,0},{2,3},{3,2},{4,5},{5,4},{6,7},{7,6},{8,9},{9,8},{10,11... | collective-permute-start | bytes 6291464 | tf_op jit(solution)/shard_map/ppermute | solution.py:761
  410.2 45.4 %collective-permute-start.51 = (bf16[2,4,512,256]{3,2,1,0:T(8,128)(2,1)}, bf16[2,4,512,256]{3,2,1,0:T(8,128)(2,1)}, u32[]{:S(2)}, u32[]{:S(2)}) collective-permute-start(bf16[2,4,512,256]{3,2,1,0:T(8,128)(2,1)} %get-tuple-element.249.refs_14_), channel_id=1, source_target_pairs={{0,16},{1,17},{2,18},{3,19},{4,20},{5,21},{6,22},{7,23},{8,24},{9,... | collective-permute-start | bytes 6291464 | tf_op jit(solution)/shard_map/ppermute | solution.py:761
  451.6 12.1 %collective-permute-start.40 = (bf16[16,16,2176]{2,1,0:T(8,128)(2,1)}, bf16[16,16,2176]{2,1,0:T(8,128)(2,1)S(1)}, u32[]{:S(2)}, u32[]{:S(2)}) collective-permute-start(bf16[16,16,2176]{2,1,0:T(8,128)(2,1)} %get-tuple-element.252), channel_id=1, source_target_pairs={{0,8},{1,9},{2,10},{3,11},{4,12},{5,13},{6,14},{7,15},{8,0},{9,1},... | collective-permute-start | bytes 3342344 | tf_op jit(solution)/shard_map/ppermute | solution.py:761
  461.7 23.0 %collective-permute-start.52 = (bf16[4,512,256]{2,1,0:T(8,128)(2,1)}, bf16[4,512,256]{2,1,0:T(8,128)(2,1)S(1)}, u32[]{:S(2)}, u32[]{:S(2)}) collective-permute-start(bf16[4,512,256]{2,1,0:T(8,128)(2,1)} %get-tuple-element.266), channel_id=1, source_target_pairs={{0,16},{1,17},{2,18},{3,19},{4,20},{5,21},{6,22},{7,23},{8,24},{9,... | collective-permute-start | bytes 3145736 | tf_op jit(solution)/shard_map/ppermute | solution.py:761
  462.2 26.3 %collective-permute-start.53 = (bf16[4,512,256]{2,1,0:T(8,128)(2,1)}, bf16[4,512,256]{2,1,0:T(8,128)(2,1)S(1)}, u32[]{:S(2)}, u32[]{:S(2)}) collective-permute-start(bf16[4,512,256]{2,1,0:T(8,128)(2,1)} %get-tuple-element.267), channel_id=1, source_target_pairs={{0,1},{1,0},{2,3},{3,2},{4,5},{5,4},{6,7},{7,6},{8,9},{9,8},{10,11... | collective-permute-start | bytes 3145736 | tf_op jit(solution)/shard_map/ppermute | solution.py:761
  467.3 31.2 %collective-permute-start.41 = (bf16[4,16,2176]{2,1,0:T(8,128)(2,1)}, bf16[4,16,2176]{2,1,0:T(8,128)(2,1)S(1)}, u32[]{:S(2)}, u32[]{:S(2)}) collective-permute-start(bf16[4,16,2176]{2,1,0:T(8,128)(2,1)} %get-tuple-element.254), channel_id=1, source_target_pairs={{0,1},{1,0},{2,3},{3,2},{4,5},{5,4},{6,7},{7,6},{8,9},{9,8},{10,11... | collective-permute-start | bytes 835592 | tf_op jit(solution)/shard_map/ppermute | solution.py:761
  493.2 19.7 %collective-permute-start.54 = (bf16[2,512,256]{2,1,0:T(8,128)(2,1)}, bf16[2,512,256]{2,1,0:T(8,128)(2,1)S(1)}, u32[]{:S(2)}, u32[]{:S(2)}) collective-permute-start(bf16[2,512,256]{2,1,0:T(8,128)(2,1)} %get-tuple-element.269), channel_id=1, source_target_pairs={{0,2},{1,3},{2,0},{3,1},{4,6},{5,7},{6,4},{7,5},{8,10},{9,11},{10,... | collective-permute-start | bytes 1572872 | tf_op jit(solution)/shard_map/ppermute | solution.py:761
  494.0 41.1 %collective-permute-start.55 = (bf16[2,512,256]{2,1,0:T(8,128)(2,1)}, bf16[2,512,256]{2,1,0:T(8,128)(2,1)S(1)}, u32[]{:S(2)}, u32[]{:S(2)}) collective-permute-start(bf16[2,512,256]{2,1,0:T(8,128)(2,1)} %get-tuple-element.270), channel_id=1, source_target_pairs={{0,4},{1,5},{2,6},{3,7},{4,0},{5,1},{6,2},{7,3},{8,12},{9,13},{10,... | collective-permute-start | bytes 1572872 | tf_op jit(solution)/shard_map/ppermute | solution.py:761
  495.9 39.2 %collective-permute-start.56 = (bf16[2,512,256]{2,1,0:T(8,128)(2,1)}, bf16[2,512,256]{2,1,0:T(8,128)(2,1)S(1)}, u32[]{:S(2)}, u32[]{:S(2)}) collective-permute-start(bf16[2,512,256]{2,1,0:T(8,128)(2,1)} %get-tuple-element.271), channel_id=1, source_target_pairs={{0,6},{1,7},{2,4},{3,5},{4,2},{5,3},{6,0},{7,1},{8,14},{9,15},{10,... | collective-permute-start | bytes 1572872 | tf_op jit(solution)/shard_map/ppermute | solution.py:761
  497.6 6.5 %collective-permute-start.42 = (bf16[4,16,2176]{2,1,0:T(8,128)(2,1)S(1)}, bf16[4,16,2176]{2,1,0:T(8,128)(2,1)S(1)}, u32[]{:S(2)}, u32[]{:S(2)}) collective-permute-start(bf16[4,16,2176]{2,1,0:T(8,128)(2,1)S(1)} %copy-done.49), channel_id=1, source_target_pairs={{0,16},{1,17},{2,18},{3,19},{4,20},{5,21},{6,22},{7,23},{8,24},{9,... | collective-permute-start | bytes 835592 | tf_op jit(solution)/shard_map/ppermute | solution.py:761
  498.4 9.0 %collective-permute-start.43 = (bf16[4,16,2176]{2,1,0:T(8,128)(2,1)S(1)}, bf16[4,16,2176]{2,1,0:T(8,128)(2,1)S(1)}, u32[]{:S(2)}, u32[]{:S(2)}) collective-permute-start(bf16[4,16,2176]{2,1,0:T(8,128)(2,1)S(1)} %copy-done.48), channel_id=1, source_target_pairs={{0,17},{1,16},{2,19},{3,18},{4,21},{5,20},{6,23},{7,22},{8,25},{9,... | collective-permute-start | bytes 835592 | tf_op jit(solution)/shard_map/ppermute | solution.py:761
  510.1 34.3 %collective-permute-start.44 = (bf16[1,16,2176]{2,1,0:T(8,128)(2,1)}, bf16[1,16,2176]{2,1,0:T(8,128)(2,1)S(1)}, u32[]{:S(2)}, u32[]{:S(2)}) collective-permute-start(bf16[1,16,2176]{2,1,0:T(8,128)(2,1)} %get-tuple-element.258), channel_id=1, source_target_pairs={{0,2},{1,3},{2,0},{3,1},{4,6},{5,7},{6,4},{7,5},{8,10},{9,11},{10,... | collective-permute-start | bytes 208904 | tf_op jit(solution)/shard_map/ppermute | solution.py:761
  510.3 34.1 %collective-permute-start.45 = (bf16[1,16,2176]{2,1,0:T(8,128)(2,1)}, bf16[1,16,2176]{2,1,0:T(8,128)(2,1)S(1)}, u32[]{:S(2)}, u32[]{:S(2)}) collective-permute-start(bf16[1,16,2176]{2,1,0:T(8,128)(2,1)} %get-tuple-element.259), channel_id=1, source_target_pairs={{0,4},{1,5},{2,6},{3,7},{4,0},{5,1},{6,2},{7,3},{8,12},{9,13},{10,... | collective-permute-start | bytes 208904 | tf_op jit(solution)/shard_map/ppermute | solution.py:761
  512.9 31.6 %collective-permute-start.46 = (bf16[1,16,2176]{2,1,0:T(8,128)(2,1)}, bf16[1,16,2176]{2,1,0:T(8,128)(2,1)S(1)}, u32[]{:S(2)}, u32[]{:S(2)}) collective-permute-start(bf16[1,16,2176]{2,1,0:T(8,128)(2,1)} %get-tuple-element.260), channel_id=1, source_target_pairs={{0,6},{1,7},{2,4},{3,5},{4,2},{5,3},{6,0},{7,1},{8,14},{9,15},{10,... | collective-permute-start | bytes 208904 | tf_op jit(solution)/shard_map/ppermute | solution.py:761
  547.3 1.4 collective-permute-start.57
  549.4 3.6 collective-permute-start.58
  553.1 3.6 collective-permute-start.59
  556.7 9.2 %collective-permute-start.60 = (f32[8,128]{1,0:T(8,128)S(1)}, f32[8,128]{1,0:T(8,128)S(1)}, u32[]{:S(2)}, u32[]{:S(2)}) collective-permute-start(f32[8,128]{1,0:T(8,128)S(1)} %add.55), channel_id=1, source_target_pairs={{0,2},{1,3},{2,0},{3,1},{4,6},{5,7},{6,4},{7,5},{8,10},{9,11},{10,... | collective-permute-start | bytes 12296 | tf_op jit(solution)/shard_map/ppermute | solution.py:761
  565.9 8.2 %collective-permute-start.61 = (f32[8,128]{1,0:T(8,128)S(1)}, f32[8,128]{1,0:T(8,128)S(1)}, u32[]{:S(2)}, u32[]{:S(2)}) collective-permute-start(f32[8,128]{1,0:T(8,128)S(1)} %add.56), channel_id=1, source_target_pairs={{0,4},{1,5},{2,6},{3,7},{4,0},{5,1},{6,2},{7,3},{8,12},{9,13},{10,... | collective-permute-start | bytes 12296 | tf_op jit(solution)/shard_map/ppermute | solution.py:761
  (52 other events, 495.8 us)

commit v4 on v3

--- a/solution.py
+++ b/solution.py
@@ -525,7 +525,7 @@
         out_shape=out_shape,
         input_output_aliases=aliases,
         compiler_params=params(),
-        cost_estimate=cost(10),
+        cost_estimate=cost(4),
         name=f"experts_{0 if first else 1}{half}",
     )(at, *args, *after)
 
@@ -857,15 +857,17 @@
         functools.partial(block_sum_kernel, parts, len(terms)),
         out_shape=[jax.ShapeDtypeStruct(shape, BF)] * parts,
         compiler_params=params(),
+        cost_estimate=cost(0.1),
         name="block_sum",
     )(*terms)
 
 
-def scatter_dense(near, far):
+def scatter_dense(near, far, beside):
     parts = block_sum([near, swap(far, CORE_BIT)], 4)
     got = [swap(parts[1], Y_BIT), swap(parts[2], X_BIT), swap(parts[3], X_BIT | Y_BIT)]
-    parts = block_sum([parts[0]] + got, 4)
-    return [parts[0]] + [swap(parts[z], Z_BITS[z - 1]) for z in (1, 2, 3)]
+    keep, beside = lax.optimization_barrier((parts[0], beside))
+    parts = block_sum([keep] + got, 4)
+    return beside, [parts[0]] + [swap(parts[z], Z_BITS[z - 1]) for z in (1, 2, 3)]
 
 
 def fold_cores_kernel(n0, n1, g0, g1, a_keep, b_keep, a_send, b_send):
@@ -933,44 +935,46 @@
     return jnp.sum(jnp.sum(array, axis=1, keepdims=True), axis=0, keepdims=True)
 
 
-def expert_update_kernel(*refs):
-    parts, (wi, fi, si, wo, fo, so), outs = refs[:8], refs[8:14], refs[14:]
-    sums = outs[6]
+def expert_update_kernel(given, *refs):
+    parts, (wi, fi, si, wo, fo, so, before), refs = refs[:4], refs[4:11], refs[11:]
+    outs, sums = refs[given : given + 6], refs[given + 6]
     lane = lane_iota(1, 128)
-    kept = jnp.zeros((1, 128), F32)
-    moved = jnp.zeros((1, 128), F32)
-    cols = parts[0].shape[2]
+    kept, moved = before[0:1, :], before[1:2, :]
     for m, (weight, first, second, new) in enumerate(((wi, fi, si, outs[0:3]), (wo, fo, so, outs[3:6]))):
-        for k in range(2):
-            grad = parts[4 * k][m].astype(F32)
-            for part in parts[4 * k + 1 : 4 * k + 4]:
-                grad = grad + part[m].astype(F32)
-            span = slice(k * cols, (k + 1) * cols)
-            if m == 0:
-                at = (0, slice(None), span)
-            else:
-                grad = grad.T
-                at = (0, span, slice(None))
-            state = moments(weight[at], grad, first[at], second[at])
-            for ref, value in zip(new, state):
-                ref[at] = value
-            slot = lane == (8 if m == 0 else 10)
-            kept += jnp.where(slot, total_of(weight[at] * weight[at]), 0.0)
-            moved += jnp.where(slot, total_of(state[2] * state[2]), 0.0)
+        grad = parts[0][m].astype(F32)
+        for part in parts[1:]:
+            grad = grad + part[m].astype(F32)
+        if m:
+            grad = grad.T
+        state = moments(weight[0], grad, first[0], second[0])
+        for ref, value in zip(new, state):
+            ref[0] = value
+        slot = lane == (10 if m else 8)
+        kept += jnp.where(slot, total_of(weight[0] * weight[0]), 0.0)
+        moved += jnp.where(slot, total_of(state[2] * state[2]), 0.0)
     sums[...] = jnp.zeros_like(sums)
     sums[0:1, :] = kept
     sums[1:2, :] = moved
 
 
-def expert_update(parts, arrays):
+def expert_update(parts, arrays, sums, slice_index, done=()):
+    rows, cols = parts[0].shape[1:]
+    part = pl.BlockSpec(parts[0].shape, lambda i: (0, 0, 0))
+    enter = pl.BlockSpec((1, rows, cols), lambda i: (0, 0, slice_index))
+    leave = pl.BlockSpec((1, cols, rows), lambda i: (0, slice_index, 0))
+    total = pl.BlockSpec((8, 128), lambda i: (0, 0))
     shape = jax.ShapeDtypeStruct(arrays[0].shape, F32)
     return pl.pallas_call(
-        expert_update_kernel,
+        functools.partial(expert_update_kernel, len(done)),
+        grid=(1,),
+        in_specs=[part] * 4 + [enter] * 3 + [leave] * 3 + [total] + unread(done),
+        out_specs=[enter] * 3 + [leave] * 3 + [total],
         out_shape=[shape] * 6 + [jax.ShapeDtypeStruct((8, 128), F32)],
-        compiler_params=params(),
-        cost_estimate=cost(6),
-        name="expert_update",
-    )(*parts, *arrays)
+        input_output_aliases={11 + j: j for j in range(len(done))},
+        compiler_params=params(),
+        cost_estimate=cost(0.1),
+        name=f"expert_update_{slice_index}",
+    )(*parts, *arrays, sums, *done)
 
 
 def narrow(row, columns, rows):
@@ -1019,7 +1023,7 @@
         dense_update_kernel,
         out_shape=[jax.ShapeDtypeStruct(a.shape, F32) for a in states] + [jax.ShapeDtypeStruct((8, 128), F32)],
         compiler_params=params(),
-        cost_estimate=cost(3),
+        cost_estimate=cost(0.1),
         name="dense_update",
     )(*terms, sums, *states)
 
@@ -1144,9 +1148,9 @@
     near, x_in = lax.optimization_barrier((near, x_in))
     crossed = cross(near), (cross(x_in), cross(x_out))
     y_part, d_part, near_a, far_a, bias_a, leave_a = expert_pass(
-        at, lists, first_half(near, far_x, crossed), bias_cut(0), after=far_xy
-    )
-    near_two, *far_xy = lax.optimization_barrier((near_two, *far_xy))
+        at, lists, first_half(near, far_x, crossed), bias_cut(0)
+    )
+    y_part, *far_xy = lax.optimization_barrier((y_part, *far_xy))
     far_x_two, far_y_two = swap(near_two, X_BIT), swap(near_two, Y_BIT)
     crossed = cross(far_y), cross(far_xy[0]), cross(far_xy[1])
     y_half, d_half, near_b, far_b, bias_b, leave_b = expert_pass(
@@ -1154,12 +1158,14 @@
     )
     got_a = swap(far_a, CORE_BIT)
     far_b, far_x_two, far_y_two = lax.optimization_barrier((far_b, far_x_two, far_y_two))
+    diagonal = far_x_two[0:1], far_y_two[1:2]
     crossed = cross(near_two), cross(far_x_two)
     got_b = swap(far_b, CORE_BIT)
     one = fold_cores((near_a, near_b), (got_a, got_b))
-    a_send, far_x_two, far_y_two = lax.optimization_barrier((one[2], far_x_two, far_y_two))
+    far_y_crossed = cross(far_y_two)
+    a_send, far_y_crossed, *diagonal = lax.optimization_barrier((one[2], far_y_crossed, *diagonal))
     one = (*one[:2], a_send, one[3])
-    far_xy_two = swap(far_x_two[0:1], Y_BIT), swap(far_y_two[1:2], X_BIT)
+    far_xy_two = swap(diagonal[0], Y_BIT), swap(diagonal[1], X_BIT)
     even = lax.bitwise_xor(jnp.arange(ep, dtype=jnp.int32), ep_me)[:, None, None] % 2 == 0
     grad_bias = [jnp.where(even, bias_a, bias_b)]
     grad_leave_bias = jnp.where(even, leave_a, leave_b)
@@ -1169,21 +1175,27 @@
         after=one[2:],
     )
     y_part, *far_xy_two = lax.optimization_barrier((y_part, *far_xy_two))
-    crossed = cross(far_y_two), cross(far_xy_two[0]), cross(far_xy_two[1])
+    crossed = far_y_crossed, cross(far_xy_two[0]), cross(far_xy_two[1])
     got_a = swap(far_a, CORE_BIT)
     y, d, near_b, far_b, bias_b = expert_pass(
         at, lists, other_half(far_y_two, far_xy_two, crossed), bias_cut(1), leave_bias, (y_half, d_half), half=1,
         done=(y_part, d_part),
     )
+    far_b, *one_got = lax.optimization_barrier((far_b, *one_got))
     one = fold_first(*one[:2], *one_got)
     one_got = swap(one[2], X_BIT), swap(one[3], Y_BIT)
     got_b = swap(far_b, CORE_BIT)
+    two = fold_cores((near_a, near_b), (got_a, got_b))
+    two_got = swap(two[2], Y_BIT), swap(two[3], X_BIT)
     output, grad_hidden, grad_mixed, grad_out, grad_router, grad_scale = combine(
         meta, y, d, lcol, gcol, hidden, cot_pad, mixed, out_matrix, router_matrix, gains,
-        after=one,
-    )
+        after=list(one) + list(two[2:]),
+    )
+    grad_mixed, *one_got = lax.optimization_barrier((grad_mixed, *one_got))
     one = fold_second(*one[:2], *one_got)
-    two = fold_cores((near_a, near_b), (got_a, got_b))
+    one_got = [swap(one[z], Z_BITS[z - 1]) for z in (1, 2, 3)]
+    two = fold_first(*two[:2], *two_got)
+    two_got = swap(two[2], X_BIT), swap(two[3], Y_BIT)
     grad_bias.append(jnp.where(even, bias_a, bias_b))
     devices = rep * ep
     by_device = lambda a: jnp.pad(
@@ -1200,27 +1212,27 @@
         axis=1,
     )
     small_grads = jnp.pad(small_grads, ((0, 0), (0, 8 - small_grads.shape[1]), (0, 0)))
-    one_got = [swap(one[z], Z_BITS[z - 1]) for z in (1, 2, 3)]
-    two_got = swap(two[2], Y_BIT), swap(two[3], X_BIT)
     input_grad, near_dense, far_dense = attention_back(
         place, proj, probs, grad_mixed, grad_hidden, tok_pad, in_matrix, gains, grad_out, small_grads,
         after=list(one[1:]) + list(two[2:]),
     )
-    two = fold_first(*two[:2], *two_got, after=one_got)
-    two_got = swap(two[2], X_BIT), swap(two[3], Y_BIT)
-    dense_terms = scatter_dense(near_dense, far_dense)
+    far_dense, *got = lax.optimization_barrier((far_dense, *one_got, *two_got))
+    one_got, two_got = got[:3], got[3:]
     two = fold_second(*two[:2], *two_got)
+    far_dense, *two = lax.optimization_barrier((far_dense, *two))
     two_got = [swap(two[z], Z_BITS[z - 1]) for z in (1, 2, 3)]
-    parts = [one[0]] + one_got + [two[0]] + two_got
-    (in_first, in_second, in_step, out_first, out_second, out_step, sums) = expert_update(
-        parts, (expert_in, expert_in_first, expert_in_second, expert_out, expert_out_first, expert_out_second)
-    )
+    expert_states = (expert_in, expert_in_first, expert_in_second, expert_out, expert_out_first, expert_out_second)
+    *expert_new, sums = expert_update([one[0]] + list(one_got), expert_states, jnp.zeros((8, 128), F32), 0)
+    sums, dense_terms = scatter_dense(near_dense, far_dense, sums)
     dense_states = (
         heads_in, heads_in_first, heads_in_second, heads_out, heads_out_first, heads_out_second,
         router, router_first, router_second, scales, scales_first, scales_second,
         bias_in, bias_in_first, bias_in_second, bias_out, bias_out_first, bias_out_second,
     )
     *dense_new, sums = dense_update(dense_terms, sums, dense_states)
+    sums, *two_got = lax.optimization_barrier((sums, *two_got))
+    *expert_new, sums = expert_update([two[0]] + two_got, expert_states, sums, 1, done=expert_new)
+    in_first, in_second, in_step, out_first, out_second, out_step = expert_new
     sums = sum_everywhere(sums)
     counts = jnp.array(
         [3 * width * width, width * width, width * experts]

time: 593 us -> 556 us (0.938)
  waiting for transfers between devices: 117 us -> 86.9 us
    ppermute x62, waiting for transfers between devices: 117 us -> 86.9 us  [swap(): return lax.ppermute(array, AXES, [(d, d ^ bits) for d in range(devices)])]
    ppermute x62, starting transfers between devices: 82.7 us -> 76.8 us  [swap(): return lax.ppermute(array, AXES, [(d, d ^ bits) for d in range(devices)])]
    unnamed x124 -> x140, local copies, waits for them, and re-layouts: 26.8 us -> 24.8 us
  transfers between devices with their start and end apart: 62 -> 62, of which waited for: 19 -> 21; matrix products, arithmetic and copies ran while one was open for 5% -> 5% of each run, Pallas kernels for 54% -> 56%
where the time goes in v4:
time: 556 us; the launch traced here: 546 us
  Pallas kernels  333 us (60%)
  waiting for transfers between devices  86.9 us (16%)
  starting transfers between devices  76.8 us (14%)
  local copies, waits for them, and re-layouts  37.9 us (7%)
  other arithmetic  9.75 us (2%)
    pallas_call x4, Pallas kernels, expert_pass(): pl.pallas_call(kernel, grid_spec=pltpu.PrefetchScalarGridSpec(num_scalar_...  96.8 us
    ppermute x62, waiting for transfers between devices, swap(): return lax.ppermute(array, AXES, [(d, d ^ bits) for d in range(devices)])  86.9 us
    ppermute x62, starting transfers between devices, swap(): return lax.ppermute(array, AXES, [(d, d ^ bits) for d in range(devices)])  76.8 us
    pallas_call x1, Pallas kernels, combine(): pl.pallas_call(behind(combine_kernel, 11, after), grid_spec=pltpu.Prefetc...  50.1 us
    pallas_call x1, Pallas kernels, attention_back(): pl.pallas_call(behind(attention_back_kernel, 10, after), grid_spec=pltpu....  41 us
    pallas_call x1, Pallas kernels, attention(): pl.pallas_call(behind(attention_kernel, 6, after), grid=(images,), in_spe...  28.1 us
    pallas_call x1, Pallas kernels, gather(): pl.pallas_call(behind(gather_kernel, 5, after), grid_spec=pltpu.PrefetchS...  27.6 us
    unnamed x140, local copies, waits for them, and re-layouts  24.8 us
  transfers between devices with their start and end apart: 62, of which 21 were waited for; matrix products, arithmetic and copies ran while one was open for 5% of the time, Pallas kernels for 56%

profile of v4, /device:TPU:0, one launch (start us, length us, event | category | flops | bytes accessed | tf_op | source)
XLA Modules:
  0.0 546.3 jit_solution(5253512593797803007)
XLA Ops:
  5.5 3.1 collective-permute-start
  8.6 2.6 collective-permute-start.1
  14.9 4.6 spread_rows.1
  21.4 1.9 stack.34.refs_0_
  23.3 1.7 collective-permute-start.3
  25.0 1.5 collective-permute-start.4
  29.7 9.6 %places.1 = (f32[10,8,208]{2,1,0:T(8,128)}, f32[2080,8]{1,0:T(8,128)}, s32[20,8]{1,0:T(8,128)}) custom-call(f32[8,2080]{1,0:T(8,128)} %pad.32.clone.rows_ref, f32[2080,8]{1,0:T(8,128)} %pad_bitcast_fusion.cols_ref), custom_call_target="tpu_custom_call" | custom-call | flops 2000000000 | bytes 200000 | tf_op jit(solution)/shard_map/places/pallas_call | solution.py:220
  40.4 2.3 stack.35
  43.2 3.5 collective-permute-start.8
  47.8 3.9 assemble.1
  51.7 28.1 %attention.1 = (bf16[2080,1536]{1,0:T(8,128)(2,1)}, bf16[10,8,208,208]{3,2,1,0:T(8,128)(2,1)}, bf16[2080,512]{1,0:T(8,128)(2,1)}, f32[2080,512]{1,0:T(8,128)}, b...) custom-call(bf16[2080,512]{1,0:T(8,128)(2,1)} %get-tuple-element.199.refs_4_.refs_0_.refs_5_, ...), custom_call_target="tpu_custom_call" | custom-call | flops 8000000000 | bytes 800000 | tf_op jit(solution)/shard_map/attention/pallas_call | solution.py:314
  79.8 1.7 collective-permute-done.8.refs_2_
  82.5 3.0 turn_stack.2.refs_5_.refs_9_
  85.6 1.7 collective-permute-start.10
  88.8 11.7 %collective-permute-start.13 = (bf16[2,512,256]{2,1,0:T(8,128)(2,1)S(1)}, bf16[2,512,256]{2,1,0:T(8,128)(2,1)S(1)}, u32[]{:S(2)}, u32[]{:S(2)}) collective-permute-start(bf16[2,512,256]{2,1,0:T(8,128)(2,1)S(1)} %pad_maximum_fusion.1.refs_0_), channel_id=1, source_target_pairs={{0,2},{1,3},{2,0},{3,1},{4,6},{5,7},{6,4},{7,5},{8,10},{9,11},{10,... | collective-permute-start | bytes 1572872 | tf_op jit(solution)/shard_map/ppermute | solution.py:761
  103.0 27.6 %gather.1 = (bf16[8,624,512]{2,1,0:T(8,128)(2,1)}, bf16[8,624,512]{2,1,0:T(8,128)(2,1)}, bf16[8,512,624]{2,1,0:T(8,128)(2,1)}, bf16[8,512,624]{2,1,0:T(8,128)(2,1)}) custom-call(s32[20,8]{1,0:T(8,128)} %get-tuple-element.198.refs_0_, bf16[2080,512]{1,0:T(8,128)(2,1)} %get-tuple-element.207.refs_1_, bf16[2080,512]{1,0:T(8,128)(2,1)} %get-tuple-element.208.refs_2_.refs_6_, ...), custom_call_target="tpu_custom_call" | custom-call | flops 8000000000 | bytes 800000 | tf_op jit(solution)/shard_map/gather/pallas_call | solution.py:378
  130.6 8.1 %collective-permute-done.14.refs_2_ = bf16[2,512,256]{2,1,0:T(8,128)(2,1)S(1)} collective-permute-done((bf16[2,512,256]{2,1,0:T(8,128)(2,1)S(1)}, bf16[2,512,256]{2,1,0:T(8,128)(2,1)S(1)}, u32[]{:S(2)}, u32[]{:S(2)}) %collective-permute-start.14) | collective-permute-done | bytes 524320 | tf_op jit(solution)/shard_map/ppermute | solution.py:761
  139.7 3.0 turn_stack.3.refs_2_.refs_5_.refs_9_
  142.7 4.1 pick.1
  148.2 6.1 %collective-permute-done.17.refs_8_ = bf16[1,4,512,256]{3,2,1,0:T(8,128)(2,1)} collective-permute-done((bf16[1,4,512,256]{3,2,1,0:T(8,128)(2,1)}, bf16[1,4,512,256]{3,2,1,0:T(8,128)(2,1)}, u32[]{:S(2)}, u32[]{:S(2)}) %collective-permute-start.17) | collective-permute-done | bytes 1048608 | tf_op jit(solution)/shard_map/ppermute | solution.py:761
  157.9 25.0 %experts_00.1 = (f32[8,624,512]{2,1,0:T(8,128)}, f32[8,624,512]{2,1,0:T(8,128)}, bf16[2,4,2,512,256]{4,3,2,1,0:T(8,128)(2,1)}, bf16[2,4,2,512,256]{4,3,2,1,0:T(8...) custom-call(s32[10]{0:T(128)} %pad_add_fusion.refs_0_, bf16[8,624,512]{2,1,0:T(8,128)(2,1)} %get-tuple-element.212.refs_4_.refs_1_, ...), custom_call_target="tpu_custom_call" | custom-call | flops 4000000000 | bytes 400000 | tf_op jit(solution)/shard_map/experts_00/pallas_call | solution.py:516
  183.6 2.8 collective-permute-done.21.refs_8_
  189.6 23.3 %experts_01.1 = (f32[8,624,512]{2,1,0:T(8,128)}, f32[8,624,512]{2,1,0:T(8,128)}, bf16[2,4,2,512,256]{4,3,2,1,0:T(8,128)(2,1)}, bf16[2,4,2,512,256]{4,3,2,1,0:T(8...) custom-call(s32[10]{0:T(128)} %pad_add_fusion.refs_0_, ...), custom_call_target="tpu_custom_call", output_to_operand_aliasing={{0}: (14, {}), {1}: (15, {})} | custom-call | flops 4000000000 | bytes 400000 | tf_op jit(solution)/shard_map/experts_01/pallas_call | solution.py:516
  212.9 5.5 %collective-permute-done.23.refs_7_.refs_11_ = bf16[2,4,512,256]{3,2,1,0:T(8,128)(2,1)} collective-permute-done((bf16[2,4,512,256]{3,2,1,0:T(8,128)(2,1)S(1)}, bf16[2,4,512,256]{3,2,1,0:T(8,128)(2,1)}, u32[]{:S(2)}, u32[]{:S(2)}) %collective-permute-start.23) | collective-permute-done | bytes 2097184 | tf_op jit(solution)/shard_map/ppermute | solution.py:761
  219.4 2.3 slice.56
  221.6 2.3 slice.57
  223.9 2.8 collective-permute-done.26.g1
  226.8 9.0 %fold_cores.2 = (bf16[2,4,512,256]{3,2,1,0:T(8,128)(2,1)}, bf16[2,4,512,256]{3,2,1,0:T(8,128)(2,1)}, bf16[2,4,512,256]{3,2,1,0:T(8,128)(2,1)}, bf16[2,4,512,256]{3,2,1,0:T(8,128)(2,1)}) custom-call(bf16[2,4,2,512,256]{4,3,2,1,0:T(8,128)(2,1)} %get-tuple-element.230.n0, bf16[2,4,2,512,256]{4,3,2,1,0:T(8,128)(2,1)} %get-tuple-element.231.n1, ...), custom_call_target="tpu_custom_call" | custom-call | flops 7000000000 | bytes 700000 | tf_op jit(solution)/shard_map/fold_cores/pallas_call | solution.py:885
  235.7 1.6 collective-permute-start.30
  238.2 1.7 collective-permute-start.35
  240.5 24.8 %experts_10.1 = (bf16[8,624,512]{2,1,0:T(8,128)(2,1)}, bf16[8,624,512]{2,1,0:T(8,128)(2,1)}, bf16[2,4,2,512,256]{4,3,2,1,0:T(8,128)(2,1)}, bf16[2,4,2,512,256]{4,3,2,1,0:T(8,128)(2,1)}, f32[8,4,256]{2,1,0:T(4,128)}) custom-call(s32[10]{0:T(128)} %pad_add_fusion.refs_0_, bf16[8,624,512]{2,1,0:T(8,128)(2,1)} %get-tuple-element.212.refs_4_.refs_1_, ...), custom_call_target="tpu_custom_call" | custom-call | flops 4000000000 | bytes 400000 | tf_op jit(solution)/shard_map/experts_10/pallas_call | solution.py:516
  266.0 2.8 collective-permute-done.32.refs_8_
  268.8 2.1 collective-permute-done.33.refs_12_
  271.9 23.6 %experts_11.1 = (bf16[8,624,512]{2,1,0:T(8,128)(2,1)}, bf16[8,624,512]{2,1,0:T(8,128)(2,1)}, bf16[2,4,2,512,256]{4,3,2,1,0:T(8,128)(2,1)}, bf16[2,4,2,512,256]{4,3,2,1,0:T(8,128)(2,1)}, f32[8,4,256]{2,1,0:T(4,128)}) custom-call(s32[10]{0:T(128)} %pad_add_fusion.refs_0_, ...), custom_call_target="tpu_custom_call", output_to_operand_aliasing={{0}: (17, {}), {1}: (18, {})} | custom-call | flops 4000000000 | bytes 400000 | tf_op jit(solution)/shard_map/experts_11/pallas_call | solution.py:516
  295.5 10.7 %collective-permute-done.34.refs_2_ = bf16[2,4,512,256]{3,2,1,0:T(8,128)(2,1)} collective-permute-done((bf16[2,4,512,256]{3,2,1,0:T(8,128)(2,1)}, bf16[2,4,512,256]{3,2,1,0:T(8,128)(2,1)}, u32[]{:S(2)}, u32[]{:S(2)}) %collective-permute-start.34) | collective-permute-done | bytes 2097184 | tf_op jit(solution)/shard_map/ppermute | solution.py:761
  307.7 5.7 %fold_first.2 = (bf16[4,512,256]{2,1,0:T(8,128)(2,1)}, bf16[4,512,256]{2,1,0:T(8,128)(2,1)}, bf16[4,512,256]{2,1,0:T(8,128)(2,1)}, bf16[4,512,256]{2,1,0:T(8,128)(2,1)}) custom-call(bf16[2,4,512,256]{3,2,1,0:T(8,128)(2,1)} %get-tuple-element.253.refs_0_, bf16[2,4,512,256]{3,2,1,0:T(8,128)(2,1)} %get-tuple-element.254.refs_1_, ...), custom_call_target="tpu_custom_call" | custom-call | flops 4000000000 | bytes 400000 | tf_op jit(solution)/shard_map/fold_first/pallas_call | solution.py:906
  315.0 9.0 %fold_cores.3 = (bf16[2,4,512,256]{3,2,1,0:T(8,128)(2,1)}, bf16[2,4,512,256]{3,2,1,0:T(8,128)(2,1)}, bf16[2,4,512,256]{3,2,1,0:T(8,128)(2,1)}, bf16[2,4,512,256]{3,2,1,0:T(8,128)(2,1)}) custom-call(bf16[2,4,2,512,256]{4,3,2,1,0:T(8,128)(2,1)} %get-tuple-element.262.n0, bf16[2,4,2,512,256]{4,3,2,1,0:T(8,128)(2,1)} %get-tuple-element.263.n1, ...), custom_call_target="tpu_custom_call" | custom-call | flops 7000000000 | bytes 700000 | tf_op jit(solution)/shard_map/fold_cores/pallas_call | solution.py:885
  326.6 50.1 %combine.1 = (f32[1970,512]{1,0:T(8,128)}, f32[2080,512]{1,0:T(8,128)}, bf16[2080,512]{1,0:T(8,128)(2,1)}, f32[512,512]{1,0:T(8,128)}, f32[8,512]{1,0:T(8,128)}, /*index=5*/f32[8,512]{1,0:T(8,128)}) custom-call(s32[20,8]{1,0:T(8,128)} %get-tuple-element.198.refs_0_, bf16[8,624,512]{2,1,0:T(8,128)(2,1)} %get-tuple-element.248.refs_1_, ...), custom_call_target="tpu_custom_call" | custom-call | flops 40000000000 | bytes 4000000 | tf_op jit(solution)/shard_map/combine/pallas_call | solution.py:616
  379.5 3.6 fold_second.2
  383.1 9.9 %collective-permute-start.42 = (bf16[2,512,256]{2,1,0:T(8,128)(2,1)}, bf16[2,512,256]{2,1,0:T(8,128)(2,1)S(1)}, u32[]{:S(2)}, u32[]{:S(2)}) collective-permute-start(bf16[2,512,256]{2,1,0:T(8,128)(2,1)} %get-tuple-element.285.refs_10_), channel_id=1, source_target_pairs={{0,2},{1,3},{2,0},{3,1},{4,6},{5,7},{6,4},{7,5},{8,10},{9,11},{10,... | collective-permute-start | bytes 1572872 | tf_op jit(solution)/shard_map/ppermute | solution.py:761
  393.6 1.7 collective-permute-start.44
  395.4 5.7 %fold_first.3 = (bf16[4,512,256]{2,1,0:T(8,128)(2,1)}, bf16[4,512,256]{2,1,0:T(8,128)(2,1)}, bf16[4,512,256]{2,1,0:T(8,128)(2,1)}, bf16[4,512,256]{2,1,0:T(8,128)(2,1)}) custom-call(bf16[2,4,512,256]{3,2,1,0:T(8,128)(2,1)} %get-tuple-element.288.refs_0_, bf16[2,4,512,256]{3,2,1,0:T(8,128)(2,1)} %get-tuple-element.289.refs_1_, ...), custom_call_target="tpu_custom_call" | custom-call | flops 4000000000 | bytes 400000 | tf_op jit(solution)/shard_map/fold_first/pallas_call | solution.py:906
  402.5 41.0 %attention_back.1 = (f32[1970,512]{1,0:T(8,128)}, bf16[16,16,2176]{2,1,0:T(8,128)(2,1)}, bf16[16,16,2176]{2,1,0:T(8,128)(2,1)}) custom-call(s32[32]{0:T(128)} %broadcast_xor_fusion.place_ref.refs_0_, bf16[2080,1536]{1,0:T(8,128)(2,1)} %get-tuple-element.269.refs_1_, bf16[10,8,208,208]{3,2,1,0:T(8,128)(2,1)} %get-tuple-element.270.refs_2_, ...), custom_call_target="tpu_custom_call" | custom-call | flops 49999998976 | bytes 5000000 | tf_op jit(solution)/shard_map/attention_back/pallas_call | solution.py:727
  444.9 3.5 fold_second.3
  448.5 3.0 collective-permute-done.47.refs_1_
  452.5 2.6 block_sum.2
  457.4 1.6 collective-permute-start.55
  459.0 1.7 collective-permute-start.56
  462.2 1.8 collective-permute-done.48.refs_1_
  464.0 2.1 collective-permute-start.50
  466.8 4.8 expert_update_0.1
  471.6 3.1 collective-permute-done.50.refs_3_
  475.4 2.0 block_sum.3
  477.6 2.4 collective-permute-start.52
  480.1 13.6 %collective-permute-done.51.refs_1_ = bf16[1,16,2176]{2,1,0:T(8,128)(2,1)S(1)} collective-permute-done((bf16[1,16,2176]{2,1,0:T(8,128)(2,1)}, bf16[1,16,2176]{2,1,0:T(8,128)(2,1)S(1)}, u32[]{:S(2)}, u32[]{:S(2)}) %collective-permute-start.51) | collective-permute-done | bytes 69664 | tf_op jit(solution)/shard_map/ppermute | solution.py:761
  493.7 2.1 collective-permute-start.53
  499.8 11.1 %collective-permute-done.52.refs_2_ = bf16[1,16,2176]{2,1,0:T(8,128)(2,1)S(1)} collective-permute-done((bf16[1,16,2176]{2,1,0:T(8,128)(2,1)}, bf16[1,16,2176]{2,1,0:T(8,128)(2,1)S(1)}, u32[]{:S(2)}, u32[]{:S(2)}) %collective-permute-start.52) | collective-permute-done | bytes 69664 | tf_op jit(solution)/shard_map/ppermute | solution.py:761
  511.5 2.2 dense_update.1
  514.9 5.0 expert_update_1.1
  522.9 2.8 collective-permute-done.58
  527.1 2.1 collective-permute-done.59
  530.5 2.3 collective-permute-done.60
  532.8 1.9 collective-permute-start.61
  538.0 4.1 new_weights.1
  (284 shorter events, 71.9 us)
Async XLA Ops:
  5.5 15.9 %collective-permute-start = (bf16[16,2304]{1,0:T(8,128)(2,1)S(1)}, bf16[16,2304]{1,0:T(8,128)(2,1)}, u32[]{:S(2)}, u32[]{:S(2)}) collective-permute-start(bf16[16,2304]{1,0:T(8,128)(2,1)S(1)} %pad_maximum_fusion.2.refs_0_), channel_id=1, source_target_pairs={{0,2},{1,3},{2,0},{3,1},{4,6},{5,7},{6,4},{7,5},{8,10},{9,11},{10,... | collective-permute-start | bytes 221192 | tf_op jit(solution)/shard_map/ppermute | solution.py:761
  8.6 12.8 %collective-permute-start.1 = (bf16[16,2304]{1,0:T(8,128)(2,1)S(1)}, bf16[16,2304]{1,0:T(8,128)(2,1)}, u32[]{:S(2)}, u32[]{:S(2)}) collective-permute-start(bf16[16,2304]{1,0:T(8,128)(2,1)S(1)} %pad_maximum_fusion.2.refs_0_), channel_id=1, source_target_pairs={{0,4},{1,5},{2,6},{3,7},{4,0},{5,1},{6,2},{7,3},{8,12},{9,13},{10,... | collective-permute-start | bytes 221192 | tf_op jit(solution)/shard_map/ppermute | solution.py:761
  11.2 10.2 %collective-permute-start.2 = (bf16[16,2304]{1,0:T(8,128)(2,1)S(1)}, bf16[16,2304]{1,0:T(8,128)(2,1)}, u32[]{:S(2)}, u32[]{:S(2)}) collective-permute-start(bf16[16,2304]{1,0:T(8,128)(2,1)S(1)} %pad_maximum_fusion.2.refs_0_), channel_id=1, source_target_pairs={{0,6},{1,7},{2,4},{3,5},{4,2},{5,3},{6,0},{7,1},{8,14},{9,15},{10,... | collective-permute-start | bytes 221192 | tf_op jit(solution)/shard_map/ppermute | solution.py:761
  23.3 16.0 %collective-permute-start.3 = (bf16[4,16,2304]{2,1,0:T(8,128)(2,1)}, bf16[4,16,2304]{2,1,0:T(8,128)(2,1)S(1)}, u32[]{:S(2)}, u32[]{:S(2)}) collective-permute-start(bf16[4,16,2304]{2,1,0:T(8,128)(2,1)} %stack.34.refs_0_), channel_id=1, source_target_pairs={{0,1},{1,0},{2,3},{3,2},{4,5},{5,4},{6,7},{7,6},{8,9},{9,8},{10,11... | collective-permute-start | bytes 884744 | tf_op jit(solution)/shard_map/ppermute | solution.py:761
  25.0 14.3 %collective-permute-start.4 = (bf16[4,16,2304]{2,1,0:T(8,128)(2,1)}, bf16[4,16,2304]{2,1,0:T(8,128)(2,1)S(1)}, u32[]{:S(2)}, u32[]{:S(2)}) collective-permute-start(bf16[4,16,2304]{2,1,0:T(8,128)(2,1)} %stack.34.refs_0_), channel_id=1, source_target_pairs={{0,16},{1,17},{2,18},{3,19},{4,20},{5,21},{6,22},{7,23},{8,24},{9,... | collective-permute-start | bytes 884744 | tf_op jit(solution)/shard_map/ppermute | solution.py:761
  26.5 12.8 %collective-permute-start.5 = (bf16[4,16,2304]{2,1,0:T(8,128)(2,1)}, bf16[4,16,2304]{2,1,0:T(8,128)(2,1)S(1)}, u32[]{:S(2)}, u32[]{:S(2)}) collective-permute-start(bf16[4,16,2304]{2,1,0:T(8,128)(2,1)} %stack.34.refs_0_), channel_id=1, source_target_pairs={{0,17},{1,16},{2,19},{3,18},{4,21},{5,20},{6,23},{7,22},{8,25},{9,... | collective-permute-start | bytes 884744 | tf_op jit(solution)/shard_map/ppermute | solution.py:761
  26.8 12.6 %collective-permute-start.6 = (bf16[2,512,256]{2,1,0:T(8,128)(2,1)S(1)}, bf16[2,512,256]{2,1,0:T(8,128)(2,1)S(1)}, u32[]{:S(2)}, u32[]{:S(2)}) collective-permute-start(bf16[2,512,256]{2,1,0:T(8,128)(2,1)S(1)} %pad_maximum_fusion.refs_0_), channel_id=1, source_target_pairs={{0,2},{1,3},{2,0},{3,1},{4,6},{5,7},{6,4},{7,5},{8,10},{9,11},{10,... | collective-permute-start | bytes 1572872 | tf_op jit(solution)/shard_map/ppermute | solution.py:761
  42.7 4.0 collective-permute-start.7
  43.2 38.3 %collective-permute-start.8 = (bf16[2,512,256]{2,1,0:T(8,128)(2,1)S(1)}, bf16[2,512,256]{2,1,0:T(8,128)(2,1)S(1)}, u32[]{:S(2)}, u32[]{:S(2)}) collective-permute-start(bf16[2,512,256]{2,1,0:T(8,128)(2,1)S(1)} %pad_maximum_fusion.refs_0_), channel_id=1, source_target_pairs={{0,4},{1,5},{2,6},{3,7},{4,0},{5,1},{6,2},{7,3},{8,12},{9,13},{10,... | collective-permute-start | bytes 1572872 | tf_op jit(solution)/shard_map/ppermute | solution.py:761
  46.7 34.8 %collective-permute-start.9 = (bf16[2,512,256]{2,1,0:T(8,128)(2,1)S(1)}, bf16[2,512,256]{2,1,0:T(8,128)(2,1)S(1)}, u32[]{:S(2)}, u32[]{:S(2)}) collective-permute-start(bf16[2,512,256]{2,1,0:T(8,128)(2,1)S(1)} %pad_maximum_fusion.refs_0_), channel_id=1, source_target_pairs={{0,6},{1,7},{2,4},{3,5},{4,2},{5,3},{6,0},{7,1},{8,14},{9,15},{10,... | collective-permute-start | bytes 1572872 | tf_op jit(solution)/shard_map/ppermute | solution.py:761
  85.6 57.1 %collective-permute-start.10 = (bf16[2,4,512,256]{3,2,1,0:T(8,128)(2,1)}, bf16[2,4,512,256]{3,2,1,0:T(8,128)(2,1)}, u32[]{:S(2)}, u32[]{:S(2)}) collective-permute-start(bf16[2,4,512,256]{3,2,1,0:T(8,128)(2,1)} %turn_stack.2.refs_5_.refs_9_), channel_id=1, source_target_pairs={{0,1},{1,0},{2,3},{3,2},{4,5},{5,4},{6,7},{7,6},{8,9},{9,8},{10,11... | collective-permute-start | bytes 6291464 | tf_op jit(solution)/shard_map/ppermute | solution.py:761
  87.2 55.4 %collective-permute-start.12 = (bf16[2,4,512,256]{3,2,1,0:T(8,128)(2,1)}, bf16[2,4,512,256]{3,2,1,0:T(8,128)(2,1)}, u32[]{:S(2)}, u32[]{:S(2)}) collective-permute-start(bf16[2,4,512,256]{3,2,1,0:T(8,128)(2,1)} %turn_stack.2.refs_5_.refs_9_), channel_id=1, source_target_pairs={{0,16},{1,17},{2,18},{3,19},{4,20},{5,21},{6,22},{7,23},{8,24},{9,... | collective-permute-start | bytes 6291464 | tf_op jit(solution)/shard_map/ppermute | solution.py:761
  88.8 41.8 %copy-start.3 = (bf16[2,512,256]{2,1,0:T(8,128)(2,1)}, bf16[2,512,256]{2,1,0:T(8,128)(2,1)S(1)}, u32[]{:S(2)}) copy-start(bf16[2,512,256]{2,1,0:T(8,128)(2,1)S(1)} %pad_maximum_fusion.1.refs_0_) | copy-start | bytes 1572868
  88.8 41.8 %collective-permute-start.13 = (bf16[2,512,256]{2,1,0:T(8,128)(2,1)S(1)}, bf16[2,512,256]{2,1,0:T(8,128)(2,1)S(1)}, u32[]{:S(2)}, u32[]{:S(2)}) collective-permute-start(bf16[2,512,256]{2,1,0:T(8,128)(2,1)S(1)} %pad_maximum_fusion.1.refs_0_), channel_id=1, source_target_pairs={{0,2},{1,3},{2,0},{3,1},{4,6},{5,7},{6,4},{7,5},{8,10},{9,11},{10,... | collective-permute-start | bytes 1572872 | tf_op jit(solution)/shard_map/ppermute | solution.py:761
  100.5 38.2 %collective-permute-start.14 = (bf16[2,512,256]{2,1,0:T(8,128)(2,1)S(1)}, bf16[2,512,256]{2,1,0:T(8,128)(2,1)S(1)}, u32[]{:S(2)}, u32[]{:S(2)}) collective-permute-start(bf16[2,512,256]{2,1,0:T(8,128)(2,1)S(1)} %pad_maximum_fusion.1.refs_0_), channel_id=1, source_target_pairs={{0,4},{1,5},{2,6},{3,7},{4,0},{5,1},{6,2},{7,3},{8,12},{9,13},{10,... | collective-permute-start | bytes 1572872 | tf_op jit(solution)/shard_map/ppermute | solution.py:761
  101.6 37.2 %collective-permute-start.15 = (bf16[2,512,256]{2,1,0:T(8,128)(2,1)S(1)}, bf16[2,512,256]{2,1,0:T(8,128)(2,1)S(1)}, u32[]{:S(2)}, u32[]{:S(2)}) collective-permute-start(bf16[2,512,256]{2,1,0:T(8,128)(2,1)S(1)} %pad_maximum_fusion.1.refs_0_), channel_id=1, source_target_pairs={{0,6},{1,7},{2,4},{3,5},{4,2},{5,3},{6,0},{7,1},{8,14},{9,15},{10,... | collective-permute-start | bytes 1572872 | tf_op jit(solution)/shard_map/ppermute | solution.py:761
  146.8 9.9 %collective-permute-start.16 = (bf16[2,4,512,256]{3,2,1,0:T(8,128)(2,1)}, bf16[2,4,512,256]{3,2,1,0:T(8,128)(2,1)}, u32[]{:S(2)}, u32[]{:S(2)}) collective-permute-start(bf16[2,4,512,256]{3,2,1,0:T(8,128)(2,1)} %turn_stack.2.refs_5_.refs_9_), channel_id=1, source_target_pairs={{0,8},{1,9},{2,10},{3,11},{4,12},{5,13},{6,14},{7,15},{8,0},{9,1},... | collective-permute-start | bytes 6291464 | tf_op jit(solution)/shard_map/ppermute | solution.py:761
  146.8 7.5 %collective-permute-start.17 = (bf16[1,4,512,256]{3,2,1,0:T(8,128)(2,1)}, bf16[1,4,512,256]{3,2,1,0:T(8,128)(2,1)}, u32[]{:S(2)}, u32[]{:S(2)}) collective-permute-start(bf16[1,4,512,256]{3,2,1,0:T(8,128)(2,1)} %get-tuple-element.219), channel_id=1, source_target_pairs={{0,8},{1,9},{2,10},{3,11},{4,12},{5,13},{6,14},{7,15},{8,0},{9,1},... | collective-permute-start | bytes 3145736 | tf_op jit(solution)/shard_map/ppermute | solution.py:761
  147.3 8.4 %collective-permute-start.18 = (bf16[1,4,512,256]{3,2,1,0:T(8,128)(2,1)}, bf16[1,4,512,256]{3,2,1,0:T(8,128)(2,1)S(1)}, u32[]{:S(2)}, u32[]{:S(2)}) collective-permute-start(bf16[1,4,512,256]{3,2,1,0:T(8,128)(2,1)} %get-tuple-element.220), channel_id=1, source_target_pairs={{0,8},{1,9},{2,10},{3,11},{4,12},{5,13},{6,14},{7,15},{8,0},{9,1},... | collective-permute-start | bytes 3145736 | tf_op jit(solution)/shard_map/ppermute | solution.py:761
  147.3 35.6 %collective-permute-start.19 = (bf16[1,4,512,256]{3,2,1,0:T(8,128)(2,1)}, bf16[1,4,512,256]{3,2,1,0:T(8,128)(2,1)S(1)}, u32[]{:S(2)}, u32[]{:S(2)}) collective-permute-start(bf16[1,4,512,256]{3,2,1,0:T(8,128)(2,1)} %get-tuple-element.219), channel_id=1, source_target_pairs={{0,1},{1,0},{2,3},{3,2},{4,5},{5,4},{6,7},{7,6},{8,9},{9,8},{10,11... | collective-permute-start | bytes 3145736 | tf_op jit(solution)/shard_map/ppermute | solution.py:761
  147.8 35.1 %collective-permute-start.20 = (bf16[1,4,512,256]{3,2,1,0:T(8,128)(2,1)}, bf16[1,4,512,256]{3,2,1,0:T(8,128)(2,1)}, u32[]{:S(2)}, u32[]{:S(2)}) collective-permute-start(bf16[1,4,512,256]{3,2,1,0:T(8,128)(2,1)} %get-tuple-element.223), channel_id=1, source_target_pairs={{0,16},{1,17},{2,18},{3,19},{4,20},{5,21},{6,22},{7,23},{8,24},{9,... | collective-permute-start | bytes 3145736 | tf_op jit(solution)/shard_map/ppermute | solution.py:761
  154.3 29.2 %collective-permute-start.11 = (bf16[2,4,512,256]{3,2,1,0:T(8,128)(2,1)}, bf16[2,4,512,256]{3,2,1,0:T(8,128)(2,1)}, u32[]{:S(2)}, u32[]{:S(2)}) collective-permute-start(bf16[2,4,512,256]{3,2,1,0:T(8,128)(2,1)} %collective-permute-done.10.refs_1_.refs_5_.refs_9_), channel_id=1, source_target_pairs={{0,8},{1,9},{2,10},{3,11},{4,12},{5,13},{6,14},{7,15},{8,0},{9,1},... | collective-permute-start | bytes 6291464 | tf_op jit(solution)/shard_map/ppermute | solution.py:761
  155.7 62.6 %collective-permute-start.23 = (bf16[2,4,512,256]{3,2,1,0:T(8,128)(2,1)S(1)}, bf16[2,4,512,256]{3,2,1,0:T(8,128)(2,1)}, u32[]{:S(2)}, u32[]{:S(2)}) collective-permute-start(bf16[2,4,512,256]{3,2,1,0:T(8,128)(2,1)S(1)} %copy-done), channel_id=1, source_target_pairs={{0,16},{1,17},{2,18},{3,19},{4,20},{5,21},{6,22},{7,23},{8,24},{9,... | collective-permute-start | bytes 6291464 | tf_op jit(solution)/shard_map/ppermute | solution.py:761
  156.7 61.6 %collective-permute-start.24 = (bf16[2,4,512,256]{3,2,1,0:T(8,128)(2,1)S(1)}, bf16[2,4,512,256]{3,2,1,0:T(8,128)(2,1)}, u32[]{:S(2)}, u32[]{:S(2)}) collective-permute-start(bf16[2,4,512,256]{3,2,1,0:T(8,128)(2,1)S(1)} %copy-done), channel_id=1, source_target_pairs={{0,1},{1,0},{2,3},{3,2},{4,5},{5,4},{6,7},{7,6},{8,9},{9,8},{10,11... | collective-permute-start | bytes 6291464 | tf_op jit(solution)/shard_map/ppermute | solution.py:761
  182.9 3.4 collective-permute-start.21
  183.1 5.5 %collective-permute-start.22 = (bf16[1,4,512,256]{3,2,1,0:T(8,128)(2,1)}, bf16[1,4,512,256]{3,2,1,0:T(8,128)(2,1)S(1)}, u32[]{:S(2)}, u32[]{:S(2)}) collective-permute-start(bf16[1,4,512,256]{3,2,1,0:T(8,128)(2,1)} %collective-permute-done.20.refs_11_), channel_id=1, source_target_pairs={{0,8},{1,9},{2,10},{3,11},{4,12},{5,13},{6,14},{7,15},{8,0},{9,1},... | collective-permute-start | bytes 3145736 | tf_op jit(solution)/shard_map/ppermute | solution.py:761
  183.5 40.4 %collective-permute-start.25 = (bf16[2,4,2,512,256]{4,3,2,1,0:T(8,128)(2,1)}, bf16[2,4,2,512,256]{4,3,2,1,0:T(8,128)(2,1)}, u32[]{:S(2)}, u32[]{:S(2)}) collective-permute-start(bf16[2,4,2,512,256]{4,3,2,1,0:T(8,128)(2,1)} %get-tuple-element.232), channel_id=1, source_target_pairs={{0,8},{1,9},{2,10},{3,11},{4,12},{5,13},{6,14},{7,15},{8,0},{9,1},... | collective-permute-start | bytes 12582920 | tf_op jit(solution)/shard_map/ppermute | solution.py:761
  218.4 8.4 %collective-permute-start.26 = (bf16[2,4,2,512,256]{4,3,2,1,0:T(8,128)(2,1)}, bf16[2,4,2,512,256]{4,3,2,1,0:T(8,128)(2,1)}, u32[]{:S(2)}, u32[]{:S(2)}) collective-permute-start(bf16[2,4,2,512,256]{4,3,2,1,0:T(8,128)(2,1)} %get-tuple-element.233), channel_id=1, source_target_pairs={{0,8},{1,9},{2,10},{3,11},{4,12},{5,13},{6,14},{7,15},{8,0},{9,1},... | collective-permute-start | bytes 12582920 | tf_op jit(solution)/shard_map/ppermute | solution.py:761
  218.4 17.4 %collective-permute-start.27 = (bf16[2,4,512,256]{3,2,1,0:T(8,128)(2,1)}, bf16[2,4,512,256]{3,2,1,0:T(8,128)(2,1)}, u32[]{:S(2)}, u32[]{:S(2)}) collective-permute-start(bf16[2,4,512,256]{3,2,1,0:T(8,128)(2,1)} %collective-permute-done.24.refs_5_.refs_9_), channel_id=1, source_target_pairs={{0,8},{1,9},{2,10},{3,11},{4,12},{5,13},{6,14},{7,15},{8,0},{9,1},... | collective-permute-start | bytes 6291464 | tf_op jit(solution)/shard_map/ppermute | solution.py:761
  218.9 19.3 %collective-permute-start.28 = (bf16[2,4,512,256]{3,2,1,0:T(8,128)(2,1)S(1)}, bf16[2,4,512,256]{3,2,1,0:T(8,128)(2,1)}, u32[]{:S(2)}, u32[]{:S(2)}) collective-permute-start(bf16[2,4,512,256]{3,2,1,0:T(8,128)(2,1)S(1)} %copy-done), channel_id=1, source_target_pairs={{0,8},{1,9},{2,10},{3,11},{4,12},{5,13},{6,14},{7,15},{8,0},{9,1},... | collective-permute-start | bytes 6291464 | tf_op jit(solution)/shard_map/ppermute | solution.py:761
  218.9 21.6 %collective-permute-start.29 = (bf16[2,4,512,256]{3,2,1,0:T(8,128)(2,1)}, bf16[2,4,512,256]{3,2,1,0:T(8,128)(2,1)}, u32[]{:S(2)}, u32[]{:S(2)}) collective-permute-start(bf16[2,4,512,256]{3,2,1,0:T(8,128)(2,1)} %collective-permute-done.23.refs_7_.refs_11_), channel_id=1, source_target_pairs={{0,8},{1,9},{2,10},{3,11},{4,12},{5,13},{6,14},{7,15},{8,0},{9,1},... | collective-permute-start | bytes 6291464 | tf_op jit(solution)/shard_map/ppermute | solution.py:761
  235.7 29.6 %collective-permute-start.30 = (bf16[1,4,512,256]{3,2,1,0:T(8,128)(2,1)}, bf16[1,4,512,256]{3,2,1,0:T(8,128)(2,1)S(1)}, u32[]{:S(2)}, u32[]{:S(2)}) collective-permute-start(bf16[1,4,512,256]{3,2,1,0:T(8,128)(2,1)} %slice.56), channel_id=1, source_target_pairs={{0,1},{1,0},{2,3},{3,2},{4,5},{5,4},{6,7},{7,6},{8,9},{9,8},{10,11... | collective-permute-start | bytes 3145736 | tf_op jit(solution)/shard_map/ppermute | solution.py:761
  237.3 28.0 %collective-permute-start.31 = (bf16[1,4,512,256]{3,2,1,0:T(8,128)(2,1)}, bf16[1,4,512,256]{3,2,1,0:T(8,128)(2,1)}, u32[]{:S(2)}, u32[]{:S(2)}) collective-permute-start(bf16[1,4,512,256]{3,2,1,0:T(8,128)(2,1)} %slice.57), channel_id=1, source_target_pairs={{0,16},{1,17},{2,18},{3,19},{4,20},{5,21},{6,22},{7,23},{8,24},{9,... | collective-permute-start | bytes 3145736 | tf_op jit(solution)/shard_map/ppermute | solution.py:761
  237.8 68.4 %collective-permute-start.34 = (bf16[2,4,512,256]{3,2,1,0:T(8,128)(2,1)}, bf16[2,4,512,256]{3,2,1,0:T(8,128)(2,1)}, u32[]{:S(2)}, u32[]{:S(2)}) collective-permute-start(bf16[2,4,512,256]{3,2,1,0:T(8,128)(2,1)} %get-tuple-element.239.refs_17_), channel_id=1, source_target_pairs={{0,1},{1,0},{2,3},{3,2},{4,5},{5,4},{6,7},{7,6},{8,9},{9,8},{10,11... | collective-permute-start | bytes 6291464 | tf_op jit(solution)/shard_map/ppermute | solution.py:761
  238.2 69.3 %collective-permute-start.35 = (bf16[2,4,512,256]{3,2,1,0:T(8,128)(2,1)}, bf16[2,4,512,256]{3,2,1,0:T(8,128)(2,1)}, u32[]{:S(2)}, u32[]{:S(2)}) collective-permute-start(bf16[2,4,512,256]{3,2,1,0:T(8,128)(2,1)} %get-tuple-element.240.refs_18_), channel_id=1, source_target_pairs={{0,16},{1,17},{2,18},{3,19},{4,20},{5,21},{6,22},{7,23},{8,24},{9,... | collective-permute-start | bytes 6291464 | tf_op jit(solution)/shard_map/ppermute | solution.py:761
  265.3 3.4 collective-permute-start.32
  265.4 5.5 %collective-permute-start.33 = (bf16[1,4,512,256]{3,2,1,0:T(8,128)(2,1)}, bf16[1,4,512,256]{3,2,1,0:T(8,128)(2,1)S(1)}, u32[]{:S(2)}, u32[]{:S(2)}) collective-permute-start(bf16[1,4,512,256]{3,2,1,0:T(8,128)(2,1)} %collective-permute-done.31.refs_11_), channel_id=1, source_target_pairs={{0,8},{1,9},{2,10},{3,11},{4,12},{5,13},{6,14},{7,15},{8,0},{9,1},... | collective-permute-start | bytes 3145736 | tf_op jit(solution)/shard_map/ppermute | solution.py:761
  265.9 48.5 %collective-permute-start.36 = (bf16[2,4,2,512,256]{4,3,2,1,0:T(8,128)(2,1)}, bf16[2,4,2,512,256]{4,3,2,1,0:T(8,128)(2,1)}, u32[]{:S(2)}, u32[]{:S(2)}) collective-permute-start(bf16[2,4,2,512,256]{4,3,2,1,0:T(8,128)(2,1)} %get-tuple-element.264), channel_id=1, source_target_pairs={{0,8},{1,9},{2,10},{3,11},{4,12},{5,13},{6,14},{7,15},{8,0},{9,1},... | collective-permute-start | bytes 12582920 | tf_op jit(solution)/shard_map/ppermute | solution.py:761
  271.9 35.6 %copy-start.37 = (f32[8,1,512]{2,1,0:T(1,128)S(1)}, f32[8,1,512]{2,1,0:T(1,128)}, u32[]{:S(2)}) copy-start(f32[8,1,512]{2,1,0:T(1,128)} %get-tuple-element.280) | copy-start | bytes 49156
  307.5 7.5 %collective-permute-start.37 = (bf16[2,4,2,512,256]{4,3,2,1,0:T(8,128)(2,1)}, bf16[2,4,2,512,256]{4,3,2,1,0:T(8,128)(2,1)}, u32[]{:S(2)}, u32[]{:S(2)}) collective-permute-start(bf16[2,4,2,512,256]{4,3,2,1,0:T(8,128)(2,1)} %get-tuple-element.265), channel_id=1, source_target_pairs={{0,8},{1,9},{2,10},{3,11},{4,12},{5,13},{6,14},{7,15},{8,0},{9,1},... | collective-permute-start | bytes 12582920 | tf_op jit(solution)/shard_map/ppermute | solution.py:761
  313.4 63.4 %collective-permute-start.38 = (bf16[4,512,256]{2,1,0:T(8,128)(2,1)}, bf16[4,512,256]{2,1,0:T(8,128)(2,1)S(1)}, u32[]{:S(2)}, u32[]{:S(2)}) collective-permute-start(bf16[4,512,256]{2,1,0:T(8,128)(2,1)} %get-tuple-element.260.refs_13_), channel_id=1, source_target_pairs={{0,16},{1,17},{2,18},{3,19},{4,20},{5,21},{6,22},{7,23},{8,24},{9,... | collective-permute-start | bytes 3145736 | tf_op jit(solution)/shard_map/ppermute | solution.py:761
  313.9 62.9 %collective-permute-start.39 = (bf16[4,512,256]{2,1,0:T(8,128)(2,1)}, bf16[4,512,256]{2,1,0:T(8,128)(2,1)S(1)}, u32[]{:S(2)}, u32[]{:S(2)}) collective-permute-start(bf16[4,512,256]{2,1,0:T(8,128)(2,1)} %get-tuple-element.261.refs_14_), channel_id=1, source_target_pairs={{0,1},{1,0},{2,3},{3,2},{4,5},{5,4},{6,7},{7,6},{8,9},{9,8},{10,11... | collective-permute-start | bytes 3145736 | tf_op jit(solution)/shard_map/ppermute | solution.py:761
  324.0 71.4 %collective-permute-start.40 = (bf16[2,4,512,256]{3,2,1,0:T(8,128)(2,1)}, bf16[2,4,512,256]{3,2,1,0:T(8,128)(2,1)}, u32[]{:S(2)}, u32[]{:S(2)}) collective-permute-start(bf16[2,4,512,256]{3,2,1,0:T(8,128)(2,1)} %get-tuple-element.266.refs_15_), channel_id=1, source_target_pairs={{0,1},{1,0},{2,3},{3,2},{4,5},{5,4},{6,7},{7,6},{8,9},{9,8},{10,11... | collective-permute-start | bytes 6291464 | tf_op jit(solution)/shard_map/ppermute | solution.py:761
  325.1 70.2 %collective-permute-start.41 = (bf16[2,4,512,256]{3,2,1,0:T(8,128)(2,1)}, bf16[2,4,512,256]{3,2,1,0:T(8,128)(2,1)}, u32[]{:S(2)}, u32[]{:S(2)}) collective-permute-start(bf16[2,4,512,256]{3,2,1,0:T(8,128)(2,1)} %get-tuple-element.267.refs_16_), channel_id=1, source_target_pairs={{0,16},{1,17},{2,18},{3,19},{4,20},{5,21},{6,22},{7,23},{8,24},{9,... | collective-permute-start | bytes 6291464 | tf_op jit(solution)/shard_map/ppermute | solution.py:761
  383.1 60.4 %collective-permute-start.42 = (bf16[2,512,256]{2,1,0:T(8,128)(2,1)}, bf16[2,512,256]{2,1,0:T(8,128)(2,1)S(1)}, u32[]{:S(2)}, u32[]{:S(2)}) collective-permute-start(bf16[2,512,256]{2,1,0:T(8,128)(2,1)} %get-tuple-element.285.refs_10_), channel_id=1, source_target_pairs={{0,2},{1,3},{2,0},{3,1},{4,6},{5,7},{6,4},{7,5},{8,10},{9,11},{10,... | collective-permute-start | bytes 1572872 | tf_op jit(solution)/shard_map/ppermute | solution.py:761
  393.0 50.5 %collective-permute-start.43 = (bf16[2,512,256]{2,1,0:T(8,128)(2,1)}, bf16[2,512,256]{2,1,0:T(8,128)(2,1)S(1)}, u32[]{:S(2)}, u32[]{:S(2)}) collective-permute-start(bf16[2,512,256]{2,1,0:T(8,128)(2,1)} %get-tuple-element.286.refs_11_), channel_id=1, source_target_pairs={{0,4},{1,5},{2,6},{3,7},{4,0},{5,1},{6,2},{7,3},{8,12},{9,13},{10,... | collective-permute-start | bytes 1572872 | tf_op jit(solution)/shard_map/ppermute | solution.py:761
  393.6 49.9 %collective-permute-start.44 = (bf16[2,512,256]{2,1,0:T(8,128)(2,1)}, bf16[2,512,256]{2,1,0:T(8,128)(2,1)S(1)}, u32[]{:S(2)}, u32[]{:S(2)}) collective-permute-start(bf16[2,512,256]{2,1,0:T(8,128)(2,1)} %get-tuple-element.287.refs_12_), channel_id=1, source_target_pairs={{0,6},{1,7},{2,4},{3,5},{4,2},{5,3},{6,0},{7,1},{8,14},{9,15},{10,... | collective-permute-start | bytes 1572872 | tf_op jit(solution)/shard_map/ppermute | solution.py:761
  401.1 42.4 %collective-permute-start.45 = (bf16[4,512,256]{2,1,0:T(8,128)(2,1)}, bf16[4,512,256]{2,1,0:T(8,128)(2,1)S(1)}, u32[]{:S(2)}, u32[]{:S(2)}) collective-permute-start(bf16[4,512,256]{2,1,0:T(8,128)(2,1)} %get-tuple-element.290.refs_13_), channel_id=1, source_target_pairs={{0,16},{1,17},{2,18},{3,19},{4,20},{5,21},{6,22},{7,23},{8,24},{9,... | collective-permute-start | bytes 3145736 | tf_op jit(solution)/shard_map/ppermute | solution.py:761
  401.6 41.9 %collective-permute-start.46 = (bf16[4,512,256]{2,1,0:T(8,128)(2,1)}, bf16[4,512,256]{2,1,0:T(8,128)(2,1)S(1)}, u32[]{:S(2)}, u32[]{:S(2)}) collective-permute-start(bf16[4,512,256]{2,1,0:T(8,128)(2,1)} %get-tuple-element.291.refs_14_), channel_id=1, source_target_pairs={{0,1},{1,0},{2,3},{3,2},{4,5},{5,4},{6,7},{7,6},{8,9},{9,8},{10,11... | collective-permute-start | bytes 3145736 | tf_op jit(solution)/shard_map/ppermute | solution.py:761
  448.4 3.0 collective-permute-start.47
  455.1 8.9 %collective-permute-start.48 = (bf16[4,16,2176]{2,1,0:T(8,128)(2,1)}, bf16[4,16,2176]{2,1,0:T(8,128)(2,1)S(1)}, u32[]{:S(2)}, u32[]{:S(2)}) collective-permute-start(bf16[4,16,2176]{2,1,0:T(8,128)(2,1)} %get-tuple-element.312), channel_id=1, source_target_pairs={{0,1},{1,0},{2,3},{3,2},{4,5},{5,4},{6,7},{7,6},{8,9},{9,8},{10,11... | collective-permute-start | bytes 835592 | tf_op jit(solution)/shard_map/ppermute | solution.py:761
  456.3 57.5 %collective-permute-start.54 = (bf16[2,512,256]{2,1,0:T(8,128)(2,1)}, bf16[2,512,256]{2,1,0:T(8,128)(2,1)S(1)}, u32[]{:S(2)}, u32[]{:S(2)}) collective-permute-start(bf16[2,512,256]{2,1,0:T(8,128)(2,1)} %get-tuple-element.324), channel_id=1, source_target_pairs={{0,2},{1,3},{2,0},{3,1},{4,6},{5,7},{6,4},{7,5},{8,10},{9,11},{10,... | collective-permute-start | bytes 1572872 | tf_op jit(solution)/shard_map/ppermute | solution.py:761
  457.4 56.4 %collective-permute-start.55 = (bf16[2,512,256]{2,1,0:T(8,128)(2,1)}, bf16[2,512,256]{2,1,0:T(8,128)(2,1)S(1)}, u32[]{:S(2)}, u32[]{:S(2)}) collective-permute-start(bf16[2,512,256]{2,1,0:T(8,128)(2,1)} %get-tuple-element.325), channel_id=1, source_target_pairs={{0,4},{1,5},{2,6},{3,7},{4,0},{5,1},{6,2},{7,3},{8,12},{9,13},{10,... | collective-permute-start | bytes 1572872 | tf_op jit(solution)/shard_map/ppermute | solution.py:761
  459.0 54.8 %collective-permute-start.56 = (bf16[2,512,256]{2,1,0:T(8,128)(2,1)S(1)}, bf16[2,512,256]{2,1,0:T(8,128)(2,1)S(1)}, u32[]{:S(2)}, u32[]{:S(2)}) collective-permute-start(bf16[2,512,256]{2,1,0:T(8,128)(2,1)S(1)} %copy-done.54), channel_id=1, source_target_pairs={{0,6},{1,7},{2,4},{3,5},{4,2},{5,3},{6,0},{7,1},{8,14},{9,15},{10,... | collective-permute-start | bytes 1572872 | tf_op jit(solution)/shard_map/ppermute | solution.py:761
  460.7 10.9 %collective-permute-start.49 = (bf16[4,16,2176]{2,1,0:T(8,128)(2,1)}, bf16[4,16,2176]{2,1,0:T(8,128)(2,1)S(1)}, u32[]{:S(2)}, u32[]{:S(2)}) collective-permute-start(bf16[4,16,2176]{2,1,0:T(8,128)(2,1)} %get-tuple-element.313), channel_id=1, source_target_pairs={{0,16},{1,17},{2,18},{3,19},{4,20},{5,21},{6,22},{7,23},{8,24},{9,... | collective-permute-start | bytes 835592 | tf_op jit(solution)/shard_map/ppermute | solution.py:761
  464.0 10.7 %collective-permute-start.50 = (bf16[4,16,2176]{2,1,0:T(8,128)(2,1)}, bf16[4,16,2176]{2,1,0:T(8,128)(2,1)S(1)}, u32[]{:S(2)}, u32[]{:S(2)}) collective-permute-start(bf16[4,16,2176]{2,1,0:T(8,128)(2,1)} %get-tuple-element.314), channel_id=1, source_target_pairs={{0,17},{1,16},{2,19},{3,18},{4,21},{5,20},{6,23},{7,22},{8,25},{9,... | collective-permute-start | bytes 835592 | tf_op jit(solution)/shard_map/ppermute | solution.py:761
  477.4 16.3 %collective-permute-start.51 = (bf16[1,16,2176]{2,1,0:T(8,128)(2,1)}, bf16[1,16,2176]{2,1,0:T(8,128)(2,1)S(1)}, u32[]{:S(2)}, u32[]{:S(2)}) collective-permute-start(bf16[1,16,2176]{2,1,0:T(8,128)(2,1)} %get-tuple-element.316), channel_id=1, source_target_pairs={{0,2},{1,3},{2,0},{3,1},{4,6},{5,7},{6,4},{7,5},{8,10},{9,11},{10,... | collective-permute-start | bytes 208904 | tf_op jit(solution)/shard_map/ppermute | solution.py:761
  477.6 33.3 %collective-permute-start.52 = (bf16[1,16,2176]{2,1,0:T(8,128)(2,1)}, bf16[1,16,2176]{2,1,0:T(8,128)(2,1)S(1)}, u32[]{:S(2)}, u32[]{:S(2)}) collective-permute-start(bf16[1,16,2176]{2,1,0:T(8,128)(2,1)} %get-tuple-element.317), channel_id=1, source_target_pairs={{0,4},{1,5},{2,6},{3,7},{4,0},{5,1},{6,2},{7,3},{8,12},{9,13},{10,... | collective-permute-start | bytes 208904 | tf_op jit(solution)/shard_map/ppermute | solution.py:761
  493.7 17.2 %collective-permute-start.53 = (bf16[1,16,2176]{2,1,0:T(8,128)(2,1)}, bf16[1,16,2176]{2,1,0:T(8,128)(2,1)S(1)}, u32[]{:S(2)}, u32[]{:S(2)}) collective-permute-start(bf16[1,16,2176]{2,1,0:T(8,128)(2,1)} %get-tuple-element.318), channel_id=1, source_target_pairs={{0,6},{1,7},{2,4},{3,5},{4,2},{5,3},{6,0},{7,1},{8,14},{9,15},{10,... | collective-permute-start | bytes 208904 | tf_op jit(solution)/shard_map/ppermute | solution.py:761
  519.9 1.4 collective-permute-start.57
  522.0 3.6 collective-permute-start.58
  525.6 3.6 collective-permute-start.59
  529.2 3.6 collective-permute-start.60
  532.8 4.6 collective-permute-start.61
  (60 other events, 533.3 us)

commit v5 on v4

--- a/solution.py
+++ b/solution.py
@@ -1157,15 +1157,17 @@
         at, lists, other_half(far_y, far_xy, crossed), bias_cut(0), half=1, done=(y_part, d_part),
     )
     got_a = swap(far_a, CORE_BIT)
-    far_b, far_x_two, far_y_two = lax.optimization_barrier((far_b, far_x_two, far_y_two))
+    near_two, bias_a = lax.optimization_barrier((near_two, bias_a))
+    near_crossed = cross(near_two)
+    far_b, far_x_two, far_y_two, near_crossed = lax.optimization_barrier((far_b, far_x_two, far_y_two, near_crossed))
     diagonal = far_x_two[0:1], far_y_two[1:2]
-    crossed = cross(near_two), cross(far_x_two)
+    crossed = near_crossed, cross(far_x_two)
+    far_xy_two = swap(diagonal[0], Y_BIT), swap(diagonal[1], X_BIT)
     got_b = swap(far_b, CORE_BIT)
     one = fold_cores((near_a, near_b), (got_a, got_b))
+    a_send, far_y_two = lax.optimization_barrier((one[2], far_y_two))
+    one = (*one[:2], a_send, one[3])
     far_y_crossed = cross(far_y_two)
-    a_send, far_y_crossed, *diagonal = lax.optimization_barrier((one[2], far_y_crossed, *diagonal))
-    one = (*one[:2], a_send, one[3])
-    far_xy_two = swap(diagonal[0], Y_BIT), swap(diagonal[1], X_BIT)
     even = lax.bitwise_xor(jnp.arange(ep, dtype=jnp.int32), ep_me)[:, None, None] % 2 == 0
     grad_bias = [jnp.where(even, bias_a, bias_b)]
     grad_leave_bias = jnp.where(even, leave_a, leave_b)

time: 556 us -> 548 us (0.986)
  waiting for transfers between devices: 86.9 us -> 78.9 us
    ppermute x62, waiting for transfers between devices: 86.9 us -> 78.9 us  [swap(): return lax.ppermute(array, AXES, [(d, d ^ bits) for d in range(devices)])]
    unnamed x140 -> x138, local copies, waits for them, and re-layouts: 24.8 us -> 24.9 us
  transfers between devices with their start and end apart: 62 -> 62, of which waited for: 21 -> 20; matrix products, arithmetic and copies ran while one was open for 5% -> 5% of each run, Pallas kernels for 56% -> 57%
where the time goes in v5:
time: 548 us; the launch traced here: 538 us
  Pallas kernels  333 us (61%)
  waiting for transfers between devices  78.9 us (14%)
  starting transfers between devices  76.8 us (14%)
  local copies, waits for them, and re-layouts  38 us (7%)
  other arithmetic  9.74 us (2%)
    pallas_call x4, Pallas kernels, expert_pass(): pl.pallas_call(kernel, grid_spec=pltpu.PrefetchScalarGridSpec(num_scalar_...  96.7 us
    ppermute x62, waiting for transfers between devices, swap(): return lax.ppermute(array, AXES, [(d, d ^ bits) for d in range(devices)])  78.9 us
    ppermute x62, starting transfers between devices, swap(): return lax.ppermute(array, AXES, [(d, d ^ bits) for d in range(devices)])  76.8 us
    pallas_call x1, Pallas kernels, combine(): pl.pallas_call(behind(combine_kernel, 11, after), grid_spec=pltpu.Prefetc...  50.1 us
    pallas_call x1, Pallas kernels, attention_back(): pl.pallas_call(behind(attention_back_kernel, 10, after), grid_spec=pltpu....  41 us
    pallas_call x1, Pallas kernels, attention(): pl.pallas_call(behind(attention_kernel, 6, after), grid=(images,), in_spe...  28.1 us
    pallas_call x1, Pallas kernels, gather(): pl.pallas_call(behind(gather_kernel, 5, after), grid_spec=pltpu.PrefetchS...  27.6 us
    unnamed x138, local copies, waits for them, and re-layouts  24.9 us
  transfers between devices with their start and end apart: 62, of which 20 were waited for; matrix products, arithmetic and copies ran while one was open for 5% of the time, Pallas kernels for 57%

profile of v5, /device:TPU:0, one launch (start us, length us, event | category | flops | bytes accessed | tf_op | source)
XLA Modules:
  0.0 538.1 jit_solution(11818135043464124582)
XLA Ops:
  5.5 3.1 collective-permute-start
  8.6 2.6 collective-permute-start.1
  11.2 1.4 copy.182
  14.9 4.6 spread_rows.1
  21.4 1.9 stack.34.refs_0_
  23.4 1.7 collective-permute-start.3
  25.1 1.5 collective-permute-start.4
  29.8 9.5 %places.1 = (f32[10,8,208]{2,1,0:T(8,128)}, f32[2080,8]{1,0:T(8,128)}, s32[20,8]{1,0:T(8,128)}) custom-call(f32[8,2080]{1,0:T(8,128)} %pad.32.clone.rows_ref, f32[2080,8]{1,0:T(8,128)} %pad_bitcast_fusion.cols_ref), custom_call_target="tpu_custom_call" | custom-call | flops 2000000000 | bytes 200000 | tf_op jit(solution)/shard_map/places/pallas_call | solution.py:220
  40.4 2.3 stack.35
  43.3 3.5 collective-permute-start.8
  47.8 3.9 assemble.1
  51.7 28.1 %attention.1 = (bf16[2080,1536]{1,0:T(8,128)(2,1)}, bf16[10,8,208,208]{3,2,1,0:T(8,128)(2,1)}, bf16[2080,512]{1,0:T(8,128)(2,1)}, f32[2080,512]{1,0:T(8,128)}, b...) custom-call(bf16[2080,512]{1,0:T(8,128)(2,1)} %get-tuple-element.200.refs_4_.refs_0_.refs_5_, ...), custom_call_target="tpu_custom_call" | custom-call | flops 8000000000 | bytes 800000 | tf_op jit(solution)/shard_map/attention/pallas_call | solution.py:314
  79.8 1.8 collective-permute-done.8.refs_2_
  82.6 3.1 turn_stack.2.refs_5_.refs_9_
  85.6 1.7 collective-permute-start.10
  87.3 1.5 collective-permute-start.11
  88.9 11.7 %collective-permute-start.12 = (bf16[2,512,256]{2,1,0:T(8,128)(2,1)S(1)}, bf16[2,512,256]{2,1,0:T(8,128)(2,1)S(1)}, u32[]{:S(2)}, u32[]{:S(2)}) collective-permute-start(bf16[2,512,256]{2,1,0:T(8,128)(2,1)S(1)} %pad_maximum_fusion.1.refs_0_), channel_id=1, source_target_pairs={{0,2},{1,3},{2,0},{3,1},{4,6},{5,7},{6,4},{7,5},{8,10},{9,11},{10,... | collective-permute-start | bytes 1572872 | tf_op jit(solution)/shard_map/ppermute | solution.py:761
  103.0 27.6 %gather.1 = (bf16[8,624,512]{2,1,0:T(8,128)(2,1)}, bf16[8,624,512]{2,1,0:T(8,128)(2,1)}, bf16[8,512,624]{2,1,0:T(8,128)(2,1)}, bf16[8,512,624]{2,1,0:T(8,128)(2,1)}) custom-call(s32[20,8]{1,0:T(8,128)} %get-tuple-element.199.refs_0_, bf16[2080,512]{1,0:T(8,128)(2,1)} %get-tuple-element.208.refs_1_, bf16[2080,512]{1,0:T(8,128)(2,1)} %get-tuple-element.209.refs_2_.refs_6_, ...), custom_call_target="tpu_custom_call" | custom-call | flops 8000000000 | bytes 800000 | tf_op jit(solution)/shard_map/gather/pallas_call | solution.py:378
  130.6 8.2 %collective-permute-done.13.refs_2_ = bf16[2,512,256]{2,1,0:T(8,128)(2,1)S(1)} collective-permute-done((bf16[2,512,256]{2,1,0:T(8,128)(2,1)S(1)}, bf16[2,512,256]{2,1,0:T(8,128)(2,1)S(1)}, u32[]{:S(2)}, u32[]{:S(2)}) %collective-permute-start.13) | collective-permute-done | bytes 524320 | tf_op jit(solution)/shard_map/ppermute | solution.py:761
  139.8 3.0 turn_stack.3.refs_2_.refs_5_.refs_9_
  142.7 4.1 pick.1
  150.4 2.5 collective-permute-done.16.refs_8_
  155.4 25.1 %experts_00.1 = (f32[8,624,512]{2,1,0:T(8,128)}, f32[8,624,512]{2,1,0:T(8,128)}, bf16[2,4,2,512,256]{4,3,2,1,0:T(8,128)(2,1)}, bf16[2,4,2,512,256]{4,3,2,1,0:T(8...) custom-call(s32[10]{0:T(128)} %pad_add_fusion.refs_0_, bf16[8,624,512]{2,1,0:T(8,128)(2,1)} %get-tuple-element.213.refs_4_.refs_1_, ...), custom_call_target="tpu_custom_call" | custom-call | flops 4000000000 | bytes 400000 | tf_op jit(solution)/shard_map/experts_00/pallas_call | solution.py:516
  181.8 6.1 %collective-permute-done.21.refs_8_ = bf16[1,4,512,256]{3,2,1,0:T(8,128)(2,1)S(1)} collective-permute-done((bf16[1,4,512,256]{3,2,1,0:T(8,128)(2,1)S(1)}, bf16[1,4,512,256]{3,2,1,0:T(8,128)(2,1)S(1)}, u32[]{:S(2)}, u32[]{:S(2)}) %collective-permute-start.21) | collective-permute-done | bytes 1048608 | tf_op jit(solution)/shard_map/ppermute | solution.py:761
  189.1 23.2 %experts_01.1 = (f32[8,624,512]{2,1,0:T(8,128)}, f32[8,624,512]{2,1,0:T(8,128)}, bf16[2,4,2,512,256]{4,3,2,1,0:T(8,128)(2,1)}, bf16[2,4,2,512,256]{4,3,2,1,0:T(8...) custom-call(s32[10]{0:T(128)} %pad_add_fusion.refs_0_, ...), custom_call_target="tpu_custom_call", output_to_operand_aliasing={{0}: (14, {}), {1}: (15, {})} | custom-call | flops 4000000000 | bytes 400000 | tf_op jit(solution)/shard_map/experts_01/pallas_call | solution.py:516
  212.3 11.0 %collective-permute-done.24.refs_7_.refs_11_ = bf16[2,4,512,256]{3,2,1,0:T(8,128)(2,1)} collective-permute-done((bf16[2,4,512,256]{3,2,1,0:T(8,128)(2,1)S(1)}, bf16[2,4,512,256]{3,2,1,0:T(8,128)(2,1)}, u32[]{:S(2)}, u32[]{:S(2)}) %collective-permute-start.24) | collective-permute-done | bytes 2097184 | tf_op jit(solution)/shard_map/ppermute | solution.py:761
  223.8 2.3 slice.58
  226.6 2.3 slice.59
  229.2 1.6 collective-permute-done.27.g1
  230.8 9.0 %fold_cores.2 = (bf16[2,4,512,256]{3,2,1,0:T(8,128)(2,1)}, bf16[2,4,512,256]{3,2,1,0:T(8,128)(2,1)}, bf16[2,4,512,256]{3,2,1,0:T(8,128)(2,1)}, bf16[2,4,512,256]{3,2,1,0:T(8,128)(2,1)}) custom-call(bf16[2,4,2,512,256]{4,3,2,1,0:T(8,128)(2,1)} %get-tuple-element.223.n0, bf16[2,4,2,512,256]{4,3,2,1,0:T(8,128)(2,1)} %get-tuple-element.230.n1, ...), custom_call_target="tpu_custom_call" | custom-call | flops 7000000000 | bytes 700000 | tf_op jit(solution)/shard_map/fold_cores/pallas_call | solution.py:885
  242.1 24.8 %experts_10.1 = (bf16[8,624,512]{2,1,0:T(8,128)(2,1)}, bf16[8,624,512]{2,1,0:T(8,128)(2,1)}, bf16[2,4,2,512,256]{4,3,2,1,0:T(8,128)(2,1)}, bf16[2,4,2,512,256]{4,3,2,1,0:T(8,128)(2,1)}, f32[8,4,256]{2,1,0:T(4,128)}) custom-call(s32[10]{0:T(128)} %pad_add_fusion.refs_0_, bf16[8,624,512]{2,1,0:T(8,128)(2,1)} %get-tuple-element.213.refs_4_.refs_1_, ...), custom_call_target="tpu_custom_call" | custom-call | flops 4000000000 | bytes 400000 | tf_op jit(solution)/shard_map/experts_10/pallas_call | solution.py:516
  266.9 1.4 collective-permute-start.32
  268.4 2.9 collective-permute-done.32.refs_8_
  274.6 23.7 %experts_11.1 = (bf16[8,624,512]{2,1,0:T(8,128)(2,1)}, bf16[8,624,512]{2,1,0:T(8,128)(2,1)}, bf16[2,4,2,512,256]{4,3,2,1,0:T(8,128)(2,1)}, bf16[2,4,2,512,256]{4,3,2,1,0:T(8,128)(2,1)}, f32[8,4,256]{2,1,0:T(4,128)}) custom-call(s32[10]{0:T(128)} %pad_add_fusion.refs_0_, ...), custom_call_target="tpu_custom_call", output_to_operand_aliasing={{0}: (17, {}), {1}: (18, {})} | custom-call | flops 4000000000 | bytes 400000 | tf_op jit(solution)/shard_map/experts_11/pallas_call | solution.py:516
  300.4 5.7 %fold_first.2 = (bf16[4,512,256]{2,1,0:T(8,128)(2,1)}, bf16[4,512,256]{2,1,0:T(8,128)(2,1)}, bf16[4,512,256]{2,1,0:T(8,128)(2,1)}, bf16[4,512,256]{2,1,0:T(8,128)(2,1)}) custom-call(bf16[2,4,512,256]{3,2,1,0:T(8,128)(2,1)} %get-tuple-element.255.refs_0_, bf16[2,4,512,256]{3,2,1,0:T(8,128)(2,1)} %get-tuple-element.256.refs_1_, ...), custom_call_target="tpu_custom_call" | custom-call | flops 4000000000 | bytes 400000 | tf_op jit(solution)/shard_map/fold_first/pallas_call | solution.py:906
  307.4 8.9 %fold_cores.3 = (bf16[2,4,512,256]{3,2,1,0:T(8,128)(2,1)}, bf16[2,4,512,256]{3,2,1,0:T(8,128)(2,1)}, bf16[2,4,512,256]{3,2,1,0:T(8,128)(2,1)}, bf16[2,4,512,256]{3,2,1,0:T(8,128)(2,1)}) custom-call(bf16[2,4,2,512,256]{4,3,2,1,0:T(8,128)(2,1)} %get-tuple-element.264.n0, bf16[2,4,2,512,256]{4,3,2,1,0:T(8,128)(2,1)} %get-tuple-element.265.n1, ...), custom_call_target="tpu_custom_call" | custom-call | flops 7000000000 | bytes 700000 | tf_op jit(solution)/shard_map/fold_cores/pallas_call | solution.py:885
  317.4 2.0 collective-permute-start.41
  319.4 50.1 %combine.1 = (f32[1970,512]{1,0:T(8,128)}, f32[2080,512]{1,0:T(8,128)}, bf16[2080,512]{1,0:T(8,128)(2,1)}, f32[512,512]{1,0:T(8,128)}, f32[8,512]{1,0:T(8,128)}, /*index=5*/f32[8,512]{1,0:T(8,128)}) custom-call(s32[20,8]{1,0:T(8,128)} %get-tuple-element.199.refs_0_, bf16[8,624,512]{2,1,0:T(8,128)(2,1)} %get-tuple-element.250.refs_1_, ...), custom_call_target="tpu_custom_call" | custom-call | flops 40000000000 | bytes 4000000 | tf_op jit(solution)/shard_map/combine/pallas_call | solution.py:616
  372.3 3.5 fold_second.2
  375.8 8.6 %collective-permute-start.42 = (bf16[2,512,256]{2,1,0:T(8,128)(2,1)}, bf16[2,512,256]{2,1,0:T(8,128)(2,1)S(1)}, u32[]{:S(2)}, u32[]{:S(2)}) collective-permute-start(bf16[2,512,256]{2,1,0:T(8,128)(2,1)} %get-tuple-element.287.refs_10_), channel_id=1, source_target_pairs={{0,2},{1,3},{2,0},{3,1},{4,6},{5,7},{6,4},{7,5},{8,10},{9,11},{10,... | collective-permute-start | bytes 1572872 | tf_op jit(solution)/shard_map/ppermute | solution.py:761
  385.1 1.7 collective-permute-start.44
  386.8 5.7 %fold_first.3 = (bf16[4,512,256]{2,1,0:T(8,128)(2,1)}, bf16[4,512,256]{2,1,0:T(8,128)(2,1)}, bf16[4,512,256]{2,1,0:T(8,128)(2,1)}, bf16[4,512,256]{2,1,0:T(8,128)(2,1)}) custom-call(bf16[2,4,512,256]{3,2,1,0:T(8,128)(2,1)} %get-tuple-element.290.refs_0_, bf16[2,4,512,256]{3,2,1,0:T(8,128)(2,1)} %get-tuple-element.291.refs_1_, ...), custom_call_target="tpu_custom_call" | custom-call | flops 4000000000 | bytes 400000 | tf_op jit(solution)/shard_map/fold_first/pallas_call | solution.py:906
  394.6 41.0 %attention_back.1 = (f32[1970,512]{1,0:T(8,128)}, bf16[16,16,2176]{2,1,0:T(8,128)(2,1)}, bf16[16,16,2176]{2,1,0:T(8,128)(2,1)}) custom-call(s32[32]{0:T(128)} %broadcast_xor_fusion.place_ref.refs_0_, bf16[2080,1536]{1,0:T(8,128)(2,1)} %get-tuple-element.271.refs_1_, bf16[10,8,208,208]{3,2,1,0:T(8,128)(2,1)} %get-tuple-element.272.refs_2_, ...), custom_call_target="tpu_custom_call" | custom-call | flops 49999998976 | bytes 5000000 | tf_op jit(solution)/shard_map/attention_back/pallas_call | solution.py:727
  437.0 3.5 fold_second.3
  440.7 3.0 collective-permute-done.47.refs_1_
  444.6 2.7 block_sum.2
  449.2 1.5 collective-permute-start.55
  450.8 1.7 collective-permute-start.56
  453.7 2.5 collective-permute-done.48.refs_1_
  456.2 1.4 collective-permute-start.50
  458.2 4.8 expert_update_0.1
  463.1 3.8 collective-permute-done.50.refs_3_
  467.6 2.0 block_sum.3
  469.8 2.4 collective-permute-start.52
  472.2 13.3 %collective-permute-done.51.refs_1_ = bf16[1,16,2176]{2,1,0:T(8,128)(2,1)S(1)} collective-permute-done((bf16[1,16,2176]{2,1,0:T(8,128)(2,1)}, bf16[1,16,2176]{2,1,0:T(8,128)(2,1)S(1)}, u32[]{:S(2)}, u32[]{:S(2)}) %collective-permute-start.51) | collective-permute-done | bytes 69664 | tf_op jit(solution)/shard_map/ppermute | solution.py:761
  485.5 2.1 collective-permute-start.53
  491.6 11.1 %collective-permute-done.52.refs_2_ = bf16[1,16,2176]{2,1,0:T(8,128)(2,1)S(1)} collective-permute-done((bf16[1,16,2176]{2,1,0:T(8,128)(2,1)}, bf16[1,16,2176]{2,1,0:T(8,128)(2,1)S(1)}, u32[]{:S(2)}, u32[]{:S(2)}) %collective-permute-start.52) | collective-permute-done | bytes 69664 | tf_op jit(solution)/shard_map/ppermute | solution.py:761
  503.4 2.2 dense_update.1
  506.8 5.0 expert_update_1.1
  515.0 2.4 collective-permute-done.58
  518.6 2.4 collective-permute-done.59
  522.3 2.3 collective-permute-done.60
  524.6 1.9 collective-permute-start.61
  529.8 4.1 new_weights.1
  (282 shorter events, 70.4 us)
Async XLA Ops:
  5.5 16.0 %collective-permute-start = (bf16[16,2304]{1,0:T(8,128)(2,1)S(1)}, bf16[16,2304]{1,0:T(8,128)(2,1)}, u32[]{:S(2)}, u32[]{:S(2)}) collective-permute-start(bf16[16,2304]{1,0:T(8,128)(2,1)S(1)} %pad_maximum_fusion.2.refs_0_), channel_id=1, source_target_pairs={{0,2},{1,3},{2,0},{3,1},{4,6},{5,7},{6,4},{7,5},{8,10},{9,11},{10,... | collective-permute-start | bytes 221192 | tf_op jit(solution)/shard_map/ppermute | solution.py:761
  8.6 12.9 %collective-permute-start.1 = (bf16[16,2304]{1,0:T(8,128)(2,1)S(1)}, bf16[16,2304]{1,0:T(8,128)(2,1)}, u32[]{:S(2)}, u32[]{:S(2)}) collective-permute-start(bf16[16,2304]{1,0:T(8,128)(2,1)S(1)} %pad_maximum_fusion.2.refs_0_), channel_id=1, source_target_pairs={{0,4},{1,5},{2,6},{3,7},{4,0},{5,1},{6,2},{7,3},{8,12},{9,13},{10,... | collective-permute-start | bytes 221192 | tf_op jit(solution)/shard_map/ppermute | solution.py:761
  11.2 10.3 %collective-permute-start.2 = (bf16[16,2304]{1,0:T(8,128)(2,1)S(1)}, bf16[16,2304]{1,0:T(8,128)(2,1)}, u32[]{:S(2)}, u32[]{:S(2)}) collective-permute-start(bf16[16,2304]{1,0:T(8,128)(2,1)S(1)} %pad_maximum_fusion.2.refs_0_), channel_id=1, source_target_pairs={{0,6},{1,7},{2,4},{3,5},{4,2},{5,3},{6,0},{7,1},{8,14},{9,15},{10,... | collective-permute-start | bytes 221192 | tf_op jit(solution)/shard_map/ppermute | solution.py:761
  23.4 16.0 %collective-permute-start.3 = (bf16[4,16,2304]{2,1,0:T(8,128)(2,1)}, bf16[4,16,2304]{2,1,0:T(8,128)(2,1)S(1)}, u32[]{:S(2)}, u32[]{:S(2)}) collective-permute-start(bf16[4,16,2304]{2,1,0:T(8,128)(2,1)} %stack.34.refs_0_), channel_id=1, source_target_pairs={{0,1},{1,0},{2,3},{3,2},{4,5},{5,4},{6,7},{7,6},{8,9},{9,8},{10,11... | collective-permute-start | bytes 884744 | tf_op jit(solution)/shard_map/ppermute | solution.py:761
  25.1 14.3 %collective-permute-start.4 = (bf16[4,16,2304]{2,1,0:T(8,128)(2,1)}, bf16[4,16,2304]{2,1,0:T(8,128)(2,1)S(1)}, u32[]{:S(2)}, u32[]{:S(2)}) collective-permute-start(bf16[4,16,2304]{2,1,0:T(8,128)(2,1)} %stack.34.refs_0_), channel_id=1, source_target_pairs={{0,16},{1,17},{2,18},{3,19},{4,20},{5,21},{6,22},{7,23},{8,24},{9,... | collective-permute-start | bytes 884744 | tf_op jit(solution)/shard_map/ppermute | solution.py:761
  26.6 12.8 %collective-permute-start.5 = (bf16[4,16,2304]{2,1,0:T(8,128)(2,1)}, bf16[4,16,2304]{2,1,0:T(8,128)(2,1)S(1)}, u32[]{:S(2)}, u32[]{:S(2)}) collective-permute-start(bf16[4,16,2304]{2,1,0:T(8,128)(2,1)} %stack.34.refs_0_), channel_id=1, source_target_pairs={{0,17},{1,16},{2,19},{3,18},{4,21},{5,20},{6,23},{7,22},{8,25},{9,... | collective-permute-start | bytes 884744 | tf_op jit(solution)/shard_map/ppermute | solution.py:761
  26.8 12.6 %collective-permute-start.6 = (bf16[2,512,256]{2,1,0:T(8,128)(2,1)S(1)}, bf16[2,512,256]{2,1,0:T(8,128)(2,1)S(1)}, u32[]{:S(2)}, u32[]{:S(2)}) collective-permute-start(bf16[2,512,256]{2,1,0:T(8,128)(2,1)S(1)} %pad_maximum_fusion.refs_0_), channel_id=1, source_target_pairs={{0,2},{1,3},{2,0},{3,1},{4,6},{5,7},{6,4},{7,5},{8,10},{9,11},{10,... | collective-permute-start | bytes 1572872 | tf_op jit(solution)/shard_map/ppermute | solution.py:761
  42.8 4.0 collective-permute-start.7
  43.3 38.3 %collective-permute-start.8 = (bf16[2,512,256]{2,1,0:T(8,128)(2,1)S(1)}, bf16[2,512,256]{2,1,0:T(8,128)(2,1)S(1)}, u32[]{:S(2)}, u32[]{:S(2)}) collective-permute-start(bf16[2,512,256]{2,1,0:T(8,128)(2,1)S(1)} %pad_maximum_fusion.refs_0_), channel_id=1, source_target_pairs={{0,4},{1,5},{2,6},{3,7},{4,0},{5,1},{6,2},{7,3},{8,12},{9,13},{10,... | collective-permute-start | bytes 1572872 | tf_op jit(solution)/shard_map/ppermute | solution.py:761
  46.8 34.8 %collective-permute-start.9 = (bf16[2,512,256]{2,1,0:T(8,128)(2,1)S(1)}, bf16[2,512,256]{2,1,0:T(8,128)(2,1)S(1)}, u32[]{:S(2)}, u32[]{:S(2)}) collective-permute-start(bf16[2,512,256]{2,1,0:T(8,128)(2,1)S(1)} %pad_maximum_fusion.refs_0_), channel_id=1, source_target_pairs={{0,6},{1,7},{2,4},{3,5},{4,2},{5,3},{6,0},{7,1},{8,14},{9,15},{10,... | collective-permute-start | bytes 1572872 | tf_op jit(solution)/shard_map/ppermute | solution.py:761
  85.6 57.1 %collective-permute-start.10 = (bf16[2,4,512,256]{3,2,1,0:T(8,128)(2,1)}, bf16[2,4,512,256]{3,2,1,0:T(8,128)(2,1)}, u32[]{:S(2)}, u32[]{:S(2)}) collective-permute-start(bf16[2,4,512,256]{3,2,1,0:T(8,128)(2,1)} %turn_stack.2.refs_5_.refs_9_), channel_id=1, source_target_pairs={{0,16},{1,17},{2,18},{3,19},{4,20},{5,21},{6,22},{7,23},{8,24},{9,... | collective-permute-start | bytes 6291464 | tf_op jit(solution)/shard_map/ppermute | solution.py:761
  87.3 55.5 %collective-permute-start.11 = (bf16[2,4,512,256]{3,2,1,0:T(8,128)(2,1)}, bf16[2,4,512,256]{3,2,1,0:T(8,128)(2,1)}, u32[]{:S(2)}, u32[]{:S(2)}) collective-permute-start(bf16[2,4,512,256]{3,2,1,0:T(8,128)(2,1)} %turn_stack.2.refs_5_.refs_9_), channel_id=1, source_target_pairs={{0,1},{1,0},{2,3},{3,2},{4,5},{5,4},{6,7},{7,6},{8,9},{9,8},{10,11... | collective-permute-start | bytes 6291464 | tf_op jit(solution)/shard_map/ppermute | solution.py:761
  88.9 41.8 %copy-start.4 = (bf16[2,512,256]{2,1,0:T(8,128)(2,1)}, bf16[2,512,256]{2,1,0:T(8,128)(2,1)S(1)}, u32[]{:S(2)}) copy-start(bf16[2,512,256]{2,1,0:T(8,128)(2,1)S(1)} %pad_maximum_fusion.1.refs_0_) | copy-start | bytes 1572868
  88.9 41.7 %collective-permute-start.12 = (bf16[2,512,256]{2,1,0:T(8,128)(2,1)S(1)}, bf16[2,512,256]{2,1,0:T(8,128)(2,1)S(1)}, u32[]{:S(2)}, u32[]{:S(2)}) collective-permute-start(bf16[2,512,256]{2,1,0:T(8,128)(2,1)S(1)} %pad_maximum_fusion.1.refs_0_), channel_id=1, source_target_pairs={{0,2},{1,3},{2,0},{3,1},{4,6},{5,7},{6,4},{7,5},{8,10},{9,11},{10,... | collective-permute-start | bytes 1572872 | tf_op jit(solution)/shard_map/ppermute | solution.py:761
  100.6 38.2 %collective-permute-start.13 = (bf16[2,512,256]{2,1,0:T(8,128)(2,1)S(1)}, bf16[2,512,256]{2,1,0:T(8,128)(2,1)S(1)}, u32[]{:S(2)}, u32[]{:S(2)}) collective-permute-start(bf16[2,512,256]{2,1,0:T(8,128)(2,1)S(1)} %pad_maximum_fusion.1.refs_0_), channel_id=1, source_target_pairs={{0,4},{1,5},{2,6},{3,7},{4,0},{5,1},{6,2},{7,3},{8,12},{9,13},{10,... | collective-permute-start | bytes 1572872 | tf_op jit(solution)/shard_map/ppermute | solution.py:761
  101.6 37.2 %collective-permute-start.14 = (bf16[2,512,256]{2,1,0:T(8,128)(2,1)S(1)}, bf16[2,512,256]{2,1,0:T(8,128)(2,1)S(1)}, u32[]{:S(2)}, u32[]{:S(2)}) collective-permute-start(bf16[2,512,256]{2,1,0:T(8,128)(2,1)S(1)} %pad_maximum_fusion.1.refs_0_), channel_id=1, source_target_pairs={{0,6},{1,7},{2,4},{3,5},{4,2},{5,3},{6,0},{7,1},{8,14},{9,15},{10,... | collective-permute-start | bytes 1572872 | tf_op jit(solution)/shard_map/ppermute | solution.py:761
  146.8 8.0 %collective-permute-start.15 = (bf16[2,4,512,256]{3,2,1,0:T(8,128)(2,1)}, bf16[2,4,512,256]{3,2,1,0:T(8,128)(2,1)}, u32[]{:S(2)}, u32[]{:S(2)}) collective-permute-start(bf16[2,4,512,256]{3,2,1,0:T(8,128)(2,1)} %turn_stack.2.refs_5_.refs_9_), channel_id=1, source_target_pairs={{0,8},{1,9},{2,10},{3,11},{4,12},{5,13},{6,14},{7,15},{8,0},{9,1},... | collective-permute-start | bytes 6291464 | tf_op jit(solution)/shard_map/ppermute | solution.py:761
  146.9 6.0 %collective-permute-start.16 = (bf16[1,4,512,256]{3,2,1,0:T(8,128)(2,1)}, bf16[1,4,512,256]{3,2,1,0:T(8,128)(2,1)}, u32[]{:S(2)}, u32[]{:S(2)}) collective-permute-start(bf16[1,4,512,256]{3,2,1,0:T(8,128)(2,1)} %get-tuple-element.220), channel_id=1, source_target_pairs={{0,8},{1,9},{2,10},{3,11},{4,12},{5,13},{6,14},{7,15},{8,0},{9,1},... | collective-permute-start | bytes 3145736 | tf_op jit(solution)/shard_map/ppermute | solution.py:761
  147.4 7.0 %collective-permute-start.17 = (bf16[1,4,512,256]{3,2,1,0:T(8,128)(2,1)}, bf16[1,4,512,256]{3,2,1,0:T(8,128)(2,1)}, u32[]{:S(2)}, u32[]{:S(2)}) collective-permute-start(bf16[1,4,512,256]{3,2,1,0:T(8,128)(2,1)} %get-tuple-element.221), channel_id=1, source_target_pairs={{0,8},{1,9},{2,10},{3,11},{4,12},{5,13},{6,14},{7,15},{8,0},{9,1},... | collective-permute-start | bytes 3145736 | tf_op jit(solution)/shard_map/ppermute | solution.py:761
  147.4 34.1 %collective-permute-start.18 = (bf16[2,4,512,256]{3,2,1,0:T(8,128)(2,1)}, bf16[2,4,512,256]{3,2,1,0:T(8,128)(2,1)}, u32[]{:S(2)}, u32[]{:S(2)}) collective-permute-start(bf16[2,4,512,256]{3,2,1,0:T(8,128)(2,1)} %collective-permute-done.11.refs_1_.refs_5_.refs_9_), channel_id=1, source_target_pairs={{0,8},{1,9},{2,10},{3,11},{4,12},{5,13},{6,14},{7,15},{8,0},{9,1},... | collective-permute-start | bytes 6291464 | tf_op jit(solution)/shard_map/ppermute | solution.py:761
  147.9 32.6 %collective-permute-start.19 = (bf16[1,4,512,256]{3,2,1,0:T(8,128)(2,1)}, bf16[1,4,512,256]{3,2,1,0:T(8,128)(2,1)S(1)}, u32[]{:S(2)}, u32[]{:S(2)}) collective-permute-start(bf16[1,4,512,256]{3,2,1,0:T(8,128)(2,1)} %get-tuple-element.220), channel_id=1, source_target_pairs={{0,1},{1,0},{2,3},{3,2},{4,5},{5,4},{6,7},{7,6},{8,9},{9,8},{10,11... | collective-permute-start | bytes 3145736 | tf_op jit(solution)/shard_map/ppermute | solution.py:761
  152.8 28.5 %collective-permute-start.20 = (bf16[1,4,512,256]{3,2,1,0:T(8,128)(2,1)}, bf16[1,4,512,256]{3,2,1,0:T(8,128)(2,1)}, u32[]{:S(2)}, u32[]{:S(2)}) collective-permute-start(bf16[1,4,512,256]{3,2,1,0:T(8,128)(2,1)} %get-tuple-element.225), channel_id=1, source_target_pairs={{0,16},{1,17},{2,18},{3,19},{4,20},{5,21},{6,22},{7,23},{8,24},{9,... | collective-permute-start | bytes 3145736 | tf_op jit(solution)/shard_map/ppermute | solution.py:761
  154.4 69.0 %collective-permute-start.24 = (bf16[2,4,512,256]{3,2,1,0:T(8,128)(2,1)S(1)}, bf16[2,4,512,256]{3,2,1,0:T(8,128)(2,1)}, u32[]{:S(2)}, u32[]{:S(2)}) collective-permute-start(bf16[2,4,512,256]{3,2,1,0:T(8,128)(2,1)S(1)} %copy-done), channel_id=1, source_target_pairs={{0,16},{1,17},{2,18},{3,19},{4,20},{5,21},{6,22},{7,23},{8,24},{9,... | collective-permute-start | bytes 6291464 | tf_op jit(solution)/shard_map/ppermute | solution.py:761
  154.9 68.4 %collective-permute-start.25 = (bf16[2,4,512,256]{3,2,1,0:T(8,128)(2,1)S(1)}, bf16[2,4,512,256]{3,2,1,0:T(8,128)(2,1)}, u32[]{:S(2)}, u32[]{:S(2)}) collective-permute-start(bf16[2,4,512,256]{3,2,1,0:T(8,128)(2,1)S(1)} %copy-done), channel_id=1, source_target_pairs={{0,1},{1,0},{2,3},{3,2},{4,5},{5,4},{6,7},{7,6},{8,9},{9,8},{10,11... | collective-permute-start | bytes 6291464 | tf_op jit(solution)/shard_map/ppermute | solution.py:761
  180.5 42.8 %collective-permute-start.26 = (bf16[2,4,512,256]{3,2,1,0:T(8,128)(2,1)S(1)}, bf16[2,4,512,256]{3,2,1,0:T(8,128)(2,1)}, u32[]{:S(2)}, u32[]{:S(2)}) collective-permute-start(bf16[2,4,512,256]{3,2,1,0:T(8,128)(2,1)S(1)} %copy-done), channel_id=1, source_target_pairs={{0,8},{1,9},{2,10},{3,11},{4,12},{5,13},{6,14},{7,15},{8,0},{9,1},... | collective-permute-start | bytes 6291464 | tf_op jit(solution)/shard_map/ppermute | solution.py:761
  181.3 6.7 %collective-permute-start.21 = (bf16[1,4,512,256]{3,2,1,0:T(8,128)(2,1)S(1)}, bf16[1,4,512,256]{3,2,1,0:T(8,128)(2,1)S(1)}, u32[]{:S(2)}, u32[]{:S(2)}) collective-permute-start(bf16[1,4,512,256]{3,2,1,0:T(8,128)(2,1)S(1)} %collective-permute-done.19.refs_7_), channel_id=1, source_target_pairs={{0,8},{1,9},{2,10},{3,11},{4,12},{5,13},{6,14},{7,15},{8,0},{9,1},... | collective-permute-start | bytes 3145736 | tf_op jit(solution)/shard_map/ppermute | solution.py:761
  181.4 7.7 %collective-permute-start.22 = (bf16[1,4,512,256]{3,2,1,0:T(8,128)(2,1)}, bf16[1,4,512,256]{3,2,1,0:T(8,128)(2,1)}, u32[]{:S(2)}, u32[]{:S(2)}) collective-permute-start(bf16[1,4,512,256]{3,2,1,0:T(8,128)(2,1)} %collective-permute-done.20.refs_11_), channel_id=1, source_target_pairs={{0,8},{1,9},{2,10},{3,11},{4,12},{5,13},{6,14},{7,15},{8,0},{9,1},... | collective-permute-start | bytes 3145736 | tf_op jit(solution)/shard_map/ppermute | solution.py:761
  189.0 40.3 %collective-permute-start.23 = (bf16[2,4,2,512,256]{4,3,2,1,0:T(8,128)(2,1)}, bf16[2,4,2,512,256]{4,3,2,1,0:T(8,128)(2,1)}, u32[]{:S(2)}, u32[]{:S(2)}) collective-permute-start(bf16[2,4,2,512,256]{4,3,2,1,0:T(8,128)(2,1)} %get-tuple-element.231), channel_id=1, source_target_pairs={{0,8},{1,9},{2,10},{3,11},{4,12},{5,13},{6,14},{7,15},{8,0},{9,1},... | collective-permute-start | bytes 12582920 | tf_op jit(solution)/shard_map/ppermute | solution.py:761
  223.3 7.5 %collective-permute-start.27 = (bf16[2,4,2,512,256]{4,3,2,1,0:T(8,128)(2,1)}, bf16[2,4,2,512,256]{4,3,2,1,0:T(8,128)(2,1)}, u32[]{:S(2)}, u32[]{:S(2)}) collective-permute-start(bf16[2,4,2,512,256]{4,3,2,1,0:T(8,128)(2,1)} %get-tuple-element.235), channel_id=1, source_target_pairs={{0,8},{1,9},{2,10},{3,11},{4,12},{5,13},{6,14},{7,15},{8,0},{9,1},... | collective-permute-start | bytes 12582920 | tf_op jit(solution)/shard_map/ppermute | solution.py:761
  223.3 17.1 %collective-permute-start.29 = (bf16[2,4,512,256]{3,2,1,0:T(8,128)(2,1)}, bf16[2,4,512,256]{3,2,1,0:T(8,128)(2,1)}, u32[]{:S(2)}, u32[]{:S(2)}) collective-permute-start(bf16[2,4,512,256]{3,2,1,0:T(8,128)(2,1)} %collective-permute-done.24.refs_7_.refs_11_), channel_id=1, source_target_pairs={{0,8},{1,9},{2,10},{3,11},{4,12},{5,13},{6,14},{7,15},{8,0},{9,1},... | collective-permute-start | bytes 6291464 | tf_op jit(solution)/shard_map/ppermute | solution.py:761
  226.1 40.8 %collective-permute-start.30 = (bf16[1,4,512,256]{3,2,1,0:T(8,128)(2,1)}, bf16[1,4,512,256]{3,2,1,0:T(8,128)(2,1)S(1)}, u32[]{:S(2)}, u32[]{:S(2)}) collective-permute-start(bf16[1,4,512,256]{3,2,1,0:T(8,128)(2,1)} %slice.58), channel_id=1, source_target_pairs={{0,1},{1,0},{2,3},{3,2},{4,5},{5,4},{6,7},{7,6},{8,9},{9,8},{10,11... | collective-permute-start | bytes 3145736 | tf_op jit(solution)/shard_map/ppermute | solution.py:761
  228.9 38.1 %collective-permute-start.31 = (bf16[1,4,512,256]{3,2,1,0:T(8,128)(2,1)}, bf16[1,4,512,256]{3,2,1,0:T(8,128)(2,1)}, u32[]{:S(2)}, u32[]{:S(2)}) collective-permute-start(bf16[1,4,512,256]{3,2,1,0:T(8,128)(2,1)} %slice.59), channel_id=1, source_target_pairs={{0,16},{1,17},{2,18},{3,19},{4,20},{5,21},{6,22},{7,23},{8,24},{9,... | collective-permute-start | bytes 3145736 | tf_op jit(solution)/shard_map/ppermute | solution.py:761
  239.8 32.6 %collective-permute-start.28 = (bf16[2,4,512,256]{3,2,1,0:T(8,128)(2,1)}, bf16[2,4,512,256]{3,2,1,0:T(8,128)(2,1)S(1)}, u32[]{:S(2)}, u32[]{:S(2)}) collective-permute-start(bf16[2,4,512,256]{3,2,1,0:T(8,128)(2,1)} %collective-permute-done.25.refs_5_.refs_9_), channel_id=1, source_target_pairs={{0,8},{1,9},{2,10},{3,11},{4,12},{5,13},{6,14},{7,15},{8,0},{9,1},... | collective-permute-start | bytes 6291464 | tf_op jit(solution)/shard_map/ppermute | solution.py:761
  239.9 58.4 %collective-permute-start.34 = (bf16[2,4,512,256]{3,2,1,0:T(8,128)(2,1)}, bf16[2,4,512,256]{3,2,1,0:T(8,128)(2,1)}, u32[]{:S(2)}, u32[]{:S(2)}) collective-permute-start(bf16[2,4,512,256]{3,2,1,0:T(8,128)(2,1)} %get-tuple-element.243.refs_17_), channel_id=1, source_target_pairs={{0,1},{1,0},{2,3},{3,2},{4,5},{5,4},{6,7},{7,6},{8,9},{9,8},{10,11... | collective-permute-start | bytes 6291464 | tf_op jit(solution)/shard_map/ppermute | solution.py:761
  240.5 58.5 %collective-permute-start.35 = (bf16[2,4,512,256]{3,2,1,0:T(8,128)(2,1)}, bf16[2,4,512,256]{3,2,1,0:T(8,128)(2,1)}, u32[]{:S(2)}, u32[]{:S(2)}) collective-permute-start(bf16[2,4,512,256]{3,2,1,0:T(8,128)(2,1)} %get-tuple-element.244.refs_18_), channel_id=1, source_target_pairs={{0,16},{1,17},{2,18},{3,19},{4,20},{5,21},{6,22},{7,23},{8,24},{9,... | collective-permute-start | bytes 6291464 | tf_op jit(solution)/shard_map/ppermute | solution.py:761
  266.9 4.4 collective-permute-start.32
  268.4 4.0 collective-permute-start.33
  271.4 35.8 %collective-permute-start.36 = (bf16[2,4,2,512,256]{4,3,2,1,0:T(8,128)(2,1)}, bf16[2,4,2,512,256]{4,3,2,1,0:T(8,128)(2,1)}, u32[]{:S(2)}, u32[]{:S(2)}) collective-permute-start(bf16[2,4,2,512,256]{4,3,2,1,0:T(8,128)(2,1)} %get-tuple-element.266), channel_id=1, source_target_pairs={{0,8},{1,9},{2,10},{3,11},{4,12},{5,13},{6,14},{7,15},{8,0},{9,1},... | collective-permute-start | bytes 12582920 | tf_op jit(solution)/shard_map/ppermute | solution.py:761
  299.0 8.4 %collective-permute-start.37 = (bf16[2,4,2,512,256]{4,3,2,1,0:T(8,128)(2,1)}, bf16[2,4,2,512,256]{4,3,2,1,0:T(8,128)(2,1)}, u32[]{:S(2)}, u32[]{:S(2)}) collective-permute-start(bf16[2,4,2,512,256]{4,3,2,1,0:T(8,128)(2,1)} %get-tuple-element.267), channel_id=1, source_target_pairs={{0,8},{1,9},{2,10},{3,11},{4,12},{5,13},{6,14},{7,15},{8,0},{9,1},... | collective-permute-start | bytes 12582920 | tf_op jit(solution)/shard_map/ppermute | solution.py:761
  306.1 63.4 %collective-permute-start.38 = (bf16[4,512,256]{2,1,0:T(8,128)(2,1)}, bf16[4,512,256]{2,1,0:T(8,128)(2,1)S(1)}, u32[]{:S(2)}, u32[]{:S(2)}) collective-permute-start(bf16[4,512,256]{2,1,0:T(8,128)(2,1)} %get-tuple-element.262.refs_13_), channel_id=1, source_target_pairs={{0,16},{1,17},{2,18},{3,19},{4,20},{5,21},{6,22},{7,23},{8,24},{9,... | collective-permute-start | bytes 3145736 | tf_op jit(solution)/shard_map/ppermute | solution.py:761
  306.1 63.4 %collective-permute-start.39 = (bf16[4,512,256]{2,1,0:T(8,128)(2,1)}, bf16[4,512,256]{2,1,0:T(8,128)(2,1)S(1)}, u32[]{:S(2)}, u32[]{:S(2)}) collective-permute-start(bf16[4,512,256]{2,1,0:T(8,128)(2,1)} %get-tuple-element.263.refs_14_), channel_id=1, source_target_pairs={{0,1},{1,0},{2,3},{3,2},{4,5},{5,4},{6,7},{7,6},{8,9},{9,8},{10,11... | collective-permute-start | bytes 3145736 | tf_op jit(solution)/shard_map/ppermute | solution.py:761
  316.3 70.5 %collective-permute-start.40 = (bf16[2,4,512,256]{3,2,1,0:T(8,128)(2,1)}, bf16[2,4,512,256]{3,2,1,0:T(8,128)(2,1)}, u32[]{:S(2)}, u32[]{:S(2)}) collective-permute-start(bf16[2,4,512,256]{3,2,1,0:T(8,128)(2,1)} %get-tuple-element.268.refs_15_), channel_id=1, source_target_pairs={{0,1},{1,0},{2,3},{3,2},{4,5},{5,4},{6,7},{7,6},{8,9},{9,8},{10,11... | collective-permute-start | bytes 6291464 | tf_op jit(solution)/shard_map/ppermute | solution.py:761
  317.4 69.4 %collective-permute-start.41 = (bf16[2,4,512,256]{3,2,1,0:T(8,128)(2,1)}, bf16[2,4,512,256]{3,2,1,0:T(8,128)(2,1)}, u32[]{:S(2)}, u32[]{:S(2)}) collective-permute-start(bf16[2,4,512,256]{3,2,1,0:T(8,128)(2,1)} %get-tuple-element.269.refs_16_), channel_id=1, source_target_pairs={{0,16},{1,17},{2,18},{3,19},{4,20},{5,21},{6,22},{7,23},{8,24},{9,... | collective-permute-start | bytes 6291464 | tf_op jit(solution)/shard_map/ppermute | solution.py:761
  375.8 59.7 %collective-permute-start.42 = (bf16[2,512,256]{2,1,0:T(8,128)(2,1)}, bf16[2,512,256]{2,1,0:T(8,128)(2,1)S(1)}, u32[]{:S(2)}, u32[]{:S(2)}) collective-permute-start(bf16[2,512,256]{2,1,0:T(8,128)(2,1)} %get-tuple-element.287.refs_10_), channel_id=1, source_target_pairs={{0,2},{1,3},{2,0},{3,1},{4,6},{5,7},{6,4},{7,5},{8,10},{9,11},{10,... | collective-permute-start | bytes 1572872 | tf_op jit(solution)/shard_map/ppermute | solution.py:761
  384.5 51.1 %collective-permute-start.43 = (bf16[2,512,256]{2,1,0:T(8,128)(2,1)}, bf16[2,512,256]{2,1,0:T(8,128)(2,1)S(1)}, u32[]{:S(2)}, u32[]{:S(2)}) collective-permute-start(bf16[2,512,256]{2,1,0:T(8,128)(2,1)} %get-tuple-element.288.refs_11_), channel_id=1, source_target_pairs={{0,4},{1,5},{2,6},{3,7},{4,0},{5,1},{6,2},{7,3},{8,12},{9,13},{10,... | collective-permute-start | bytes 1572872 | tf_op jit(solution)/shard_map/ppermute | solution.py:761
  385.1 50.5 %collective-permute-start.44 = (bf16[2,512,256]{2,1,0:T(8,128)(2,1)}, bf16[2,512,256]{2,1,0:T(8,128)(2,1)S(1)}, u32[]{:S(2)}, u32[]{:S(2)}) collective-permute-start(bf16[2,512,256]{2,1,0:T(8,128)(2,1)} %get-tuple-element.289.refs_12_), channel_id=1, source_target_pairs={{0,6},{1,7},{2,4},{3,5},{4,2},{5,3},{6,0},{7,1},{8,14},{9,15},{10,... | collective-permute-start | bytes 1572872 | tf_op jit(solution)/shard_map/ppermute | solution.py:761
  392.6 43.1 %collective-permute-start.45 = (bf16[4,512,256]{2,1,0:T(8,128)(2,1)}, bf16[4,512,256]{2,1,0:T(8,128)(2,1)S(1)}, u32[]{:S(2)}, u32[]{:S(2)}) collective-permute-start(bf16[4,512,256]{2,1,0:T(8,128)(2,1)} %get-tuple-element.292.refs_13_), channel_id=1, source_target_pairs={{0,16},{1,17},{2,18},{3,19},{4,20},{5,21},{6,22},{7,23},{8,24},{9,... | collective-permute-start | bytes 3145736 | tf_op jit(solution)/shard_map/ppermute | solution.py:761
  393.4 42.2 %collective-permute-start.46 = (bf16[4,512,256]{2,1,0:T(8,128)(2,1)}, bf16[4,512,256]{2,1,0:T(8,128)(2,1)S(1)}, u32[]{:S(2)}, u32[]{:S(2)}) collective-permute-start(bf16[4,512,256]{2,1,0:T(8,128)(2,1)} %get-tuple-element.293.refs_14_), channel_id=1, source_target_pairs={{0,1},{1,0},{2,3},{3,2},{4,5},{5,4},{6,7},{7,6},{8,9},{9,8},{10,11... | collective-permute-start | bytes 3145736 | tf_op jit(solution)/shard_map/ppermute | solution.py:761
  440.6 3.0 collective-permute-start.47
  447.3 8.9 %collective-permute-start.48 = (bf16[4,16,2176]{2,1,0:T(8,128)(2,1)}, bf16[4,16,2176]{2,1,0:T(8,128)(2,1)S(1)}, u32[]{:S(2)}, u32[]{:S(2)}) collective-permute-start(bf16[4,16,2176]{2,1,0:T(8,128)(2,1)} %get-tuple-element.314), channel_id=1, source_target_pairs={{0,1},{1,0},{2,3},{3,2},{4,5},{5,4},{6,7},{7,6},{8,9},{9,8},{10,11... | collective-permute-start | bytes 835592 | tf_op jit(solution)/shard_map/ppermute | solution.py:761
  448.1 57.5 %collective-permute-start.54 = (bf16[2,512,256]{2,1,0:T(8,128)(2,1)}, bf16[2,512,256]{2,1,0:T(8,128)(2,1)S(1)}, u32[]{:S(2)}, u32[]{:S(2)}) collective-permute-start(bf16[2,512,256]{2,1,0:T(8,128)(2,1)} %get-tuple-element.326), channel_id=1, source_target_pairs={{0,2},{1,3},{2,0},{3,1},{4,6},{5,7},{6,4},{7,5},{8,10},{9,11},{10,... | collective-permute-start | bytes 1572872 | tf_op jit(solution)/shard_map/ppermute | solution.py:761
  449.2 56.4 %collective-permute-start.55 = (bf16[2,512,256]{2,1,0:T(8,128)(2,1)}, bf16[2,512,256]{2,1,0:T(8,128)(2,1)S(1)}, u32[]{:S(2)}, u32[]{:S(2)}) collective-permute-start(bf16[2,512,256]{2,1,0:T(8,128)(2,1)} %get-tuple-element.327), channel_id=1, source_target_pairs={{0,4},{1,5},{2,6},{3,7},{4,0},{5,1},{6,2},{7,3},{8,12},{9,13},{10,... | collective-permute-start | bytes 1572872 | tf_op jit(solution)/shard_map/ppermute | solution.py:761
  450.8 54.9 %collective-permute-start.56 = (bf16[2,512,256]{2,1,0:T(8,128)(2,1)S(1)}, bf16[2,512,256]{2,1,0:T(8,128)(2,1)S(1)}, u32[]{:S(2)}, u32[]{:S(2)}) collective-permute-start(bf16[2,512,256]{2,1,0:T(8,128)(2,1)S(1)} %copy-done.53), channel_id=1, source_target_pairs={{0,6},{1,7},{2,4},{3,5},{4,2},{5,3},{6,0},{7,1},{8,14},{9,15},{10,... | collective-permute-start | bytes 1572872 | tf_op jit(solution)/shard_map/ppermute | solution.py:761
  452.5 10.6 %collective-permute-start.49 = (bf16[4,16,2176]{2,1,0:T(8,128)(2,1)}, bf16[4,16,2176]{2,1,0:T(8,128)(2,1)S(1)}, u32[]{:S(2)}, u32[]{:S(2)}) collective-permute-start(bf16[4,16,2176]{2,1,0:T(8,128)(2,1)} %get-tuple-element.315), channel_id=1, source_target_pairs={{0,16},{1,17},{2,18},{3,19},{4,20},{5,21},{6,22},{7,23},{8,24},{9,... | collective-permute-start | bytes 835592 | tf_op jit(solution)/shard_map/ppermute | solution.py:761
  456.2 10.7 %collective-permute-start.50 = (bf16[4,16,2176]{2,1,0:T(8,128)(2,1)}, bf16[4,16,2176]{2,1,0:T(8,128)(2,1)S(1)}, u32[]{:S(2)}, u32[]{:S(2)}) collective-permute-start(bf16[4,16,2176]{2,1,0:T(8,128)(2,1)} %get-tuple-element.316), channel_id=1, source_target_pairs={{0,17},{1,16},{2,19},{3,18},{4,21},{5,20},{6,23},{7,22},{8,25},{9,... | collective-permute-start | bytes 835592 | tf_op jit(solution)/shard_map/ppermute | solution.py:761
  458.2 32.7 %copy-start.47 = (f32[16,5]{0,1:T(8,128)S(1)}, f32[16,5]{0,1:T(8,128)}, u32[]{:S(2)}) copy-start(f32[16,5]{0,1:T(8,128)} %param.45) | copy-start | bytes 964
  469.6 15.9 %collective-permute-start.51 = (bf16[1,16,2176]{2,1,0:T(8,128)(2,1)}, bf16[1,16,2176]{2,1,0:T(8,128)(2,1)S(1)}, u32[]{:S(2)}, u32[]{:S(2)}) collective-permute-start(bf16[1,16,2176]{2,1,0:T(8,128)(2,1)} %get-tuple-element.318), channel_id=1, source_target_pairs={{0,2},{1,3},{2,0},{3,1},{4,6},{5,7},{6,4},{7,5},{8,10},{9,11},{10,... | collective-permute-start | bytes 208904 | tf_op jit(solution)/shard_map/ppermute | solution.py:761
  469.8 32.9 %collective-permute-start.52 = (bf16[1,16,2176]{2,1,0:T(8,128)(2,1)}, bf16[1,16,2176]{2,1,0:T(8,128)(2,1)S(1)}, u32[]{:S(2)}, u32[]{:S(2)}) collective-permute-start(bf16[1,16,2176]{2,1,0:T(8,128)(2,1)} %get-tuple-element.319), channel_id=1, source_target_pairs={{0,4},{1,5},{2,6},{3,7},{4,0},{5,1},{6,2},{7,3},{8,12},{9,13},{10,... | collective-permute-start | bytes 208904 | tf_op jit(solution)/shard_map/ppermute | solution.py:761
  485.5 17.2 %collective-permute-start.53 = (bf16[1,16,2176]{2,1,0:T(8,128)(2,1)}, bf16[1,16,2176]{2,1,0:T(8,128)(2,1)S(1)}, u32[]{:S(2)}, u32[]{:S(2)}) collective-permute-start(bf16[1,16,2176]{2,1,0:T(8,128)(2,1)} %get-tuple-element.320), channel_id=1, source_target_pairs={{0,6},{1,7},{2,4},{3,5},{4,2},{5,3},{6,0},{7,1},{8,14},{9,15},{10,... | collective-permute-start | bytes 208904 | tf_op jit(solution)/shard_map/ppermute | solution.py:761
  511.7 1.4 collective-permute-start.57
  513.8 3.6 collective-permute-start.58
  517.4 3.6 collective-permute-start.59
  521.0 3.6 collective-permute-start.60
  524.6 4.6 collective-permute-start.61
  (59 other events, 511.0 us)

commit v6 on v5

--- a/solution.py
+++ b/solution.py
@@ -884,9 +884,9 @@
     out = jax.ShapeDtypeStruct((2, 4, rows, cols), BF)
     return pl.pallas_call(
         fold_cores_kernel,
-        grid=(4,),
-        in_specs=[pl.BlockSpec((2, 1, 2, rows, cols), lambda z: (0, z, 0, 0, 0))] * 4,
-        out_specs=[pl.BlockSpec((2, 1, rows, cols), lambda z: (0, z, 0, 0))] * 4,
+        grid=(4, 2),
+        in_specs=[pl.BlockSpec((2, 1, 2, rows // 2, cols), lambda z, r: (0, z, 0, r, 0))] * 4,
+        out_specs=[pl.BlockSpec((2, 1, rows // 2, cols), lambda z, r: (0, z, r, 0))] * 4,
         out_shape=[out] * 4,
         compiler_params=params(),
         cost_estimate=cost(7),

time: 548 us -> 551 us (level)
  transfers between devices with their start and end apart: 62 -> 62, of which waited for: 20 -> 18; matrix products, arithmetic and copies ran while one was open for 5% -> 5% of each run, Pallas kernels for 57% -> 57%
where the time goes in v6:
time: 551 us; the launch traced here: 542 us
  Pallas kernels  337 us (61%)
  waiting for transfers between devices  78.9 us (14%)
  starting transfers between devices  77 us (14%)
  local copies, waits for them, and re-layouts  38 us (7%)
  other arithmetic  9.74 us (2%)
    pallas_call x4, Pallas kernels, expert_pass(): pl.pallas_call(kernel, grid_spec=pltpu.PrefetchScalarGridSpec(num_scalar_...  96.8 us
    ppermute x62, waiting for transfers between devices, swap(): return lax.ppermute(array, AXES, [(d, d ^ bits) for d in range(devices)])  78.9 us
    ppermute x62, starting transfers between devices, swap(): return lax.ppermute(array, AXES, [(d, d ^ bits) for d in range(devices)])  77 us
    pallas_call x1, Pallas kernels, combine(): pl.pallas_call(behind(combine_kernel, 11, after), grid_spec=pltpu.Prefetc...  50.1 us
    pallas_call x1, Pallas kernels, attention_back(): pl.pallas_call(behind(attention_back_kernel, 10, after), grid_spec=pltpu....  40.9 us
    pallas_call x1, Pallas kernels, attention(): pl.pallas_call(behind(attention_kernel, 6, after), grid=(images,), in_spe...  28.1 us
    pallas_call x1, Pallas kernels, gather(): pl.pallas_call(behind(gather_kernel, 5, after), grid_spec=pltpu.PrefetchS...  27.6 us
    unnamed x138, local copies, waits for them, and re-layouts  24.9 us
  transfers between devices with their start and end apart: 62, of which 18 were waited for; matrix products, arithmetic and copies ran while one was open for 5% of the time, Pallas kernels for 57%

profile of v6, /device:TPU:0, one launch (start us, length us, event | category | flops | bytes accessed | tf_op | source)
XLA Modules:
  0.0 542.0 jit_solution(11599977457777667561)
XLA Ops:
  5.5 3.1 collective-permute-start
  8.6 2.6 collective-permute-start.1
  11.2 1.4 copy.182
  14.9 4.6 spread_rows.1
  21.4 1.9 stack.34.refs_0_
  23.4 1.7 collective-permute-start.3
  25.1 1.5 collective-permute-start.4
  29.8 9.5 %places.1 = (f32[10,8,208]{2,1,0:T(8,128)}, f32[2080,8]{1,0:T(8,128)}, s32[20,8]{1,0:T(8,128)}) custom-call(f32[8,2080]{1,0:T(8,128)} %pad.32.clone.rows_ref, f32[2080,8]{1,0:T(8,128)} %pad_bitcast_fusion.cols_ref), custom_call_target="tpu_custom_call" | custom-call | flops 2000000000 | bytes 200000 | tf_op jit(solution)/shard_map/places/pallas_call | solution.py:220
  40.4 2.3 stack.35
  43.3 3.5 collective-permute-start.8
  47.8 3.9 assemble.1
  51.7 28.1 %attention.1 = (bf16[2080,1536]{1,0:T(8,128)(2,1)}, bf16[10,8,208,208]{3,2,1,0:T(8,128)(2,1)}, bf16[2080,512]{1,0:T(8,128)(2,1)}, f32[2080,512]{1,0:T(8,128)}, b...) custom-call(bf16[2080,512]{1,0:T(8,128)(2,1)} %get-tuple-element.200.refs_4_.refs_0_.refs_5_, ...), custom_call_target="tpu_custom_call" | custom-call | flops 8000000000 | bytes 800000 | tf_op jit(solution)/shard_map/attention/pallas_call | solution.py:314
  79.8 1.8 collective-permute-done.8.refs_2_
  82.6 3.1 turn_stack.2.refs_5_.refs_9_
  85.6 1.7 collective-permute-start.10
  87.3 1.5 collective-permute-start.11
  88.9 11.7 %collective-permute-start.12 = (bf16[2,512,256]{2,1,0:T(8,128)(2,1)S(1)}, bf16[2,512,256]{2,1,0:T(8,128)(2,1)S(1)}, u32[]{:S(2)}, u32[]{:S(2)}) collective-permute-start(bf16[2,512,256]{2,1,0:T(8,128)(2,1)S(1)} %pad_maximum_fusion.1.refs_0_), channel_id=1, source_target_pairs={{0,2},{1,3},{2,0},{3,1},{4,6},{5,7},{6,4},{7,5},{8,10},{9,11},{10,... | collective-permute-start | bytes 1572872 | tf_op jit(solution)/shard_map/ppermute | solution.py:761
  103.0 27.6 %gather.1 = (bf16[8,624,512]{2,1,0:T(8,128)(2,1)}, bf16[8,624,512]{2,1,0:T(8,128)(2,1)}, bf16[8,512,624]{2,1,0:T(8,128)(2,1)}, bf16[8,512,624]{2,1,0:T(8,128)(2,1)}) custom-call(s32[20,8]{1,0:T(8,128)} %get-tuple-element.199.refs_0_, bf16[2080,512]{1,0:T(8,128)(2,1)} %get-tuple-element.208.refs_1_, bf16[2080,512]{1,0:T(8,128)(2,1)} %get-tuple-element.209.refs_2_.refs_6_, ...), custom_call_target="tpu_custom_call" | custom-call | flops 8000000000 | bytes 800000 | tf_op jit(solution)/shard_map/gather/pallas_call | solution.py:378
  130.6 8.2 %collective-permute-done.13.refs_2_ = bf16[2,512,256]{2,1,0:T(8,128)(2,1)S(1)} collective-permute-done((bf16[2,512,256]{2,1,0:T(8,128)(2,1)S(1)}, bf16[2,512,256]{2,1,0:T(8,128)(2,1)S(1)}, u32[]{:S(2)}, u32[]{:S(2)}) %collective-permute-start.13) | collective-permute-done | bytes 524320 | tf_op jit(solution)/shard_map/ppermute | solution.py:761
  139.8 3.0 turn_stack.3.refs_2_.refs_5_.refs_9_
  142.7 4.1 pick.1
  150.4 2.5 collective-permute-done.16.refs_8_
  155.4 23.7 %experts_00.1 = (f32[8,624,512]{2,1,0:T(8,128)}, f32[8,624,512]{2,1,0:T(8,128)}, bf16[2,4,2,512,256]{4,3,2,1,0:T(8,128)(2,1)}, bf16[2,4,2,512,256]{4,3,2,1,0:T(8...) custom-call(s32[10]{0:T(128)} %pad_add_fusion.refs_0_, bf16[8,624,512]{2,1,0:T(8,128)(2,1)} %get-tuple-element.213.refs_4_.refs_1_, ...), custom_call_target="tpu_custom_call" | custom-call | flops 4000000000 | bytes 400000 | tf_op jit(solution)/shard_map/experts_00/pallas_call | solution.py:516
  179.8 6.2 %collective-permute-done.21.refs_8_ = bf16[1,4,512,256]{3,2,1,0:T(8,128)(2,1)S(1)} collective-permute-done((bf16[1,4,512,256]{3,2,1,0:T(8,128)(2,1)S(1)}, bf16[1,4,512,256]{3,2,1,0:T(8,128)(2,1)S(1)}, u32[]{:S(2)}, u32[]{:S(2)}) %collective-permute-start.21) | collective-permute-done | bytes 1048608 | tf_op jit(solution)/shard_map/ppermute | solution.py:761
  187.3 24.6 %experts_01.1 = (f32[8,624,512]{2,1,0:T(8,128)}, f32[8,624,512]{2,1,0:T(8,128)}, bf16[2,4,2,512,256]{4,3,2,1,0:T(8,128)(2,1)}, bf16[2,4,2,512,256]{4,3,2,1,0:T(8...) custom-call(s32[10]{0:T(128)} %pad_add_fusion.refs_0_, ...), custom_call_target="tpu_custom_call", output_to_operand_aliasing={{0}: (14, {}), {1}: (15, {})} | custom-call | flops 4000000000 | bytes 400000 | tf_op jit(solution)/shard_map/experts_01/pallas_call | solution.py:516
  211.9 11.4 %collective-permute-done.24.refs_7_.refs_11_ = bf16[2,4,512,256]{3,2,1,0:T(8,128)(2,1)} collective-permute-done((bf16[2,4,512,256]{3,2,1,0:T(8,128)(2,1)S(1)}, bf16[2,4,512,256]{3,2,1,0:T(8,128)(2,1)}, u32[]{:S(2)}, u32[]{:S(2)}) %collective-permute-start.24) | collective-permute-done | bytes 2097184 | tf_op jit(solution)/shard_map/ppermute | solution.py:761
  223.8 2.3 slice.58
  226.6 2.3 slice.59
  229.2 1.6 collective-permute-done.27.g1
  230.8 10.7 %fold_cores.2 = (bf16[2,4,512,256]{3,2,1,0:T(8,128)(2,1)}, bf16[2,4,512,256]{3,2,1,0:T(8,128)(2,1)}, bf16[2,4,512,256]{3,2,1,0:T(8,128)(2,1)}, bf16[2,4,512,256]{3,2,1,0:T(8,128)(2,1)}) custom-call(bf16[2,4,2,512,256]{4,3,2,1,0:T(8,128)(2,1)} %get-tuple-element.223.n0, bf16[2,4,2,512,256]{4,3,2,1,0:T(8,128)(2,1)} %get-tuple-element.230.n1, ...), custom_call_target="tpu_custom_call" | custom-call | flops 7000000000 | bytes 700000 | tf_op jit(solution)/shard_map/fold_cores/pallas_call | solution.py:885
  243.8 23.3 %experts_10.1 = (bf16[8,624,512]{2,1,0:T(8,128)(2,1)}, bf16[8,624,512]{2,1,0:T(8,128)(2,1)}, bf16[2,4,2,512,256]{4,3,2,1,0:T(8,128)(2,1)}, bf16[2,4,2,512,256]{4,3,2,1,0:T(8,128)(2,1)}, f32[8,4,256]{2,1,0:T(4,128)}) custom-call(s32[10]{0:T(128)} %pad_add_fusion.refs_0_, bf16[8,624,512]{2,1,0:T(8,128)(2,1)} %get-tuple-element.213.refs_4_.refs_1_, ...), custom_call_target="tpu_custom_call" | custom-call | flops 4000000000 | bytes 400000 | tf_op jit(solution)/shard_map/experts_10/pallas_call | solution.py:516
  267.8 2.9 collective-permute-done.32.refs_8_
  273.9 25.2 %experts_11.1 = (bf16[8,624,512]{2,1,0:T(8,128)(2,1)}, bf16[8,624,512]{2,1,0:T(8,128)(2,1)}, bf16[2,4,2,512,256]{4,3,2,1,0:T(8,128)(2,1)}, bf16[2,4,2,512,256]{4,3,2,1,0:T(8,128)(2,1)}, f32[8,4,256]{2,1,0:T(4,128)}) custom-call(s32[10]{0:T(128)} %pad_add_fusion.refs_0_, ...), custom_call_target="tpu_custom_call", output_to_operand_aliasing={{0}: (17, {}), {1}: (18, {})} | custom-call | flops 4000000000 | bytes 400000 | tf_op jit(solution)/shard_map/experts_11/pallas_call | solution.py:516
  299.5 5.7 %fold_first.2 = (bf16[4,512,256]{2,1,0:T(8,128)(2,1)}, bf16[4,512,256]{2,1,0:T(8,128)(2,1)}, bf16[4,512,256]{2,1,0:T(8,128)(2,1)}, bf16[4,512,256]{2,1,0:T(8,128)(2,1)}) custom-call(bf16[2,4,512,256]{3,2,1,0:T(8,128)(2,1)} %get-tuple-element.255.refs_0_, bf16[2,4,512,256]{3,2,1,0:T(8,128)(2,1)} %get-tuple-element.256.refs_1_, ...), custom_call_target="tpu_custom_call" | custom-call | flops 4000000000 | bytes 400000 | tf_op jit(solution)/shard_map/fold_first/pallas_call | solution.py:906
  306.2 1.5 collective-permute-start.39
  307.9 10.7 %fold_cores.3 = (bf16[2,4,512,256]{3,2,1,0:T(8,128)(2,1)}, bf16[2,4,512,256]{3,2,1,0:T(8,128)(2,1)}, bf16[2,4,512,256]{3,2,1,0:T(8,128)(2,1)}, bf16[2,4,512,256]{3,2,1,0:T(8,128)(2,1)}) custom-call(bf16[2,4,2,512,256]{4,3,2,1,0:T(8,128)(2,1)} %get-tuple-element.264.n0, bf16[2,4,2,512,256]{4,3,2,1,0:T(8,128)(2,1)} %get-tuple-element.265.n1, ...), custom_call_target="tpu_custom_call" | custom-call | flops 7000000000 | bytes 700000 | tf_op jit(solution)/shard_map/fold_cores/pallas_call | solution.py:885
  320.2 50.1 %combine.1 = (f32[1970,512]{1,0:T(8,128)}, f32[2080,512]{1,0:T(8,128)}, bf16[2080,512]{1,0:T(8,128)(2,1)}, f32[512,512]{1,0:T(8,128)}, f32[8,512]{1,0:T(8,128)}, /*index=5*/f32[8,512]{1,0:T(8,128)}) custom-call(s32[20,8]{1,0:T(8,128)} %get-tuple-element.199.refs_0_, bf16[8,624,512]{2,1,0:T(8,128)(2,1)} %get-tuple-element.250.refs_1_, ...), custom_call_target="tpu_custom_call" | custom-call | flops 40000000000 | bytes 4000000 | tf_op jit(solution)/shard_map/combine/pallas_call | solution.py:616
  373.1 3.5 fold_second.2
  376.7 10.1 %collective-permute-start.42 = (bf16[2,512,256]{2,1,0:T(8,128)(2,1)}, bf16[2,512,256]{2,1,0:T(8,128)(2,1)S(1)}, u32[]{:S(2)}, u32[]{:S(2)}) collective-permute-start(bf16[2,512,256]{2,1,0:T(8,128)(2,1)} %get-tuple-element.287.refs_10_), channel_id=1, source_target_pairs={{0,2},{1,3},{2,0},{3,1},{4,6},{5,7},{6,4},{7,5},{8,10},{9,11},{10,... | collective-permute-start | bytes 1572872 | tf_op jit(solution)/shard_map/ppermute | solution.py:761
  386.7 1.8 collective-permute-start.43
  388.5 1.5 collective-permute-start.44
  390.0 5.7 %fold_first.3 = (bf16[4,512,256]{2,1,0:T(8,128)(2,1)}, bf16[4,512,256]{2,1,0:T(8,128)(2,1)}, bf16[4,512,256]{2,1,0:T(8,128)(2,1)}, bf16[4,512,256]{2,1,0:T(8,128)(2,1)}) custom-call(bf16[2,4,512,256]{3,2,1,0:T(8,128)(2,1)} %get-tuple-element.290.refs_0_, bf16[2,4,512,256]{3,2,1,0:T(8,128)(2,1)} %get-tuple-element.291.refs_1_, ...), custom_call_target="tpu_custom_call" | custom-call | flops 4000000000 | bytes 400000 | tf_op jit(solution)/shard_map/fold_first/pallas_call | solution.py:906
  397.8 40.9 %attention_back.1 = (f32[1970,512]{1,0:T(8,128)}, bf16[16,16,2176]{2,1,0:T(8,128)(2,1)}, bf16[16,16,2176]{2,1,0:T(8,128)(2,1)}) custom-call(s32[32]{0:T(128)} %broadcast_xor_fusion.place_ref.refs_0_, bf16[2080,1536]{1,0:T(8,128)(2,1)} %get-tuple-element.271.refs_1_, bf16[10,8,208,208]{3,2,1,0:T(8,128)(2,1)} %get-tuple-element.272.refs_2_, ...), custom_call_target="tpu_custom_call" | custom-call | flops 49999998976 | bytes 5000000 | tf_op jit(solution)/shard_map/attention_back/pallas_call | solution.py:727
  440.2 3.5 fold_second.3
  443.8 3.0 collective-permute-done.47.refs_1_
  447.8 2.7 block_sum.2
  452.6 2.0 collective-permute-start.55
  454.6 1.5 collective-permute-start.56
  456.8 2.5 collective-permute-done.48.refs_1_
  459.3 1.7 collective-permute-start.50
  461.6 4.8 expert_update_0.1
  466.5 3.8 collective-permute-done.50.refs_3_
  471.0 2.0 block_sum.3
  472.9 2.9 collective-permute-start.52
  475.8 13.0 %collective-permute-done.51.refs_1_ = bf16[1,16,2176]{2,1,0:T(8,128)(2,1)S(1)} collective-permute-done((bf16[1,16,2176]{2,1,0:T(8,128)(2,1)}, bf16[1,16,2176]{2,1,0:T(8,128)(2,1)S(1)}, u32[]{:S(2)}, u32[]{:S(2)}) %collective-permute-start.51) | collective-permute-done | bytes 69664 | tf_op jit(solution)/shard_map/ppermute | solution.py:761
  488.9 2.6 collective-permute-start.53
  495.5 10.5 %collective-permute-done.52.refs_2_ = bf16[1,16,2176]{2,1,0:T(8,128)(2,1)S(1)} collective-permute-done((bf16[1,16,2176]{2,1,0:T(8,128)(2,1)}, bf16[1,16,2176]{2,1,0:T(8,128)(2,1)S(1)}, u32[]{:S(2)}, u32[]{:S(2)}) %collective-permute-start.52) | collective-permute-done | bytes 69664 | tf_op jit(solution)/shard_map/ppermute | solution.py:761
  506.7 2.2 dense_update.1
  510.1 5.0 expert_update_1.1
  517.7 3.1 collective-permute-done.58
  521.4 2.9 collective-permute-done.59
  525.7 2.3 collective-permute-done.60
  528.0 2.4 collective-permute-start.61
  533.7 4.1 new_weights.1
  (282 shorter events, 66.9 us)
Async XLA Ops:
  5.5 16.0 %collective-permute-start = (bf16[16,2304]{1,0:T(8,128)(2,1)S(1)}, bf16[16,2304]{1,0:T(8,128)(2,1)}, u32[]{:S(2)}, u32[]{:S(2)}) collective-permute-start(bf16[16,2304]{1,0:T(8,128)(2,1)S(1)} %pad_maximum_fusion.2.refs_0_), channel_id=1, source_target_pairs={{0,2},{1,3},{2,0},{3,1},{4,6},{5,7},{6,4},{7,5},{8,10},{9,11},{10,... | collective-permute-start | bytes 221192 | tf_op jit(solution)/shard_map/ppermute | solution.py:761
  8.6 12.9 %collective-permute-start.1 = (bf16[16,2304]{1,0:T(8,128)(2,1)S(1)}, bf16[16,2304]{1,0:T(8,128)(2,1)}, u32[]{:S(2)}, u32[]{:S(2)}) collective-permute-start(bf16[16,2304]{1,0:T(8,128)(2,1)S(1)} %pad_maximum_fusion.2.refs_0_), channel_id=1, source_target_pairs={{0,4},{1,5},{2,6},{3,7},{4,0},{5,1},{6,2},{7,3},{8,12},{9,13},{10,... | collective-permute-start | bytes 221192 | tf_op jit(solution)/shard_map/ppermute | solution.py:761
  11.2 10.3 %collective-permute-start.2 = (bf16[16,2304]{1,0:T(8,128)(2,1)S(1)}, bf16[16,2304]{1,0:T(8,128)(2,1)}, u32[]{:S(2)}, u32[]{:S(2)}) collective-permute-start(bf16[16,2304]{1,0:T(8,128)(2,1)S(1)} %pad_maximum_fusion.2.refs_0_), channel_id=1, source_target_pairs={{0,6},{1,7},{2,4},{3,5},{4,2},{5,3},{6,0},{7,1},{8,14},{9,15},{10,... | collective-permute-start | bytes 221192 | tf_op jit(solution)/shard_map/ppermute | solution.py:761
  23.4 16.0 %collective-permute-start.3 = (bf16[4,16,2304]{2,1,0:T(8,128)(2,1)}, bf16[4,16,2304]{2,1,0:T(8,128)(2,1)S(1)}, u32[]{:S(2)}, u32[]{:S(2)}) collective-permute-start(bf16[4,16,2304]{2,1,0:T(8,128)(2,1)} %stack.34.refs_0_), channel_id=1, source_target_pairs={{0,1},{1,0},{2,3},{3,2},{4,5},{5,4},{6,7},{7,6},{8,9},{9,8},{10,11... | collective-permute-start | bytes 884744 | tf_op jit(solution)/shard_map/ppermute | solution.py:761
  25.1 14.3 %collective-permute-start.4 = (bf16[4,16,2304]{2,1,0:T(8,128)(2,1)}, bf16[4,16,2304]{2,1,0:T(8,128)(2,1)S(1)}, u32[]{:S(2)}, u32[]{:S(2)}) collective-permute-start(bf16[4,16,2304]{2,1,0:T(8,128)(2,1)} %stack.34.refs_0_), channel_id=1, source_target_pairs={{0,16},{1,17},{2,18},{3,19},{4,20},{5,21},{6,22},{7,23},{8,24},{9,... | collective-permute-start | bytes 884744 | tf_op jit(solution)/shard_map/ppermute | solution.py:761
  26.6 12.8 %collective-permute-start.5 = (bf16[4,16,2304]{2,1,0:T(8,128)(2,1)}, bf16[4,16,2304]{2,1,0:T(8,128)(2,1)S(1)}, u32[]{:S(2)}, u32[]{:S(2)}) collective-permute-start(bf16[4,16,2304]{2,1,0:T(8,128)(2,1)} %stack.34.refs_0_), channel_id=1, source_target_pairs={{0,17},{1,16},{2,19},{3,18},{4,21},{5,20},{6,23},{7,22},{8,25},{9,... | collective-permute-start | bytes 884744 | tf_op jit(solution)/shard_map/ppermute | solution.py:761
  26.8 12.6 %collective-permute-start.6 = (bf16[2,512,256]{2,1,0:T(8,128)(2,1)S(1)}, bf16[2,512,256]{2,1,0:T(8,128)(2,1)S(1)}, u32[]{:S(2)}, u32[]{:S(2)}) collective-permute-start(bf16[2,512,256]{2,1,0:T(8,128)(2,1)S(1)} %pad_maximum_fusion.refs_0_), channel_id=1, source_target_pairs={{0,2},{1,3},{2,0},{3,1},{4,6},{5,7},{6,4},{7,5},{8,10},{9,11},{10,... | collective-permute-start | bytes 1572872 | tf_op jit(solution)/shard_map/ppermute | solution.py:761
  42.8 4.0 collective-permute-start.7
  43.3 38.3 %collective-permute-start.8 = (bf16[2,512,256]{2,1,0:T(8,128)(2,1)S(1)}, bf16[2,512,256]{2,1,0:T(8,128)(2,1)S(1)}, u32[]{:S(2)}, u32[]{:S(2)}) collective-permute-start(bf16[2,512,256]{2,1,0:T(8,128)(2,1)S(1)} %pad_maximum_fusion.refs_0_), channel_id=1, source_target_pairs={{0,4},{1,5},{2,6},{3,7},{4,0},{5,1},{6,2},{7,3},{8,12},{9,13},{10,... | collective-permute-start | bytes 1572872 | tf_op jit(solution)/shard_map/ppermute | solution.py:761
  46.8 34.8 %collective-permute-start.9 = (bf16[2,512,256]{2,1,0:T(8,128)(2,1)S(1)}, bf16[2,512,256]{2,1,0:T(8,128)(2,1)S(1)}, u32[]{:S(2)}, u32[]{:S(2)}) collective-permute-start(bf16[2,512,256]{2,1,0:T(8,128)(2,1)S(1)} %pad_maximum_fusion.refs_0_), channel_id=1, source_target_pairs={{0,6},{1,7},{2,4},{3,5},{4,2},{5,3},{6,0},{7,1},{8,14},{9,15},{10,... | collective-permute-start | bytes 1572872 | tf_op jit(solution)/shard_map/ppermute | solution.py:761
  85.6 57.1 %collective-permute-start.10 = (bf16[2,4,512,256]{3,2,1,0:T(8,128)(2,1)}, bf16[2,4,512,256]{3,2,1,0:T(8,128)(2,1)}, u32[]{:S(2)}, u32[]{:S(2)}) collective-permute-start(bf16[2,4,512,256]{3,2,1,0:T(8,128)(2,1)} %turn_stack.2.refs_5_.refs_9_), channel_id=1, source_target_pairs={{0,16},{1,17},{2,18},{3,19},{4,20},{5,21},{6,22},{7,23},{8,24},{9,... | collective-permute-start | bytes 6291464 | tf_op jit(solution)/shard_map/ppermute | solution.py:761
  87.3 55.5 %collective-permute-start.11 = (bf16[2,4,512,256]{3,2,1,0:T(8,128)(2,1)}, bf16[2,4,512,256]{3,2,1,0:T(8,128)(2,1)}, u32[]{:S(2)}, u32[]{:S(2)}) collective-permute-start(bf16[2,4,512,256]{3,2,1,0:T(8,128)(2,1)} %turn_stack.2.refs_5_.refs_9_), channel_id=1, source_target_pairs={{0,1},{1,0},{2,3},{3,2},{4,5},{5,4},{6,7},{7,6},{8,9},{9,8},{10,11... | collective-permute-start | bytes 6291464 | tf_op jit(solution)/shard_map/ppermute | solution.py:761
  88.9 41.8 %copy-start.4 = (bf16[2,512,256]{2,1,0:T(8,128)(2,1)}, bf16[2,512,256]{2,1,0:T(8,128)(2,1)S(1)}, u32[]{:S(2)}) copy-start(bf16[2,512,256]{2,1,0:T(8,128)(2,1)S(1)} %pad_maximum_fusion.1.refs_0_) | copy-start | bytes 1572868
  88.9 41.7 %collective-permute-start.12 = (bf16[2,512,256]{2,1,0:T(8,128)(2,1)S(1)}, bf16[2,512,256]{2,1,0:T(8,128)(2,1)S(1)}, u32[]{:S(2)}, u32[]{:S(2)}) collective-permute-start(bf16[2,512,256]{2,1,0:T(8,128)(2,1)S(1)} %pad_maximum_fusion.1.refs_0_), channel_id=1, source_target_pairs={{0,2},{1,3},{2,0},{3,1},{4,6},{5,7},{6,4},{7,5},{8,10},{9,11},{10,... | collective-permute-start | bytes 1572872 | tf_op jit(solution)/shard_map/ppermute | solution.py:761
  100.6 38.2 %collective-permute-start.13 = (bf16[2,512,256]{2,1,0:T(8,128)(2,1)S(1)}, bf16[2,512,256]{2,1,0:T(8,128)(2,1)S(1)}, u32[]{:S(2)}, u32[]{:S(2)}) collective-permute-start(bf16[2,512,256]{2,1,0:T(8,128)(2,1)S(1)} %pad_maximum_fusion.1.refs_0_), channel_id=1, source_target_pairs={{0,4},{1,5},{2,6},{3,7},{4,0},{5,1},{6,2},{7,3},{8,12},{9,13},{10,... | collective-permute-start | bytes 1572872 | tf_op jit(solution)/shard_map/ppermute | solution.py:761
  101.6 37.2 %collective-permute-start.14 = (bf16[2,512,256]{2,1,0:T(8,128)(2,1)S(1)}, bf16[2,512,256]{2,1,0:T(8,128)(2,1)S(1)}, u32[]{:S(2)}, u32[]{:S(2)}) collective-permute-start(bf16[2,512,256]{2,1,0:T(8,128)(2,1)S(1)} %pad_maximum_fusion.1.refs_0_), channel_id=1, source_target_pairs={{0,6},{1,7},{2,4},{3,5},{4,2},{5,3},{6,0},{7,1},{8,14},{9,15},{10,... | collective-permute-start | bytes 1572872 | tf_op jit(solution)/shard_map/ppermute | solution.py:761
  146.8 8.0 %collective-permute-start.15 = (bf16[2,4,512,256]{3,2,1,0:T(8,128)(2,1)}, bf16[2,4,512,256]{3,2,1,0:T(8,128)(2,1)}, u32[]{:S(2)}, u32[]{:S(2)}) collective-permute-start(bf16[2,4,512,256]{3,2,1,0:T(8,128)(2,1)} %turn_stack.2.refs_5_.refs_9_), channel_id=1, source_target_pairs={{0,8},{1,9},{2,10},{3,11},{4,12},{5,13},{6,14},{7,15},{8,0},{9,1},... | collective-permute-start | bytes 6291464 | tf_op jit(solution)/shard_map/ppermute | solution.py:761
  146.9 6.0 %collective-permute-start.16 = (bf16[1,4,512,256]{3,2,1,0:T(8,128)(2,1)}, bf16[1,4,512,256]{3,2,1,0:T(8,128)(2,1)}, u32[]{:S(2)}, u32[]{:S(2)}) collective-permute-start(bf16[1,4,512,256]{3,2,1,0:T(8,128)(2,1)} %get-tuple-element.220), channel_id=1, source_target_pairs={{0,8},{1,9},{2,10},{3,11},{4,12},{5,13},{6,14},{7,15},{8,0},{9,1},... | collective-permute-start | bytes 3145736 | tf_op jit(solution)/shard_map/ppermute | solution.py:761
  147.4 7.0 %collective-permute-start.17 = (bf16[1,4,512,256]{3,2,1,0:T(8,128)(2,1)}, bf16[1,4,512,256]{3,2,1,0:T(8,128)(2,1)}, u32[]{:S(2)}, u32[]{:S(2)}) collective-permute-start(bf16[1,4,512,256]{3,2,1,0:T(8,128)(2,1)} %get-tuple-element.221), channel_id=1, source_target_pairs={{0,8},{1,9},{2,10},{3,11},{4,12},{5,13},{6,14},{7,15},{8,0},{9,1},... | collective-permute-start | bytes 3145736 | tf_op jit(solution)/shard_map/ppermute | solution.py:761
  147.4 32.3 %collective-permute-start.18 = (bf16[2,4,512,256]{3,2,1,0:T(8,128)(2,1)}, bf16[2,4,512,256]{3,2,1,0:T(8,128)(2,1)}, u32[]{:S(2)}, u32[]{:S(2)}) collective-permute-start(bf16[2,4,512,256]{3,2,1,0:T(8,128)(2,1)} %collective-permute-done.11.refs_1_.refs_5_.refs_9_), channel_id=1, source_target_pairs={{0,8},{1,9},{2,10},{3,11},{4,12},{5,13},{6,14},{7,15},{8,0},{9,1},... | collective-permute-start | bytes 6291464 | tf_op jit(solution)/shard_map/ppermute | solution.py:761
  147.9 31.2 %collective-permute-start.19 = (bf16[1,4,512,256]{3,2,1,0:T(8,128)(2,1)}, bf16[1,4,512,256]{3,2,1,0:T(8,128)(2,1)S(1)}, u32[]{:S(2)}, u32[]{:S(2)}) collective-permute-start(bf16[1,4,512,256]{3,2,1,0:T(8,128)(2,1)} %get-tuple-element.220), channel_id=1, source_target_pairs={{0,1},{1,0},{2,3},{3,2},{4,5},{5,4},{6,7},{7,6},{8,9},{9,8},{10,11... | collective-permute-start | bytes 3145736 | tf_op jit(solution)/shard_map/ppermute | solution.py:761
  152.8 26.4 %collective-permute-start.20 = (bf16[1,4,512,256]{3,2,1,0:T(8,128)(2,1)}, bf16[1,4,512,256]{3,2,1,0:T(8,128)(2,1)}, u32[]{:S(2)}, u32[]{:S(2)}) collective-permute-start(bf16[1,4,512,256]{3,2,1,0:T(8,128)(2,1)} %get-tuple-element.225), channel_id=1, source_target_pairs={{0,16},{1,17},{2,18},{3,19},{4,20},{5,21},{6,22},{7,23},{8,24},{9,... | collective-permute-start | bytes 3145736 | tf_op jit(solution)/shard_map/ppermute | solution.py:761
  154.4 69.0 %collective-permute-start.24 = (bf16[2,4,512,256]{3,2,1,0:T(8,128)(2,1)S(1)}, bf16[2,4,512,256]{3,2,1,0:T(8,128)(2,1)}, u32[]{:S(2)}, u32[]{:S(2)}) collective-permute-start(bf16[2,4,512,256]{3,2,1,0:T(8,128)(2,1)S(1)} %copy-done), channel_id=1, source_target_pairs={{0,16},{1,17},{2,18},{3,19},{4,20},{5,21},{6,22},{7,23},{8,24},{9,... | collective-permute-start | bytes 6291464 | tf_op jit(solution)/shard_map/ppermute | solution.py:761
  154.9 68.4 %collective-permute-start.25 = (bf16[2,4,512,256]{3,2,1,0:T(8,128)(2,1)S(1)}, bf16[2,4,512,256]{3,2,1,0:T(8,128)(2,1)}, u32[]{:S(2)}, u32[]{:S(2)}) collective-permute-start(bf16[2,4,512,256]{3,2,1,0:T(8,128)(2,1)S(1)} %copy-done), channel_id=1, source_target_pairs={{0,1},{1,0},{2,3},{3,2},{4,5},{5,4},{6,7},{7,6},{8,9},{9,8},{10,11... | collective-permute-start | bytes 6291464 | tf_op jit(solution)/shard_map/ppermute | solution.py:761
  179.1 44.2 %collective-permute-start.26 = (bf16[2,4,512,256]{3,2,1,0:T(8,128)(2,1)S(1)}, bf16[2,4,512,256]{3,2,1,0:T(8,128)(2,1)}, u32[]{:S(2)}, u32[]{:S(2)}) collective-permute-start(bf16[2,4,512,256]{3,2,1,0:T(8,128)(2,1)S(1)} %copy-done), channel_id=1, source_target_pairs={{0,8},{1,9},{2,10},{3,11},{4,12},{5,13},{6,14},{7,15},{8,0},{9,1},... | collective-permute-start | bytes 6291464 | tf_op jit(solution)/shard_map/ppermute | solution.py:761
  179.2 6.8 %collective-permute-start.21 = (bf16[1,4,512,256]{3,2,1,0:T(8,128)(2,1)S(1)}, bf16[1,4,512,256]{3,2,1,0:T(8,128)(2,1)S(1)}, u32[]{:S(2)}, u32[]{:S(2)}) collective-permute-start(bf16[1,4,512,256]{3,2,1,0:T(8,128)(2,1)S(1)} %collective-permute-done.19.refs_7_), channel_id=1, source_target_pairs={{0,8},{1,9},{2,10},{3,11},{4,12},{5,13},{6,14},{7,15},{8,0},{9,1},... | collective-permute-start | bytes 3145736 | tf_op jit(solution)/shard_map/ppermute | solution.py:761
  179.7 7.6 %collective-permute-start.22 = (bf16[1,4,512,256]{3,2,1,0:T(8,128)(2,1)}, bf16[1,4,512,256]{3,2,1,0:T(8,128)(2,1)}, u32[]{:S(2)}, u32[]{:S(2)}) collective-permute-start(bf16[1,4,512,256]{3,2,1,0:T(8,128)(2,1)} %collective-permute-done.20.refs_11_), channel_id=1, source_target_pairs={{0,8},{1,9},{2,10},{3,11},{4,12},{5,13},{6,14},{7,15},{8,0},{9,1},... | collective-permute-start | bytes 3145736 | tf_op jit(solution)/shard_map/ppermute | solution.py:761
  187.0 42.3 %collective-permute-start.23 = (bf16[2,4,2,512,256]{4,3,2,1,0:T(8,128)(2,1)}, bf16[2,4,2,512,256]{4,3,2,1,0:T(8,128)(2,1)}, u32[]{:S(2)}, u32[]{:S(2)}) collective-permute-start(bf16[2,4,2,512,256]{4,3,2,1,0:T(8,128)(2,1)} %get-tuple-element.231), channel_id=1, source_target_pairs={{0,8},{1,9},{2,10},{3,11},{4,12},{5,13},{6,14},{7,15},{8,0},{9,1},... | collective-permute-start | bytes 12582920 | tf_op jit(solution)/shard_map/ppermute | solution.py:761
  223.3 7.5 %collective-permute-start.27 = (bf16[2,4,2,512,256]{4,3,2,1,0:T(8,128)(2,1)}, bf16[2,4,2,512,256]{4,3,2,1,0:T(8,128)(2,1)}, u32[]{:S(2)}, u32[]{:S(2)}) collective-permute-start(bf16[2,4,2,512,256]{4,3,2,1,0:T(8,128)(2,1)} %get-tuple-element.235), channel_id=1, source_target_pairs={{0,8},{1,9},{2,10},{3,11},{4,12},{5,13},{6,14},{7,15},{8,0},{9,1},... | collective-permute-start | bytes 12582920 | tf_op jit(solution)/shard_map/ppermute | solution.py:761
  223.3 18.8 %collective-permute-start.29 = (bf16[2,4,512,256]{3,2,1,0:T(8,128)(2,1)}, bf16[2,4,512,256]{3,2,1,0:T(8,128)(2,1)}, u32[]{:S(2)}, u32[]{:S(2)}) collective-permute-start(bf16[2,4,512,256]{3,2,1,0:T(8,128)(2,1)} %collective-permute-done.24.refs_7_.refs_11_), channel_id=1, source_target_pairs={{0,8},{1,9},{2,10},{3,11},{4,12},{5,13},{6,14},{7,15},{8,0},{9,1},... | collective-permute-start | bytes 6291464 | tf_op jit(solution)/shard_map/ppermute | solution.py:761
  226.1 41.1 %collective-permute-start.30 = (bf16[1,4,512,256]{3,2,1,0:T(8,128)(2,1)}, bf16[1,4,512,256]{3,2,1,0:T(8,128)(2,1)S(1)}, u32[]{:S(2)}, u32[]{:S(2)}) collective-permute-start(bf16[1,4,512,256]{3,2,1,0:T(8,128)(2,1)} %slice.58), channel_id=1, source_target_pairs={{0,1},{1,0},{2,3},{3,2},{4,5},{5,4},{6,7},{7,6},{8,9},{9,8},{10,11... | collective-permute-start | bytes 3145736 | tf_op jit(solution)/shard_map/ppermute | solution.py:761
  228.9 38.3 %collective-permute-start.31 = (bf16[1,4,512,256]{3,2,1,0:T(8,128)(2,1)}, bf16[1,4,512,256]{3,2,1,0:T(8,128)(2,1)}, u32[]{:S(2)}, u32[]{:S(2)}) collective-permute-start(bf16[1,4,512,256]{3,2,1,0:T(8,128)(2,1)} %slice.59), channel_id=1, source_target_pairs={{0,16},{1,17},{2,18},{3,19},{4,20},{5,21},{6,22},{7,23},{8,24},{9,... | collective-permute-start | bytes 3145736 | tf_op jit(solution)/shard_map/ppermute | solution.py:761
  241.5 30.1 %collective-permute-start.28 = (bf16[2,4,512,256]{3,2,1,0:T(8,128)(2,1)}, bf16[2,4,512,256]{3,2,1,0:T(8,128)(2,1)S(1)}, u32[]{:S(2)}, u32[]{:S(2)}) collective-permute-start(bf16[2,4,512,256]{3,2,1,0:T(8,128)(2,1)} %collective-permute-done.25.refs_5_.refs_9_), channel_id=1, source_target_pairs={{0,8},{1,9},{2,10},{3,11},{4,12},{5,13},{6,14},{7,15},{8,0},{9,1},... | collective-permute-start | bytes 6291464 | tf_op jit(solution)/shard_map/ppermute | solution.py:761
  241.6 57.4 %collective-permute-start.34 = (bf16[2,4,512,256]{3,2,1,0:T(8,128)(2,1)}, bf16[2,4,512,256]{3,2,1,0:T(8,128)(2,1)}, u32[]{:S(2)}, u32[]{:S(2)}) collective-permute-start(bf16[2,4,512,256]{3,2,1,0:T(8,128)(2,1)} %get-tuple-element.243.refs_17_), channel_id=1, source_target_pairs={{0,1},{1,0},{2,3},{3,2},{4,5},{5,4},{6,7},{7,6},{8,9},{9,8},{10,11... | collective-permute-start | bytes 6291464 | tf_op jit(solution)/shard_map/ppermute | solution.py:761
  242.2 56.9 %collective-permute-start.35 = (bf16[2,4,512,256]{3,2,1,0:T(8,128)(2,1)}, bf16[2,4,512,256]{3,2,1,0:T(8,128)(2,1)}, u32[]{:S(2)}, u32[]{:S(2)}) collective-permute-start(bf16[2,4,512,256]{3,2,1,0:T(8,128)(2,1)} %get-tuple-element.244.refs_18_), channel_id=1, source_target_pairs={{0,16},{1,17},{2,18},{3,19},{4,20},{5,21},{6,22},{7,23},{8,24},{9,... | collective-permute-start | bytes 6291464 | tf_op jit(solution)/shard_map/ppermute | solution.py:761
  267.2 3.4 collective-permute-start.32
  267.3 4.4 collective-permute-start.33
  270.6 37.2 %collective-permute-start.36 = (bf16[2,4,2,512,256]{4,3,2,1,0:T(8,128)(2,1)}, bf16[2,4,2,512,256]{4,3,2,1,0:T(8,128)(2,1)}, u32[]{:S(2)}, u32[]{:S(2)}) collective-permute-start(bf16[2,4,2,512,256]{4,3,2,1,0:T(8,128)(2,1)} %get-tuple-element.266), channel_id=1, source_target_pairs={{0,8},{1,9},{2,10},{3,11},{4,12},{5,13},{6,14},{7,15},{8,0},{9,1},... | collective-permute-start | bytes 12582920 | tf_op jit(solution)/shard_map/ppermute | solution.py:761
  299.1 8.8 %collective-permute-start.37 = (bf16[2,4,2,512,256]{4,3,2,1,0:T(8,128)(2,1)}, bf16[2,4,2,512,256]{4,3,2,1,0:T(8,128)(2,1)}, u32[]{:S(2)}, u32[]{:S(2)}) collective-permute-start(bf16[2,4,2,512,256]{4,3,2,1,0:T(8,128)(2,1)} %get-tuple-element.267), channel_id=1, source_target_pairs={{0,8},{1,9},{2,10},{3,11},{4,12},{5,13},{6,14},{7,15},{8,0},{9,1},... | collective-permute-start | bytes 12582920 | tf_op jit(solution)/shard_map/ppermute | solution.py:761
  305.2 65.1 %collective-permute-start.38 = (bf16[4,512,256]{2,1,0:T(8,128)(2,1)}, bf16[4,512,256]{2,1,0:T(8,128)(2,1)S(1)}, u32[]{:S(2)}, u32[]{:S(2)}) collective-permute-start(bf16[4,512,256]{2,1,0:T(8,128)(2,1)} %get-tuple-element.262.refs_13_), channel_id=1, source_target_pairs={{0,16},{1,17},{2,18},{3,19},{4,20},{5,21},{6,22},{7,23},{8,24},{9,... | collective-permute-start | bytes 3145736 | tf_op jit(solution)/shard_map/ppermute | solution.py:761
  306.2 64.1 %collective-permute-start.39 = (bf16[4,512,256]{2,1,0:T(8,128)(2,1)}, bf16[4,512,256]{2,1,0:T(8,128)(2,1)S(1)}, u32[]{:S(2)}, u32[]{:S(2)}) collective-permute-start(bf16[4,512,256]{2,1,0:T(8,128)(2,1)} %get-tuple-element.263.refs_14_), channel_id=1, source_target_pairs={{0,1},{1,0},{2,3},{3,2},{4,5},{5,4},{6,7},{7,6},{8,9},{9,8},{10,11... | collective-permute-start | bytes 3145736 | tf_op jit(solution)/shard_map/ppermute | solution.py:761
  318.6 71.4 %collective-permute-start.40 = (bf16[2,4,512,256]{3,2,1,0:T(8,128)(2,1)}, bf16[2,4,512,256]{3,2,1,0:T(8,128)(2,1)}, u32[]{:S(2)}, u32[]{:S(2)}) collective-permute-start(bf16[2,4,512,256]{3,2,1,0:T(8,128)(2,1)} %get-tuple-element.268.refs_15_), channel_id=1, source_target_pairs={{0,1},{1,0},{2,3},{3,2},{4,5},{5,4},{6,7},{7,6},{8,9},{9,8},{10,11... | collective-permute-start | bytes 6291464 | tf_op jit(solution)/shard_map/ppermute | solution.py:761
  319.2 70.8 %collective-permute-start.41 = (bf16[2,4,512,256]{3,2,1,0:T(8,128)(2,1)}, bf16[2,4,512,256]{3,2,1,0:T(8,128)(2,1)}, u32[]{:S(2)}, u32[]{:S(2)}) collective-permute-start(bf16[2,4,512,256]{3,2,1,0:T(8,128)(2,1)} %get-tuple-element.269.refs_16_), channel_id=1, source_target_pairs={{0,16},{1,17},{2,18},{3,19},{4,20},{5,21},{6,22},{7,23},{8,24},{9,... | collective-permute-start | bytes 6291464 | tf_op jit(solution)/shard_map/ppermute | solution.py:761
  376.7 62.0 %collective-permute-start.42 = (bf16[2,512,256]{2,1,0:T(8,128)(2,1)}, bf16[2,512,256]{2,1,0:T(8,128)(2,1)S(1)}, u32[]{:S(2)}, u32[]{:S(2)}) collective-permute-start(bf16[2,512,256]{2,1,0:T(8,128)(2,1)} %get-tuple-element.287.refs_10_), channel_id=1, source_target_pairs={{0,2},{1,3},{2,0},{3,1},{4,6},{5,7},{6,4},{7,5},{8,10},{9,11},{10,... | collective-permute-start | bytes 1572872 | tf_op jit(solution)/shard_map/ppermute | solution.py:761
  386.7 52.0 %collective-permute-start.43 = (bf16[2,512,256]{2,1,0:T(8,128)(2,1)}, bf16[2,512,256]{2,1,0:T(8,128)(2,1)S(1)}, u32[]{:S(2)}, u32[]{:S(2)}) collective-permute-start(bf16[2,512,256]{2,1,0:T(8,128)(2,1)} %get-tuple-element.288.refs_11_), channel_id=1, source_target_pairs={{0,4},{1,5},{2,6},{3,7},{4,0},{5,1},{6,2},{7,3},{8,12},{9,13},{10,... | collective-permute-start | bytes 1572872 | tf_op jit(solution)/shard_map/ppermute | solution.py:761
  388.5 50.2 %collective-permute-start.44 = (bf16[2,512,256]{2,1,0:T(8,128)(2,1)}, bf16[2,512,256]{2,1,0:T(8,128)(2,1)S(1)}, u32[]{:S(2)}, u32[]{:S(2)}) collective-permute-start(bf16[2,512,256]{2,1,0:T(8,128)(2,1)} %get-tuple-element.289.refs_12_), channel_id=1, source_target_pairs={{0,6},{1,7},{2,4},{3,5},{4,2},{5,3},{6,0},{7,1},{8,14},{9,15},{10,... | collective-permute-start | bytes 1572872 | tf_op jit(solution)/shard_map/ppermute | solution.py:761
  395.7 43.0 %collective-permute-start.45 = (bf16[4,512,256]{2,1,0:T(8,128)(2,1)}, bf16[4,512,256]{2,1,0:T(8,128)(2,1)S(1)}, u32[]{:S(2)}, u32[]{:S(2)}) collective-permute-start(bf16[4,512,256]{2,1,0:T(8,128)(2,1)} %get-tuple-element.292.refs_13_), channel_id=1, source_target_pairs={{0,16},{1,17},{2,18},{3,19},{4,20},{5,21},{6,22},{7,23},{8,24},{9,... | collective-permute-start | bytes 3145736 | tf_op jit(solution)/shard_map/ppermute | solution.py:761
  397.0 41.8 %collective-permute-start.46 = (bf16[4,512,256]{2,1,0:T(8,128)(2,1)}, bf16[4,512,256]{2,1,0:T(8,128)(2,1)S(1)}, u32[]{:S(2)}, u32[]{:S(2)}) collective-permute-start(bf16[4,512,256]{2,1,0:T(8,128)(2,1)} %get-tuple-element.293.refs_14_), channel_id=1, source_target_pairs={{0,1},{1,0},{2,3},{3,2},{4,5},{5,4},{6,7},{7,6},{8,9},{9,8},{10,11... | collective-permute-start | bytes 3145736 | tf_op jit(solution)/shard_map/ppermute | solution.py:761
  443.7 3.0 collective-permute-start.47
  450.4 8.9 %collective-permute-start.48 = (bf16[4,16,2176]{2,1,0:T(8,128)(2,1)}, bf16[4,16,2176]{2,1,0:T(8,128)(2,1)S(1)}, u32[]{:S(2)}, u32[]{:S(2)}) collective-permute-start(bf16[4,16,2176]{2,1,0:T(8,128)(2,1)} %get-tuple-element.314), channel_id=1, source_target_pairs={{0,1},{1,0},{2,3},{3,2},{4,5},{5,4},{6,7},{7,6},{8,9},{9,8},{10,11... | collective-permute-start | bytes 835592 | tf_op jit(solution)/shard_map/ppermute | solution.py:761
  451.7 57.2 %collective-permute-start.54 = (bf16[2,512,256]{2,1,0:T(8,128)(2,1)}, bf16[2,512,256]{2,1,0:T(8,128)(2,1)S(1)}, u32[]{:S(2)}, u32[]{:S(2)}) collective-permute-start(bf16[2,512,256]{2,1,0:T(8,128)(2,1)} %get-tuple-element.326), channel_id=1, source_target_pairs={{0,2},{1,3},{2,0},{3,1},{4,6},{5,7},{6,4},{7,5},{8,10},{9,11},{10,... | collective-permute-start | bytes 1572872 | tf_op jit(solution)/shard_map/ppermute | solution.py:761
  452.6 56.4 %collective-permute-start.55 = (bf16[2,512,256]{2,1,0:T(8,128)(2,1)}, bf16[2,512,256]{2,1,0:T(8,128)(2,1)S(1)}, u32[]{:S(2)}, u32[]{:S(2)}) collective-permute-start(bf16[2,512,256]{2,1,0:T(8,128)(2,1)} %get-tuple-element.327), channel_id=1, source_target_pairs={{0,4},{1,5},{2,6},{3,7},{4,0},{5,1},{6,2},{7,3},{8,12},{9,13},{10,... | collective-permute-start | bytes 1572872 | tf_op jit(solution)/shard_map/ppermute | solution.py:761
  454.6 54.4 %collective-permute-start.56 = (bf16[2,512,256]{2,1,0:T(8,128)(2,1)S(1)}, bf16[2,512,256]{2,1,0:T(8,128)(2,1)S(1)}, u32[]{:S(2)}, u32[]{:S(2)}) collective-permute-start(bf16[2,512,256]{2,1,0:T(8,128)(2,1)S(1)} %copy-done.53), channel_id=1, source_target_pairs={{0,6},{1,7},{2,4},{3,5},{4,2},{5,3},{6,0},{7,1},{8,14},{9,15},{10,... | collective-permute-start | bytes 1572872 | tf_op jit(solution)/shard_map/ppermute | solution.py:761
  456.1 10.4 %collective-permute-start.49 = (bf16[4,16,2176]{2,1,0:T(8,128)(2,1)}, bf16[4,16,2176]{2,1,0:T(8,128)(2,1)S(1)}, u32[]{:S(2)}, u32[]{:S(2)}) collective-permute-start(bf16[4,16,2176]{2,1,0:T(8,128)(2,1)} %get-tuple-element.315), channel_id=1, source_target_pairs={{0,16},{1,17},{2,18},{3,19},{4,20},{5,21},{6,22},{7,23},{8,24},{9,... | collective-permute-start | bytes 835592 | tf_op jit(solution)/shard_map/ppermute | solution.py:761
  459.3 10.9 %collective-permute-start.50 = (bf16[4,16,2176]{2,1,0:T(8,128)(2,1)}, bf16[4,16,2176]{2,1,0:T(8,128)(2,1)S(1)}, u32[]{:S(2)}, u32[]{:S(2)}) collective-permute-start(bf16[4,16,2176]{2,1,0:T(8,128)(2,1)} %get-tuple-element.316), channel_id=1, source_target_pairs={{0,17},{1,16},{2,19},{3,18},{4,21},{5,20},{6,23},{7,22},{8,25},{9,... | collective-permute-start | bytes 835592 | tf_op jit(solution)/shard_map/ppermute | solution.py:761
  461.6 33.2 %copy-start.47 = (f32[16,5]{0,1:T(8,128)S(1)}, f32[16,5]{0,1:T(8,128)}, u32[]{:S(2)}) copy-start(f32[16,5]{0,1:T(8,128)} %param.45) | copy-start | bytes 964
  472.9 15.9 %collective-permute-start.51 = (bf16[1,16,2176]{2,1,0:T(8,128)(2,1)}, bf16[1,16,2176]{2,1,0:T(8,128)(2,1)S(1)}, u32[]{:S(2)}, u32[]{:S(2)}) collective-permute-start(bf16[1,16,2176]{2,1,0:T(8,128)(2,1)} %get-tuple-element.318), channel_id=1, source_target_pairs={{0,2},{1,3},{2,0},{3,1},{4,6},{5,7},{6,4},{7,5},{8,10},{9,11},{10,... | collective-permute-start | bytes 208904 | tf_op jit(solution)/shard_map/ppermute | solution.py:761
  472.9 33.1 %collective-permute-start.52 = (bf16[1,16,2176]{2,1,0:T(8,128)(2,1)}, bf16[1,16,2176]{2,1,0:T(8,128)(2,1)S(1)}, u32[]{:S(2)}, u32[]{:S(2)}) collective-permute-start(bf16[1,16,2176]{2,1,0:T(8,128)(2,1)} %get-tuple-element.319), channel_id=1, source_target_pairs={{0,4},{1,5},{2,6},{3,7},{4,0},{5,1},{6,2},{7,3},{8,12},{9,13},{10,... | collective-permute-start | bytes 208904 | tf_op jit(solution)/shard_map/ppermute | solution.py:761
  488.9 17.2 %collective-permute-start.53 = (bf16[1,16,2176]{2,1,0:T(8,128)(2,1)}, bf16[1,16,2176]{2,1,0:T(8,128)(2,1)S(1)}, u32[]{:S(2)}, u32[]{:S(2)}) collective-permute-start(bf16[1,16,2176]{2,1,0:T(8,128)(2,1)} %get-tuple-element.320), channel_id=1, source_target_pairs={{0,6},{1,7},{2,4},{3,5},{4,2},{5,3},{6,0},{7,1},{8,14},{9,15},{10,... | collective-permute-start | bytes 208904 | tf_op jit(solution)/shard_map/ppermute | solution.py:761
  515.1 1.4 collective-permute-start.57
  517.2 3.6 collective-permute-start.58
  520.8 3.6 collective-permute-start.59
  524.4 3.6 collective-permute-start.60
  528.0 5.1 collective-permute-start.61
  (59 other events, 521.3 us)
